TPU v7x, 32 devices: a whole 2x2x4 slice. The times are simulated.
32 devices in a mesh: grp: 2 (over x), tile: 8 (over z, y), wave: 2 (over core).
Axes of the slice: x: 2, y: 2, z: 4, core: 2. Of those that a mesh axis runs over, the one named last changes fastest.
Arguments:
- residual: float32 [16, 8, 2, 8, 128], P(('grp', 'tile'), 'wave'), parts along dimension 0, may hold values from -210 to 210
- kernel: bfloat16 [16, 8, 9, 2, 128, 128], P(('grp', 'tile'), 'wave'), parts along dimension 0, may hold values from -0.125 to 0.125
- offsets: float32 [16, 8, 2, 128], P(('grp', 'tile'), 'wave'), parts along dimension 0, may hold values from 0 to 1
- neighbor: int32 [16, 8, 9], P(('grp', 'tile'), 'wave'), parts along dimension 0, may hold values from 0 to 8, each once within a row
- frequency: int32 [16], P('grp'), parts along dimension 0, may hold values from 0 to 7, each once
- lattice_x: int32 [128], replicated, may hold values from 0 to 127, each once
- lattice_y: int32 [128], replicated, may hold values from 0 to 127, each once
- spectral_weight: float32 [8, 128, 128], replicated, may hold values from 0.1 to 3
Outputs:
- image_two: float32 [16, 8, 2, 8, 128], P(('grp', 'tile'), 'wave'), parts along dimension 0
- arnoldi: float32 [8, 8], P('grp'), parts along dimension 0
There are 2 independent parts, one for each index of `grp`. A program takes and returns all parts, laid end to end along the dimension named above; an argument that names none is the same for every part. Nothing has to cross between parts.
Inputs may be any that keep to these rules, and one draw needn't show every extreme that they name: `neighbor`: each row names each of the nine neighbour slots once. `frequency`: each index appears once. `lattice_x`: each index appears once. `lattice_y`: each index appears once.
All inputs are finite; a program needn't handle non-finite values.
Results may differ from a plain program's by a relative error of at most 0.013.
Values may be sent and summed in bfloat16 or wider, within the bound.
No kernel may reach another device: no remote copies, remote signals or barrier semaphores. Data moves between devices by JAX's collectives and lax.ppermute only.
A program may use at most 64 MiB of HBM per device.

v0:
```python
import math

import jax
import jax.numpy as jnp
from jax import lax
from jax.sharding import PartitionSpec as P

two_pi = 2.0 * math.pi
eps_norm = 1e-06


def padded_2(array, sides, width):
    for axis, dim in sides:
        size, length = (lax.axis_size(axis), array.shape[dim])
        up = [(i, (i + 1) % size) for i in range(size)]
        down = [(j, i) for i, j in up]
        last = lax.slice_in_dim(array, length - width, length, axis=dim)
        initial = lax.slice_in_dim(array, 0, width, axis=dim)
        before = lax.ppermute(last, axis, up)
        after = lax.ppermute(initial, axis, down)
        array = jnp.concatenate([before, array, after], axis=dim)
    return array


def phase_table(position, harmonic):
    phase_angle = two_pi * (position[:, None] * harmonic[None, :])
    return (jnp.cos(phase_angle).astype(jnp.bfloat16), jnp.sin(phase_angle).astype(jnp.bfloat16))


def project_rows(cosine_cols, sine_cols, twisted):
    row_count = cosine_cols.shape[1]
    stacked = jnp.concatenate([cosine_cols, sine_cols], 1)
    gram_matrix = lax.dot_general(
        stacked, twisted, (((0,), (0,)), ((), ())), preferred_element_type=jnp.float32
    )
    gram_matrix = gram_matrix.reshape(2, row_count, 2, -1)
    coef_real = gram_matrix[0, :, 0] + gram_matrix[1, :, 1]
    coef_imag = gram_matrix[0, :, 1] - gram_matrix[1, :, 0]
    return jnp.stack([coef_real, coef_imag], 1)


def expand_rows(cosine_cols, sine_cols, scaled):
    row_count = scaled.shape[0]
    upper_rows = scaled.reshape(row_count, -1)
    lower_rows = jnp.stack([-scaled[:, 1], scaled[:, 0]], 1).reshape(row_count, -1)
    matrix = jnp.concatenate([upper_rows, lower_rows], 0)
    stacked = jnp.concatenate([cosine_cols, sine_cols], 1)
    return jnp.dot(stacked, matrix, preferred_element_type=jnp.float32)


def twist_density(panel_density, cosine_y, sine_y):
    density_real = panel_density[:, 0, :, None].astype(jnp.float32)
    density_imag = panel_density[:, 1, :, None].astype(jnp.float32)
    wave_cos = cosine_y.astype(jnp.float32)[:, None, :]
    wave_sin = sine_y.astype(jnp.float32)[:, None, :]
    part_real = wave_cos * density_real + wave_sin * density_imag
    part_imag = wave_cos * density_imag - wave_sin * density_real
    return (
        jnp.stack([part_real, part_imag], 1)
        .reshape(panel_density.shape[0], -1)
        .astype(jnp.bfloat16)
    )


def finish(summed, cosine_y, sine_y, vectors):
    shaped = summed.reshape(summed.shape[0], 2, vectors, -1)
    wave_cos = cosine_y.astype(jnp.float32)[:, None, :]
    wave_sin = sine_y.astype(jnp.float32)[:, None, :]
    far_real = jnp.sum(shaped[:, 0] * wave_cos - shaped[:, 1] * wave_sin, -1)
    far_imag = jnp.sum(shaped[:, 0] * wave_sin + shaped[:, 1] * wave_cos, -1)
    return jnp.stack([far_real, far_imag], 1)


def combine_near(product, vectors):
    first_half = product[:, 0]
    second = product[:, 1]
    near_real = first_half[:, :vectors] - second[:, vectors:]
    near_imag = second[:, :vectors] + first_half[:, vectors:]
    return jnp.stack([near_real, near_imag], 1)


def panel_sum(values):
    return jnp.sum(values, axis=(0, 1, 3))


def per_device(
    residual, kernel, offsets, neighbor, frequency, lattice_x, lattice_y, spectral_weight
):
    strips = residual.shape[0]
    tiles_y = residual.shape[1]
    vectors = residual.shape[3]
    panels_t = residual.shape[4]
    modes_x = spectral_weight.shape[1]
    modes_y = spectral_weight.shape[2]
    count_x = lax.axis_size("tile") * strips
    count_y = lax.axis_size("wave") * tiles_y
    devices = lax.axis_size("tile") * lax.axis_size("wave")
    panels = count_x * count_y * panels_t
    local_rows = strips * tiles_y * panels_t
    column = (lax.axis_index("tile") * strips + jnp.arange(strips)).astype(jnp.float32)
    row_index = (lax.axis_index("wave") * tiles_y + jnp.arange(tiles_y)).astype(jnp.float32)
    position_x = ((column[:, None, None] + offsets[:, :, 0, :]) / count_x).reshape(-1)
    position_y = ((row_index[None, :, None] + offsets[:, :, 1, :]) / count_y).reshape(-1)
    harmonic_x = (lattice_x - modes_x // 2).astype(jnp.float32)
    harmonic_y = (lattice_y - modes_y // 2).astype(jnp.float32)
    cosine_x, sine_x = phase_table(position_x, harmonic_x)
    cosine_y, sine_y = phase_table(position_y, harmonic_y)
    weight_rows = jnp.take(spectral_weight, frequency, axis=0)
    factor = weight_rows * (1.0 / math.sqrt(modes_x * modes_y * panels))
    factor_wide = jnp.transpose(factor, (1, 0, 2)).reshape(modes_x, vectors * modes_y)[:, None, :]

    def near_field(density):
        padded = padded_2(density, (("tile", 0), ("wave", 1)), 1)
        candidates = []
        for slot_index in range(9):
            shift_x = slot_index // 3 - 1
            shift_y = slot_index % 3 - 1
            candidates.append(
                padded[1 + shift_x : 1 + shift_x + strips, 1 + shift_y : 1 + shift_y + tiles_y]
            )
        stacked = jnp.stack(candidates, 2).reshape(strips * tiles_y, 9, -1)
        picked = jnp.take_along_axis(stacked, neighbor.reshape(strips * tiles_y, 9, 1), axis=1)
        picked = picked.reshape(strips * tiles_y, 9, 2 * vectors, panels_t)
        blocks = kernel.reshape(strips * tiles_y, 9, 2, panels_t, panels_t)
        product = jnp.einsum("tjmp,tjcpq->tcmq", picked, blocks, preferred_element_type=jnp.float32)
        return combine_near(product, vectors).reshape(strips, tiles_y, 2, vectors, panels_t)

    def far_field(density):
        panel_density = jnp.transpose(density, (0, 1, 4, 2, 3)).reshape(local_rows, 2, vectors)
        twisted = twist_density(panel_density, cosine_y, sine_y)
        partial_coeffs = project_rows(cosine_x, sine_x, twisted)
        share_rows = modes_x // devices
        shares = lax.psum_scatter(partial_coeffs, ("tile", "wave"), scatter_dimension=0, tiled=True)
        owner_index = lax.axis_index("tile") * lax.axis_size("wave") + lax.axis_index("wave")
        owner_factor = lax.dynamic_slice_in_dim(
            factor_wide, owner_index * share_rows, share_rows, 0
        )
        owner_scaled = (shares * owner_factor).astype(jnp.bfloat16)
        scaled = lax.all_gather(owner_scaled, ("tile", "wave"), axis=0, tiled=True)
        summed = expand_rows(cosine_x, sine_x, scaled)
        far_panel = finish(summed, cosine_y, sine_y, vectors)
        return far_panel.reshape(strips, tiles_y, panels_t, 2, vectors).transpose(0, 1, 3, 4, 2)

    def apply_operator(density):
        return 0.5 * density.astype(jnp.float32) + near_field(density) + far_field(density)

    local_sq = panel_sum(
        residual[:, :, 0] * residual[:, :, 0] + residual[:, :, 1] * residual[:, :, 1]
    )
    squares = lax.psum(local_sq, ("tile", "wave"))
    basis_scale = jnp.sqrt(squares / panels + eps_norm)
    basis_one = (residual / basis_scale[None, None, None, :, None]).astype(jnp.bfloat16)
    image_one = apply_operator(basis_one)
    basis_real = basis_one[:, :, 0].astype(jnp.float32)
    basis_imag = basis_one[:, :, 1].astype(jnp.float32)
    image_real = image_one[:, :, 0]
    image_imag = image_one[:, :, 1]
    inner_real, inner_imag = lax.psum(
        (
            panel_sum(basis_real * image_real + basis_imag * image_imag),
            panel_sum(basis_real * image_imag - basis_imag * image_real),
        ),
        ("tile", "wave"),
    )
    coef_real = inner_real / panels
    coef_imag = inner_imag / panels
    wide_real = coef_real[None, None, :, None]
    wide_imag = coef_imag[None, None, :, None]
    update_real = image_real - (wide_real * basis_real - wide_imag * basis_imag)
    update_imag = image_imag - (wide_real * basis_imag + wide_imag * basis_real)
    update_sq = lax.psum(
        panel_sum(update_real * update_real + update_imag * update_imag), ("tile", "wave")
    )
    update_scale = jnp.sqrt(update_sq / panels + eps_norm)
    next_basis = (
        jnp.stack([update_real, update_imag], 2) / update_scale[None, None, None, :, None]
    ).astype(jnp.bfloat16)
    image_two = apply_operator(next_basis)
    arnoldi = jnp.stack([basis_scale, coef_real, coef_imag, update_scale])
    return (image_two, arnoldi)


def solution(mesh):
    return jax.shard_map(
        per_device,
        mesh=mesh,
        in_specs=(
            P(("grp", "tile"), "wave", None, None, None),
            P(("grp", "tile"), "wave", None, None, None, None),
            P(("grp", "tile"), "wave", None, None),
            P(("grp", "tile"), "wave", None),
            P("grp"),
            P(),
            P(),
            P(),
        ),
        out_specs=(P(("grp", "tile"), "wave", None, None, None), P("grp", None)),
        check_vma=False,
    )
```

profile of v0, /device:TPU:0, one launch (start us, length us, event | category | flops | bytes accessed | tf_op | source)
XLA Modules:
  0.0 307.0 jit_solution(9363511399105179548)
XLA Ops:
  8.2 34.9 %psum.28 = f32[8]{0:T(128)S(1)} all-reduce(f32[8]{0:T(128)S(1)} %add_reduce_fusion.2), channel_id=1, replica_groups=mesh['grp'=2,'tile'=8,'wave'=2] {'tile','wave'}, use_global_device_ids=true, to_apply=%region_1.2 | all-reduce | flops 8 | bytes 64 | tf_op jit(solution)/shard_map/psum | solution.py:150
  43.7 1.4 fusion.22
  45.2 4.7 %collective-permute-start.1 = (bf16[1,4,2,8,128]{4,3,1,2,0:T(8,128)(2,1)}, bf16[1,4,2,8,128]{4,3,1,2,0:T(8,128)(2,1)}, u32[]{:S(2)}, u32[]{:S(2)}) collective-permute-start(bf16[1,4,2,8,128]{4,3,1,2,0:T(8,128)(2,1)} %fusion.22), channel_id=1, source_target_pairs={{2,0},{4,2},{6,4},{8,6},{10,8},{12,10},{14,12},{0,14},{3,1},{5,3},... | collective-permute-start | bytes 49160 | tf_op jit(solution)/shard_map/ppermute | solution.py:20
  54.7 1.1 cosine_convert_fusion.1
  56.9 1.1 pad_maximum_fusion.2
  58.7 1.6 gather_fusion
  61.7 1.2 copy.121
  63.0 1.3 pad_maximum_fusion.31
  67.8 1.2 copy.122
  73.7 1.5 gather_fusion.1
  76.5 36.3 %reduce-scatter.3.cloned.1.call-done = f32[8,2,1024]{2,0,1:T(8,128)} async-done(((f32[128,2,1024]{2,0,1:T(8,128)}), f32[8,2,1024]{2,0,1:T(8,128)}) %reduce-scatter.3.cloned.1.call-update) | async-done | bytes 65552 | tf_op jit(solution)/shard_map/reduce_scatter | solution.py:133
  113.7 20.8 %all_gather.6 = bf16[128,2,1024]{2,0,1:T(8,128)(2,1)S(1)} all-gather(bf16[8,2,1024]{2,0,1:T(8,128)(2,1)S(1)} %multiply_convert_fusion.1), channel_id=1, replica_groups=mesh['grp'=2,'tile'=8,'wave'=2] {'tile','wave'}, dimensions={0}, use_global_device_ids=true | all-gather | bytes 557056 | tf_op jit(solution)/shard_map/all_gather | solution.py:139
  136.3 1.1 pad_maximum_fusion.4
  138.4 2.0 convolution_bitcast_fusion.1
  141.4 1.2 subtract_reduce_fusion.1
  145.2 29.8 %all-reduce = (f32[8]{0:T(128)S(1)}, f32[8]{0:T(128)S(1)}) all-reduce(f32[8]{0:T(128)S(1)} %get-tuple-element.16, f32[8]{0:T(128)S(1)} %get-tuple-element.15), channel_id=1, replica_groups=mesh['grp'=2,'tile'=8,'wave'=2] {'tile','wave'}, use_global_device_ids=true, to_apply=%region_8.10 | all-reduce | flops 16 | bytes 128 | tf_op jit(solution)/shard_map/psum | solution.py:158
  176.7 29.5 %psum.31 = f32[8]{0:T(128)S(1)} all-reduce(f32[8]{0:T(128)S(1)} %fusion.40), channel_id=1, replica_groups=mesh['grp'=2,'tile'=8,'wave'=2] {'tile','wave'}, use_global_device_ids=true, to_apply=%region_10.12 | all-reduce | flops 8 | bytes 64 | tf_op jit(solution)/shard_map/psum | solution.py:171
  206.4 4.7 %collective-permute-start.5 = (bf16[1,4,2,8,128]{4,3,1,2,0:T(8,128)(2,1)S(1)}, bf16[1,4,2,8,128]{4,3,1,2,0:T(8,128)(2,1)S(1)}, u32[]{:S(2)}, u32[]{:S(2)}) collective-permute-start(bf16[1,4,2,8,128]{4,3,1,2,0:T(8,128)(2,1)S(1)} %fusion.20), channel_id=1, source_target_pairs={{2,0},{4,2},{6,4},{8,6},{10,8},{12,10},{14,12},{0,14},{3,1},{5,3},... | collective-permute-start | bytes 49160 | tf_op jit(solution)/shard_map/ppermute | solution.py:20
  213.7 1.1 pad_maximum_fusion.3
  217.2 1.5 gather_fusion.2
  219.4 50.2 %reduce-scatter.5.cloned.1.call-done = f32[8,2,1024]{2,0,1:T(8,128)} async-done(((f32[128,2,1024]{2,0,1:T(8,128)}), f32[8,2,1024]{2,0,1:T(8,128)}) %reduce-scatter.5.cloned.1.call-update) | async-done | bytes 65552 | tf_op jit(solution)/shard_map/reduce_scatter | solution.py:133
  270.5 20.8 %all_gather.7 = bf16[128,2,1024]{2,0,1:T(8,128)(2,1)S(1)} all-gather(bf16[8,2,1024]{2,0,1:T(8,128)(2,1)S(1)} %multiply_convert_fusion), channel_id=1, replica_groups=mesh['grp'=2,'tile'=8,'wave'=2] {'tile','wave'}, dimensions={0}, use_global_device_ids=true | all-gather | bytes 557056 | tf_op jit(solution)/shard_map/all_gather | solution.py:139
  295.1 2.0 convolution_bitcast_fusion
  298.1 1.2 subtract_reduce_fusion
  (197 shorter events, 39.9 us)
Async XLA Ops:
  7.2 68.3 %copy-start = (bf16[1,4,9,2,128,128]{5,4,3,2,1,0:T(8,128)(2,1)S(1)}, bf16[1,4,9,2,128,128]{5,4,3,2,1,0:T(8,128)(2,1)}, u32[]{:S(2)}) copy-start(bf16[1,4,9,2,128,128]{5,4,3,2,1,0:T(8,128)(2,1)} %param.11) | copy-start | bytes 7077892
  7.2 105.6 %reduce-scatter.3.cloned.1.call-start = ((), (), s32[]{:S(2)}) async-start(), calls=%async_computation.2 | async-start | bytes 1114112 | tf_op jit(solution)/shard_map/reduce_scatter | solution.py:133
  43.7 7.0 %copy-start.19 = (f32[8]{0:T(128)}, f32[8]{0:T(128)S(1)}, u32[]{:S(2)}) copy-start(f32[8]{0:T(128)S(1)} %get-tuple-element.68) | copy-start | bytes 100
  45.2 17.8 %collective-permute-start = (bf16[1,4,2,8,128]{4,3,1,2,0:T(8,128)(2,1)}, bf16[1,4,2,8,128]{4,3,1,2,0:T(8,128)(2,1)}, u32[]{:S(2)}, u32[]{:S(2)}) collective-permute-start(bf16[1,4,2,8,128]{4,3,1,2,0:T(8,128)(2,1)} %fusion.22), channel_id=1, source_target_pairs={{0,2},{2,4},{4,6},{6,8},{8,10},{10,12},{12,14},{14,0},{1,3},{3,5},... | collective-permute-start | bytes 49160 | tf_op jit(solution)/shard_map/ppermute | solution.py:19
  45.2 17.8 %collective-permute-start.1 = (bf16[1,4,2,8,128]{4,3,1,2,0:T(8,128)(2,1)}, bf16[1,4,2,8,128]{4,3,1,2,0:T(8,128)(2,1)}, u32[]{:S(2)}, u32[]{:S(2)}) collective-permute-start(bf16[1,4,2,8,128]{4,3,1,2,0:T(8,128)(2,1)} %fusion.22), channel_id=1, source_target_pairs={{2,0},{4,2},{6,4},{8,6},{10,8},{12,10},{14,12},{0,14},{3,1},{5,3},... | collective-permute-start | bytes 49160 | tf_op jit(solution)/shard_map/ppermute | solution.py:20
  53.9 12.3 %copy-start.1 = (f32[512,128]{0,1:T(8,128)}, f32[512,128]{0,1:T(8,128)S(1)}, u32[]{:S(2)}) copy-start(f32[512,128]{0,1:T(8,128)S(1)} %get-tuple-element.64) | copy-start | bytes 786436
  58.0 211.7 %reduce-scatter.5.cloned.1.call-start = ((), (), s32[]{:S(2)}) async-start(), calls=%async_computation.3 | async-start | bytes 1114112 | tf_op jit(solution)/shard_map/reduce_scatter | solution.py:133
  64.3 7.5 %collective-permute-start.2 = (bf16[3,1,2,8,128]{4,3,1,2,0:T(8,128)(2,1)}, bf16[3,1,2,8,128]{4,3,1,2,0:T(8,128)(2,1)}, u32[]{:S(2)}, u32[]{:S(2)}) collective-permute-start(bf16[3,1,2,8,128]{4,3,1,2,0:T(8,128)(2,1)} %get-tuple-element.56), channel_id=1, source_target_pairs={{0,1},{1,0},{2,3},{3,2},{4,5},{5,4},{6,7},{7,6},{8,9},{9,8},{10,11... | collective-permute-start | bytes 36872 | tf_op jit(solution)/shard_map/ppermute | solution.py:19
  67.7 7.5 %copy-start.21 = (pred[4,9]{1,0:T(4,128)(4,1)S(1)}, pred[4,9]{1,0:T(4,128)(4,1)}, u32[]{:S(2)}) copy-start(pred[4,9]{1,0:T(4,128)(4,1)} %and_bitcast_fusion) | copy-start | bytes 112
  69.0 43.9 %copy-start.16 = (f32[8,1,1024]{2,0,1:T(8,128)}, f32[8,1,1024]{2,0,1:T(8,128)S(1)}, u32[]{:S(2)}) copy-start(f32[8,1,1024]{2,0,1:T(8,128)S(1)} %copy.122) | copy-start | bytes 98308
  70.5 2.1 collective-permute-start.3
  134.4 4.0 %copy-start.10 = (bf16[512,128]{0,1:T(8,128)(2,1)S(1)}, bf16[512,128]{0,1:T(8,128)(2,1)}, u32[]{:S(2)}) copy-start(bf16[512,128]{0,1:T(8,128)(2,1)} %copy-done.9) | copy-start | bytes 393220
  141.4 2.0 copy-start.20
  141.4 69.8 %copy-start.2 = (f32[512,128]{0,1:T(8,128)S(1)}, f32[512,128]{0,1:T(8,128)}, u32[]{:S(2)}) copy-start(f32[512,128]{0,1:T(8,128)} %copy-done.1) | copy-start | bytes 786436
  176.7 38.0 %copy-start.12 = (f32[1,4,1,8,128]{4,3,1,2,0:T(8,128)}, f32[1,4,1,8,128]{4,3,1,2,0:T(8,128)S(1)}, u32[]{:S(2)}) copy-start(f32[1,4,1,8,128]{4,3,1,2,0:T(8,128)S(1)} %get-tuple-element.51) | copy-start | bytes 49156
  176.7 38.0 %copy-start.14 = (f32[1,4,1,8,128]{4,3,1,2,0:T(8,128)}, f32[1,4,1,8,128]{4,3,1,2,0:T(8,128)S(1)}, u32[]{:S(2)}) copy-start(f32[1,4,1,8,128]{4,3,1,2,0:T(8,128)S(1)} %get-tuple-element.52) | copy-start | bytes 49156
  206.4 8.4 %collective-permute-start.4 = (bf16[1,4,2,8,128]{4,3,1,2,0:T(8,128)(2,1)S(1)}, bf16[1,4,2,8,128]{4,3,1,2,0:T(8,128)(2,1)S(1)}, u32[]{:S(2)}, u32[]{:S(2)}) collective-permute-start(bf16[1,4,2,8,128]{4,3,1,2,0:T(8,128)(2,1)S(1)} %fusion.20), channel_id=1, source_target_pairs={{0,2},{2,4},{4,6},{6,8},{8,10},{10,12},{12,14},{14,0},{1,3},{3,5},... | collective-permute-start | bytes 49160 | tf_op jit(solution)/shard_map/ppermute | solution.py:19
  206.4 8.4 %collective-permute-start.5 = (bf16[1,4,2,8,128]{4,3,1,2,0:T(8,128)(2,1)S(1)}, bf16[1,4,2,8,128]{4,3,1,2,0:T(8,128)(2,1)S(1)}, u32[]{:S(2)}, u32[]{:S(2)}) collective-permute-start(bf16[1,4,2,8,128]{4,3,1,2,0:T(8,128)(2,1)S(1)} %fusion.20), channel_id=1, source_target_pairs={{2,0},{4,2},{6,4},{8,6},{10,8},{12,10},{14,12},{0,14},{3,1},{5,3},... | collective-permute-start | bytes 49160 | tf_op jit(solution)/shard_map/ppermute | solution.py:20
  214.8 4.0 %copy-start.22 = (pred[4,9]{1,0:T(4,128)(4,1)S(1)}, pred[4,9]{1,0:T(4,128)(4,1)}, u32[]{:S(2)}) copy-start(pred[4,9]{1,0:T(4,128)(4,1)} %and_bitcast_fusion) | copy-start | bytes 112
  214.8 1.2 collective-permute-start.7
  215.5 1.3 collective-permute-start.6
  218.7 51.0 %copy-start.17 = (f32[8,1,1024]{2,0,1:T(8,128)S(1)}, f32[8,1,1024]{2,0,1:T(8,128)}, u32[]{:S(2)}) copy-start(f32[8,1,1024]{2,0,1:T(8,128)} %copy-done.16) | copy-start | bytes 98308
  291.3 3.8 %copy-start.11 = (bf16[512,128]{0,1:T(8,128)(2,1)S(1)}, bf16[512,128]{0,1:T(8,128)(2,1)}, u32[]{:S(2)}) copy-start(bf16[512,128]{0,1:T(8,128)(2,1)} %copy-done.9) | copy-start | bytes 393220
  298.0 1.4 copy-start.15
  (11 other events, 11.5 us)
Sparse Core Ops, SparseCore 0:
  58.1 54.6 reduce-scatter.2
  214.9 54.7 reduce-scatter.4
where the time goes:
time: 308 us; the launch traced here: 307 us
  blocking collectives  136 us (44%)
  waiting for transfers between devices  87.3 us (28%)
  other arithmetic  30 us (10%)
  local copies, waits for them, and re-layouts  22.2 us (7%)
  between operations  14.9 us (5%)
  starting transfers between devices  10.7 us (3%)
  matrix products  6.26 us (2%)
    reduce_scatter x2, waiting for transfers between devices, far_field(): lax.psum_scatter(partial_coeffs, ('tile', 'wave'), scatter_dimension=0, t...  86.5 us
    all_gather x2, blocking collectives, far_field(): scaled = lax.all_gather(owner_scaled, ('tile', 'wave'), axis=0, tiled=True)  41.5 us
    psum x1, blocking collectives, per_device(): squares = lax.psum(local_sq, ('tile', 'wave'))  34.9 us
    psum x1, blocking collectives, per_device(): lax.psum((panel_sum(basis_real * image_real + basis_imag * image_imag), p...  29.8 us
    psum x1, blocking collectives, per_device(): lax.psum(panel_sum(update_real * update_real + update_imag * update_imag)...  29.5 us
    ppermute x4, starting transfers between devices, padded_2(): after = lax.ppermute(initial, axis, down)  10.1 us
  transfers between devices with their start and end apart: 10, of which 3 were waited for; matrix products, arithmetic and copies ran while one was open for 10% of the time, Pallas kernels for 0%

commit v1 on v0

v1 whole, which is shorter than its diff:
```python
import math

import jax
import jax.numpy as jnp
from jax import lax
from jax.experimental import pallas as pl
from jax.experimental.pallas import tpu as pltpu
from jax.sharding import PartitionSpec as P

eps_norm = 1e-06
f32 = jnp.float32
bf16 = jnp.bfloat16
lanes = 128
vmem_bytes = 56 * 1024 * 1024

sine_terms = (6.283185160087918, -10.3354137577709, 5.100062753380459, -1.1960903419427114, 0.1544402466966843)
cosine_terms = (0.9999999534659573, -4.93479285858416, 4.058411912342187, -1.331880149557601, 0.21969677520430975)


def horner(terms, value):
    total = jnp.full_like(value, terms[-1])
    for term in terms[-2::-1]:
        total = total * value + term
    return total


def cos_sin(turns):
    turn = turns - jnp.round(turns)
    square = turn * turn
    double = turn * horner(sine_terms, square)
    return 1.0 - 0.5 * (double * double), double * horner(cosine_terms, square)


class Layout:
    def __init__(self, strips, tiles_y, vectors, modes):
        self.strips, self.tiles_y, self.vectors = strips, tiles_y, vectors
        self.tiles = strips * tiles_y
        self.columns, self.waves = lax.axis_size("tile"), lax.axis_size("wave")
        self.devices = self.columns * self.waves
        self.count_x, self.count_y = self.columns * strips, self.waves * tiles_y
        self.panels = self.count_x * self.count_y * lanes
        self.local = self.tiles * lanes
        self.rows = self.tiles * 2 * vectors
        self.offset_rows = -(-6 * self.tiles // 16) * 16
        self.half = modes // 2
        self.quarter = modes // 4
        chip_bits = (self.columns - 1).bit_length()
        wave_bits = (self.waves - 1).bit_length()
        assert self.columns == 1 << chip_bits and self.waves == 1 << wave_bits
        other = 1 if wave_bits else 0
        self.chip_masks = [(1 << b) * self.waves + other for b in reversed(range(chip_bits))]
        self.masks = self.chip_masks + [1 << b for b in reversed(range(wave_bits))]
        self.wave_bits = wave_bits
        self.phase_row = 2 * self.quarter + 5

    def me(self):
        return lax.axis_index("tile") * self.waves + lax.axis_index("wave")

    def device_of(self, block):
        device = self.me()
        for k, mask in enumerate(self.masks):
            device = device ^ (((block >> k) & 1) * mask)
        return device

    def block_of(self, device):
        rest = device ^ self.me()
        block = 0
        for k, mask in enumerate(self.chip_masks):
            bit = (rest >> (mask.bit_length() - 1)) & 1
            block = block | (bit << k)
            rest = rest ^ (bit * mask)
        for b in range(self.wave_bits):
            bit = (rest >> (self.wave_bits - 1 - b)) & 1
            block = block | (bit << (len(self.chip_masks) + b))
        return block


def gather_blocks(array, layout):
    array = array[None]
    for mask in layout.masks:
        pairs = [(i, i ^ mask) for i in range(layout.devices)]
        array = jnp.concatenate([array, lax.ppermute(array, ("tile", "wave"), pairs)])
    return array


def pack_kernel(layout, residual, offsets, out):
    rows = layout.rows
    out[:rows, :] = residual[...].astype(bf16)
    value = offsets[...]
    first = value.astype(bf16)
    value = value - first.astype(f32)
    second = value.astype(bf16)
    third = (value - second.astype(f32)).astype(bf16)
    pieces = [first.astype(f32), second.astype(f32), third.astype(f32)]
    pad = layout.offset_rows - 6 * layout.tiles
    if pad:
        pieces.append(jnp.zeros((pad, lanes), f32))
    out[rows:, :] = jnp.concatenate(pieces, 0).astype(bf16)


def split_dot(weights, value, dims):
    total = 0.0
    for _ in range(3):
        part = value.astype(bf16)
        total = total + lax.dot_general(weights, part, dims, preferred_element_type=f32)
        value = value - part.astype(f32)
    return total


def spectral_kernel(layout, scale, frequency, lattice_x, lattice_y, weight, out, guess):
    size = 2 * layout.half
    spot = lax.broadcasted_iota(jnp.int32, (size, size), 0)
    wanted = jnp.where(spot < layout.half, spot + layout.half, size - 1 - spot)
    pick_x = jnp.where(wanted == lattice_x[...], 1.0, 0.0).astype(bf16)
    pick_y = jnp.where(wanted == lattice_y[...], 1.0, 0.0).astype(bf16)
    rows = []
    for v in range(layout.vectors):
        table = weight[frequency[v]] * scale
        moved = split_dot(pick_x, table, (((1,), (0,)), ((), ())))
        moved = split_dot(pick_y, moved, (((1,), (1,)), ((), ())))
        out[v] = moved
        mean = jnp.sum(jnp.sum(moved, 0, keepdims=True), 1, keepdims=True)
        rows.append(jnp.broadcast_to(0.5 + mean, (1, lanes)))
    guess[...] = jnp.concatenate(rows + rows, 0)


def make_tables(layout, block, offsets_of, table_x, table_y):
    tiles, half, quarter = layout.tiles, layout.half, layout.quarter
    device = layout.device_of(block)
    column, row_index = device // layout.waves, device % layout.waves
    pieces = offsets_of(block)
    offset = pieces[: 2 * tiles] + pieces[2 * tiles : 4 * tiles] + pieces[4 * tiles : 6 * tiles]
    eight = lax.broadcasted_iota(jnp.int32, (8, lanes), 0).astype(f32)
    coarse_y = jnp.where(eight < 4, quarter / 2 + 0.5 + 8 * eight, jnp.where(eight < 5, quarter / 2.0, 0.5))
    for i in range(tiles):
        g = (column * layout.strips + i // layout.tiles_y).astype(f32)
        h = (row_index * layout.tiles_y + i % layout.tiles_y).astype(f32)
        x = jnp.broadcast_to((offset[2 * i : 2 * i + 1] + g) * (1.0 / layout.count_x), (8, lanes))
        y = jnp.broadcast_to((offset[2 * i + 1 : 2 * i + 2] + h) * (1.0 / layout.count_y), (8, lanes))
        fine_xc, fine_xs = cos_sin(eight * x)
        big_xc, big_xs = cos_sin((8 * eight + 0.5) * x)
        fine_yc, fine_ys = cos_sin(eight * y)
        big_yc, big_ys = cos_sin(coarse_y * y + jnp.where(eight == 5, 0.5, 0.0) * x)
        shift_c, shift_s = big_yc[4:5], big_ys[4:5]
        span = slice(i * lanes, (i + 1) * lanes)
        for e, sign in ((0, 1.0), (1, -1.0)):
            both_c = big_xc * shift_c - sign * (big_xs * shift_s)
            both_s = big_xs * shift_c + sign * (big_xc * shift_s)
            cosines, sines = [], []
            for a in range(half // 8):
                c, s = both_c[a : a + 1], both_s[a : a + 1]
                cosines.append(c * fine_xc - s * fine_xs)
                sines.append(s * fine_xc + c * fine_xs)
            table_x[block, 2 * half * e : 2 * half * (e + 1), span] = jnp.concatenate(cosines + sines, 0).astype(bf16)
        cosines, sines = [], []
        for a in range(quarter // 8):
            c, s = big_yc[a : a + 1], big_ys[a : a + 1]
            cosines.append(c * fine_yc - s * fine_ys)
            sines.append(s * fine_yc + c * fine_ys)
        last = jnp.concatenate([big_yc[5:6], big_ys[5:6], jnp.zeros((6, lanes), f32)], 0)
        table_y[block, :, span] = jnp.concatenate(cosines + sines + [last], 0)


def twist(layout, block, density, table_y, out):
    vectors, group = layout.vectors, 2 * layout.quarter
    for i in range(layout.tiles):
        span = slice(i * lanes, (i + 1) * lanes)
        values = density[block, i * 2 * vectors : (i + 1) * 2 * vectors, :].astype(f32)
        waves = table_y[block, :group, span]
        c, s = table_y[block, group : group + 1, span], table_y[block, group + 1 : group + 2, span]
        real, imag = values[:vectors], values[vectors:]
        turned = (real * c - imag * s, imag * c + real * s)
        for part in range(2):
            for v in range(vectors):
                start = (part * vectors + v) * group
                out[start : start + group, span] = (turned[part][v : v + 1] * waves).astype(bf16)


def project(layout, density, table_x, table_y, twisted, total, before):
    def step(block, carry):
        before(block)
        twist(layout, block, density, table_y, twisted)
        product = lax.dot_general(
            twisted[...], table_x[block], (((1,), (1,)), ((), ())), preferred_element_type=f32
        )
        total[...] += product
        return carry

    total[...] = jnp.zeros_like(total)
    lax.fori_loop(0, layout.devices, step, 0)


def swap(value):
    return pltpu.roll(value, lanes // 2, 1)


def weigh(layout, total, weight, scaled):
    vectors, quarter = layout.vectors, layout.quarter
    low = lax.broadcasted_iota(jnp.int32, (quarter, lanes), 1) < layout.half
    sign = jnp.where(low, -1.0, 1.0)
    for v in range(vectors):
        table = weight[v]
        part = [table[k * quarter : (k + 1) * quarter] for k in range(4)]
        choices = ((part[1], part[3]), (part[2], part[0]), (part[0], part[2]), (part[3], part[1]))
        for e in range(2):
            span = slice(e * lanes, (e + 1) * lanes)
            real = v * 2 * quarter
            imag = (vectors + v) * 2 * quarter
            cos_r = total[real : real + quarter, span]
            sin_r = swap(total[real + quarter : real + 2 * quarter, span]) * sign
            cos_i = total[imag : imag + quarter, span]
            sin_i = swap(total[imag + quarter : imag + 2 * quarter, span]) * sign
            out = []
            for k, (mr, mi) in enumerate(((cos_r + sin_r, cos_i + sin_i), (cos_r - sin_r, cos_i - sin_i))):
                chosen = jnp.where(low, *choices[2 * e + k])
                turned = swap(chosen)
                plus, minus = chosen + turned, chosen - turned
                out.append((plus * mr + minus * swap(mi), plus * mi - minus * swap(mr)))
            for start, k in ((real, 0), (imag, 1)):
                scaled[start : start + quarter, span] = (out[0][k] + out[1][k]).astype(bf16)
                scaled[start + quarter : start + 2 * quarter, span] = swap(sign * (out[0][k] - out[1][k])).astype(bf16)


def expand(layout, scaled, table_x, table_y, summed):
    vectors, group = layout.vectors, 2 * layout.quarter
    summed[...] = jnp.dot(scaled[...], table_x[0], preferred_element_type=f32)
    result = []
    for i in range(layout.tiles):
        span = slice(i * lanes, (i + 1) * lanes)
        waves = table_y[0, :group, span]
        rows = []
        for k in range(2 * vectors):
            rows.append(jnp.sum(summed[k * group : (k + 1) * group, span] * waves, 0, keepdims=True))
        real, imag = jnp.concatenate(rows[:vectors], 0), jnp.concatenate(rows[vectors:], 0)
        c, s = table_y[0, group : group + 1, span], table_y[0, group + 1 : group + 2, span]
        result.append(jnp.concatenate([real * c + imag * s, imag * c - real * s], 0))
    return result


def near(layout, i, neighbor, density, kernel):
    vectors = layout.vectors
    g = lax.axis_index("tile") * layout.strips + i // layout.tiles_y
    h = lax.axis_index("wave") * layout.tiles_y + i % layout.tiles_y
    by_real, by_imag = 0.0, 0.0
    for j in range(9):
        slot = neighbor[i, j]
        step_x = lax.div(slot, 3)
        gx = lax.rem(g + step_x - 1 + layout.count_x, layout.count_x)
        hy = lax.rem(h + slot - 3 * step_x - 1 + layout.count_y, layout.count_y)
        block = layout.block_of(lax.div(gx, layout.strips) * layout.waves + lax.div(hy, layout.tiles_y))
        tile = lax.rem(gx, layout.strips) * layout.tiles_y + lax.rem(hy, layout.tiles_y)
        start = pl.multiple_of(tile * 2 * vectors, 2 * vectors)
        values = density[block, pl.ds(start, 2 * vectors), :]
        by_real += jnp.dot(values, kernel[i, j, 0], preferred_element_type=f32)
        by_imag += jnp.dot(values, kernel[i, j, 1], preferred_element_type=f32)
    return jnp.concatenate(
        [by_real[:vectors] - by_imag[vectors:], by_imag[:vectors] + by_real[vectors:]], 0
    )


def first_kernel(layout, neighbor, density, kernel, weight, guess, basis, image, table_x, table_y, twisted, total, scaled, summed):
    rows, tall = layout.rows, 2 * layout.vectors

    def tables(block):
        make_tables(layout, block, lambda b: density[b, rows:, :].astype(f32), table_x, table_y)

    project(layout, density, table_x, table_y, twisted, total, tables)
    weigh(layout, total, weight, scaled)
    far = expand(layout, scaled, table_x, table_y, summed)
    for i in range(layout.tiles):
        span = slice(i * tall, (i + 1) * tall)
        own = density[0, span, :].astype(f32)
        value = 0.5 * own + near(layout, i, neighbor, density, kernel) + far[i]
        image[span, :] = value
        basis[span, :] = (value - guess[...] * own).astype(bf16)


def second_kernel(layout, neighbor, density, start, kernel, weight, guess, image, table_x, table_y, result, scalars, twisted, total, scaled, summed):
    vectors, tall, tiles = layout.vectors, 2 * layout.vectors, layout.tiles
    project(layout, density, table_x, table_y, twisted, total, lambda block: None)
    weigh(layout, total, weight, scaled)
    far = expand(layout, scaled, table_x, table_y, summed)

    def pieces(device):
        block = layout.block_of(device)
        for i in range(tiles):
            r = start[block, i * tall : (i + 1) * tall, :].astype(f32)
            z = density[block, i * tall : (i + 1) * tall, :].astype(f32)
            yield r[:vectors], r[vectors:], z[:vectors], z[vectors:]

    def products(device, sums):
        squares, real, imag = sums
        for rr, ri, zr, zi in pieces(device):
            squares = squares + rr * rr + ri * ri
            real = real + rr * zr + ri * zi
            imag = imag + rr * zi - ri * zr
        return squares, real, imag

    zero = jnp.zeros((vectors, lanes), f32)
    sums = lax.fori_loop(0, layout.devices, products, (zero, zero, zero))
    squares, real, imag = [jnp.sum(s, 1, keepdims=True) * (1.0 / layout.panels) for s in sums]
    scale_sq = squares + eps_norm
    hint = guess[:vectors, :1]
    more_real = (real - hint * eps_norm) / scale_sq
    more_imag = imag / scale_sq
    wide_real = jnp.broadcast_to(more_real, (vectors, lanes))
    wide_imag = jnp.broadcast_to(more_imag, (vectors, lanes))

    def lengths(device, total_sq):
        for rr, ri, zr, zi in pieces(device):
            ur = zr - (wide_real * rr - wide_imag * ri)
            ui = zi - (wide_real * ri + wide_imag * rr)
            total_sq = total_sq + ur * ur + ui * ui
        return total_sq

    update_sq = jnp.sum(lax.fori_loop(0, layout.devices, lengths, zero), 1, keepdims=True)
    scale = jnp.sqrt(scale_sq)
    update_scale = jnp.sqrt(update_sq * (1.0 / layout.panels) / scale_sq + eps_norm)
    inverse = jnp.broadcast_to(1.0 / (scale * update_scale), (vectors, lanes))
    spot = lax.broadcasted_iota(jnp.int32, (vectors, lanes), 0)
    lane = lax.broadcasted_iota(jnp.int32, (vectors, lanes), 1)
    rows = [
        jnp.sum(jnp.where(spot == lane, jnp.broadcast_to(value, (vectors, lanes)), 0.0), 0, keepdims=True)
        for value in (scale, hint + more_real, more_imag, update_scale)
    ]
    scalars[...] = jnp.concatenate(rows, 0)[:, :vectors]
    for i in range(tiles):
        first = i * tall
        own = density[0, first : first + tall, :].astype(f32)
        value = 0.5 * own + near(layout, i, neighbor, density, kernel) + far[i]
        wr, wi = image[first : first + vectors, :], image[first + vectors : first + tall, :]
        result[first : first + vectors, :] = (value[:vectors] - (wide_real * wr - wide_imag * wi)) * inverse
        result[first + vectors : first + tall, :] = (value[vectors:] - (wide_real * wi + wide_imag * wr)) * inverse


def per_device(residual, kernel, offsets, neighbor, frequency, lattice_x, lattice_y, spectral_weight):
    strips, tiles_y, _, vectors, _ = residual.shape
    modes_x, modes_y = spectral_weight.shape[1:]
    layout = Layout(strips, tiles_y, vectors, modes_x)
    tiles, rows, devices = layout.tiles, layout.rows, layout.devices
    vmem, smem = pl.BlockSpec(memory_space=pltpu.VMEM), pl.BlockSpec(memory_space=pltpu.SMEM)
    shape = jax.ShapeDtypeStruct
    params = pltpu.CompilerParams(vmem_limit_bytes=vmem_bytes)

    def call(body, name, out_shape, in_specs, scratch=()):
        return pl.pallas_call(
            body,
            out_shape=out_shape,
            in_specs=in_specs,
            out_specs=jax.tree.map(lambda _: vmem, out_shape),
            scratch_shapes=scratch,
            compiler_params=params,
            name=name,
        )

    packed = call(
        lambda *refs: pack_kernel(layout, *refs),
        "pack",
        shape((rows + layout.offset_rows, lanes), bf16),
        [vmem, vmem],
    )(residual.reshape(rows, lanes), offsets.reshape(2 * tiles, lanes))
    scale = 1.0 / math.sqrt(modes_x * modes_y * layout.panels)
    weight, guess = call(
        lambda *refs: spectral_kernel(layout, scale, *refs),
        "spectral",
        (shape((vectors, modes_y, modes_x), f32), shape((2 * vectors, lanes), f32)),
        [smem, vmem, vmem, vmem],
    )(frequency, lattice_x.reshape(1, -1), lattice_y.reshape(1, -1), spectral_weight)
    blocks = kernel.reshape(tiles, 9, 2, lanes, lanes)
    neighbor = neighbor.reshape(tiles, 9)
    tall = 2 * vectors * 2 * layout.quarter
    wide = 4 * layout.half
    scratch = [
        pltpu.VMEM((tall, layout.local), bf16),
        pltpu.VMEM((tall, wide), f32),
        pltpu.VMEM((tall, wide), bf16),
        pltpu.VMEM((tall, layout.local), f32),
    ]
    gathered = gather_blocks(packed, layout)
    basis, image, table_x, table_y = call(
        lambda *refs: first_kernel(layout, *refs),
        "first",
        (
            shape((rows, lanes), bf16),
            shape((rows, lanes), f32),
            shape((devices, wide, layout.local), bf16),
            shape((devices, 2 * layout.quarter + 8, layout.local), f32),
        ),
        [smem, vmem, vmem, vmem, vmem],
        scratch,
    )(neighbor, gathered, blocks, weight, guess)
    second = gather_blocks(basis, layout)
    result, scalars = call(
        lambda *refs: second_kernel(layout, *refs),
        "second",
        (shape((rows, lanes), f32), shape((4, vectors), f32)),
        [smem] + [vmem] * 8,
        scratch,
    )(neighbor, second, gathered, blocks, weight, guess, image, table_x, table_y)
    return result.reshape(residual.shape), scalars


def solution(mesh):
    return jax.shard_map(
        per_device,
        mesh=mesh,
        in_specs=(
            P(("grp", "tile"), "wave", None, None, None),
            P(("grp", "tile"), "wave", None, None, None, None),
            P(("grp", "tile"), "wave", None, None),
            P(("grp", "tile"), "wave", None),
            P("grp"),
            P(),
            P(),
            P(),
        ),
        out_specs=(P(("grp", "tile"), "wave", None, None, None), P("grp", None)),
        check_vma=False,
    )
```

time: 308 us -> 72.5 us (0.24)
  blocking collectives: 136 us -> 0 us
  waiting for transfers between devices: 87.3 us -> 13.6 us
  Pallas kernels: 0 us -> 37.6 us
  other arithmetic: 30 us -> 4.43 us
  local copies, waits for them, and re-layouts: 22.2 us -> 3.02 us
  between operations: 14.9 us -> 0.69 us
  matrix products: 6.26 us -> 0 us
    psum x3 -> x0, blocking collectives: 94.2 us -> none  [the longest x1 34.9 us: per_device(): squares = lax.psum(local_sq, ('tile', 'wave'))]
    reduce_scatter x2 -> x0, waiting for transfers between devices: 86.5 us -> none  [far_field(): lax.psum_scatter(partial_coeffs, ('tile', 'wave'), scatter_dimension=0, t...]
    all_gather x2 -> x0, blocking collectives: 41.5 us -> none  [far_field(): scaled = lax.all_gather(owner_scaled, ('tile', 'wave'), axis=0, tiled=True)]
    pallas_call x0 -> x4, Pallas kernels: none -> 37.6 us  [the longest x1 17 us: per_device(): call(lambda *refs: first_kernel(layout, *refs), 'first', (shape((rows, la...]
    ppermute x8, waiting for transfers between devices: 0.76 us -> 13.6 us  [gather_blocks(): lax.ppermute(array, ('tile', 'wave'), pairs)]
    another operation x15 -> x0, other arithmetic: 7.55 us -> none  [the longest x2 2.13 us: project_rows(): return jnp.stack([coef_real, coef_imag], 1)]
    convert_element_type x11 -> x0, other arithmetic: 6.68 us -> none  [the longest x2 1.7 us: far_field(): owner_scaled = (shares * owner_factor).astype(jnp.bfloat16)]
    dot_general x6 -> x0, matrix products: 6.26 us -> none  [the longest x2 3.93 us: expand_rows(): return jnp.dot(stacked, matrix, preferred_element_type=jnp.float32)]
  transfers between devices with their start and end apart: 10 -> 8, of which waited for: 3 -> 7; matrix products, arithmetic and copies ran while one was open for 10% -> 2% of each run, Pallas kernels for 0% -> 4%
where the time goes in v1:
time: 72.5 us; the launch traced here: 71.8 us
  Pallas kernels  37.6 us (52%)
  waiting for transfers between devices  13.6 us (19%)
  starting transfers between devices  12.5 us (17%)
  other arithmetic  4.43 us (6%)
  local copies, waits for them, and re-layouts  3.02 us (4%)
    pallas_call x1, Pallas kernels, per_device(): call(lambda *refs: first_kernel(layout, *refs), 'first', (shape((rows, la...  17 us
    pallas_call x1, Pallas kernels, per_device(): call(lambda *refs: second_kernel(layout, *refs), 'second', (shape((rows,...  16.1 us
    ppermute x8, waiting for transfers between devices, gather_blocks(): lax.ppermute(array, ('tile', 'wave'), pairs)  13.6 us
    ppermute x8, starting transfers between devices, gather_blocks(): lax.ppermute(array, ('tile', 'wave'), pairs)  12.5 us
    concatenate x6, other arithmetic, gather_blocks(): jnp.concatenate([array, lax.ppermute(array, ('tile', 'wave'), pairs)])  4.43 us
    pallas_call x1, Pallas kernels, per_device(): call(lambda *refs: spectral_kernel(layout, scale, *refs), 'spectral', (sh...  3.18 us
    unnamed x12, local copies, waits for them, and re-layouts  2.97 us
  transfers between devices with their start and end apart: 8, of which 7 were waited for; matrix products, arithmetic and copies ran while one was open for 2% of the time, Pallas kernels for 4%

profile of v1, /device:TPU:0, one launch (start us, length us, event | category | flops | bytes accessed | tf_op | source)
XLA Modules:
  0.0 71.8 jit_solution(3688316493322667388)
XLA Ops:
  0.6 1.4 %pack.1 = bf16[96,128]{1,0:T(8,128)(2,1)} custom-call(f32[64,128]{1,0:T(8,128)} %bitcast.21, f32[8,128]{1,0:T(8,128)} %bitcast.24), custom_call_target="tpu_custom_call" | custom-call | tf_op jit(solution)/shard_map/pack/pallas_call | solution.py:356
  2.0 3.5 %collective-permute-start = (bf16[1,96,128]{2,1,0:T(8,128)(2,1)}, bf16[1,96,128]{2,1,0:T(8,128)(2,1)S(1)}, u32[]{:S(2)}, u32[]{:S(2)}) collective-permute-start(bf16[1,96,128]{2,1,0:T(8,128)(2,1)} %bitcast.13), channel_id=1, source_target_pairs={{0,9},{1,8},{2,11},{3,10},{4,13},{5,12},{6,15},{7,14},{8,1},{9,0},... | collective-permute-start | bytes 73736 | tf_op jit(solution)/shard_map/ppermute | solution.py:82
  5.5 1.8 %collective-permute-done = bf16[1,96,128]{2,1,0:T(8,128)(2,1)S(1)} collective-permute-done((bf16[1,96,128]{2,1,0:T(8,128)(2,1)}, bf16[1,96,128]{2,1,0:T(8,128)(2,1)S(1)}, u32[]{:S(2)}, u32[]{:S(2)}) %collective-permute-start) | collective-permute-done | bytes 24608 | tf_op jit(solution)/shard_map/ppermute | solution.py:82
  7.3 0.7 %pad_maximum_fusion.4 = bf16[2,96,128]{2,1,0:T(8,128)(2,1)S(1)} fusion(bf16[1,96,128]{2,1,0:T(8,128)(2,1)S(1)} %collective-permute-done, bf16[1,96,128]{2,1,0:T(8,128)(2,1)} %bitcast.14), kind=kLoop, calls=%fused_computation.4 | loop fusion | flops 24576 | bytes 98304 | tf_op jit(solution)/shard_map/concatenate | solution.py:82
  8.0 1.8 %collective-permute-start.1 = (bf16[2,96,128]{2,1,0:T(8,128)(2,1)S(1)}, bf16[2,96,128]{2,1,0:T(8,128)(2,1)S(1)}, u32[]{:S(2)}, u32[]{:S(2)}) collective-permute-start(bf16[2,96,128]{2,1,0:T(8,128)(2,1)S(1)} %pad_maximum_fusion.4), channel_id=1, source_target_pairs={{0,5},{1,4},{2,7},{3,6},{4,1},{5,0},{6,3},{7,2},{8,13},{9,12},{10,... | collective-permute-start | bytes 147464 | tf_op jit(solution)/shard_map/ppermute | solution.py:82
  9.9 0.7 %constant_dynamic-update-slice_fusion.4 = bf16[16,96,128]{2,1,0:T(8,128)(2,1)S(1)} fusion(bf16[96,128]{1,0:T(8,128)(2,1)} %pack.1), kind=kLoop, calls=%fused_computation.10 | loop fusion | bytes 49152
  10.6 3.2 %spectral.1 = (f32[8,128,128]{2,1,0:T(8,128)}, f32[16,128]{1,0:T(8,128)}) custom-call(s32[8]{0:T(128)} %refs_0_.1, s32[1,128]{1,0:T(1,128)} %bitcast.25, s32[1,128]{1,0:T(1,128)} %bitcast.26, f32[8,128,128]{2,1,0:T(8,128)} %refs_3_.1), custom_call_target="tpu_custom_call" | custom-call | tf_op jit(solution)/shard_map/spectral/pallas_call | solution.py:363
  13.8 0.7 %pad_maximum_fusion.2 = bf16[4,96,128]{2,1,0:T(8,128)(2,1)S(1)} fusion(bf16[2,96,128]{2,1,0:T(8,128)(2,1)S(1)} %collective-permute-done.1, bf16[1,96,128]{2,1,0:T(8,128)(2,1)S(1)} %collective-permute-done, bf16[1,96,128]{2,1,0:T(8,128)(2,1)} %bitcast.15), kind=kLoop, calls=%fused_computation.2 | loop fusion | flops 98304 | bytes 196608 | tf_op jit(solution)/shard_map/concatenate | solution.py:82
  14.5 1.6 %collective-permute-start.2 = (bf16[4,96,128]{2,1,0:T(8,128)(2,1)S(1)}, bf16[4,96,128]{2,1,0:T(8,128)(2,1)S(1)}, u32[]{:S(2)}, u32[]{:S(2)}) collective-permute-start(bf16[4,96,128]{2,1,0:T(8,128)(2,1)S(1)} %pad_maximum_fusion.2), channel_id=1, source_target_pairs={{0,3},{1,2},{2,1},{3,0},{4,7},{5,6},{6,5},{7,4},{8,11},{9,10},{10,... | collective-permute-start | bytes 294920 | tf_op jit(solution)/shard_map/ppermute | solution.py:82
  16.1 3.1 %collective-permute-done.2 = bf16[4,96,128]{2,1,0:T(8,128)(2,1)S(1)} collective-permute-done((bf16[4,96,128]{2,1,0:T(8,128)(2,1)S(1)}, bf16[4,96,128]{2,1,0:T(8,128)(2,1)S(1)}, u32[]{:S(2)}, u32[]{:S(2)}) %collective-permute-start.2) | collective-permute-done | bytes 98336 | tf_op jit(solution)/shard_map/ppermute | solution.py:82
  19.3 0.8 %pad_maximum_fusion = bf16[8,96,128]{2,1,0:T(8,128)(2,1)S(1)} fusion(bf16[4,96,128]{2,1,0:T(8,128)(2,1)S(1)} %collective-permute-done.2, bf16[2,96,128]{2,1,0:T(8,128)(2,1)S(1)} %collective-permute-done.1, bf16[1,96,128]{2,1,0:T(8,128)(2,1)S(1)} %collective-permute-done, bf16[1,96,128]{2,1,0:T(8,128)(2,1)} %bitcast.16), kind=kLoop, calls=%fused_computation | loop fusion | flops 294912 | bytes 393216 | tf_op jit(solution)/shard_map/concatenate | solution.py:82
  20.4 1.1 %collective-permute-done.3 = bf16[8,96,128]{2,1,0:T(8,128)(2,1)S(1)} collective-permute-done((bf16[8,96,128]{2,1,0:T(8,128)(2,1)S(1)}, bf16[8,96,128]{2,1,0:T(8,128)(2,1)S(1)}, u32[]{:S(2)}, u32[]{:S(2)}) %collective-permute-start.3) | collective-permute-done | bytes 196640 | tf_op jit(solution)/shard_map/ppermute | solution.py:82
  21.6 0.8 %copy-done = bf16[16,96,128]{2,1,0:T(8,128)(2,1)} copy-done((bf16[16,96,128]{2,1,0:T(8,128)(2,1)}, bf16[16,96,128]{2,1,0:T(8,128)(2,1)S(1)}, u32[]{:S(2)}) %copy-start) | copy-done | bytes 393240
  22.3 17.0 %first.1 = (bf16[64,128]{1,0:T(8,128)(2,1)}, f32[64,128]{1,0:T(8,128)}, bf16[16,256,512]{2,1,0:T(8,128)(2,1)}, f32[16,72,512]{2,1,0:T(8,128)}) custom-call(s32[4,9]{1,0:T(4,128)} %bitcast.22, bf16[16,96,128]{2,1,0:T(8,128)(2,1)} %copy-done, bf16[4,9,2,128,128]{4,3,2,1,0:T(8,128)(2,1)} %bitcast.11, f32[8,128,128]{2,1,0:T(8,128)} %get-tuple-element.10.refs_3_.refs_4_, ...), custom_call_target="tpu_custom_call" | custom-call | tf_op jit(solution)/shard_map/first/pallas_call | solution.py:380
  39.3 3.1 %collective-permute-start.4 = (bf16[1,64,128]{2,1,0:T(8,128)(2,1)}, bf16[1,64,128]{2,1,0:T(8,128)(2,1)S(1)}, u32[]{:S(2)}, u32[]{:S(2)}) collective-permute-start(bf16[1,64,128]{2,1,0:T(8,128)(2,1)} %bitcast.17), channel_id=1, source_target_pairs={{0,9},{1,8},{2,11},{3,10},{4,13},{5,12},{6,15},{7,14},{8,1},{9,0},... | collective-permute-start | bytes 49160 | tf_op jit(solution)/shard_map/ppermute | solution.py:82
  42.4 1.7 %collective-permute-done.4 = bf16[1,64,128]{2,1,0:T(8,128)(2,1)S(1)} collective-permute-done((bf16[1,64,128]{2,1,0:T(8,128)(2,1)}, bf16[1,64,128]{2,1,0:T(8,128)(2,1)S(1)}, u32[]{:S(2)}, u32[]{:S(2)}) %collective-permute-start.4) | collective-permute-done | bytes 16416 | tf_op jit(solution)/shard_map/ppermute | solution.py:82
  44.1 0.7 %pad_maximum_fusion.5 = bf16[2,64,128]{2,1,0:T(8,128)(2,1)S(1)} fusion(bf16[1,64,128]{2,1,0:T(8,128)(2,1)S(1)} %collective-permute-done.4, bf16[1,64,128]{2,1,0:T(8,128)(2,1)} %bitcast.18), kind=kLoop, calls=%fused_computation.5 | loop fusion | flops 16384 | bytes 65536 | tf_op jit(solution)/shard_map/concatenate | solution.py:82
  45.9 2.2 %collective-permute-done.5 = bf16[2,64,128]{2,1,0:T(8,128)(2,1)S(1)} collective-permute-done((bf16[2,64,128]{2,1,0:T(8,128)(2,1)S(1)}, bf16[2,64,128]{2,1,0:T(8,128)(2,1)S(1)}, u32[]{:S(2)}, u32[]{:S(2)}) %collective-permute-start.5) | collective-permute-done | bytes 32800 | tf_op jit(solution)/shard_map/ppermute | solution.py:82
  48.1 0.7 %pad_maximum_fusion.3 = bf16[4,64,128]{2,1,0:T(8,128)(2,1)S(1)} fusion(bf16[2,64,128]{2,1,0:T(8,128)(2,1)S(1)} %collective-permute-done.5, bf16[1,64,128]{2,1,0:T(8,128)(2,1)S(1)} %collective-permute-done.4, bf16[1,64,128]{2,1,0:T(8,128)(2,1)} %bitcast.19), kind=kLoop, calls=%fused_computation.3 | loop fusion | flops 65536 | bytes 131072 | tf_op jit(solution)/shard_map/concatenate | solution.py:82
  48.9 1.4 %collective-permute-start.6 = (bf16[4,64,128]{2,1,0:T(8,128)(2,1)S(1)}, bf16[4,64,128]{2,1,0:T(8,128)(2,1)S(1)}, u32[]{:S(2)}, u32[]{:S(2)}) collective-permute-start(bf16[4,64,128]{2,1,0:T(8,128)(2,1)S(1)} %pad_maximum_fusion.3), channel_id=1, source_target_pairs={{0,3},{1,2},{2,1},{3,0},{4,7},{5,6},{6,5},{7,4},{8,11},{9,10},{10,... | collective-permute-start | bytes 196616 | tf_op jit(solution)/shard_map/ppermute | solution.py:82
  50.3 2.6 %collective-permute-done.6 = bf16[4,64,128]{2,1,0:T(8,128)(2,1)S(1)} collective-permute-done((bf16[4,64,128]{2,1,0:T(8,128)(2,1)S(1)}, bf16[4,64,128]{2,1,0:T(8,128)(2,1)S(1)}, u32[]{:S(2)}, u32[]{:S(2)}) %collective-permute-start.6) | collective-permute-done | bytes 65568 | tf_op jit(solution)/shard_map/ppermute | solution.py:82
  52.8 0.7 %pad_maximum_fusion.1 = bf16[8,64,128]{2,1,0:T(8,128)(2,1)S(1)} fusion(bf16[4,64,128]{2,1,0:T(8,128)(2,1)S(1)} %collective-permute-done.6, bf16[2,64,128]{2,1,0:T(8,128)(2,1)S(1)} %collective-permute-done.5, bf16[1,64,128]{2,1,0:T(8,128)(2,1)S(1)} %collective-permute-done.4, bf16[1,64,128]{2,1,0:T(8,128)(2,1)} %bitcast.20), kind=kLoop, calls=%fused_computation.1 | loop fusion | flops 196608 | bytes 262144 | tf_op jit(solution)/shard_map/concatenate | solution.py:82
  53.9 1.1 %collective-permute-done.7 = bf16[8,64,128]{2,1,0:T(8,128)(2,1)S(1)} collective-permute-done((bf16[8,64,128]{2,1,0:T(8,128)(2,1)S(1)}, bf16[8,64,128]{2,1,0:T(8,128)(2,1)S(1)}, u32[]{:S(2)}, u32[]{:S(2)}) %collective-permute-start.7) | collective-permute-done | bytes 131104 | tf_op jit(solution)/shard_map/ppermute | solution.py:82
  55.7 16.1 %second.1 = (f32[64,128]{1,0:T(8,128)}, f32[4,8]{1,0:T(4,128)}) custom-call(s32[4,9]{1,0:T(4,128)} %bitcast.23, bf16[16,64,128]{2,1,0:T(8,128)(2,1)} %copy-done.1, bf16[16,96,128]{2,1,0:T(8,128)(2,1)} %copy-done, bf16[4,9,2,128,128]{4,3,2,1,0:T(8,128)(2,1)} %bitcast.12, f32[8,128,128]{2,1,0:T(8,128)} %get-tuple-element.10.refs_3_.refs_4_, ...), custom_call_target="tpu_custom_call" | custom-call | tf_op jit(solution)/shard_map/second/pallas_call | solution.py:393
  (16 shorter events, 2.6 us)
Async XLA Ops:
  2.0 5.3 %collective-permute-start = (bf16[1,96,128]{2,1,0:T(8,128)(2,1)}, bf16[1,96,128]{2,1,0:T(8,128)(2,1)S(1)}, u32[]{:S(2)}, u32[]{:S(2)}) collective-permute-start(bf16[1,96,128]{2,1,0:T(8,128)(2,1)} %bitcast.13), channel_id=1, source_target_pairs={{0,9},{1,8},{2,11},{3,10},{4,13},{5,12},{6,15},{7,14},{8,1},{9,0},... | collective-permute-start | bytes 73736 | tf_op jit(solution)/shard_map/ppermute | solution.py:82
  8.0 5.8 %collective-permute-start.1 = (bf16[2,96,128]{2,1,0:T(8,128)(2,1)S(1)}, bf16[2,96,128]{2,1,0:T(8,128)(2,1)S(1)}, u32[]{:S(2)}, u32[]{:S(2)}) collective-permute-start(bf16[2,96,128]{2,1,0:T(8,128)(2,1)S(1)} %pad_maximum_fusion.4), channel_id=1, source_target_pairs={{0,5},{1,4},{2,7},{3,6},{4,1},{5,0},{6,3},{7,2},{8,13},{9,12},{10,... | collective-permute-start | bytes 147464 | tf_op jit(solution)/shard_map/ppermute | solution.py:82
  14.5 4.7 %collective-permute-start.2 = (bf16[4,96,128]{2,1,0:T(8,128)(2,1)S(1)}, bf16[4,96,128]{2,1,0:T(8,128)(2,1)S(1)}, u32[]{:S(2)}, u32[]{:S(2)}) collective-permute-start(bf16[4,96,128]{2,1,0:T(8,128)(2,1)S(1)} %pad_maximum_fusion.2), channel_id=1, source_target_pairs={{0,3},{1,2},{2,1},{3,0},{4,7},{5,6},{6,5},{7,4},{8,11},{9,10},{10,... | collective-permute-start | bytes 294920 | tf_op jit(solution)/shard_map/ppermute | solution.py:82
  20.0 1.5 %collective-permute-start.3 = (bf16[8,96,128]{2,1,0:T(8,128)(2,1)S(1)}, bf16[8,96,128]{2,1,0:T(8,128)(2,1)S(1)}, u32[]{:S(2)}, u32[]{:S(2)}) collective-permute-start(bf16[8,96,128]{2,1,0:T(8,128)(2,1)S(1)} %pad_maximum_fusion), channel_id=1, source_target_pairs={{0,1},{1,0},{2,3},{3,2},{4,5},{5,4},{6,7},{7,6},{8,9},{9,8},{10,11... | collective-permute-start | bytes 589832 | tf_op jit(solution)/shard_map/ppermute | solution.py:82
  21.6 0.8 %copy-start = (bf16[16,96,128]{2,1,0:T(8,128)(2,1)}, bf16[16,96,128]{2,1,0:T(8,128)(2,1)S(1)}, u32[]{:S(2)}) copy-start(bf16[16,96,128]{2,1,0:T(8,128)(2,1)S(1)} %constant_dynamic-update-slice_fusion.refs_1_.refs_2_) | copy-start | bytes 1179652
  39.3 4.8 %collective-permute-start.4 = (bf16[1,64,128]{2,1,0:T(8,128)(2,1)}, bf16[1,64,128]{2,1,0:T(8,128)(2,1)S(1)}, u32[]{:S(2)}, u32[]{:S(2)}) collective-permute-start(bf16[1,64,128]{2,1,0:T(8,128)(2,1)} %bitcast.17), channel_id=1, source_target_pairs={{0,9},{1,8},{2,11},{3,10},{4,13},{5,12},{6,15},{7,14},{8,1},{9,0},... | collective-permute-start | bytes 49160 | tf_op jit(solution)/shard_map/ppermute | solution.py:82
  44.8 3.3 %collective-permute-start.5 = (bf16[2,64,128]{2,1,0:T(8,128)(2,1)S(1)}, bf16[2,64,128]{2,1,0:T(8,128)(2,1)S(1)}, u32[]{:S(2)}, u32[]{:S(2)}) collective-permute-start(bf16[2,64,128]{2,1,0:T(8,128)(2,1)S(1)} %pad_maximum_fusion.5), channel_id=1, source_target_pairs={{0,5},{1,4},{2,7},{3,6},{4,1},{5,0},{6,3},{7,2},{8,13},{9,12},{10,... | collective-permute-start | bytes 98312 | tf_op jit(solution)/shard_map/ppermute | solution.py:82
  48.9 4.0 %collective-permute-start.6 = (bf16[4,64,128]{2,1,0:T(8,128)(2,1)S(1)}, bf16[4,64,128]{2,1,0:T(8,128)(2,1)S(1)}, u32[]{:S(2)}, u32[]{:S(2)}) collective-permute-start(bf16[4,64,128]{2,1,0:T(8,128)(2,1)S(1)} %pad_maximum_fusion.3), channel_id=1, source_target_pairs={{0,3},{1,2},{2,1},{3,0},{4,7},{5,6},{6,5},{7,4},{8,11},{9,10},{10,... | collective-permute-start | bytes 196616 | tf_op jit(solution)/shard_map/ppermute | solution.py:82
  53.6 1.4 %collective-permute-start.7 = (bf16[8,64,128]{2,1,0:T(8,128)(2,1)S(1)}, bf16[8,64,128]{2,1,0:T(8,128)(2,1)S(1)}, u32[]{:S(2)}, u32[]{:S(2)}) collective-permute-start(bf16[8,64,128]{2,1,0:T(8,128)(2,1)S(1)} %pad_maximum_fusion.1), channel_id=1, source_target_pairs={{0,1},{1,0},{2,3},{3,2},{4,5},{5,4},{6,7},{7,6},{8,9},{9,8},{10,11... | collective-permute-start | bytes 393224 | tf_op jit(solution)/shard_map/ppermute | solution.py:82
  55.0 0.7 copy-start.1

commit v2 on v1

--- a/solution.py
+++ b/solution.py
@@ -11,7 +11,7 @@
 f32 = jnp.float32
 bf16 = jnp.bfloat16
 lanes = 128
-vmem_bytes = 56 * 1024 * 1024
+mib = 1024 * 1024
 
 sine_terms = (6.283185160087918, -10.3354137577709, 5.100062753380459, -1.1960903419427114, 0.1544402466966843)
 cosine_terms = (0.9999999534659573, -4.93479285858416, 4.058411912342187, -1.331880149557601, 0.21969677520430975)
@@ -340,16 +340,15 @@
     tiles, rows, devices = layout.tiles, layout.rows, layout.devices
     vmem, smem = pl.BlockSpec(memory_space=pltpu.VMEM), pl.BlockSpec(memory_space=pltpu.SMEM)
     shape = jax.ShapeDtypeStruct
-    params = pltpu.CompilerParams(vmem_limit_bytes=vmem_bytes)
-
-    def call(body, name, out_shape, in_specs, scratch=()):
+
+    def call(body, name, out_shape, in_specs, limit, scratch=()):
         return pl.pallas_call(
             body,
             out_shape=out_shape,
             in_specs=in_specs,
             out_specs=jax.tree.map(lambda _: vmem, out_shape),
             scratch_shapes=scratch,
-            compiler_params=params,
+            compiler_params=pltpu.CompilerParams(vmem_limit_bytes=limit),
             name=name,
         )
 
@@ -358,6 +357,7 @@
         "pack",
         shape((rows + layout.offset_rows, lanes), bf16),
         [vmem, vmem],
+        mib,
     )(residual.reshape(rows, lanes), offsets.reshape(2 * tiles, lanes))
     scale = 1.0 / math.sqrt(modes_x * modes_y * layout.panels)
     weight, guess = call(
@@ -365,6 +365,7 @@
         "spectral",
         (shape((vectors, modes_y, modes_x), f32), shape((2 * vectors, lanes), f32)),
         [smem, vmem, vmem, vmem],
+        4 * mib,
     )(frequency, lattice_x.reshape(1, -1), lattice_y.reshape(1, -1), spectral_weight)
     blocks = kernel.reshape(tiles, 9, 2, lanes, lanes)
     neighbor = neighbor.reshape(tiles, 9)
@@ -376,6 +377,7 @@
         pltpu.VMEM((tall, wide), bf16),
         pltpu.VMEM((tall, layout.local), f32),
     ]
+    limit = int(24 * mib)
     gathered = gather_blocks(packed, layout)
     basis, image, table_x, table_y = call(
         lambda *refs: first_kernel(layout, *refs),
@@ -387,6 +389,7 @@
             shape((devices, 2 * layout.quarter + 8, layout.local), f32),
         ),
         [smem, vmem, vmem, vmem, vmem],
+        limit,
         scratch,
     )(neighbor, gathered, blocks, weight, guess)
     second = gather_blocks(basis, layout)
@@ -395,6 +398,7 @@
         "second",
         (shape((rows, lanes), f32), shape((4, vectors), f32)),
         [smem] + [vmem] * 8,
+        limit,
         scratch,
     )(neighbor, second, gathered, blocks, weight, guess, image, table_x, table_y)
     return result.reshape(residual.shape), scalars

time: 72.5 us -> 62.3 us (0.86)
  Pallas kernels: 37.6 us -> 27.7 us
  other arithmetic: 4.43 us -> 0.08 us
  local copies, waits for them, and re-layouts: 3.02 us -> 6.9 us
    concatenate x6, other arithmetic: 4.43 us -> 0.08 us  [gather_blocks(): jnp.concatenate([array, lax.ppermute(array, ('tile', 'wave'), pairs)])]
    unnamed x12 -> x24, local copies, waits for them, and re-layouts: 2.97 us -> 6.85 us
    pallas_call x1, Pallas kernels: 17 us -> 13.1 us  [per_device(): call(lambda *refs: first_kernel(layout, *refs), 'first', (shape((rows, la...]
    pallas_call x1, Pallas kernels: 16.1 us -> 12.7 us  [per_device(): call(lambda *refs: second_kernel(layout, *refs), 'second', (shape((rows,...]
    pallas_call x1, Pallas kernels: 1.38 us -> 0.01 us  [per_device(): call(lambda *refs: pack_kernel(layout, *refs), 'pack', shape((rows + layo...]
    pallas_call x1, Pallas kernels: 3.18 us -> 1.89 us  [per_device(): call(lambda *refs: spectral_kernel(layout, scale, *refs), 'spectral', (sh...]
  transfers between devices with their start and end apart: 8 -> 8, of which waited for: 7 -> 7; matrix products, arithmetic and copies ran while one was open for 2% -> 0% of each run, Pallas kernels for 4% -> 3%
where the time goes in v2:
time: 62.3 us; the launch traced here: 61.9 us
  Pallas kernels  27.7 us (44%)
  waiting for transfers between devices  14 us (22%)
  starting transfers between devices  12.6 us (20%)
  local copies, waits for them, and re-layouts  6.9 us (11%)
  between operations  0.7 us (1%)
    ppermute x8, waiting for transfers between devices, gather_blocks(): lax.ppermute(array, ('tile', 'wave'), pairs)  14 us
    pallas_call x1, Pallas kernels, per_device(): call(lambda *refs: first_kernel(layout, *refs), 'first', (shape((rows, la...  13.1 us
    pallas_call x1, Pallas kernels, per_device(): call(lambda *refs: second_kernel(layout, *refs), 'second', (shape((rows,...  12.7 us
    ppermute x8, starting transfers between devices, gather_blocks(): lax.ppermute(array, ('tile', 'wave'), pairs)  12.6 us
    unnamed x24, local copies, waits for them, and re-layouts  6.85 us
    pallas_call x1, Pallas kernels, per_device(): call(lambda *refs: spectral_kernel(layout, scale, *refs), 'spectral', (sh...  1.89 us
  transfers between devices with their start and end apart: 8, of which 7 were waited for; matrix products, arithmetic and copies ran while one was open for 0% of the time, Pallas kernels for 3%

profile of v2, /device:TPU:0, one launch (start us, length us, event | category | flops | bytes accessed | tf_op | source)
XLA Modules:
  0.0 61.9 jit_solution(14751252852174927029)
XLA Ops:
  0.6 0.7 %copy-done.2 = f32[1,4,2,8,128]{4,3,2,1,0:T(8,128)S(1)} copy-done((f32[1,4,2,8,128]{4,3,2,1,0:T(8,128)S(1)}, f32[1,4,2,8,128]{4,3,2,1,0:T(8,128)}, u32[]{:S(2)}) %copy-start.2) | copy-done | bytes 32792
  1.4 0.7 %copy-done.4 = f32[1,4,2,128]{3,2,1,0:T(2,128)S(1)} copy-done((f32[1,4,2,128]{3,2,1,0:T(2,128)S(1)}, f32[1,4,2,128]{3,2,1,0:T(2,128)}, u32[]{:S(2)}) %copy-start.4) | copy-done | bytes 4120
  2.1 3.5 %collective-permute-start = (bf16[1,96,128]{2,1,0:T(8,128)(2,1)S(1)}, bf16[1,96,128]{2,1,0:T(8,128)(2,1)S(1)}, u32[]{:S(2)}, u32[]{:S(2)}) collective-permute-start(bf16[1,96,128]{2,1,0:T(8,128)(2,1)S(1)} %bitcast.13), channel_id=1, source_target_pairs={{0,9},{1,8},{2,11},{3,10},{4,13},{5,12},{6,15},{7,14},{8,1},{9,0},... | collective-permute-start | bytes 73736 | tf_op jit(solution)/shard_map/ppermute | solution.py:82
  5.6 1.6 %collective-permute-done = bf16[1,96,128]{2,1,0:T(8,128)(2,1)S(1)} collective-permute-done((bf16[1,96,128]{2,1,0:T(8,128)(2,1)S(1)}, bf16[1,96,128]{2,1,0:T(8,128)(2,1)S(1)}, u32[]{:S(2)}, u32[]{:S(2)}) %collective-permute-start) | collective-permute-done | bytes 24608 | tf_op jit(solution)/shard_map/ppermute | solution.py:82
  7.2 1.8 %collective-permute-start.1 = (bf16[2,96,128]{2,1,0:T(8,128)(2,1)S(1)}, bf16[2,96,128]{2,1,0:T(8,128)(2,1)S(1)}, u32[]{:S(2)}, u32[]{:S(2)}) collective-permute-start(bf16[2,96,128]{2,1,0:T(8,128)(2,1)S(1)} %pad_maximum_fusion.4), channel_id=1, source_target_pairs={{0,5},{1,4},{2,7},{3,6},{4,1},{5,0},{6,3},{7,2},{8,13},{9,12},{10,... | collective-permute-start | bytes 147464 | tf_op jit(solution)/shard_map/ppermute | solution.py:82
  9.1 1.0 %copy-done.1 = f32[8,128,128]{2,1,0:T(8,128)S(1)} copy-done((f32[8,128,128]{2,1,0:T(8,128)S(1)}, f32[8,128,128]{2,1,0:T(8,128)}, u32[]{:S(2)}) %copy-start.1) | copy-done | bytes 524312
  10.1 0.7 %copy-done.5 = s32[8]{0:T(128)S(1)} copy-done((s32[8]{0:T(128)S(1)}, s32[8]{0:T(128)}, u32[]{:S(2)}) %copy-start.5) | copy-done | bytes 56
  10.8 0.7 %copy-done.6 = s32[128]{0:T(128)S(1)} copy-done((s32[128]{0:T(128)S(1)}, s32[128]{0:T(128)}, u32[]{:S(2)}) %copy-start.6) | copy-done | bytes 536
  11.4 0.7 %copy-done.7 = s32[128]{0:T(128)S(1)} copy-done((s32[128]{0:T(128)S(1)}, s32[128]{0:T(128)}, u32[]{:S(2)}) %copy-start.7) | copy-done | bytes 536
  12.1 1.9 %spectral.1 = (f32[8,128,128]{2,1,0:T(8,128)S(1)}, f32[16,128]{1,0:T(8,128)S(1)}) custom-call(s32[8]{0:T(128)S(1)} %copy-done.5, s32[1,128]{1,0:T(1,128)S(1)} %bitcast.25, s32[1,128]{1,0:T(1,128)S(1)} %bitcast.26, f32[8,128,128]{2,1,0:T(8,128)S(1)} %copy-done.1), custom_call_target="tpu_custom_call" | custom-call | tf_op jit(solution)/shard_map/spectral/pallas_call | solution.py:363
  14.0 1.6 %collective-permute-start.2 = (bf16[4,96,128]{2,1,0:T(8,128)(2,1)S(1)}, bf16[4,96,128]{2,1,0:T(8,128)(2,1)S(1)}, u32[]{:S(2)}, u32[]{:S(2)}) collective-permute-start(bf16[4,96,128]{2,1,0:T(8,128)(2,1)S(1)} %pad_maximum_fusion.2), channel_id=1, source_target_pairs={{0,3},{1,2},{2,1},{3,0},{4,7},{5,6},{6,5},{7,4},{8,11},{9,10},{10,... | collective-permute-start | bytes 294920 | tf_op jit(solution)/shard_map/ppermute | solution.py:82
  15.6 3.0 %collective-permute-done.2 = bf16[4,96,128]{2,1,0:T(8,128)(2,1)S(1)} collective-permute-done((bf16[4,96,128]{2,1,0:T(8,128)(2,1)S(1)}, bf16[4,96,128]{2,1,0:T(8,128)(2,1)S(1)}, u32[]{:S(2)}, u32[]{:S(2)}) %collective-permute-start.2) | collective-permute-done | bytes 98336 | tf_op jit(solution)/shard_map/ppermute | solution.py:82
  18.6 0.4 collective-permute-start.3
  19.1 1.0 %collective-permute-done.3 = bf16[8,96,128]{2,1,0:T(8,128)(2,1)S(1)} collective-permute-done((bf16[8,96,128]{2,1,0:T(8,128)(2,1)S(1)}, bf16[8,96,128]{2,1,0:T(8,128)(2,1)S(1)}, u32[]{:S(2)}, u32[]{:S(2)}) %collective-permute-start.3) | collective-permute-done | bytes 196640 | tf_op jit(solution)/shard_map/ppermute | solution.py:82
  20.2 1.7 %copy-done = bf16[1,4,9,2,128,128]{5,4,3,2,1,0:T(8,128)(2,1)S(1)} copy-done((bf16[1,4,9,2,128,128]{5,4,3,2,1,0:T(8,128)(2,1)S(1)}, bf16[1,4,9,2,128,128]{5,4,3,2,1,0:T(8,128)(2,1)}, u32[]{:S(2)}) %copy-start) | copy-done | bytes 2359320
  21.8 0.7 %copy-done.3 = s32[1,4,9]{2,1,0:T(4,128)S(1)} copy-done((s32[1,4,9]{2,1,0:T(4,128)S(1)}, s32[1,4,9]{2,1,0:T(4,128)}, u32[]{:S(2)}) %copy-start.3) | copy-done | bytes 168
  22.5 13.1 %first.1 = (bf16[64,128]{1,0:T(8,128)(2,1)S(1)}, f32[64,128]{1,0:T(8,128)S(1)}, bf16[16,256,512]{2,1,0:T(8,128)(2,1)S(1)}, f32[16,72,512]{2,1,0:T(8,128)S(1)}) custom-call(s32[4,9]{1,0:T(4,128)S(1)} %bitcast.22, bf16[16,96,128]{2,1,0:T(8,128)(2,1)S(1)} %constant_dynamic-update-slice_fusion.refs_1_.refs_2_, bf16[4,9,2,128,128]{4,3,2,1,0:T(8,128)(2,1)S(1)} %bitcast.11, ...), custom_call_target="tpu_custom_call" | custom-call | tf_op jit(solution)/shard_map/first/pallas_call | solution.py:382
  35.6 3.2 %collective-permute-start.4 = (bf16[1,64,128]{2,1,0:T(8,128)(2,1)S(1)}, bf16[1,64,128]{2,1,0:T(8,128)(2,1)S(1)}, u32[]{:S(2)}, u32[]{:S(2)}) collective-permute-start(bf16[1,64,128]{2,1,0:T(8,128)(2,1)S(1)} %bitcast.17), channel_id=1, source_target_pairs={{0,9},{1,8},{2,11},{3,10},{4,13},{5,12},{6,15},{7,14},{8,1},{9,0},... | collective-permute-start | bytes 49160 | tf_op jit(solution)/shard_map/ppermute | solution.py:82
  38.9 1.4 %collective-permute-done.4 = bf16[1,64,128]{2,1,0:T(8,128)(2,1)S(1)} collective-permute-done((bf16[1,64,128]{2,1,0:T(8,128)(2,1)S(1)}, bf16[1,64,128]{2,1,0:T(8,128)(2,1)S(1)}, u32[]{:S(2)}, u32[]{:S(2)}) %collective-permute-start.4) | collective-permute-done | bytes 16416 | tf_op jit(solution)/shard_map/ppermute | solution.py:82
  40.6 3.1 %collective-permute-done.5 = bf16[2,64,128]{2,1,0:T(8,128)(2,1)S(1)} collective-permute-done((bf16[2,64,128]{2,1,0:T(8,128)(2,1)S(1)}, bf16[2,64,128]{2,1,0:T(8,128)(2,1)S(1)}, u32[]{:S(2)}, u32[]{:S(2)}) %collective-permute-start.5) | collective-permute-done | bytes 32800 | tf_op jit(solution)/shard_map/ppermute | solution.py:82
  43.7 1.4 %collective-permute-start.6 = (bf16[4,64,128]{2,1,0:T(8,128)(2,1)S(1)}, bf16[4,64,128]{2,1,0:T(8,128)(2,1)S(1)}, u32[]{:S(2)}, u32[]{:S(2)}) collective-permute-start(bf16[4,64,128]{2,1,0:T(8,128)(2,1)S(1)} %pad_maximum_fusion.3), channel_id=1, source_target_pairs={{0,3},{1,2},{2,1},{3,0},{4,7},{5,6},{6,5},{7,4},{8,11},{9,10},{10,... | collective-permute-start | bytes 196616 | tf_op jit(solution)/shard_map/ppermute | solution.py:82
  45.1 2.7 %collective-permute-done.6 = bf16[4,64,128]{2,1,0:T(8,128)(2,1)S(1)} collective-permute-done((bf16[4,64,128]{2,1,0:T(8,128)(2,1)S(1)}, bf16[4,64,128]{2,1,0:T(8,128)(2,1)S(1)}, u32[]{:S(2)}, u32[]{:S(2)}) %collective-permute-start.6) | collective-permute-done | bytes 65568 | tf_op jit(solution)/shard_map/ppermute | solution.py:82
  48.1 1.2 %collective-permute-done.7 = bf16[8,64,128]{2,1,0:T(8,128)(2,1)S(1)} collective-permute-done((bf16[8,64,128]{2,1,0:T(8,128)(2,1)S(1)}, bf16[8,64,128]{2,1,0:T(8,128)(2,1)S(1)}, u32[]{:S(2)}, u32[]{:S(2)}) %collective-permute-start.7) | collective-permute-done | bytes 131104 | tf_op jit(solution)/shard_map/ppermute | solution.py:82
  49.2 12.7 %second.1 = (f32[64,128]{1,0:T(8,128)}, f32[4,8]{1,0:T(4,128)}) custom-call(s32[4,9]{1,0:T(4,128)S(1)} %bitcast.23, bf16[16,64,128]{2,1,0:T(8,128)(2,1)S(1)} %constant_dynamic-update-slice_fusion.5.refs_1_, bf16[16,96,128]{2,1,0:T(8,128)(2,1)S(1)} %constant_dynamic-update-slice_fusion.refs_1_.refs_2_, bf16[4,9,2,128,128]{4,3,2,1,0:T(8,128)(2,1)S(1)} %bitcast.12, ...), custom_call_target="tpu_custom_call" | custom-call | tf_op jit(solution)/shard_map/second/pallas_call | solution.py:396
  (28 shorter events, 0.7 us)
Async XLA Ops:
  0.6 0.8 %copy-start.2 = (f32[1,4,2,8,128]{4,3,2,1,0:T(8,128)S(1)}, f32[1,4,2,8,128]{4,3,2,1,0:T(8,128)}, u32[]{:S(2)}) copy-start(f32[1,4,2,8,128]{4,3,2,1,0:T(8,128)} %param.8) | copy-start | bytes 98308
  1.4 0.7 %copy-start.4 = (f32[1,4,2,128]{3,2,1,0:T(2,128)S(1)}, f32[1,4,2,128]{3,2,1,0:T(2,128)}, u32[]{:S(2)}) copy-start(f32[1,4,2,128]{3,2,1,0:T(2,128)} %param.10) | copy-start | bytes 12292
  2.1 5.1 %collective-permute-start = (bf16[1,96,128]{2,1,0:T(8,128)(2,1)S(1)}, bf16[1,96,128]{2,1,0:T(8,128)(2,1)S(1)}, u32[]{:S(2)}, u32[]{:S(2)}) collective-permute-start(bf16[1,96,128]{2,1,0:T(8,128)(2,1)S(1)} %bitcast.13), channel_id=1, source_target_pairs={{0,9},{1,8},{2,11},{3,10},{4,13},{5,12},{6,15},{7,14},{8,1},{9,0},... | collective-permute-start | bytes 73736 | tf_op jit(solution)/shard_map/ppermute | solution.py:82
  7.2 6.7 %collective-permute-start.1 = (bf16[2,96,128]{2,1,0:T(8,128)(2,1)S(1)}, bf16[2,96,128]{2,1,0:T(8,128)(2,1)S(1)}, u32[]{:S(2)}, u32[]{:S(2)}) collective-permute-start(bf16[2,96,128]{2,1,0:T(8,128)(2,1)S(1)} %pad_maximum_fusion.4), channel_id=1, source_target_pairs={{0,5},{1,4},{2,7},{3,6},{4,1},{5,0},{6,3},{7,2},{8,13},{9,12},{10,... | collective-permute-start | bytes 147464 | tf_op jit(solution)/shard_map/ppermute | solution.py:82
  9.1 1.0 %copy-start.1 = (f32[8,128,128]{2,1,0:T(8,128)S(1)}, f32[8,128,128]{2,1,0:T(8,128)}, u32[]{:S(2)}) copy-start(f32[8,128,128]{2,1,0:T(8,128)} %refs_3_.1) | copy-start | bytes 1572868
  10.1 0.7 %copy-start.5 = (s32[8]{0:T(128)S(1)}, s32[8]{0:T(128)}, u32[]{:S(2)}) copy-start(s32[8]{0:T(128)} %refs_0_.1) | copy-start | bytes 100
  10.8 0.7 %copy-start.6 = (s32[128]{0:T(128)S(1)}, s32[128]{0:T(128)}, u32[]{:S(2)}) copy-start(s32[128]{0:T(128)} %param.13) | copy-start | bytes 1540
  11.4 0.7 %copy-start.7 = (s32[128]{0:T(128)S(1)}, s32[128]{0:T(128)}, u32[]{:S(2)}) copy-start(s32[128]{0:T(128)} %param.14) | copy-start | bytes 1540
  14.0 4.6 %collective-permute-start.2 = (bf16[4,96,128]{2,1,0:T(8,128)(2,1)S(1)}, bf16[4,96,128]{2,1,0:T(8,128)(2,1)S(1)}, u32[]{:S(2)}, u32[]{:S(2)}) collective-permute-start(bf16[4,96,128]{2,1,0:T(8,128)(2,1)S(1)} %pad_maximum_fusion.2), channel_id=1, source_target_pairs={{0,3},{1,2},{2,1},{3,0},{4,7},{5,6},{6,5},{7,4},{8,11},{9,10},{10,... | collective-permute-start | bytes 294920 | tf_op jit(solution)/shard_map/ppermute | solution.py:82
  18.6 1.5 %collective-permute-start.3 = (bf16[8,96,128]{2,1,0:T(8,128)(2,1)S(1)}, bf16[8,96,128]{2,1,0:T(8,128)(2,1)S(1)}, u32[]{:S(2)}, u32[]{:S(2)}) collective-permute-start(bf16[8,96,128]{2,1,0:T(8,128)(2,1)S(1)} %pad_maximum_fusion), channel_id=1, source_target_pairs={{0,1},{1,0},{2,3},{3,2},{4,5},{5,4},{6,7},{7,6},{8,9},{9,8},{10,11... | collective-permute-start | bytes 589832 | tf_op jit(solution)/shard_map/ppermute | solution.py:82
  20.2 1.7 %copy-start = (bf16[1,4,9,2,128,128]{5,4,3,2,1,0:T(8,128)(2,1)S(1)}, bf16[1,4,9,2,128,128]{5,4,3,2,1,0:T(8,128)(2,1)}, u32[]{:S(2)}) copy-start(bf16[1,4,9,2,128,128]{5,4,3,2,1,0:T(8,128)(2,1)} %param.9) | copy-start | bytes 7077892
  21.8 0.7 %copy-start.3 = (s32[1,4,9]{2,1,0:T(4,128)S(1)}, s32[1,4,9]{2,1,0:T(4,128)}, u32[]{:S(2)}) copy-start(s32[1,4,9]{2,1,0:T(4,128)} %param.11) | copy-start | bytes 436
  35.6 4.7 %collective-permute-start.4 = (bf16[1,64,128]{2,1,0:T(8,128)(2,1)S(1)}, bf16[1,64,128]{2,1,0:T(8,128)(2,1)S(1)}, u32[]{:S(2)}, u32[]{:S(2)}) collective-permute-start(bf16[1,64,128]{2,1,0:T(8,128)(2,1)S(1)} %bitcast.17), channel_id=1, source_target_pairs={{0,9},{1,8},{2,11},{3,10},{4,13},{5,12},{6,15},{7,14},{8,1},{9,0},... | collective-permute-start | bytes 49160 | tf_op jit(solution)/shard_map/ppermute | solution.py:82
  40.3 3.3 %collective-permute-start.5 = (bf16[2,64,128]{2,1,0:T(8,128)(2,1)S(1)}, bf16[2,64,128]{2,1,0:T(8,128)(2,1)S(1)}, u32[]{:S(2)}, u32[]{:S(2)}) collective-permute-start(bf16[2,64,128]{2,1,0:T(8,128)(2,1)S(1)} %pad_maximum_fusion.5), channel_id=1, source_target_pairs={{0,5},{1,4},{2,7},{3,6},{4,1},{5,0},{6,3},{7,2},{8,13},{9,12},{10,... | collective-permute-start | bytes 98312 | tf_op jit(solution)/shard_map/ppermute | solution.py:82
  43.7 4.1 %collective-permute-start.6 = (bf16[4,64,128]{2,1,0:T(8,128)(2,1)S(1)}, bf16[4,64,128]{2,1,0:T(8,128)(2,1)S(1)}, u32[]{:S(2)}, u32[]{:S(2)}) collective-permute-start(bf16[4,64,128]{2,1,0:T(8,128)(2,1)S(1)} %pad_maximum_fusion.3), channel_id=1, source_target_pairs={{0,3},{1,2},{2,1},{3,0},{4,7},{5,6},{6,5},{7,4},{8,11},{9,10},{10,... | collective-permute-start | bytes 196616 | tf_op jit(solution)/shard_map/ppermute | solution.py:82
  47.8 1.4 %collective-permute-start.7 = (bf16[8,64,128]{2,1,0:T(8,128)(2,1)S(1)}, bf16[8,64,128]{2,1,0:T(8,128)(2,1)S(1)}, u32[]{:S(2)}, u32[]{:S(2)}) collective-permute-start(bf16[8,64,128]{2,1,0:T(8,128)(2,1)S(1)} %pad_maximum_fusion.1), channel_id=1, source_target_pairs={{0,1},{1,0},{2,3},{3,2},{4,5},{5,4},{6,7},{7,6},{8,9},{9,8},{10,11... | collective-permute-start | bytes 393224 | tf_op jit(solution)/shard_map/ppermute | solution.py:82

commit v3 on v1

v3 whole, which is shorter than its diff:
```python
import math

import jax
import jax.numpy as jnp
from jax import lax
from jax.experimental import pallas as pl
from jax.experimental.pallas import tpu as pltpu
from jax.sharding import PartitionSpec as P

eps_norm = 1e-06
f32 = jnp.float32
bf16 = jnp.bfloat16
lanes = 128
mib = 1024 * 1024

sine_terms = (6.283185160087918, -10.3354137577709, 5.100062753380459, -1.1960903419427114, 0.1544402466966843)
cosine_terms = (0.9999999534659573, -4.93479285858416, 4.058411912342187, -1.331880149557601, 0.21969677520430975)


def horner(terms, value):
    total = jnp.full_like(value, terms[-1])
    for term in terms[-2::-1]:
        total = total * value + term
    return total


def cos_sin(turns):
    turn = turns - jnp.round(turns)
    square = turn * turn
    double = turn * horner(sine_terms, square)
    return 1.0 - 0.5 * (double * double), double * horner(cosine_terms, square)


class Layout:
    def __init__(self, strips, tiles_y, vectors, modes):
        self.strips, self.tiles_y, self.vectors = strips, tiles_y, vectors
        self.tiles = strips * tiles_y
        self.columns, self.waves = lax.axis_size("tile"), lax.axis_size("wave")
        self.devices = self.columns * self.waves
        self.count_x, self.count_y = self.columns * strips, self.waves * tiles_y
        self.panels = self.count_x * self.count_y * lanes
        self.local = self.tiles * lanes
        self.rows = self.tiles * 2 * vectors
        self.offset_rows = -(-6 * self.tiles // 16) * 16
        self.sum_rows = 16
        self.part_v = vectors // 2
        self.half = modes // 2
        self.quarter = modes // 4
        chip_bits = (self.columns - 1).bit_length()
        assert self.columns == 1 << chip_bits and self.waves == 2
        self.chip_masks = [(1 << b) * self.waves + 1 for b in reversed(range(chip_bits))]
        self.masks = self.chip_masks + [1]

    def me(self):
        return lax.axis_index("tile") * self.waves + lax.axis_index("wave")

    def device_of(self, block):
        device = self.me()
        for k, mask in enumerate(self.masks):
            device = device ^ (((block >> k) & 1) * mask)
        return device

    def block_of(self, device):
        rest = device ^ self.me()
        block = 0
        for k, mask in enumerate(self.chip_masks):
            bit = (rest >> (mask.bit_length() - 1)) & 1
            block = block | (bit << k)
            rest = rest ^ (bit * mask)
        block = block | (rest << len(self.chip_masks))
        return block


def swap_cores(array):
    return lax.ppermute(array, "wave", [(0, 1), (1, 0)])


def gather_parts(array, layout):
    array = array[None]
    parts = []
    for mask in layout.chip_masks:
        pairs = [(i, i ^ mask) for i in range(layout.devices)]
        arrived = lax.ppermute(array, ("tile", "wave"), pairs)
        array = jnp.concatenate([array, arrived])
        parts.append(arrived if parts else array)
    return array, parts


def three_parts(value, pad):
    first = value.astype(bf16).astype(f32)
    value = value - first
    second = value.astype(bf16).astype(f32)
    pieces = [first, second, value - second]
    if pad:
        pieces.append(jnp.zeros((pad, lanes), f32))
    return jnp.concatenate(pieces, 0).astype(bf16)


def add_three(rows, count):
    return rows[:count] + rows[count : 2 * count] + rows[2 * count : 3 * count]


def pack_kernel(layout, head, out, squares):
    rows, vectors = layout.rows, layout.vectors
    out[:rows, :] = head[:rows, :].astype(bf16)
    out[rows:, :] = three_parts(head[rows:, :], layout.offset_rows - 6 * layout.tiles)
    total = 0.0
    for k in range(2 * layout.tiles):
        piece = head[k * vectors : (k + 1) * vectors, :]
        total = total + piece * piece
    squares[...] = total


def split_dot(weights, value, dims):
    total = 0.0
    for _ in range(3):
        part = value.astype(bf16)
        total = total + lax.dot_general(weights, part, dims, preferred_element_type=f32)
        value = value - part.astype(f32)
    return total


def spectral_kernel(layout, scale, table, frequency, out, guess, order, moved_all, sem):
    size = 2 * layout.half
    count = moved_all.shape[0]
    copy = pltpu.make_async_copy(frequency, order, sem)
    copy.start()
    spot = lax.broadcasted_iota(jnp.int32, (size, size), 0)
    wanted = jnp.where(spot < layout.half, spot + layout.half, size - 1 - spot).astype(f32)
    pick_x = jnp.where(wanted == table[count * size : count * size + 1], 1.0, 0.0).astype(bf16)
    pick_y = jnp.where(wanted == table[count * size + 1 : count * size + 2], 1.0, 0.0).astype(bf16)
    for f in range(count):
        moved = split_dot(pick_x, table[f * size : (f + 1) * size] * scale, (((1,), (0,)), ((), ())))
        moved_all[f] = split_dot(pick_y, moved, (((1,), (1,)), ((), ())))
    copy.wait()
    rows = []
    for v in range(layout.vectors):
        moved = moved_all[order[v]]
        out[v] = moved
        mean = jnp.sum(jnp.sum(moved, 0, keepdims=True), 1, keepdims=True)
        rows.append(jnp.broadcast_to(0.5 + mean, (1, lanes)))
    guess[...] = jnp.concatenate(rows, 0)


def make_tables(layout, base, pair, half_block, density, table_x, table_y):
    tiles, half, quarter = layout.tiles, layout.half, layout.quarter
    block = 2 * pair + half_block
    device = layout.device_of(base + block)
    column, row_index = device // layout.waves, device % layout.waves
    offset = add_three(density[block, layout.rows :, :].astype(f32), 2 * tiles)
    eight = lax.broadcasted_iota(jnp.int32, (8, lanes), 0).astype(f32)
    coarse_y = jnp.where(eight < 4, quarter / 2 + 0.5 + 8 * eight, jnp.where(eight < 5, quarter / 2.0, 0.5))
    for i in range(tiles):
        g = (column * layout.strips + i // layout.tiles_y).astype(f32)
        h = (row_index * layout.tiles_y + i % layout.tiles_y).astype(f32)
        x = jnp.broadcast_to((offset[2 * i : 2 * i + 1] + g) * (1.0 / layout.count_x), (8, lanes))
        y = jnp.broadcast_to((offset[2 * i + 1 : 2 * i + 2] + h) * (1.0 / layout.count_y), (8, lanes))
        fine_xc, fine_xs = cos_sin(eight * x)
        big_xc, big_xs = cos_sin((8 * eight + 0.5) * x)
        fine_yc, fine_ys = cos_sin(eight * y)
        big_yc, big_ys = cos_sin(coarse_y * y + jnp.where(eight == 5, 0.5, 0.0) * x)
        shift_c, shift_s = big_yc[4:5], big_ys[4:5]
        span = slice(i * lanes, (i + 1) * lanes)
        wide = slice(half_block * layout.local + i * lanes, half_block * layout.local + (i + 1) * lanes)
        for e, sign in ((0, 1.0), (1, -1.0)):
            both_c = big_xc * shift_c - sign * (big_xs * shift_s)
            both_s = big_xs * shift_c + sign * (big_xc * shift_s)
            cosines, sines = [], []
            for a in range(half // 8):
                c, s = both_c[a : a + 1], both_s[a : a + 1]
                cosines.append(c * fine_xc - s * fine_xs)
                sines.append(s * fine_xc + c * fine_xs)
            table_x[pair, 2 * half * e : 2 * half * (e + 1), wide] = jnp.concatenate(cosines + sines, 0).astype(bf16)
        cosines, sines = [], []
        for a in range(quarter // 8):
            c, s = big_yc[a : a + 1], big_ys[a : a + 1]
            cosines.append(c * fine_yc - s * fine_ys)
            sines.append(s * fine_yc + c * fine_ys)
        last = jnp.concatenate([big_yc[5:6], big_ys[5:6], jnp.zeros((6, lanes), f32)], 0)
        table_y[block, :, span] = jnp.concatenate(cosines + sines + [last], 0)


def pick_half(layout, rows, other):
    count = layout.part_v
    core = lax.axis_index("wave")
    upper = jnp.broadcast_to(1 - core if other else core, (count, lanes)) == 1
    return jnp.where(upper, rows[count:], rows[:count])


def both_halves(layout, own, other):
    upper = jnp.broadcast_to(lax.axis_index("wave"), own.shape) == 1
    return jnp.concatenate([jnp.where(upper, other, own), jnp.where(upper, own, other)], 0)


def twist(layout, pair, half_block, density, table_y, out, halves):
    vectors, group = layout.vectors, 2 * layout.quarter
    block = 2 * pair + half_block
    for i in range(layout.tiles):
        span = slice(i * lanes, (i + 1) * lanes)
        wide = slice(half_block * layout.local + i * lanes, half_block * layout.local + (i + 1) * lanes)
        values = density[block, i * 2 * vectors : (i + 1) * 2 * vectors, :].astype(f32)
        waves = table_y[block, :group, span]
        c, s = table_y[block, group : group + 1, span], table_y[block, group + 1 : group + 2, span]
        start = 0
        for other in halves:
            real, imag = pick_half(layout, values[:vectors], other), pick_half(layout, values[vectors:], other)
            turned = (real * c - imag * s, imag * c + real * s)
            for v in range(layout.part_v):
                for part in range(2):
                    out[start : start + group, wide] = (turned[part][v : v + 1] * waves).astype(bf16)
                    start += group


def project(layout, base, density, table_x, table_y, twisted, total, start, halves, with_tables):
    def step(pair, before):
        for half_block in range(2):
            if with_tables:
                make_tables(layout, base, pair, half_block, density, table_x, table_y)
            twist(layout, pair, half_block, density, table_y, twisted, halves)
        product = lax.dot_general(
            twisted[...], table_x[pair], (((1,), (1,)), ((), ())), preferred_element_type=f32
        )
        total[...] = product if before is None else before[...] + product

    step(0, start)
    pairs = density.shape[0] // 2
    if pairs > 1:
        lax.fori_loop(1, pairs, lambda pair, carry: step(pair, total) or carry, 0)


def part_kernel(layout, base, with_start, with_tables, halves, *refs):
    refs = list(refs)
    density = refs.pop(0)
    tables = None if with_tables else (refs.pop(0), refs.pop(0))
    start = refs.pop(0) if with_start else None
    total = refs.pop(0)
    table_x, table_y = tables or (refs.pop(0), refs.pop(0))
    twisted = refs.pop(0)
    if len(halves) == 1:
        size = twisted.shape[0]
        start = start.at[size * halves[0] : size * (halves[0] + 1)]
    held = refs.pop(0) if refs else total
    project(layout, base, density, table_x, table_y, twisted, held, start, halves, with_tables)
    if held is not total:
        total[...] = held[...].astype(total.dtype)


def table_kernel(layout, base, density, table_x, table_y):
    make_tables(layout, base, 0, 0, density, table_x, table_y)


def swap(value):
    return pltpu.roll(value, lanes // 2, 1)


def weigh(layout, total, weight, scaled):
    quarter = layout.quarter
    first = lax.axis_index("wave") * layout.part_v
    low = lax.broadcasted_iota(jnp.int32, (quarter, lanes), 1) < layout.half
    sign = jnp.where(low, -1.0, 1.0)
    for v in range(layout.part_v):
        table = weight[first + v]
        part = [table[k * quarter : (k + 1) * quarter] for k in range(4)]
        choices = ((part[1], part[3]), (part[2], part[0]), (part[0], part[2]), (part[3], part[1]))
        for e in range(2):
            span = slice(e * lanes, (e + 1) * lanes)
            real = v * 4 * quarter
            imag = real + 2 * quarter
            cos_r = total[real : real + quarter, span]
            sin_r = swap(total[real + quarter : real + 2 * quarter, span]) * sign
            cos_i = total[imag : imag + quarter, span]
            sin_i = swap(total[imag + quarter : imag + 2 * quarter, span]) * sign
            out = []
            for k, (mr, mi) in enumerate(((cos_r + sin_r, cos_i + sin_i), (cos_r - sin_r, cos_i - sin_i))):
                chosen = jnp.where(low, *choices[2 * e + k])
                turned = swap(chosen)
                plus, minus = chosen + turned, chosen - turned
                out.append((plus * mr + minus * swap(mi), plus * mi - minus * swap(mr)))
            for start, k in ((real, 0), (imag, 1)):
                scaled[start : start + quarter, span] = (out[0][k] + out[1][k]).astype(bf16)
                scaled[start + quarter : start + 2 * quarter, span] = swap(sign * (out[0][k] - out[1][k])).astype(bf16)


def expand(layout, scaled, table_x, table_y, summed, result):
    count, group = layout.part_v, 2 * layout.quarter
    summed[...] = jnp.dot(scaled[...], table_x[0, :, : layout.local], preferred_element_type=f32)
    for i in range(layout.tiles):
        span = slice(i * lanes, (i + 1) * lanes)
        waves = table_y[0, :group, span]
        rows = []
        for k in range(2 * count):
            rows.append(jnp.sum(summed[k * group : (k + 1) * group, span] * waves, 0, keepdims=True))
        real, imag = jnp.concatenate(rows[0::2], 0), jnp.concatenate(rows[1::2], 0)
        c, s = table_y[0, group : group + 1, span], table_y[0, group + 1 : group + 2, span]
        result[2 * count * i : 2 * count * (i + 1), :] = jnp.concatenate([real * c + imag * s, imag * c - real * s], 0)


def far_kernel(layout, own, arrived, weight, own_x, own_y, other_x, other_y, far_own, far_other, total, scaled, summed):
    total[...] = own[...] + arrived[...].astype(f32)
    weigh(layout, total, weight, scaled)
    expand(layout, scaled, other_x, other_y, summed, far_other)
    expand(layout, scaled, own_x, own_y, summed, far_own)


def far_rows(layout, i, own, other):
    count = layout.part_v
    real, imag = [
        both_halves(layout, own[start : start + count, :], other[start : start + count, :])
        for start in (2 * count * i, 2 * count * i + count)
    ]
    return real, imag


def near_tile(layout, i, neighbor, density, kernel):
    vectors = layout.vectors
    g = lax.axis_index("tile") * layout.strips + i // layout.tiles_y
    h = lax.axis_index("wave") * layout.tiles_y + i % layout.tiles_y
    by_real, by_imag = 0.0, 0.0
    for j in range(9):
        slot = neighbor[i, j]
        step_x = lax.div(slot, 3)
        gx = lax.rem(g + step_x - 1 + layout.count_x, layout.count_x)
        hy = lax.rem(h + slot - 3 * step_x - 1 + layout.count_y, layout.count_y)
        block = layout.block_of(lax.div(gx, layout.strips) * layout.waves + lax.div(hy, layout.tiles_y))
        tile = lax.rem(gx, layout.strips) * layout.tiles_y + lax.rem(hy, layout.tiles_y)
        start = pl.multiple_of(tile * 2 * vectors, 2 * vectors)
        values = density[block, pl.ds(start, 2 * vectors), :]
        by_real += jnp.dot(values, kernel[i, j, 0], preferred_element_type=f32)
        by_imag += jnp.dot(values, kernel[i, j, 1], preferred_element_type=f32)
    return jnp.concatenate(
        [by_real[:vectors] - by_imag[vectors:], by_imag[:vectors] + by_real[vectors:]], 0
    )


def near_kernel(layout, density, blocks, neighbor, out, places, sem):
    copy = pltpu.make_async_copy(neighbor, places, sem)
    copy.start()
    copy.wait()
    tall = 2 * layout.vectors
    for i in range(layout.tiles):
        out[i * tall : (i + 1) * tall, :] = near_tile(layout, i, places, density, blocks)


def spread(layout, row_of):
    spot = lax.broadcasted_iota(jnp.int32, (layout.vectors, lanes), 0)
    lane = lax.broadcasted_iota(jnp.int32, (layout.vectors, lanes), 1)
    return [lane == spot + k * layout.vectors for k in row_of]


def first_kernel(layout, density, near, far_own, far_other, guess, squares, basis, image):
    vectors, tall, rows = layout.vectors, 2 * layout.vectors, layout.rows
    hint = guess[...]
    sums = [squares[...]] + [0.0] * 4
    for i in range(layout.tiles):
        first = i * tall
        far_real, far_imag = far_rows(layout, i, far_own, far_other)
        own = density[first : first + tall, :].astype(f32)
        rr, ri = own[:vectors], own[vectors:]
        wr = 0.5 * rr + near[first : first + vectors, :] + far_real
        wi = 0.5 * ri + near[first + vectors : first + tall, :] + far_imag
        zr, zi = wr - hint * rr, wi - hint * ri
        image[first : first + tall, :] = jnp.concatenate([wr, wi], 0)
        basis[first : first + tall, :] = jnp.concatenate([zr, zi], 0).astype(bf16)
        terms = (rr * rr + ri * ri, rr * zr + ri * zi, rr * zi - ri * zr, zr * zr + zi * zi)
        sums = sums[:1] + [a + b for a, b in zip(sums[1:], terms)]
    line = jnp.zeros((vectors, lanes), f32)
    for value, place in zip(sums, spread(layout, range(5))):
        line = line + jnp.where(place, jnp.sum(value, 1, keepdims=True), 0.0)
    basis[rows:, :] = three_parts(jnp.sum(line, 0, keepdims=True), layout.sum_rows - 3)


def scalar_kernel(layout, density, guess, scalars, factors):
    vectors, rows = layout.vectors, layout.rows
    line = jnp.zeros((1, lanes), f32)
    for device in range(layout.devices):
        line = line + add_three(density[layout.block_of(device), rows:, :].astype(f32), 1)
    line = jnp.broadcast_to(line * (1.0 / layout.panels), (vectors, lanes))
    exact, squares, real, imag, rest = [
        jnp.broadcast_to(jnp.sum(jnp.where(place, line, 0.0), 1, keepdims=True), (vectors, lanes))
        for place in spread(layout, range(5))
    ]
    hint = guess[...]
    scale_sq = exact + eps_norm
    coef_real = (real + hint * squares) / scale_sq
    coef_imag = imag / scale_sq
    more_real, more_imag = coef_real - hint, coef_imag
    update_sq = rest - 2.0 * (more_real * real + more_imag * imag) + (more_real * more_real + more_imag * more_imag) * squares
    scale = jnp.sqrt(scale_sq)
    update_scale = jnp.sqrt(jnp.maximum(update_sq, 0.0) / scale_sq + eps_norm)
    here = spread(layout, [0])[0]
    lines = [
        jnp.sum(jnp.where(here, value, 0.0), 0, keepdims=True)
        for value in (scale, coef_real, coef_imag, update_scale)
    ]
    scalars[...] = jnp.concatenate(lines, 0)[:, :vectors]
    factors[...] = jnp.concatenate([more_real, more_imag, 1.0 / (scale * update_scale)], 0)


def second_kernel(layout, density, near, far_own, far_other, image, factors, result):
    vectors, tall = layout.vectors, 2 * layout.vectors
    more_real, more_imag = factors[:vectors, :], factors[vectors : 2 * vectors, :]
    inverse = factors[2 * vectors :, :]
    for i in range(layout.tiles):
        first = i * tall
        far_real, far_imag = far_rows(layout, i, far_own, far_other)
        own = density[first : first + tall, :].astype(f32)
        wr, wi = image[first : first + vectors, :], image[first + vectors : first + tall, :]
        real = 0.5 * own[:vectors] + near[first : first + vectors, :] + far_real
        imag = 0.5 * own[vectors:] + near[first + vectors : first + tall, :] + far_imag
        result[first : first + vectors, :] = (real - (more_real * wr - more_imag * wi)) * inverse
        result[first + vectors : first + tall, :] = (imag - (more_real * wi + more_imag * wr)) * inverse


def per_device(residual, kernel, offsets, neighbor, frequency, lattice_x, lattice_y, spectral_weight):
    strips, tiles_y, _, vectors, _ = residual.shape
    modes_x, modes_y = spectral_weight.shape[1:]
    layout = Layout(strips, tiles_y, vectors, modes_x)
    tiles, rows, devices = layout.tiles, layout.rows, layout.devices
    vmem, hbm = pl.BlockSpec(memory_space=pltpu.VMEM), pl.BlockSpec(memory_space=pltpu.HBM)
    shape = jax.ShapeDtypeStruct
    tall = 2 * vectors * 2 * layout.quarter
    wide = 4 * layout.half
    count = spectral_weight.shape[0]

    def call(body, name, out_shape, in_specs, limit, scratch=(), flops=0, aliases=None):
        return pl.pallas_call(
            body,
            out_shape=out_shape,
            in_specs=in_specs,
            out_specs=jax.tree.map(lambda _: vmem, out_shape),
            scratch_shapes=scratch,
            input_output_aliases=aliases or {},
            compiler_params=pltpu.CompilerParams(vmem_limit_bytes=int(limit * mib)),
            cost_estimate=pl.CostEstimate(flops=flops, bytes_accessed=0, transcendentals=0),
            name=name,
        )

    head = jnp.concatenate([residual.reshape(rows, lanes), offsets.reshape(2 * tiles, lanes)], 0)
    packed, squares = call(
        lambda *refs: pack_kernel(layout, *refs),
        "pack",
        (shape((rows + layout.offset_rows, lanes), bf16), shape((vectors, lanes), f32)),
        [vmem],
        1,
    )(head)
    scale = 1.0 / math.sqrt(modes_x * modes_y * layout.panels)
    table = jnp.concatenate(
        [spectral_weight.reshape(-1, lanes), lattice_x.astype(f32)[None], lattice_y.astype(f32)[None]], 0
    )
    weight, guess = call(
        lambda *refs: spectral_kernel(layout, scale, *refs),
        "spectral",
        (shape((vectors, modes_y, modes_x), f32), shape((vectors, lanes), f32)),
        [vmem, hbm],
        4,
        [
            pltpu.SMEM(frequency.shape, jnp.int32),
            pltpu.VMEM(spectral_weight.shape, f32),
            pltpu.SemaphoreType.DMA,
        ],
        flops=12 * count * modes_x**3,
    )(table, frequency)
    blocks = kernel.reshape(tiles, 9, 2, lanes, lanes)
    neighbor = neighbor.reshape(tiles, 9)

    def table_shapes(size):
        return (
            shape((-(-size // 2), wide, min(size, 2) * layout.local), bf16),
            shape((size, 2 * layout.quarter + 8, layout.local), f32),
        )

    def part_call(name, base, part, tables, total, halves, dtype):
        size = part.shape[0]
        high = len(halves) * tall // 2
        given = [part] + list(tables or ()) + ([] if total is None else [total])
        scratch = [pltpu.VMEM((high, 2 * layout.local), bf16)]
        if dtype != f32:
            scratch.append(pltpu.VMEM((high, wide), f32))
        with_start = total is not None
        return call(
            lambda *refs: part_kernel(layout, base, with_start, not tables, halves, *refs),
            name,
            (shape((high, wide), dtype), *(() if tables else table_shapes(size))),
            [vmem] * len(given),
            24,
            scratch,
            flops=size * 2 * layout.local * high * wide,
            aliases={len(given) - 1: 0} if with_start and len(halves) == 2 else None,
        )(*given)

    def far_field(parts, tables, arrive):
        total, base, made = None, 0, []
        for k, part in enumerate(parts[:-1]):
            total, *new = part_call("part", base, part, tables and tables[k], total, (0, 1), f32)
            base += part.shape[0]
            made.append(new or tables[k])
        leaving, *new = part_call("leaving", base, parts[-1], tables and tables[-1], total, (1,), bf16)
        made.append(new or tables[-1])
        arrived = swap_cores(leaving)
        (staying,) = part_call("staying", base, parts[-1], made[-1], total, (0,), f32)
        far_own, far_other = call(
            lambda *refs: far_kernel(layout, *refs),
            "far",
            tuple([shape((rows // 2, lanes), f32)] * 2),
            [vmem] * 7,
            24,
            [
                pltpu.VMEM((tall // 2, wide), f32),
                pltpu.VMEM((tall // 2, wide), bf16),
                pltpu.VMEM((tall // 2, layout.local), f32),
            ],
            flops=2 * tall * wide * layout.local,
        )(staying, arrived, weight, *made[0], *arrive)
        return far_own, swap_cores(far_other), made

    def near_field(density):
        return call(
            lambda *refs: near_kernel(layout, *refs),
            "near",
            shape((rows, lanes), f32),
            [vmem, vmem, hbm],
            12,
            [pltpu.SMEM(neighbor.shape, jnp.int32), pltpu.SemaphoreType.DMA],
            flops=2 * tiles * 9 * 2 * lanes * lanes * 2 * vectors,
        )(density, blocks, neighbor)

    def with_other_core(array):
        return jnp.concatenate([array, swap_cores(array)])

    other_tables = call(
        lambda *refs: table_kernel(layout, devices // 2, *refs),
        "other_tables",
        table_shapes(1),
        [vmem],
        8,
        flops=layout.local * wide * 100,
    )(swap_cores(packed)[None])
    gathered, parts = gather_parts(packed, layout)
    near_one = near_field(with_other_core(gathered))
    far_own, far_other, tables = far_field(parts, None, other_tables)
    basis, image = call(
        lambda *refs: first_kernel(layout, *refs),
        "first",
        (shape((rows + layout.sum_rows, lanes), bf16), shape((rows, lanes), f32)),
        [vmem] * 6,
        2,
    )(packed, near_one, far_own, far_other, guess, squares)
    gathered, parts = gather_parts(basis, layout)
    everything = with_other_core(gathered)
    scalars, factors = call(
        lambda *refs: scalar_kernel(layout, *refs),
        "scalars",
        (shape((4, vectors), f32), shape((3 * vectors, lanes), f32)),
        [vmem] * 2,
        2,
    )(everything, guess)
    near_two = near_field(everything)
    far_own, far_other, _ = far_field(parts, tables, other_tables)
    result = call(
        lambda *refs: second_kernel(layout, *refs),
        "second",
        shape((rows, lanes), f32),
        [vmem] * 6,
        2,
    )(basis, near_two, far_own, far_other, image, factors)
    return result.reshape(residual.shape), scalars


def solution(mesh):
    return jax.shard_map(
        per_device,
        mesh=mesh,
        in_specs=(
            P(("grp", "tile"), "wave", None, None, None),
            P(("grp", "tile"), "wave", None, None, None, None),
            P(("grp", "tile"), "wave", None, None),
            P(("grp", "tile"), "wave", None),
            P("grp"),
            P(),
            P(),
            P(),
        ),
        out_specs=(P(("grp", "tile"), "wave", None, None, None), P("grp", None)),
        check_vma=False,
    )
```

time: 72.5 us -> 43.7 us (0.60)
  Pallas kernels: 37.6 us -> 16.1 us
  other arithmetic: 4.43 us -> 1.53 us
  waiting for transfers between devices: 13.6 us -> 11.4 us
  starting transfers between devices: 12.5 us -> 11.2 us
    pallas_call x3 -> x17, Pallas kernels: 34.4 us -> 14.7 us  [the longest x8 8.58 us: part_call(): call(lambda *refs: part_kernel(layout, base, with_start, not tables, halv...]
    concatenate x6 -> x7, other arithmetic: 4.43 us -> 0.86 us  [the longest x1 0.78 us: per_device(): jnp.concatenate([residual.reshape(rows, lanes), offsets.reshape(2 * tiles...]
    ppermute x8 -> x13, waiting for transfers between devices: 13.6 us -> 11.4 us  [the longest x6 11.4 us: gather_parts(): arrived = lax.ppermute(array, ('tile', 'wave'), pairs)]
    pallas_call x1, Pallas kernels: 3.18 us -> 1.42 us  [per_device(): call(lambda *refs: spectral_kernel(layout, scale, *refs), 'spectral', (sh...]
    unnamed x12 -> x14, local copies, waits for them, and re-layouts: 2.97 us -> 1.27 us
    ppermute x8 -> x13, starting transfers between devices: 12.5 us -> 11.2 us  [the longest x6 9.01 us: gather_parts(): arrived = lax.ppermute(array, ('tile', 'wave'), pairs)]
    concatenate x2 -> x3, local copies, waits for them, and re-layouts: 0.05 us -> 1.13 us  [the longest x1 1.08 us: per_device(): jnp.concatenate([spectral_weight.reshape(-1, lanes), lattice_x.astype(f32...]
  transfers between devices with their start and end apart: 8 -> 13, of which waited for: 7 -> 5; matrix products, arithmetic and copies ran while one was open for 2% -> 4% of each run, Pallas kernels for 4% -> 29%
where the time goes in v3:
time: 43.7 us; the launch traced here: 43.5 us
  Pallas kernels  16.1 us (37%)
  waiting for transfers between devices  11.4 us (26%)
  starting transfers between devices  11.2 us (26%)
  local copies, waits for them, and re-layouts  2.4 us (5%)
  other arithmetic  1.53 us (4%)
  between operations  0.88 us (2%)
    ppermute x6, waiting for transfers between devices, gather_parts(): arrived = lax.ppermute(array, ('tile', 'wave'), pairs)  11.4 us
    ppermute x6, starting transfers between devices, gather_parts(): arrived = lax.ppermute(array, ('tile', 'wave'), pairs)  9.01 us
    pallas_call x8, Pallas kernels, part_call(): call(lambda *refs: part_kernel(layout, base, with_start, not tables, halv...  8.58 us
    pallas_call x2, Pallas kernels, near_field(): call(lambda *refs: near_kernel(layout, *refs), 'near', shape((rows, lanes...  2.63 us
    ppermute x7, starting transfers between devices, swap_cores(): return lax.ppermute(array, 'wave', [(0, 1), (1, 0)])  2.17 us
    pallas_call x2, Pallas kernels, far_field(): call(lambda *refs: far_kernel(layout, *refs), 'far', tuple([shape((rows /...  1.69 us
    pallas_call x1, Pallas kernels, per_device(): call(lambda *refs: spectral_kernel(layout, scale, *refs), 'spectral', (sh...  1.42 us
    unnamed x14, local copies, waits for them, and re-layouts  1.27 us
  transfers between devices with their start and end apart: 13, of which 5 were waited for; matrix products, arithmetic and copies ran while one was open for 4% of the time, Pallas kernels for 29%

profile of v3, /device:TPU:0, one launch (start us, length us, event | category | flops | bytes accessed | tf_op | source)
XLA Modules:
  0.0 43.5 jit_solution(1104297906557801288)
XLA Ops:
  1.9 3.7 %collective-permute-start = (bf16[1,96,128]{2,1,0:T(8,128)(2,1)S(1)}, bf16[1,96,128]{2,1,0:T(8,128)(2,1)S(1)}, u32[]{:S(2)}, u32[]{:S(2)}) collective-permute-start(bf16[1,96,128]{2,1,0:T(8,128)(2,1)S(1)} %bitcast.17), channel_id=1, source_target_pairs={{0,9},{1,8},{2,11},{3,10},{4,13},{5,12},{6,15},{7,14},{8,1},{9,0},... | collective-permute-start | bytes 73736 | tf_op jit(solution)/shard_map/ppermute | solution.py:83
  6.3 1.1 %concatenate.41.refs_0_ = f32[1026,128]{1,0:T(8,128)S(1)} concatenate(f32[1024,128]{1,0:T(8,128)} %bitcast.28, f32[1,128]{1,0:T(1,128)S(1)} %get-tuple-element.49, f32[1,128]{1,0:T(1,128)S(1)} %get-tuple-element.48), dimensions={0} | concatenate | bytes 1050624 | tf_op jit(solution)/shard_map/concatenate | solution.py:447
  8.1 1.4 %spectral.1 = (f32[8,128,128]{2,1,0:T(8,128)S(1)}, f32[8,128]{1,0:T(8,128)S(1)}) custom-call(f32[1026,128]{1,0:T(8,128)S(1)} %concatenate.41.refs_0_, s32[8]{0:T(128)S(1)} %copy-done.2), custom_call_target="tpu_custom_call" | custom-call | flops 201326592 | tf_op jit(solution)/shard_map/spectral/pallas_call | solution.py:450
  9.5 1.3 %collective-permute-start.1 = (bf16[2,96,128]{2,1,0:T(8,128)(2,1)S(1)}, bf16[2,96,128]{2,1,0:T(8,128)(2,1)S(1)}, u32[]{:S(2)}, u32[]{:S(2)}) collective-permute-start(bf16[2,96,128]{2,1,0:T(8,128)(2,1)S(1)} %pad_maximum_fusion.4.refs_0_), channel_id=1, source_target_pairs={{0,5},{1,4},{2,7},{3,6},{4,1},{5,0},{6,3},{7,2},{8,13},{9,12},{10,... | collective-permute-start | bytes 147464 | tf_op jit(solution)/shard_map/ppermute | solution.py:83
  11.0 2.3 %collective-permute-done.1.refs_0_ = bf16[2,96,128]{2,1,0:T(8,128)(2,1)S(1)} collective-permute-done((bf16[2,96,128]{2,1,0:T(8,128)(2,1)S(1)}, bf16[2,96,128]{2,1,0:T(8,128)(2,1)S(1)}, u32[]{:S(2)}, u32[]{:S(2)}) %collective-permute-start.1) | collective-permute-done | bytes 49184 | tf_op jit(solution)/shard_map/ppermute | solution.py:83
  13.4 1.3 %collective-permute-start.2 = (bf16[4,96,128]{2,1,0:T(8,128)(2,1)S(1)}, bf16[4,96,128]{2,1,0:T(8,128)(2,1)S(1)}, u32[]{:S(2)}, u32[]{:S(2)}) collective-permute-start(bf16[4,96,128]{2,1,0:T(8,128)(2,1)S(1)} %pad_maximum_fusion.2), channel_id=1, source_target_pairs={{0,3},{1,2},{2,1},{3,0},{4,7},{5,6},{6,5},{7,4},{8,11},{9,10},{10,... | collective-permute-start | bytes 294920 | tf_op jit(solution)/shard_map/ppermute | solution.py:83
  14.7 1.2 %part.4 = (f32[1024,256]{1,0:T(8,128)S(1)}, bf16[1,256,1024]{2,1,0:T(8,128)(2,1)S(1)}, f32[2,72,512]{2,1,0:T(8,128)S(1)}) custom-call(bf16[2,96,128]{2,1,0:T(8,128)(2,1)S(1)} %pad_maximum_fusion.4.refs_0_), custom_call_target="tpu_custom_call" | custom-call | flops 536870912 | tf_op jit(solution)/shard_map/part/pallas_call | solution.py:480
  15.9 1.3 %part.5 = (f32[1024,256]{1,0:T(8,128)S(1)}, bf16[1,256,1024]{2,1,0:T(8,128)(2,1)S(1)}, f32[2,72,512]{2,1,0:T(8,128)S(1)}) custom-call(bf16[2,96,128]{2,1,0:T(8,128)(2,1)S(1)} %collective-permute-done.1.refs_0_, f32[1024,256]{1,0:T(8,128)S(1)} %get-tuple-element.26.refs_1_), custom_call_target="tpu_custom_call", output_to_operand_aliasing={{0}: (1, {})} | custom-call | flops 536870912 | tf_op jit(solution)/shard_map/part/pallas_call | solution.py:480
  17.2 1.1 %collective-permute-done.2.refs_0_ = bf16[4,96,128]{2,1,0:T(8,128)(2,1)S(1)} collective-permute-done((bf16[4,96,128]{2,1,0:T(8,128)(2,1)S(1)}, bf16[4,96,128]{2,1,0:T(8,128)(2,1)S(1)}, u32[]{:S(2)}, u32[]{:S(2)}) %collective-permute-start.2) | collective-permute-done | bytes 98336 | tf_op jit(solution)/shard_map/ppermute | solution.py:83
  18.3 1.7 %leaving.2 = (bf16[512,256]{1,0:T(8,128)(2,1)S(1)}, bf16[2,256,1024]{2,1,0:T(8,128)(2,1)S(1)}, f32[4,72,512]{2,1,0:T(8,128)S(1)}) custom-call(bf16[4,96,128]{2,1,0:T(8,128)(2,1)S(1)} %collective-permute-done.2.refs_0_, f32[1024,256]{1,0:T(8,128)S(1)} %get-tuple-element.27.refs_1_.refs_3_), custom_call_target="tpu_custom_call" | custom-call | flops 536870912 | tf_op jit(solution)/shard_map/leaving/pallas_call | solution.py:480
  20.7 0.9 %staying.2.refs_0_ = f32[512,256]{1,0:T(8,128)S(1)} custom-call(bf16[4,96,128]{2,1,0:T(8,128)(2,1)S(1)} %collective-permute-done.2.refs_0_, bf16[2,256,1024]{2,1,0:T(8,128)(2,1)S(1)} %get-tuple-element.28.refs_1_, f32[4,72,512]{2,1,0:T(8,128)S(1)} %get-tuple-element.29.refs_2_, f32[1024,256]{1,0:T(8,128)S(1)} %get-tuple-element.27.refs_1_.refs_3_), custom_call_target="tpu_custom_call" | custom-call | flops 536870912 | tf_op jit(solution)/shard_map/staying/pallas_call | solution.py:480
  21.7 0.8 %far.2 = (f32[32,128]{1,0:T(8,128)S(1)}, f32[32,128]{1,0:T(8,128)S(1)}) custom-call(f32[512,256]{1,0:T(8,128)S(1)} %staying.2.refs_0_, bf16[512,256]{1,0:T(8,128)(2,1)S(1)} %collective-permute-done.4.refs_1_, f32[8,128,128]{2,1,0:T(8,128)S(1)} %get-tuple-element.31.refs_2_, bf16[1,256,1024]{2,1,0:T(8,128)(2,1)S(1)} %get-tuple-element.32.refs_3_.refs_1_, ...), custom_call_target="tpu_custom_call" | custom-call | flops 268435456 | tf_op jit(solution)/shard_map/far/pallas_call | solution.py:501
  23.3 1.3 %near.2.refs_1_ = f32[64,128]{1,0:T(8,128)S(1)} custom-call(bf16[16,96,128]{2,1,0:T(8,128)(2,1)S(1)} %constant_dynamic-update-slice_fusion.refs_0_, bf16[4,9,2,128,128]{4,3,2,1,0:T(8,128)(2,1)S(1)} %bitcast.15, s32[4,9]{1,0:T(4,128)S(1)} %bitcast.25), custom_call_target="tpu_custom_call" | custom-call | flops 37748736 | tf_op jit(solution)/shard_map/near/pallas_call | solution.py:517
  24.8 4.1 %collective-permute-done.7 = bf16[1,80,128]{2,1,0:T(8,128)(2,1)S(1)} collective-permute-done((bf16[1,80,128]{2,1,0:T(8,128)(2,1)S(1)}, bf16[1,80,128]{2,1,0:T(8,128)(2,1)S(1)}, u32[]{:S(2)}, u32[]{:S(2)}) %collective-permute-start.7) | collective-permute-done | bytes 20512 | tf_op jit(solution)/shard_map/ppermute | solution.py:83
  28.9 1.3 %collective-permute-start.8 = (bf16[2,80,128]{2,1,0:T(8,128)(2,1)S(1)}, bf16[2,80,128]{2,1,0:T(8,128)(2,1)S(1)}, u32[]{:S(2)}, u32[]{:S(2)}) collective-permute-start(bf16[2,80,128]{2,1,0:T(8,128)(2,1)S(1)} %pad_maximum_fusion.5.refs_0_), channel_id=1, source_target_pairs={{0,5},{1,4},{2,7},{3,6},{4,1},{5,0},{6,3},{7,2},{8,13},{9,12},{10,... | collective-permute-start | bytes 122888 | tf_op jit(solution)/shard_map/ppermute | solution.py:83
  31.0 1.5 %collective-permute-done.8.refs_0_ = bf16[2,80,128]{2,1,0:T(8,128)(2,1)S(1)} collective-permute-done((bf16[2,80,128]{2,1,0:T(8,128)(2,1)S(1)}, bf16[2,80,128]{2,1,0:T(8,128)(2,1)S(1)}, u32[]{:S(2)}, u32[]{:S(2)}) %collective-permute-start.8) | collective-permute-done | bytes 40992 | tf_op jit(solution)/shard_map/ppermute | solution.py:83
  32.5 1.3 %collective-permute-start.9 = (bf16[4,80,128]{2,1,0:T(8,128)(2,1)S(1)}, bf16[4,80,128]{2,1,0:T(8,128)(2,1)S(1)}, u32[]{:S(2)}, u32[]{:S(2)}) collective-permute-start(bf16[4,80,128]{2,1,0:T(8,128)(2,1)S(1)} %pad_maximum_fusion.3), channel_id=1, source_target_pairs={{0,3},{1,2},{2,1},{3,0},{4,7},{5,6},{6,5},{7,4},{8,11},{9,10},{10,... | collective-permute-start | bytes 245768 | tf_op jit(solution)/shard_map/ppermute | solution.py:83
  33.8 0.8 %part.7.refs_3_ = f32[1024,256]{1,0:T(8,128)S(1)} custom-call(bf16[2,80,128]{2,1,0:T(8,128)(2,1)S(1)} %collective-permute-done.8.refs_0_, bf16[1,256,1024]{2,1,0:T(8,128)(2,1)S(1)} %get-tuple-element.41.refs_1_, f32[2,72,512]{2,1,0:T(8,128)S(1)} %get-tuple-element.42.refs_2_, f32[1024,256]{1,0:T(8,128)S(1)} %part.6.refs_3_), custom_call_target="tpu_custom_call", output_to_operand_aliasing={{}: (3, {})} | custom-call | flops 536870912 | tf_op jit(solution)/shard_map/part/pallas_call | solution.py:480
  34.6 2.4 %collective-permute-done.9.refs_0_ = bf16[4,80,128]{2,1,0:T(8,128)(2,1)S(1)} collective-permute-done((bf16[4,80,128]{2,1,0:T(8,128)(2,1)S(1)}, bf16[4,80,128]{2,1,0:T(8,128)(2,1)S(1)}, u32[]{:S(2)}, u32[]{:S(2)}) %collective-permute-start.9) | collective-permute-done | bytes 81952 | tf_op jit(solution)/shard_map/ppermute | solution.py:83
  37.0 0.9 %leaving.3 = bf16[512,256]{1,0:T(8,128)(2,1)S(1)} custom-call(bf16[4,80,128]{2,1,0:T(8,128)(2,1)S(1)} %collective-permute-done.9.refs_0_, bf16[2,256,1024]{2,1,0:T(8,128)(2,1)S(1)} %get-tuple-element.28.refs_1_, f32[4,72,512]{2,1,0:T(8,128)S(1)} %get-tuple-element.29.refs_2_, f32[1024,256]{1,0:T(8,128)S(1)} %part.7.refs_3_), custom_call_target="tpu_custom_call" | custom-call | flops 536870912 | tf_op jit(solution)/shard_map/leaving/pallas_call | solution.py:480
  38.6 0.9 %staying.3.refs_0_ = f32[512,256]{1,0:T(8,128)S(1)} custom-call(bf16[4,80,128]{2,1,0:T(8,128)(2,1)S(1)} %collective-permute-done.9.refs_0_, bf16[2,256,1024]{2,1,0:T(8,128)(2,1)S(1)} %get-tuple-element.28.refs_1_, f32[4,72,512]{2,1,0:T(8,128)S(1)} %get-tuple-element.29.refs_2_, f32[1024,256]{1,0:T(8,128)S(1)} %part.7.refs_3_), custom_call_target="tpu_custom_call" | custom-call | flops 536870912 | tf_op jit(solution)/shard_map/staying/pallas_call | solution.py:480
  39.6 0.8 %far.3 = (f32[32,128]{1,0:T(8,128)S(1)}, f32[32,128]{1,0:T(8,128)S(1)}) custom-call(f32[512,256]{1,0:T(8,128)S(1)} %staying.3.refs_0_, bf16[512,256]{1,0:T(8,128)(2,1)S(1)} %collective-permute-done.11.refs_1_, f32[8,128,128]{2,1,0:T(8,128)S(1)} %get-tuple-element.31.refs_2_, bf16[1,256,1024]{2,1,0:T(8,128)(2,1)S(1)} %get-tuple-element.32.refs_3_.refs_1_, ...), custom_call_target="tpu_custom_call" | custom-call | flops 268435456 | tf_op jit(solution)/shard_map/far/pallas_call | solution.py:501
  40.7 0.8 %scalars.1 = (f32[4,8]{1,0:T(4,128)}, f32[24,128]{1,0:T(8,128)S(1)}) custom-call(bf16[16,80,128]{2,1,0:T(8,128)(2,1)S(1)} %constant_dynamic-update-slice_fusion.5.refs_0_, f32[8,128]{1,0:T(8,128)S(1)} %get-tuple-element.38.refs_4_.refs_1_), custom_call_target="tpu_custom_call" | custom-call | tf_op jit(solution)/shard_map/scalars/pallas_call | solution.py:550
  41.5 1.3 %near.3.refs_1_ = f32[64,128]{1,0:T(8,128)S(1)} custom-call(bf16[16,80,128]{2,1,0:T(8,128)(2,1)S(1)} %constant_dynamic-update-slice_fusion.5.refs_0_, bf16[4,9,2,128,128]{4,3,2,1,0:T(8,128)(2,1)S(1)} %bitcast.16, s32[4,9]{1,0:T(4,128)S(1)} %bitcast.26), custom_call_target="tpu_custom_call" | custom-call | flops 37748736 | tf_op jit(solution)/shard_map/near/pallas_call | solution.py:517
  (45 shorter events, 6.8 us)
Async XLA Ops:
  1.4 9.4 %collective-permute-start.5 = (bf16[96,128]{1,0:T(8,128)(2,1)S(1)}, bf16[96,128]{1,0:T(8,128)(2,1)S(1)}, u32[]{:S(2)}, u32[]{:S(2)}) collective-permute-start(bf16[96,128]{1,0:T(8,128)(2,1)S(1)} %get-tuple-element.25.refs_0_), channel_id=1, source_target_pairs={{0,1},{1,0},{2,3},{3,2},{4,5},{5,4},{6,7},{7,6},{8,9},{9,8},{10,11... | collective-permute-start | bytes 73736 | tf_op jit(solution)/shard_map/ppermute | solution.py:75
  1.9 7.6 %collective-permute-start = (bf16[1,96,128]{2,1,0:T(8,128)(2,1)S(1)}, bf16[1,96,128]{2,1,0:T(8,128)(2,1)S(1)}, u32[]{:S(2)}, u32[]{:S(2)}) collective-permute-start(bf16[1,96,128]{2,1,0:T(8,128)(2,1)S(1)} %bitcast.17), channel_id=1, source_target_pairs={{0,9},{1,8},{2,11},{3,10},{4,13},{5,12},{6,15},{7,14},{8,1},{9,0},... | collective-permute-start | bytes 73736 | tf_op jit(solution)/shard_map/ppermute | solution.py:83
  7.4 0.7 %copy-start.2 = (s32[8]{0:T(128)S(1)}, s32[8]{0:T(128)}, u32[]{:S(2)}) copy-start(s32[8]{0:T(128)} %refs_1_.1) | copy-start | bytes 100
  9.5 3.9 %collective-permute-start.1 = (bf16[2,96,128]{2,1,0:T(8,128)(2,1)S(1)}, bf16[2,96,128]{2,1,0:T(8,128)(2,1)S(1)}, u32[]{:S(2)}, u32[]{:S(2)}) collective-permute-start(bf16[2,96,128]{2,1,0:T(8,128)(2,1)S(1)} %pad_maximum_fusion.4.refs_0_), channel_id=1, source_target_pairs={{0,5},{1,4},{2,7},{3,6},{4,1},{5,0},{6,3},{7,2},{8,13},{9,12},{10,... | collective-permute-start | bytes 147464 | tf_op jit(solution)/shard_map/ppermute | solution.py:83
  13.4 4.9 %collective-permute-start.2 = (bf16[4,96,128]{2,1,0:T(8,128)(2,1)S(1)}, bf16[4,96,128]{2,1,0:T(8,128)(2,1)S(1)}, u32[]{:S(2)}, u32[]{:S(2)}) collective-permute-start(bf16[4,96,128]{2,1,0:T(8,128)(2,1)S(1)} %pad_maximum_fusion.2), channel_id=1, source_target_pairs={{0,3},{1,2},{2,1},{3,0},{4,7},{5,6},{6,5},{7,4},{8,11},{9,10},{10,... | collective-permute-start | bytes 294920 | tf_op jit(solution)/shard_map/ppermute | solution.py:83
  20.0 1.7 %collective-permute-start.4 = (bf16[512,256]{1,0:T(8,128)(2,1)S(1)}, bf16[512,256]{1,0:T(8,128)(2,1)S(1)}, u32[]{:S(2)}, u32[]{:S(2)}) collective-permute-start(bf16[512,256]{1,0:T(8,128)(2,1)S(1)} %get-tuple-element.30), channel_id=1, source_target_pairs={{0,1},{1,0},{2,3},{3,2},{4,5},{5,4},{6,7},{7,6},{8,9},{9,8},{10,11... | collective-permute-start | bytes 786440 | tf_op jit(solution)/shard_map/ppermute | solution.py:75
  20.2 2.5 %collective-permute-start.3 = (bf16[8,96,128]{2,1,0:T(8,128)(2,1)S(1)}, bf16[8,96,128]{2,1,0:T(8,128)(2,1)S(1)}, u32[]{:S(2)}, u32[]{:S(2)}) collective-permute-start(bf16[8,96,128]{2,1,0:T(8,128)(2,1)S(1)} %pad_maximum_fusion), channel_id=1, source_target_pairs={{0,1},{1,0},{2,3},{3,2},{4,5},{5,4},{6,7},{7,6},{8,9},{9,8},{10,11... | collective-permute-start | bytes 589832 | tf_op jit(solution)/shard_map/ppermute | solution.py:75
  21.6 1.7 %copy-start = (bf16[1,4,9,2,128,128]{5,4,3,2,1,0:T(8,128)(2,1)S(1)}, bf16[1,4,9,2,128,128]{5,4,3,2,1,0:T(8,128)(2,1)}, u32[]{:S(2)}) copy-start(bf16[1,4,9,2,128,128]{5,4,3,2,1,0:T(8,128)(2,1)} %param.9) | copy-start | bytes 7077892
  21.6 1.7 %copy-start.1 = (s32[1,4,9]{2,1,0:T(4,128)S(1)}, s32[1,4,9]{2,1,0:T(4,128)}, u32[]{:S(2)}) copy-start(s32[1,4,9]{2,1,0:T(4,128)} %param.11) | copy-start | bytes 436
  22.5 2.1 %collective-permute-start.6 = (f32[32,128]{1,0:T(8,128)S(1)}, f32[32,128]{1,0:T(8,128)S(1)}, u32[]{:S(2)}, u32[]{:S(2)}) collective-permute-start(f32[32,128]{1,0:T(8,128)S(1)} %get-tuple-element.37), channel_id=1, source_target_pairs={{0,1},{1,0},{2,3},{3,2},{4,5},{5,4},{6,7},{7,6},{8,9},{9,8},{10,11... | collective-permute-start | bytes 49160 | tf_op jit(solution)/shard_map/ppermute | solution.py:75
  24.8 4.2 %collective-permute-start.7 = (bf16[1,80,128]{2,1,0:T(8,128)(2,1)S(1)}, bf16[1,80,128]{2,1,0:T(8,128)(2,1)S(1)}, u32[]{:S(2)}, u32[]{:S(2)}) collective-permute-start(bf16[1,80,128]{2,1,0:T(8,128)(2,1)S(1)} %bitcast.21), channel_id=1, source_target_pairs={{0,9},{1,8},{2,11},{3,10},{4,13},{5,12},{6,15},{7,14},{8,1},{9,0},... | collective-permute-start | bytes 61448 | tf_op jit(solution)/shard_map/ppermute | solution.py:83
  28.9 3.6 %collective-permute-start.8 = (bf16[2,80,128]{2,1,0:T(8,128)(2,1)S(1)}, bf16[2,80,128]{2,1,0:T(8,128)(2,1)S(1)}, u32[]{:S(2)}, u32[]{:S(2)}) collective-permute-start(bf16[2,80,128]{2,1,0:T(8,128)(2,1)S(1)} %pad_maximum_fusion.5.refs_0_), channel_id=1, source_target_pairs={{0,5},{1,4},{2,7},{3,6},{4,1},{5,0},{6,3},{7,2},{8,13},{9,12},{10,... | collective-permute-start | bytes 122888 | tf_op jit(solution)/shard_map/ppermute | solution.py:83
  32.5 4.5 %collective-permute-start.9 = (bf16[4,80,128]{2,1,0:T(8,128)(2,1)S(1)}, bf16[4,80,128]{2,1,0:T(8,128)(2,1)S(1)}, u32[]{:S(2)}, u32[]{:S(2)}) collective-permute-start(bf16[4,80,128]{2,1,0:T(8,128)(2,1)S(1)} %pad_maximum_fusion.3), channel_id=1, source_target_pairs={{0,3},{1,2},{2,1},{3,0},{4,7},{5,6},{6,5},{7,4},{8,11},{9,10},{10,... | collective-permute-start | bytes 245768 | tf_op jit(solution)/shard_map/ppermute | solution.py:83
  38.0 1.6 %collective-permute-start.11 = (bf16[512,256]{1,0:T(8,128)(2,1)S(1)}, bf16[512,256]{1,0:T(8,128)(2,1)S(1)}, u32[]{:S(2)}, u32[]{:S(2)}) collective-permute-start(bf16[512,256]{1,0:T(8,128)(2,1)S(1)} %leaving.3), channel_id=1, source_target_pairs={{0,1},{1,0},{2,3},{3,2},{4,5},{5,4},{6,7},{7,6},{8,9},{9,8},{10,11... | collective-permute-start | bytes 786440 | tf_op jit(solution)/shard_map/ppermute | solution.py:75
  38.2 2.5 %collective-permute-start.10 = (bf16[8,80,128]{2,1,0:T(8,128)(2,1)S(1)}, bf16[8,80,128]{2,1,0:T(8,128)(2,1)S(1)}, u32[]{:S(2)}, u32[]{:S(2)}) collective-permute-start(bf16[8,80,128]{2,1,0:T(8,128)(2,1)S(1)} %pad_maximum_fusion.1), channel_id=1, source_target_pairs={{0,1},{1,0},{2,3},{3,2},{4,5},{5,4},{6,7},{7,6},{8,9},{9,8},{10,11... | collective-permute-start | bytes 491528 | tf_op jit(solution)/shard_map/ppermute | solution.py:75
  40.5 2.3 %collective-permute-start.12 = (f32[32,128]{1,0:T(8,128)S(1)}, f32[32,128]{1,0:T(8,128)S(1)}, u32[]{:S(2)}, u32[]{:S(2)}) collective-permute-start(f32[32,128]{1,0:T(8,128)S(1)} %get-tuple-element.44), channel_id=1, source_target_pairs={{0,1},{1,0},{2,3},{3,2},{4,5},{5,4},{6,7},{7,6},{8,9},{9,8},{10,11... | collective-permute-start | bytes 49160 | tf_op jit(solution)/shard_map/ppermute | solution.py:75

commit v4 on v3

--- a/solution.py
+++ b/solution.py
@@ -8,6 +8,7 @@
 from jax.sharding import PartitionSpec as P
 
 eps_norm = 1e-06
+lengths = {"part": 1, "leaving": 1, "staying": 2, "spectral": 2, "other_tables": 0.5, "far": 1, "near": 2}
 f32 = jnp.float32
 bf16 = jnp.bfloat16
 lanes = 128
@@ -60,6 +61,9 @@
             device = device ^ (((block >> k) & 1) * mask)
         return device
 
+    def group_of(self, density):
+        return min(density.shape[0], 4)
+
     def block_of(self, device):
         rest = device ^ self.me()
         block = 0
@@ -75,15 +79,8 @@
     return lax.ppermute(array, "wave", [(0, 1), (1, 0)])
 
 
-def gather_parts(array, layout):
-    array = array[None]
-    parts = []
-    for mask in layout.chip_masks:
-        pairs = [(i, i ^ mask) for i in range(layout.devices)]
-        arrived = lax.ppermute(array, ("tile", "wave"), pairs)
-        array = jnp.concatenate([array, arrived])
-        parts.append(arrived if parts else array)
-    return array, parts
+def after(value, *others):
+    return lax.optimization_barrier((value, *others))[0]
 
 
 def three_parts(value, pad):
@@ -120,31 +117,31 @@
     return total
 
 
-def spectral_kernel(layout, scale, table, frequency, out, guess, order, moved_all, sem):
+def spectral_kernel(layout, scale, integers, table, out, guess, order, moved_all, sem):
     size = 2 * layout.half
     count = moved_all.shape[0]
-    copy = pltpu.make_async_copy(frequency, order, sem)
+    copy = pltpu.make_async_copy(integers.at[2:3], order, sem)
     copy.start()
     spot = lax.broadcasted_iota(jnp.int32, (size, size), 0)
-    wanted = jnp.where(spot < layout.half, spot + layout.half, size - 1 - spot).astype(f32)
-    pick_x = jnp.where(wanted == table[count * size : count * size + 1], 1.0, 0.0).astype(bf16)
-    pick_y = jnp.where(wanted == table[count * size + 1 : count * size + 2], 1.0, 0.0).astype(bf16)
+    wanted = jnp.where(spot < layout.half, spot + layout.half, size - 1 - spot)
+    pick_x = jnp.where(wanted == integers[0:1], 1.0, 0.0).astype(bf16)
+    pick_y = jnp.where(wanted == integers[1:2], 1.0, 0.0).astype(bf16)
     for f in range(count):
-        moved = split_dot(pick_x, table[f * size : (f + 1) * size] * scale, (((1,), (0,)), ((), ())))
+        moved = split_dot(pick_x, table[f] * scale, (((1,), (0,)), ((), ())))
         moved_all[f] = split_dot(pick_y, moved, (((1,), (1,)), ((), ())))
     copy.wait()
     rows = []
     for v in range(layout.vectors):
-        moved = moved_all[order[v]]
+        moved = moved_all[order[0, v]]
         out[v] = moved
         mean = jnp.sum(jnp.sum(moved, 0, keepdims=True), 1, keepdims=True)
         rows.append(jnp.broadcast_to(0.5 + mean, (1, lanes)))
     guess[...] = jnp.concatenate(rows, 0)
 
 
-def make_tables(layout, base, pair, half_block, density, table_x, table_y):
+def make_tables(layout, base, group, k, density, table_x, table_y):
     tiles, half, quarter = layout.tiles, layout.half, layout.quarter
-    block = 2 * pair + half_block
+    block = layout.group_of(density) * group + k
     device = layout.device_of(base + block)
     column, row_index = device // layout.waves, device % layout.waves
     offset = add_three(density[block, layout.rows :, :].astype(f32), 2 * tiles)
@@ -161,7 +158,7 @@
         big_yc, big_ys = cos_sin(coarse_y * y + jnp.where(eight == 5, 0.5, 0.0) * x)
         shift_c, shift_s = big_yc[4:5], big_ys[4:5]
         span = slice(i * lanes, (i + 1) * lanes)
-        wide = slice(half_block * layout.local + i * lanes, half_block * layout.local + (i + 1) * lanes)
+        wide = slice(k * layout.local + i * lanes, k * layout.local + (i + 1) * lanes)
         for e, sign in ((0, 1.0), (1, -1.0)):
             both_c = big_xc * shift_c - sign * (big_xs * shift_s)
             both_s = big_xs * shift_c + sign * (big_xc * shift_s)
@@ -170,7 +167,7 @@
                 c, s = both_c[a : a + 1], both_s[a : a + 1]
                 cosines.append(c * fine_xc - s * fine_xs)
                 sines.append(s * fine_xc + c * fine_xs)
-            table_x[pair, 2 * half * e : 2 * half * (e + 1), wide] = jnp.concatenate(cosines + sines, 0).astype(bf16)
+            table_x[group, 2 * half * e : 2 * half * (e + 1), wide] = jnp.concatenate(cosines + sines, 0).astype(bf16)
         cosines, sines = [], []
         for a in range(quarter // 8):
             c, s = big_yc[a : a + 1], big_ys[a : a + 1]
@@ -192,12 +189,11 @@
     return jnp.concatenate([jnp.where(upper, other, own), jnp.where(upper, own, other)], 0)
 
 
-def twist(layout, pair, half_block, density, table_y, out, halves):
+def twist(layout, block, k, density, table_y, out, halves):
     vectors, group = layout.vectors, 2 * layout.quarter
-    block = 2 * pair + half_block
     for i in range(layout.tiles):
         span = slice(i * lanes, (i + 1) * lanes)
-        wide = slice(half_block * layout.local + i * lanes, half_block * layout.local + (i + 1) * lanes)
+        wide = slice(k * layout.local + i * lanes, k * layout.local + (i + 1) * lanes)
         values = density[block, i * 2 * vectors : (i + 1) * 2 * vectors, :].astype(f32)
         waves = table_y[block, :group, span]
         c, s = table_y[block, group : group + 1, span], table_y[block, group + 1 : group + 2, span]
@@ -212,20 +208,22 @@
 
 
 def project(layout, base, density, table_x, table_y, twisted, total, start, halves, with_tables):
-    def step(pair, before):
-        for half_block in range(2):
+    size = layout.group_of(density)
+
+    def step(group, before):
+        for k in range(size):
             if with_tables:
-                make_tables(layout, base, pair, half_block, density, table_x, table_y)
-            twist(layout, pair, half_block, density, table_y, twisted, halves)
+                make_tables(layout, base, group, k, density, table_x, table_y)
+            twist(layout, size * group + k, k, density, table_y, twisted, halves)
         product = lax.dot_general(
-            twisted[...], table_x[pair], (((1,), (1,)), ((), ())), preferred_element_type=f32
+            twisted[...], table_x[group], (((1,), (1,)), ((), ())), preferred_element_type=f32
         )
         total[...] = product if before is None else before[...] + product
 
     step(0, start)
-    pairs = density.shape[0] // 2
-    if pairs > 1:
-        lax.fori_loop(1, pairs, lambda pair, carry: step(pair, total) or carry, 0)
+    groups = density.shape[0] // size
+    if groups > 1:
+        lax.fori_loop(1, groups, lambda group, carry: step(group, total) or carry, 0)
 
 
 def part_kernel(layout, base, with_start, with_tables, halves, *refs):
@@ -295,10 +293,10 @@
         result[2 * count * i : 2 * count * (i + 1), :] = jnp.concatenate([real * c + imag * s, imag * c - real * s], 0)
 
 
-def far_kernel(layout, own, arrived, weight, own_x, own_y, other_x, other_y, far_own, far_other, total, scaled, summed):
+def far_kernel(layout, own, arrived, weight, own_x, own_y, other_x, other_y, far_own, far_other, total, scaled, summed, summed_other):
     total[...] = own[...] + arrived[...].astype(f32)
     weigh(layout, total, weight, scaled)
-    expand(layout, scaled, other_x, other_y, summed, far_other)
+    expand(layout, scaled, other_x, other_y, summed_other, far_other)
     expand(layout, scaled, own_x, own_y, summed, far_own)
 
 
@@ -315,7 +313,7 @@
     vectors = layout.vectors
     g = lax.axis_index("tile") * layout.strips + i // layout.tiles_y
     h = lax.axis_index("wave") * layout.tiles_y + i % layout.tiles_y
-    by_real, by_imag = 0.0, 0.0
+    values = []
     for j in range(9):
         slot = neighbor[i, j]
         step_x = lax.div(slot, 3)
@@ -324,18 +322,19 @@
         block = layout.block_of(lax.div(gx, layout.strips) * layout.waves + lax.div(hy, layout.tiles_y))
         tile = lax.rem(gx, layout.strips) * layout.tiles_y + lax.rem(hy, layout.tiles_y)
         start = pl.multiple_of(tile * 2 * vectors, 2 * vectors)
-        values = density[block, pl.ds(start, 2 * vectors), :]
-        by_real += jnp.dot(values, kernel[i, j, 0], preferred_element_type=f32)
-        by_imag += jnp.dot(values, kernel[i, j, 1], preferred_element_type=f32)
-    return jnp.concatenate(
-        [by_real[:vectors] - by_imag[vectors:], by_imag[:vectors] + by_real[vectors:]], 0
-    )
-
-
-def near_kernel(layout, density, blocks, neighbor, out, places, sem):
-    copy = pltpu.make_async_copy(neighbor, places, sem)
-    copy.start()
-    copy.wait()
+        values.append(density[block, pl.ds(start, 2 * vectors), :])
+    total = 0.0
+    for j in range(0, 9, 2):
+        span = range(j, min(j + 2, 9))
+        left = jnp.concatenate([values[k] for k in span], 1)
+        right = jnp.concatenate([jnp.concatenate([kernel[i, k, 0], kernel[i, k, 1]], 1) for k in span], 0)
+        total += jnp.dot(left, right, preferred_element_type=f32)
+    upper, lower = total[:vectors], total[vectors:]
+    return jnp.concatenate([upper[:, :lanes] - lower[:, lanes:], upper[:, lanes:] + lower[:, :lanes]], 0)
+
+
+def near_kernel(layout, density, blocks, neighbor, out):
+    places = neighbor[...]
     tall = 2 * layout.vectors
     for i in range(layout.tiles):
         out[i * tall : (i + 1) * tall, :] = near_tile(layout, i, places, density, blocks)
@@ -369,7 +368,7 @@
     basis[rows:, :] = three_parts(jnp.sum(line, 0, keepdims=True), layout.sum_rows - 3)
 
 
-def scalar_kernel(layout, density, guess, scalars, factors):
+def scalar_kernel(layout, density, guess, factors):
     vectors, rows = layout.vectors, layout.rows
     line = jnp.zeros((1, lanes), f32)
     for device in range(layout.devices):
@@ -392,14 +391,15 @@
         jnp.sum(jnp.where(here, value, 0.0), 0, keepdims=True)
         for value in (scale, coef_real, coef_imag, update_scale)
     ]
-    scalars[...] = jnp.concatenate(lines, 0)[:, :vectors]
-    factors[...] = jnp.concatenate([more_real, more_imag, 1.0 / (scale * update_scale)], 0)
-
-
-def second_kernel(layout, density, near, far_own, far_other, image, factors, result):
+    lines.append(jnp.zeros((vectors - 4, lanes), f32))
+    factors[...] = jnp.concatenate([more_real, more_imag, 1.0 / (scale * update_scale)] + lines, 0)
+
+
+def second_kernel(layout, density, near, far_own, far_other, image, factors, result, scalars):
     vectors, tall = layout.vectors, 2 * layout.vectors
     more_real, more_imag = factors[:vectors, :], factors[vectors : 2 * vectors, :]
-    inverse = factors[2 * vectors :, :]
+    inverse = factors[2 * vectors : 3 * vectors, :]
+    scalars[...] = factors[3 * vectors : 3 * vectors + 4, :vectors]
     for i in range(layout.tiles):
         first = i * tall
         far_real, far_imag = far_rows(layout, i, far_own, far_other)
@@ -416,13 +416,13 @@
     modes_x, modes_y = spectral_weight.shape[1:]
     layout = Layout(strips, tiles_y, vectors, modes_x)
     tiles, rows, devices = layout.tiles, layout.rows, layout.devices
-    vmem, hbm = pl.BlockSpec(memory_space=pltpu.VMEM), pl.BlockSpec(memory_space=pltpu.HBM)
+    vmem = pl.BlockSpec(memory_space=pltpu.VMEM)
     shape = jax.ShapeDtypeStruct
     tall = 2 * vectors * 2 * layout.quarter
     wide = 4 * layout.half
     count = spectral_weight.shape[0]
 
-    def call(body, name, out_shape, in_specs, limit, scratch=(), flops=0, aliases=None):
+    def call(body, name, out_shape, in_specs, limit, scratch=(), aliases=None):
         return pl.pallas_call(
             body,
             out_shape=out_shape,
@@ -431,7 +431,9 @@
             scratch_shapes=scratch,
             input_output_aliases=aliases or {},
             compiler_params=pltpu.CompilerParams(vmem_limit_bytes=int(limit * mib)),
-            cost_estimate=pl.CostEstimate(flops=flops, bytes_accessed=0, transcendentals=0),
+            cost_estimate=pl.CostEstimate(
+                flops=int(lengths.get(name, 0) * 1e9), bytes_accessed=0, transcendentals=0
+            ),
             name=name,
         )
 
@@ -444,28 +446,28 @@
         1,
     )(head)
     scale = 1.0 / math.sqrt(modes_x * modes_y * layout.panels)
-    table = jnp.concatenate(
-        [spectral_weight.reshape(-1, lanes), lattice_x.astype(f32)[None], lattice_y.astype(f32)[None]], 0
-    )
-    weight, guess = call(
-        lambda *refs: spectral_kernel(layout, scale, *refs),
-        "spectral",
-        (shape((vectors, modes_y, modes_x), f32), shape((vectors, lanes), f32)),
-        [vmem, hbm],
-        4,
-        [
-            pltpu.SMEM(frequency.shape, jnp.int32),
-            pltpu.VMEM(spectral_weight.shape, f32),
-            pltpu.SemaphoreType.DMA,
-        ],
-        flops=12 * count * modes_x**3,
-    )(table, frequency)
+    integers = jnp.stack([lattice_x, lattice_y, jnp.pad(frequency, (0, lanes - frequency.shape[0]))])
+
+    def spectral(integers):
+        return call(
+            lambda *refs: spectral_kernel(layout, scale, *refs),
+            "spectral",
+            (shape((vectors, modes_y, modes_x), f32), shape((vectors, lanes), f32)),
+            [vmem, vmem],
+            4,
+            [
+                pltpu.SMEM((1, lanes), jnp.int32),
+                pltpu.VMEM(spectral_weight.shape, f32),
+                pltpu.SemaphoreType.DMA,
+            ],
+        )(integers, spectral_weight)
+
     blocks = kernel.reshape(tiles, 9, 2, lanes, lanes)
     neighbor = neighbor.reshape(tiles, 9)
 
     def table_shapes(size):
         return (
-            shape((-(-size // 2), wide, min(size, 2) * layout.local), bf16),
+            shape((size // min(size, 4), wide, min(size, 4) * layout.local), bf16),
             shape((size, 2 * layout.quarter + 8, layout.local), f32),
         )
 
@@ -473,7 +475,7 @@
         size = part.shape[0]
         high = len(halves) * tall // 2
         given = [part] + list(tables or ()) + ([] if total is None else [total])
-        scratch = [pltpu.VMEM((high, 2 * layout.local), bf16)]
+        scratch = [pltpu.VMEM((high, min(size, 4) * layout.local), bf16)]
         if dtype != f32:
             scratch.append(pltpu.VMEM((high, wide), f32))
         with_start = total is not None
@@ -484,20 +486,28 @@
             [vmem] * len(given),
             24,
             scratch,
-            flops=size * 2 * layout.local * high * wide,
             aliases={len(given) - 1: 0} if with_start and len(halves) == 2 else None,
         )(*given)
 
-    def far_field(parts, tables, arrive):
-        total, base, made = None, 0, []
-        for k, part in enumerate(parts[:-1]):
-            total, *new = part_call("part", base, part, tables and tables[k], total, (0, 1), f32)
-            base += part.shape[0]
-            made.append(new or tables[k])
-        leaving, *new = part_call("leaving", base, parts[-1], tables and tables[-1], total, (1,), bf16)
+    def gather_and_project(array, tables):
+        array = array[None]
+        total, base, made, seen = None, 0, [], []
+        for k, mask in enumerate(layout.chip_masks):
+            pairs = [(i, i ^ mask) for i in range(devices)]
+            arrived = lax.ppermute(array, ("tile", "wave"), pairs)
+            array = jnp.concatenate([array, arrived])
+            seen.append(array)
+            part = arrived if k else array
+            if k < len(layout.chip_masks) - 1:
+                total, *new = part_call("part", base, part, tables and tables[k], total, (0, 1), f32)
+                base += part.shape[0]
+                made.append(new or tables[k])
+        leaving, *new = part_call("leaving", base, part, tables and tables[-1], total, (1,), bf16)
         made.append(new or tables[-1])
-        arrived = swap_cores(leaving)
-        (staying,) = part_call("staying", base, parts[-1], made[-1], total, (0,), f32)
+        (staying,) = part_call("staying", base, part, made[-1], total, (0,), f32)
+        return seen, leaving, staying, made
+
+    def far_field(leaving, staying, weight, own_tables, other_tables):
         far_own, far_other = call(
             lambda *refs: far_kernel(layout, *refs),
             "far",
@@ -508,36 +518,34 @@
                 pltpu.VMEM((tall // 2, wide), f32),
                 pltpu.VMEM((tall // 2, wide), bf16),
                 pltpu.VMEM((tall // 2, layout.local), f32),
+                pltpu.VMEM((tall // 2, layout.local), f32),
             ],
-            flops=2 * tall * wide * layout.local,
-        )(staying, arrived, weight, *made[0], *arrive)
-        return far_own, swap_cores(far_other), made
+        )(staying, swap_cores(leaving), weight, *own_tables, *other_tables)
+        return far_own, swap_cores(far_other)
 
     def near_field(density):
         return call(
             lambda *refs: near_kernel(layout, *refs),
             "near",
             shape((rows, lanes), f32),
-            [vmem, vmem, hbm],
+            [vmem] * 3,
             12,
-            [pltpu.SMEM(neighbor.shape, jnp.int32), pltpu.SemaphoreType.DMA],
-            flops=2 * tiles * 9 * 2 * lanes * lanes * 2 * vectors,
         )(density, blocks, neighbor)
 
     def with_other_core(array):
         return jnp.concatenate([array, swap_cores(array)])
 
+    seen, leaving, staying, tables = gather_and_project(packed, None)
     other_tables = call(
         lambda *refs: table_kernel(layout, devices // 2, *refs),
         "other_tables",
         table_shapes(1),
         [vmem],
         8,
-        flops=layout.local * wide * 100,
-    )(swap_cores(packed)[None])
-    gathered, parts = gather_parts(packed, layout)
-    near_one = near_field(with_other_core(gathered))
-    far_own, far_other, tables = far_field(parts, None, other_tables)
+    )(swap_cores(after(packed, seen[0]))[None])
+    weight, guess = spectral(after(integers, seen[1]))
+    near_one = near_field(with_other_core(seen[-1]))
+    far_own, far_other = far_field(leaving, staying, weight, tables[0], other_tables)
     basis, image = call(
         lambda *refs: first_kernel(layout, *refs),
         "first",
@@ -545,21 +553,21 @@
         [vmem] * 6,
         2,
     )(packed, near_one, far_own, far_other, guess, squares)
-    gathered, parts = gather_parts(basis, layout)
-    everything = with_other_core(gathered)
-    scalars, factors = call(
+    seen, leaving, staying, _ = gather_and_project(basis, tables)
+    everything = with_other_core(seen[-1])
+    factors = call(
         lambda *refs: scalar_kernel(layout, *refs),
         "scalars",
-        (shape((4, vectors), f32), shape((3 * vectors, lanes), f32)),
+        shape((4 * vectors, lanes), f32),
         [vmem] * 2,
         2,
     )(everything, guess)
     near_two = near_field(everything)
-    far_own, far_other, _ = far_field(parts, tables, other_tables)
-    result = call(
+    far_own, far_other = far_field(leaving, staying, weight, tables[0], other_tables)
+    result, scalars = call(
         lambda *refs: second_kernel(layout, *refs),
         "second",
-        shape((rows, lanes), f32),
+        (shape((rows, lanes), f32), shape((4, vectors), f32)),
         [vmem] * 6,
         2,
     )(basis, near_two, far_own, far_other, image, factors)

time: 43.7 us -> 39.7 us (0.908)
  waiting for transfers between devices: 11.4 us -> 6.02 us
  starting transfers between devices: 11.2 us -> 16.2 us
  Pallas kernels: 16.1 us -> 14.1 us
  local copies, waits for them, and re-layouts: 2.4 us -> 0.8 us
    ppermute x6, waiting for transfers between devices: 11.4 us -> 5.21 us  [gather_and_project(): arrived = lax.ppermute(array, ('tile', 'wave'), pairs)]
    ppermute x6, starting transfers between devices: 9.01 us -> 13.9 us  [gather_and_project(): arrived = lax.ppermute(array, ('tile', 'wave'), pairs)]
    unnamed x14, local copies, waits for them, and re-layouts: 1.27 us -> 0.09 us
    concatenate x1 -> x0, local copies, waits for them, and re-layouts: 1.08 us -> none  [per_device(): jnp.concatenate([spectral_weight.reshape(-1, lanes), lattice_x.astype(f32...]
    pallas_call x2, Pallas kernels: 2.63 us -> 1.73 us  [near_field(): call(lambda *refs: near_kernel(layout, *refs), 'near', shape((rows, lanes...]
    ppermute x7, waiting for transfers between devices: 0.02 us -> 0.81 us  [swap_cores(): return lax.ppermute(array, 'wave', [(0, 1), (1, 0)])]
    another operation x0 -> x1, other arithmetic: none -> 0.68 us  [per_device(): jnp.stack([lattice_x, lattice_y, jnp.pad(frequency, (0, lanes - frequency...]
    broadcast_in_dim x1 -> x0, other arithmetic: 0.67 us -> none  [per_device(): lattice_y.astype(f32)[None]]
  transfers between devices with their start and end apart: 13 -> 13, of which waited for: 5 -> 7; matrix products, arithmetic and copies ran while one was open for 4% -> 4% of each run, Pallas kernels for 29% -> 23%
where the time goes in v4:
time: 39.7 us; the launch traced here: 39.5 us
  starting transfers between devices  16.2 us (41%)
  Pallas kernels  14.1 us (36%)
  waiting for transfers between devices  6.02 us (15%)
  other arithmetic  1.54 us (4%)
  between operations  0.85 us (2%)
  local copies, waits for them, and re-layouts  0.8 us (2%)
    ppermute x6, starting transfers between devices, gather_and_project(): arrived = lax.ppermute(array, ('tile', 'wave'), pairs)  13.9 us
    pallas_call x8, Pallas kernels, part_call(): call(lambda *refs: part_kernel(layout, base, with_start, not tables, halv...  8.06 us
    ppermute x6, waiting for transfers between devices, gather_and_project(): arrived = lax.ppermute(array, ('tile', 'wave'), pairs)  5.21 us
    ppermute x7, starting transfers between devices, swap_cores(): return lax.ppermute(array, 'wave', [(0, 1), (1, 0)])  2.31 us
    pallas_call x2, Pallas kernels, near_field(): call(lambda *refs: near_kernel(layout, *refs), 'near', shape((rows, lanes...  1.73 us
    pallas_call x2, Pallas kernels, far_field(): call(lambda *refs: far_kernel(layout, *refs), 'far', tuple([shape((rows /...  1.7 us
    pallas_call x1, Pallas kernels, spectral(): call(lambda *refs: spectral_kernel(layout, scale, *refs), 'spectral', (sh...  1.42 us
    ppermute x7, waiting for transfers between devices, swap_cores(): return lax.ppermute(array, 'wave', [(0, 1), (1, 0)])  0.81 us
  transfers between devices with their start and end apart: 13, of which 7 were waited for; matrix products, arithmetic and copies ran while one was open for 4% of the time, Pallas kernels for 23%

profile of v4, /device:TPU:0, one launch (start us, length us, event | category | flops | bytes accessed | tf_op | source)
XLA Modules:
  0.0 39.5 jit_solution(3356488653801792247)
XLA Ops:
  0.6 0.8 %pad_maximum_fusion.6.refs_0_ = f32[72,128]{1,0:T(8,128)S(1)} fusion(f32[8,128]{1,0:T(8,128)} %bitcast.28, f32[64,128]{1,0:T(8,128)} %bitcast.27), kind=kLoop, calls=%fused_computation.6 | loop fusion | flops 9216 | bytes 73728 | tf_op jit(solution)/shard_map/concatenate | solution.py:440
  1.4 3.5 %collective-permute-start = (bf16[1,96,128]{2,1,0:T(8,128)(2,1)S(1)}, bf16[1,96,128]{2,1,0:T(8,128)(2,1)S(1)}, u32[]{:S(2)}, u32[]{:S(2)}) collective-permute-start(bf16[1,96,128]{2,1,0:T(8,128)(2,1)S(1)} %bitcast.14), channel_id=1, source_target_pairs={{0,9},{1,8},{2,11},{3,10},{4,13},{5,12},{6,15},{7,14},{8,1},{9,0},... | collective-permute-start | bytes 73736 | tf_op jit(solution)/shard_map/ppermute | solution.py:497
  5.6 0.7 %pad_add_fusion.refs_0_ = s32[3,128]{1,0:T(4,128)S(1)} fusion(s32[1,128]{1,0:T(1,128)S(1)} %pad_bitcast_fusion, s32[1,128]{1,0:T(1,128)} %bitcast.29, s32[1,128]{1,0:T(1,128)} %bitcast.30), kind=kLoop, calls=%fused_computation.17 | loop fusion | flops 768 | bytes 3072 | tf_op jit(solution)/shard_map/stack | solution.py:449
  6.6 1.8 %collective-permute-start.1 = (bf16[2,96,128]{2,1,0:T(8,128)(2,1)S(1)}, bf16[2,96,128]{2,1,0:T(8,128)(2,1)S(1)}, u32[]{:S(2)}, u32[]{:S(2)}) collective-permute-start(bf16[2,96,128]{2,1,0:T(8,128)(2,1)S(1)} %pad_maximum_fusion.4.refs_0_), channel_id=1, source_target_pairs={{0,5},{1,4},{2,7},{3,6},{4,1},{5,0},{6,3},{7,2},{8,13},{9,12},{10,... | collective-permute-start | bytes 147464 | tf_op jit(solution)/shard_map/ppermute | solution.py:497
  8.8 1.2 %part.4 = (f32[1024,256]{1,0:T(8,128)S(1)}, bf16[1,256,1024]{2,1,0:T(8,128)(2,1)S(1)}, f32[2,72,512]{2,1,0:T(8,128)S(1)}) custom-call(bf16[2,96,128]{2,1,0:T(8,128)(2,1)S(1)} %pad_maximum_fusion.4.refs_0_), custom_call_target="tpu_custom_call" | custom-call | flops 1000000000 | tf_op jit(solution)/shard_map/part/pallas_call | solution.py:482
  10.3 1.9 %collective-permute-start.2 = (bf16[4,96,128]{2,1,0:T(8,128)(2,1)S(1)}, bf16[4,96,128]{2,1,0:T(8,128)(2,1)S(1)}, u32[]{:S(2)}, u32[]{:S(2)}) collective-permute-start(bf16[4,96,128]{2,1,0:T(8,128)(2,1)S(1)} %pad_maximum_fusion.2), channel_id=1, source_target_pairs={{0,3},{1,2},{2,1},{3,0},{4,7},{5,6},{6,5},{7,4},{8,11},{9,10},{10,... | collective-permute-start | bytes 294920 | tf_op jit(solution)/shard_map/ppermute | solution.py:497
  12.2 1.4 %spectral.1 = (f32[8,128,128]{2,1,0:T(8,128)S(1)}, f32[8,128]{1,0:T(8,128)S(1)}) custom-call(s32[3,128]{1,0:T(4,128)S(1)} %pad_add_fusion.refs_0_, f32[8,128,128]{2,1,0:T(8,128)S(1)} %copy-done.1), custom_call_target="tpu_custom_call" | custom-call | flops 2000000000 | tf_op jit(solution)/shard_map/spectral/pallas_call | solution.py:452
  13.6 1.3 %part.5 = (f32[1024,256]{1,0:T(8,128)S(1)}, bf16[1,256,1024]{2,1,0:T(8,128)(2,1)S(1)}, f32[2,72,512]{2,1,0:T(8,128)S(1)}) custom-call(bf16[2,96,128]{2,1,0:T(8,128)(2,1)S(1)} %collective-permute-done.1.refs_0_, f32[1024,256]{1,0:T(8,128)S(1)} %get-tuple-element.28.refs_1_), custom_call_target="tpu_custom_call", output_to_operand_aliasing={{0}: (1, {})} | custom-call | flops 1000000000 | tf_op jit(solution)/shard_map/part/pallas_call | solution.py:482
  15.1 1.7 %leaving.2 = (bf16[512,256]{1,0:T(8,128)(2,1)S(1)}, bf16[1,256,2048]{2,1,0:T(8,128)(2,1)S(1)}, f32[4,72,512]{2,1,0:T(8,128)S(1)}) custom-call(bf16[4,96,128]{2,1,0:T(8,128)(2,1)S(1)} %collective-permute-done.2.refs_0_, f32[1024,256]{1,0:T(8,128)S(1)} %get-tuple-element.29.refs_1_.refs_3_), custom_call_target="tpu_custom_call" | custom-call | flops 1000000000 | tf_op jit(solution)/shard_map/leaving/pallas_call | solution.py:482
  17.4 0.8 %staying.2.refs_0_ = f32[512,256]{1,0:T(8,128)S(1)} custom-call(bf16[4,96,128]{2,1,0:T(8,128)(2,1)S(1)} %collective-permute-done.2.refs_0_, bf16[1,256,2048]{2,1,0:T(8,128)(2,1)S(1)} %get-tuple-element.30.refs_1_, f32[4,72,512]{2,1,0:T(8,128)S(1)} %get-tuple-element.31.refs_2_, f32[1024,256]{1,0:T(8,128)S(1)} %get-tuple-element.29.refs_1_.refs_3_), custom_call_target="tpu_custom_call" | custom-call | flops 2000000000 | tf_op jit(solution)/shard_map/staying/pallas_call | solution.py:482
  18.7 0.9 %far.2 = (f32[32,128]{1,0:T(8,128)S(1)}, f32[32,128]{1,0:T(8,128)S(1)}) custom-call(f32[512,256]{1,0:T(8,128)S(1)} %staying.2.refs_0_, bf16[512,256]{1,0:T(8,128)(2,1)S(1)} %collective-permute-done.4.refs_1_, f32[8,128,128]{2,1,0:T(8,128)S(1)} %get-tuple-element.34.refs_2_, bf16[1,256,1024]{2,1,0:T(8,128)(2,1)S(1)} %get-tuple-element.35.refs_3_.refs_1_, ...), custom_call_target="tpu_custom_call" | custom-call | flops 1000000000 | tf_op jit(solution)/shard_map/far/pallas_call | solution.py:511
  19.9 0.9 %near.2.refs_1_ = f32[64,128]{1,0:T(8,128)S(1)} custom-call(bf16[16,96,128]{2,1,0:T(8,128)(2,1)S(1)} %constant_dynamic-update-slice_fusion.refs_0_, bf16[4,9,2,128,128]{4,3,2,1,0:T(8,128)(2,1)S(1)} %bitcast.22, s32[4,9]{1,0:T(4,128)S(1)} %bitcast.25), custom_call_target="tpu_custom_call" | custom-call | flops 2000000000 | tf_op jit(solution)/shard_map/near/pallas_call | solution.py:527
  20.9 3.2 %collective-permute-start.7 = (bf16[1,80,128]{2,1,0:T(8,128)(2,1)S(1)}, bf16[1,80,128]{2,1,0:T(8,128)(2,1)S(1)}, u32[]{:S(2)}, u32[]{:S(2)}) collective-permute-start(bf16[1,80,128]{2,1,0:T(8,128)(2,1)S(1)} %bitcast.18), channel_id=1, source_target_pairs={{0,9},{1,8},{2,11},{3,10},{4,13},{5,12},{6,15},{7,14},{8,1},{9,0},... | collective-permute-start | bytes 61448 | tf_op jit(solution)/shard_map/ppermute | solution.py:497
  24.1 1.5 %collective-permute-done.7 = bf16[1,80,128]{2,1,0:T(8,128)(2,1)S(1)} collective-permute-done((bf16[1,80,128]{2,1,0:T(8,128)(2,1)S(1)}, bf16[1,80,128]{2,1,0:T(8,128)(2,1)S(1)}, u32[]{:S(2)}, u32[]{:S(2)}) %collective-permute-start.7) | collective-permute-done | bytes 20512 | tf_op jit(solution)/shard_map/ppermute | solution.py:497
  25.6 2.1 %collective-permute-start.8 = (bf16[2,80,128]{2,1,0:T(8,128)(2,1)S(1)}, bf16[2,80,128]{2,1,0:T(8,128)(2,1)S(1)}, u32[]{:S(2)}, u32[]{:S(2)}) collective-permute-start(bf16[2,80,128]{2,1,0:T(8,128)(2,1)S(1)} %pad_maximum_fusion.5.refs_0_), channel_id=1, source_target_pairs={{0,5},{1,4},{2,7},{3,6},{4,1},{5,0},{6,3},{7,2},{8,13},{9,12},{10,... | collective-permute-start | bytes 122888 | tf_op jit(solution)/shard_map/ppermute | solution.py:497
  27.7 0.8 %part.6.refs_3_ = f32[1024,256]{1,0:T(8,128)S(1)} custom-call(bf16[2,80,128]{2,1,0:T(8,128)(2,1)S(1)} %pad_maximum_fusion.5.refs_0_, bf16[1,256,1024]{2,1,0:T(8,128)(2,1)S(1)} %get-tuple-element.35.refs_3_.refs_1_, f32[2,72,512]{2,1,0:T(8,128)S(1)} %get-tuple-element.36.refs_4_.refs_2_), custom_call_target="tpu_custom_call" | custom-call | flops 1000000000 | tf_op jit(solution)/shard_map/part/pallas_call | solution.py:482
  28.5 1.0 %collective-permute-done.8.refs_0_ = bf16[2,80,128]{2,1,0:T(8,128)(2,1)S(1)} collective-permute-done((bf16[2,80,128]{2,1,0:T(8,128)(2,1)S(1)}, bf16[2,80,128]{2,1,0:T(8,128)(2,1)S(1)}, u32[]{:S(2)}, u32[]{:S(2)}) %collective-permute-start.8) | collective-permute-done | bytes 40992 | tf_op jit(solution)/shard_map/ppermute | solution.py:497
  29.5 1.3 %collective-permute-start.9 = (bf16[4,80,128]{2,1,0:T(8,128)(2,1)S(1)}, bf16[4,80,128]{2,1,0:T(8,128)(2,1)S(1)}, u32[]{:S(2)}, u32[]{:S(2)}) collective-permute-start(bf16[4,80,128]{2,1,0:T(8,128)(2,1)S(1)} %pad_maximum_fusion.3), channel_id=1, source_target_pairs={{0,3},{1,2},{2,1},{3,0},{4,7},{5,6},{6,5},{7,4},{8,11},{9,10},{10,... | collective-permute-start | bytes 245768 | tf_op jit(solution)/shard_map/ppermute | solution.py:497
  30.9 0.8 %part.7.refs_3_ = f32[1024,256]{1,0:T(8,128)S(1)} custom-call(bf16[2,80,128]{2,1,0:T(8,128)(2,1)S(1)} %collective-permute-done.8.refs_0_, bf16[1,256,1024]{2,1,0:T(8,128)(2,1)S(1)} %get-tuple-element.45.refs_1_, f32[2,72,512]{2,1,0:T(8,128)S(1)} %get-tuple-element.46.refs_2_, f32[1024,256]{1,0:T(8,128)S(1)} %part.6.refs_3_), custom_call_target="tpu_custom_call", output_to_operand_aliasing={{}: (3, {})} | custom-call | flops 1000000000 | tf_op jit(solution)/shard_map/part/pallas_call | solution.py:482
  31.7 2.3 %collective-permute-done.9.refs_0_ = bf16[4,80,128]{2,1,0:T(8,128)(2,1)S(1)} collective-permute-done((bf16[4,80,128]{2,1,0:T(8,128)(2,1)S(1)}, bf16[4,80,128]{2,1,0:T(8,128)(2,1)S(1)}, u32[]{:S(2)}, u32[]{:S(2)}) %collective-permute-start.9) | collective-permute-done | bytes 81952 | tf_op jit(solution)/shard_map/ppermute | solution.py:497
  34.0 0.8 %leaving.3 = bf16[512,256]{1,0:T(8,128)(2,1)S(1)} custom-call(bf16[4,80,128]{2,1,0:T(8,128)(2,1)S(1)} %collective-permute-done.9.refs_0_, bf16[1,256,2048]{2,1,0:T(8,128)(2,1)S(1)} %get-tuple-element.30.refs_1_, f32[4,72,512]{2,1,0:T(8,128)S(1)} %get-tuple-element.31.refs_2_, f32[1024,256]{1,0:T(8,128)S(1)} %part.7.refs_3_), custom_call_target="tpu_custom_call" | custom-call | flops 1000000000 | tf_op jit(solution)/shard_map/leaving/pallas_call | solution.py:482
  35.4 0.8 %staying.3.refs_0_ = f32[512,256]{1,0:T(8,128)S(1)} custom-call(bf16[4,80,128]{2,1,0:T(8,128)(2,1)S(1)} %collective-permute-done.9.refs_0_, bf16[1,256,2048]{2,1,0:T(8,128)(2,1)S(1)} %get-tuple-element.30.refs_1_, f32[4,72,512]{2,1,0:T(8,128)S(1)} %get-tuple-element.31.refs_2_, f32[1024,256]{1,0:T(8,128)S(1)} %part.7.refs_3_), custom_call_target="tpu_custom_call" | custom-call | flops 2000000000 | tf_op jit(solution)/shard_map/staying/pallas_call | solution.py:482
  36.6 0.8 %far.3 = (f32[32,128]{1,0:T(8,128)S(1)}, f32[32,128]{1,0:T(8,128)S(1)}) custom-call(f32[512,256]{1,0:T(8,128)S(1)} %staying.3.refs_0_, bf16[512,256]{1,0:T(8,128)(2,1)S(1)} %collective-permute-done.11.refs_1_, f32[8,128,128]{2,1,0:T(8,128)S(1)} %get-tuple-element.34.refs_2_, bf16[1,256,1024]{2,1,0:T(8,128)(2,1)S(1)} %get-tuple-element.35.refs_3_.refs_1_, ...), custom_call_target="tpu_custom_call" | custom-call | flops 1000000000 | tf_op jit(solution)/shard_map/far/pallas_call | solution.py:511
  37.8 0.9 %near.3.refs_1_ = f32[64,128]{1,0:T(8,128)S(1)} custom-call(bf16[16,80,128]{2,1,0:T(8,128)(2,1)S(1)} %constant_dynamic-update-slice_fusion.5.refs_0_, bf16[4,9,2,128,128]{4,3,2,1,0:T(8,128)(2,1)S(1)} %bitcast.23, s32[4,9]{1,0:T(4,128)S(1)} %bitcast.26), custom_call_target="tpu_custom_call" | custom-call | flops 2000000000 | tf_op jit(solution)/shard_map/near/pallas_call | solution.py:527
  (45 shorter events, 5.6 us)
Async XLA Ops:
  1.4 5.1 %collective-permute-start = (bf16[1,96,128]{2,1,0:T(8,128)(2,1)S(1)}, bf16[1,96,128]{2,1,0:T(8,128)(2,1)S(1)}, u32[]{:S(2)}, u32[]{:S(2)}) collective-permute-start(bf16[1,96,128]{2,1,0:T(8,128)(2,1)S(1)} %bitcast.14), channel_id=1, source_target_pairs={{0,9},{1,8},{2,11},{3,10},{4,13},{5,12},{6,15},{7,14},{8,1},{9,0},... | collective-permute-start | bytes 73736 | tf_op jit(solution)/shard_map/ppermute | solution.py:497
  6.6 3.7 %collective-permute-start.1 = (bf16[2,96,128]{2,1,0:T(8,128)(2,1)S(1)}, bf16[2,96,128]{2,1,0:T(8,128)(2,1)S(1)}, u32[]{:S(2)}, u32[]{:S(2)}) collective-permute-start(bf16[2,96,128]{2,1,0:T(8,128)(2,1)S(1)} %pad_maximum_fusion.4.refs_0_), channel_id=1, source_target_pairs={{0,5},{1,4},{2,7},{3,6},{4,1},{5,0},{6,3},{7,2},{8,13},{9,12},{10,... | collective-permute-start | bytes 147464 | tf_op jit(solution)/shard_map/ppermute | solution.py:497
  8.4 1.6 %collective-permute-start.5 = (bf16[96,128]{1,0:T(8,128)(2,1)S(1)}, bf16[96,128]{1,0:T(8,128)(2,1)S(1)}, u32[]{:S(2)}, u32[]{:S(2)}) collective-permute-start(bf16[96,128]{1,0:T(8,128)(2,1)S(1)} %get-tuple-element.37.refs_0_), channel_id=1, source_target_pairs={{0,1},{1,0},{2,3},{3,2},{4,5},{5,4},{6,7},{7,6},{8,9},{9,8},{10,11... | collective-permute-start | bytes 73736 | tf_op jit(solution)/shard_map/ppermute | solution.py:79
  8.8 3.4 %copy-start.1 = (f32[8,128,128]{2,1,0:T(8,128)S(1)}, f32[8,128,128]{2,1,0:T(8,128)}, u32[]{:S(2)}) copy-start(f32[8,128,128]{2,1,0:T(8,128)} %refs_1_.1) | copy-start | bytes 1572868
  10.3 4.8 %collective-permute-start.2 = (bf16[4,96,128]{2,1,0:T(8,128)(2,1)S(1)}, bf16[4,96,128]{2,1,0:T(8,128)(2,1)S(1)}, u32[]{:S(2)}, u32[]{:S(2)}) collective-permute-start(bf16[4,96,128]{2,1,0:T(8,128)(2,1)S(1)} %pad_maximum_fusion.2), channel_id=1, source_target_pairs={{0,3},{1,2},{2,1},{3,0},{4,7},{5,6},{6,5},{7,4},{8,11},{9,10},{10,... | collective-permute-start | bytes 294920 | tf_op jit(solution)/shard_map/ppermute | solution.py:497
  16.8 1.9 %collective-permute-start.4 = (bf16[512,256]{1,0:T(8,128)(2,1)S(1)}, bf16[512,256]{1,0:T(8,128)(2,1)S(1)}, u32[]{:S(2)}, u32[]{:S(2)}) collective-permute-start(bf16[512,256]{1,0:T(8,128)(2,1)S(1)} %get-tuple-element.32), channel_id=1, source_target_pairs={{0,1},{1,0},{2,3},{3,2},{4,5},{5,4},{6,7},{7,6},{8,9},{9,8},{10,11... | collective-permute-start | bytes 786440 | tf_op jit(solution)/shard_map/ppermute | solution.py:79
  17.2 1.5 %collective-permute-start.3 = (bf16[8,96,128]{2,1,0:T(8,128)(2,1)S(1)}, bf16[8,96,128]{2,1,0:T(8,128)(2,1)S(1)}, u32[]{:S(2)}, u32[]{:S(2)}) collective-permute-start(bf16[8,96,128]{2,1,0:T(8,128)(2,1)S(1)} %pad_maximum_fusion), channel_id=1, source_target_pairs={{0,1},{1,0},{2,3},{3,2},{4,5},{5,4},{6,7},{7,6},{8,9},{9,8},{10,11... | collective-permute-start | bytes 589832 | tf_op jit(solution)/shard_map/ppermute | solution.py:79
  18.2 1.7 %copy-start = (bf16[1,4,9,2,128,128]{5,4,3,2,1,0:T(8,128)(2,1)S(1)}, bf16[1,4,9,2,128,128]{5,4,3,2,1,0:T(8,128)(2,1)}, u32[]{:S(2)}) copy-start(bf16[1,4,9,2,128,128]{5,4,3,2,1,0:T(8,128)(2,1)} %param.9) | copy-start | bytes 7077892
  18.2 1.7 %copy-start.2 = (s32[1,4,9]{2,1,0:T(4,128)S(1)}, s32[1,4,9]{2,1,0:T(4,128)}, u32[]{:S(2)}) copy-start(s32[1,4,9]{2,1,0:T(4,128)} %param.11) | copy-start | bytes 436
  19.6 1.2 %collective-permute-start.6 = (f32[32,128]{1,0:T(8,128)S(1)}, f32[32,128]{1,0:T(8,128)S(1)}, u32[]{:S(2)}, u32[]{:S(2)}) collective-permute-start(f32[32,128]{1,0:T(8,128)S(1)} %get-tuple-element.41), channel_id=1, source_target_pairs={{0,1},{1,0},{2,3},{3,2},{4,5},{5,4},{6,7},{7,6},{8,9},{9,8},{10,11... | collective-permute-start | bytes 49160 | tf_op jit(solution)/shard_map/ppermute | solution.py:79
  20.9 4.7 %collective-permute-start.7 = (bf16[1,80,128]{2,1,0:T(8,128)(2,1)S(1)}, bf16[1,80,128]{2,1,0:T(8,128)(2,1)S(1)}, u32[]{:S(2)}, u32[]{:S(2)}) collective-permute-start(bf16[1,80,128]{2,1,0:T(8,128)(2,1)S(1)} %bitcast.18), channel_id=1, source_target_pairs={{0,9},{1,8},{2,11},{3,10},{4,13},{5,12},{6,15},{7,14},{8,1},{9,0},... | collective-permute-start | bytes 61448 | tf_op jit(solution)/shard_map/ppermute | solution.py:497
  25.6 3.9 %collective-permute-start.8 = (bf16[2,80,128]{2,1,0:T(8,128)(2,1)S(1)}, bf16[2,80,128]{2,1,0:T(8,128)(2,1)S(1)}, u32[]{:S(2)}, u32[]{:S(2)}) collective-permute-start(bf16[2,80,128]{2,1,0:T(8,128)(2,1)S(1)} %pad_maximum_fusion.5.refs_0_), channel_id=1, source_target_pairs={{0,5},{1,4},{2,7},{3,6},{4,1},{5,0},{6,3},{7,2},{8,13},{9,12},{10,... | collective-permute-start | bytes 122888 | tf_op jit(solution)/shard_map/ppermute | solution.py:497
  29.5 4.5 %collective-permute-start.9 = (bf16[4,80,128]{2,1,0:T(8,128)(2,1)S(1)}, bf16[4,80,128]{2,1,0:T(8,128)(2,1)S(1)}, u32[]{:S(2)}, u32[]{:S(2)}) collective-permute-start(bf16[4,80,128]{2,1,0:T(8,128)(2,1)S(1)} %pad_maximum_fusion.3), channel_id=1, source_target_pairs={{0,3},{1,2},{2,1},{3,0},{4,7},{5,6},{6,5},{7,4},{8,11},{9,10},{10,... | collective-permute-start | bytes 245768 | tf_op jit(solution)/shard_map/ppermute | solution.py:497
  34.7 1.9 %collective-permute-start.11 = (bf16[512,256]{1,0:T(8,128)(2,1)S(1)}, bf16[512,256]{1,0:T(8,128)(2,1)S(1)}, u32[]{:S(2)}, u32[]{:S(2)}) collective-permute-start(bf16[512,256]{1,0:T(8,128)(2,1)S(1)} %leaving.3), channel_id=1, source_target_pairs={{0,1},{1,0},{2,3},{3,2},{4,5},{5,4},{6,7},{7,6},{8,9},{9,8},{10,11... | collective-permute-start | bytes 786440 | tf_op jit(solution)/shard_map/ppermute | solution.py:79
  35.0 1.6 %collective-permute-start.10 = (bf16[8,80,128]{2,1,0:T(8,128)(2,1)S(1)}, bf16[8,80,128]{2,1,0:T(8,128)(2,1)S(1)}, u32[]{:S(2)}, u32[]{:S(2)}) collective-permute-start(bf16[8,80,128]{2,1,0:T(8,128)(2,1)S(1)} %pad_maximum_fusion.1), channel_id=1, source_target_pairs={{0,1},{1,0},{2,3},{3,2},{4,5},{5,4},{6,7},{7,6},{8,9},{9,8},{10,11... | collective-permute-start | bytes 491528 | tf_op jit(solution)/shard_map/ppermute | solution.py:79
  37.5 1.4 %collective-permute-start.12 = (f32[32,128]{1,0:T(8,128)S(1)}, f32[32,128]{1,0:T(8,128)S(1)}, u32[]{:S(2)}, u32[]{:S(2)}) collective-permute-start(f32[32,128]{1,0:T(8,128)S(1)} %get-tuple-element.48), channel_id=1, source_target_pairs={{0,1},{1,0},{2,3},{3,2},{4,5},{5,4},{6,7},{7,6},{8,9},{9,8},{10,11... | collective-permute-start | bytes 49160 | tf_op jit(solution)/shard_map/ppermute | solution.py:79

commit v5 on v4

--- a/solution.py
+++ b/solution.py
@@ -42,8 +42,7 @@
         self.panels = self.count_x * self.count_y * lanes
         self.local = self.tiles * lanes
         self.rows = self.tiles * 2 * vectors
-        self.offset_rows = -(-6 * self.tiles // 16) * 16
-        self.sum_rows = 16
+        self.offset_rows = -(-4 * self.tiles // 16) * 16
         self.part_v = vectors // 2
         self.half = modes // 2
         self.quarter = modes // 4
@@ -83,59 +82,58 @@
     return lax.optimization_barrier((value, *others))[0]
 
 
-def three_parts(value, pad):
-    first = value.astype(bf16).astype(f32)
-    value = value - first
-    second = value.astype(bf16).astype(f32)
-    pieces = [first, second, value - second]
-    if pad:
-        pieces.append(jnp.zeros((pad, lanes), f32))
-    return jnp.concatenate(pieces, 0).astype(bf16)
-
-
-def add_three(rows, count):
-    return rows[:count] + rows[count : 2 * count] + rows[2 * count : 3 * count]
-
-
-def pack_kernel(layout, head, out, squares):
-    rows, vectors = layout.rows, layout.vectors
+def two_parts(value):
+    first = value.astype(bf16)
+    return first, (value - first.astype(f32)).astype(bf16)
+
+
+def pack_kernel(layout, head, out):
+    rows, count = layout.rows, 2 * layout.tiles
     out[:rows, :] = head[:rows, :].astype(bf16)
-    out[rows:, :] = three_parts(head[rows:, :], layout.offset_rows - 6 * layout.tiles)
-    total = 0.0
-    for k in range(2 * layout.tiles):
-        piece = head[k * vectors : (k + 1) * vectors, :]
-        total = total + piece * piece
-    squares[...] = total
-
-
-def split_dot(weights, value, dims):
-    total = 0.0
-    for _ in range(3):
-        part = value.astype(bf16)
-        total = total + lax.dot_general(weights, part, dims, preferred_element_type=f32)
-        value = value - part.astype(f32)
-    return total
+    first, second = two_parts(head[rows:, :])
+    pieces = [first.astype(f32), second.astype(f32)]
+    if layout.offset_rows > 2 * count:
+        pieces.append(jnp.zeros((layout.offset_rows - 2 * count, lanes), f32))
+    out[rows:, :] = jnp.concatenate(pieces, 0).astype(bf16)
+
+
+def swap(value):
+    return pltpu.roll(value, lanes // 2, 1)
 
 
 def spectral_kernel(layout, scale, integers, table, out, guess, order, moved_all, sem):
-    size = 2 * layout.half
+    half, quarter = layout.half, layout.quarter
+    size = 2 * half
     count = moved_all.shape[0]
     copy = pltpu.make_async_copy(integers.at[2:3], order, sem)
     copy.start()
     spot = lax.broadcasted_iota(jnp.int32, (size, size), 0)
-    wanted = jnp.where(spot < layout.half, spot + layout.half, size - 1 - spot)
-    pick_x = jnp.where(wanted == integers[0:1], 1.0, 0.0).astype(bf16)
-    pick_y = jnp.where(wanted == integers[1:2], 1.0, 0.0).astype(bf16)
-    for f in range(count):
-        moved = split_dot(pick_x, table[f] * scale, (((1,), (0,)), ((), ())))
-        moved_all[f] = split_dot(pick_y, moved, (((1,), (1,)), ((), ())))
+    wanted = jnp.where(spot < half, spot + half, size - 1 - spot)
+    pick_x, pick_y = [jnp.where(wanted == integers[k : k + 1], 1.0, 0.0).astype(bf16) for k in range(2)]
+    pick_x, pick_y = [jnp.concatenate([pick, pick], 1) for pick in (pick_x, pick_y)]
+    for f in range(0, count, 2):
+        pair = range(f, min(f + 2, count))
+        columns = [jnp.concatenate(two_parts(table[k] * scale), 0) for k in pair]
+        moved = jnp.dot(pick_x, jnp.concatenate(columns, 1), preferred_element_type=f32)
+        rows = [jnp.concatenate(two_parts(moved[:, n * size : (n + 1) * size]), 1) for n in range(len(pair))]
+        moved = lax.dot_general(
+            pick_y, jnp.concatenate(rows, 0), (((1,), (1,)), ((), ())), preferred_element_type=f32
+        )
+        for n, k in enumerate(pair):
+            moved_all[k] = moved[:, n * size : (n + 1) * size]
     copy.wait()
+    low = lax.broadcasted_iota(jnp.int32, (quarter, lanes), 1) < half
     rows = []
     for v in range(layout.vectors):
         moved = moved_all[order[0, v]]
-        out[v] = moved
         mean = jnp.sum(jnp.sum(moved, 0, keepdims=True), 1, keepdims=True)
         rows.append(jnp.broadcast_to(0.5 + mean, (1, lanes)))
+        part = [moved[k * quarter : (k + 1) * quarter] for k in range(4)]
+        for k, (one, other) in enumerate(((part[1], part[3]), (part[2], part[0]), (part[0], part[2]), (part[3], part[1]))):
+            chosen = jnp.where(low, one, other)
+            turned = swap(chosen)
+            out[v, 2 * k * quarter : (2 * k + 1) * quarter, :] = chosen + turned
+            out[v, (2 * k + 1) * quarter : (2 * k + 2) * quarter, :] = chosen - turned
     guess[...] = jnp.concatenate(rows, 0)
 
 
@@ -144,7 +142,8 @@
     block = layout.group_of(density) * group + k
     device = layout.device_of(base + block)
     column, row_index = device // layout.waves, device % layout.waves
-    offset = add_three(density[block, layout.rows :, :].astype(f32), 2 * tiles)
+    pieces = density[block, layout.rows :, :].astype(f32)
+    offset = pieces[: 2 * tiles] + pieces[2 * tiles : 4 * tiles]
     eight = lax.broadcasted_iota(jnp.int32, (8, lanes), 0).astype(f32)
     coarse_y = jnp.where(eight < 4, quarter / 2 + 0.5 + 8 * eight, jnp.where(eight < 5, quarter / 2.0, 0.5))
     for i in range(tiles):
@@ -247,19 +246,12 @@
     make_tables(layout, base, 0, 0, density, table_x, table_y)
 
 
-def swap(value):
-    return pltpu.roll(value, lanes // 2, 1)
-
-
 def weigh(layout, total, weight, scaled):
     quarter = layout.quarter
     first = lax.axis_index("wave") * layout.part_v
     low = lax.broadcasted_iota(jnp.int32, (quarter, lanes), 1) < layout.half
     sign = jnp.where(low, -1.0, 1.0)
     for v in range(layout.part_v):
-        table = weight[first + v]
-        part = [table[k * quarter : (k + 1) * quarter] for k in range(4)]
-        choices = ((part[1], part[3]), (part[2], part[0]), (part[0], part[2]), (part[3], part[1]))
         for e in range(2):
             span = slice(e * lanes, (e + 1) * lanes)
             real = v * 4 * quarter
@@ -270,9 +262,9 @@
             sin_i = swap(total[imag + quarter : imag + 2 * quarter, span]) * sign
             out = []
             for k, (mr, mi) in enumerate(((cos_r + sin_r, cos_i + sin_i), (cos_r - sin_r, cos_i - sin_i))):
-                chosen = jnp.where(low, *choices[2 * e + k])
-                turned = swap(chosen)
-                plus, minus = chosen + turned, chosen - turned
+                start = 2 * (2 * e + k) * quarter
+                plus = weight[first + v, start : start + quarter, :]
+                minus = weight[first + v, start + quarter : start + 2 * quarter, :]
                 out.append((plus * mr + minus * swap(mi), plus * mi - minus * swap(mr)))
             for start, k in ((real, 0), (imag, 1)):
                 scaled[start : start + quarter, span] = (out[0][k] + out[1][k]).astype(bf16)
@@ -340,16 +332,9 @@
         out[i * tall : (i + 1) * tall, :] = near_tile(layout, i, places, density, blocks)
 
 
-def spread(layout, row_of):
-    spot = lax.broadcasted_iota(jnp.int32, (layout.vectors, lanes), 0)
-    lane = lax.broadcasted_iota(jnp.int32, (layout.vectors, lanes), 1)
-    return [lane == spot + k * layout.vectors for k in row_of]
-
-
-def first_kernel(layout, density, near, far_own, far_other, guess, squares, basis, image):
-    vectors, tall, rows = layout.vectors, 2 * layout.vectors, layout.rows
+def first_kernel(layout, density, near, far_own, far_other, guess, basis, image):
+    vectors, tall = layout.vectors, 2 * layout.vectors
     hint = guess[...]
-    sums = [squares[...]] + [0.0] * 4
     for i in range(layout.tiles):
         first = i * tall
         far_real, far_imag = far_rows(layout, i, far_own, far_other)
@@ -357,38 +342,48 @@
         rr, ri = own[:vectors], own[vectors:]
         wr = 0.5 * rr + near[first : first + vectors, :] + far_real
         wi = 0.5 * ri + near[first + vectors : first + tall, :] + far_imag
-        zr, zi = wr - hint * rr, wi - hint * ri
         image[first : first + tall, :] = jnp.concatenate([wr, wi], 0)
-        basis[first : first + tall, :] = jnp.concatenate([zr, zi], 0).astype(bf16)
+        basis[first : first + tall, :] = jnp.concatenate([wr - hint * rr, wi - hint * ri], 0).astype(bf16)
+
+
+def block_sums(layout, start, density, block):
+    vectors, tall = layout.vectors, 2 * layout.vectors
+    total = None
+    for i in range(layout.tiles):
+        r = start[block, i * tall : (i + 1) * tall, :].astype(f32)
+        z = density[block, i * tall : (i + 1) * tall, :].astype(f32)
+        rr, ri, zr, zi = r[:vectors], r[vectors:], z[:vectors], z[vectors:]
         terms = (rr * rr + ri * ri, rr * zr + ri * zi, rr * zi - ri * zr, zr * zr + zi * zi)
-        sums = sums[:1] + [a + b for a, b in zip(sums[1:], terms)]
-    line = jnp.zeros((vectors, lanes), f32)
-    for value, place in zip(sums, spread(layout, range(5))):
-        line = line + jnp.where(place, jnp.sum(value, 1, keepdims=True), 0.0)
-    basis[rows:, :] = three_parts(jnp.sum(line, 0, keepdims=True), layout.sum_rows - 3)
-
-
-def scalar_kernel(layout, density, guess, factors):
-    vectors, rows = layout.vectors, layout.rows
-    line = jnp.zeros((1, lanes), f32)
-    for device in range(layout.devices):
-        line = line + add_three(density[layout.block_of(device), rows:, :].astype(f32), 1)
-    line = jnp.broadcast_to(line * (1.0 / layout.panels), (vectors, lanes))
-    exact, squares, real, imag, rest = [
-        jnp.broadcast_to(jnp.sum(jnp.where(place, line, 0.0), 1, keepdims=True), (vectors, lanes))
-        for place in spread(layout, range(5))
+        total = terms if total is None else [a + b for a, b in zip(total, terms)]
+    return total
+
+
+def tree_sums(layout, start, density, block, count):
+    if count == 1:
+        return block_sums(layout, start, density, block)
+    lower = tree_sums(layout, start, density, block, count // 2)
+    upper = tree_sums(layout, start, density, block + count // 2, count // 2)
+    return [a + b for a, b in zip(lower, upper)]
+
+
+def scalar_kernel(layout, start, density, guess, factors):
+    vectors = layout.vectors
+    sums = tree_sums(layout, start, density, 0, layout.devices)
+    squares, real, imag, rest = [
+        jnp.broadcast_to(jnp.sum(value, 1, keepdims=True) * (1.0 / layout.panels), (vectors, lanes)) for value in sums
     ]
     hint = guess[...]
-    scale_sq = exact + eps_norm
+    scale_sq = squares + eps_norm
     coef_real = (real + hint * squares) / scale_sq
     coef_imag = imag / scale_sq
     more_real, more_imag = coef_real - hint, coef_imag
     update_sq = rest - 2.0 * (more_real * real + more_imag * imag) + (more_real * more_real + more_imag * more_imag) * squares
     scale = jnp.sqrt(scale_sq)
     update_scale = jnp.sqrt(jnp.maximum(update_sq, 0.0) / scale_sq + eps_norm)
-    here = spread(layout, [0])[0]
+    spot = lax.broadcasted_iota(jnp.int32, (vectors, lanes), 0)
+    lane = lax.broadcasted_iota(jnp.int32, (vectors, lanes), 1)
     lines = [
-        jnp.sum(jnp.where(here, value, 0.0), 0, keepdims=True)
+        jnp.sum(jnp.where(spot == lane, value, 0.0), 0, keepdims=True)
         for value in (scale, coef_real, coef_imag, update_scale)
     ]
     lines.append(jnp.zeros((vectors - 4, lanes), f32))
@@ -438,10 +433,10 @@
         )
 
     head = jnp.concatenate([residual.reshape(rows, lanes), offsets.reshape(2 * tiles, lanes)], 0)
-    packed, squares = call(
+    packed = call(
         lambda *refs: pack_kernel(layout, *refs),
         "pack",
-        (shape((rows + layout.offset_rows, lanes), bf16), shape((vectors, lanes), f32)),
+        shape((rows + layout.offset_rows, lanes), bf16),
         [vmem],
         1,
     )(head)
@@ -452,7 +447,7 @@
         return call(
             lambda *refs: spectral_kernel(layout, scale, *refs),
             "spectral",
-            (shape((vectors, modes_y, modes_x), f32), shape((vectors, lanes), f32)),
+            (shape((vectors, 2 * modes_y, modes_x), f32), shape((vectors, lanes), f32)),
             [vmem, vmem],
             4,
             [
@@ -544,26 +539,27 @@
         8,
     )(swap_cores(after(packed, seen[0]))[None])
     weight, guess = spectral(after(integers, seen[1]))
-    near_one = near_field(with_other_core(seen[-1]))
+    start = with_other_core(seen[-1])
+    near_one = near_field(start)
     far_own, far_other = far_field(leaving, staying, weight, tables[0], other_tables)
     basis, image = call(
         lambda *refs: first_kernel(layout, *refs),
         "first",
-        (shape((rows + layout.sum_rows, lanes), bf16), shape((rows, lanes), f32)),
-        [vmem] * 6,
+        (shape((rows, lanes), bf16), shape((rows, lanes), f32)),
+        [vmem] * 5,
         2,
-    )(packed, near_one, far_own, far_other, guess, squares)
+    )(packed, near_one, far_own, far_other, guess)
     seen, leaving, staying, _ = gather_and_project(basis, tables)
     everything = with_other_core(seen[-1])
     factors = call(
         lambda *refs: scalar_kernel(layout, *refs),
         "scalars",
         shape((4 * vectors, lanes), f32),
-        [vmem] * 2,
-        2,
-    )(everything, guess)
+        [vmem] * 3,
+        1 + devices / 8,
+    )(start, everything, guess)
     near_two = near_field(everything)
-    far_own, far_other = far_field(leaving, staying, weight, tables[0], other_tables)
+    far_own, far_other = far_field(leaving, after(staying, factors), weight, tables[0], other_tables)
     result, scalars = call(
         lambda *refs: second_kernel(layout, *refs),
         "second",

time: 39.7 us -> 38.3 us (0.965)
  waiting for transfers between devices: 6.02 us -> 5.07 us
  Pallas kernels: 14.1 us -> 13.7 us
    ppermute x6, waiting for transfers between devices: 5.21 us -> 4.69 us  [gather_and_project(): arrived = lax.ppermute(array, ('tile', 'wave'), pairs)]
    pallas_call x1, Pallas kernels: 1.42 us -> 0.98 us  [spectral(): call(lambda *refs: spectral_kernel(layout, scale, *refs), 'spectral', (sh...]
    ppermute x7, waiting for transfers between devices: 0.81 us -> 0.38 us  [swap_cores(): return lax.ppermute(array, 'wave', [(0, 1), (1, 0)])]
  transfers between devices with their start and end apart: 13 -> 13, of which waited for: 7 -> 6; matrix products, arithmetic and copies ran while one was open for 4% -> 4% of each run, Pallas kernels for 23% -> 30%
where the time goes in v5:
time: 38.3 us; the launch traced here: 38 us
  starting transfers between devices  16 us (42%)
  Pallas kernels  13.7 us (36%)
  waiting for transfers between devices  5.07 us (13%)
  other arithmetic  1.52 us (4%)
  local copies, waits for them, and re-layouts  0.87 us (2%)
  between operations  0.85 us (2%)
    ppermute x6, starting transfers between devices, gather_and_project(): arrived = lax.ppermute(array, ('tile', 'wave'), pairs)  13.6 us
    pallas_call x8, Pallas kernels, part_call(): call(lambda *refs: part_kernel(layout, base, with_start, not tables, halv...  8.29 us
    ppermute x6, waiting for transfers between devices, gather_and_project(): arrived = lax.ppermute(array, ('tile', 'wave'), pairs)  4.69 us
    ppermute x7, starting transfers between devices, swap_cores(): return lax.ppermute(array, 'wave', [(0, 1), (1, 0)])  2.41 us
    pallas_call x2, Pallas kernels, near_field(): call(lambda *refs: near_kernel(layout, *refs), 'near', shape((rows, lanes...  1.72 us
    pallas_call x2, Pallas kernels, far_field(): call(lambda *refs: far_kernel(layout, *refs), 'far', tuple([shape((rows /...  1.6 us
    pallas_call x1, Pallas kernels, spectral(): call(lambda *refs: spectral_kernel(layout, scale, *refs), 'spectral', (sh...  0.98 us
    concatenate x1, other arithmetic, per_device(): jnp.concatenate([residual.reshape(rows, lanes), offsets.reshape(2 * tiles...  0.78 us
  transfers between devices with their start and end apart: 13, of which 6 were waited for; matrix products, arithmetic and copies ran while one was open for 4% of the time, Pallas kernels for 30%

profile of v5, /device:TPU:0, one launch (start us, length us, event | category | flops | bytes accessed | tf_op | source)
XLA Modules:
  0.0 38.0 jit_solution(5980160568919910683)
XLA Ops:
  0.6 0.8 %pad_maximum_fusion.5.refs_0_ = f32[72,128]{1,0:T(8,128)S(1)} fusion(f32[8,128]{1,0:T(8,128)} %bitcast.28, f32[64,128]{1,0:T(8,128)} %bitcast.27), kind=kLoop, calls=%fused_computation.5 | loop fusion | flops 9216 | bytes 73728 | tf_op jit(solution)/shard_map/concatenate | solution.py:435
  1.4 3.5 %collective-permute-start = (bf16[1,80,128]{2,1,0:T(8,128)(2,1)S(1)}, bf16[1,80,128]{2,1,0:T(8,128)(2,1)S(1)}, u32[]{:S(2)}, u32[]{:S(2)}) collective-permute-start(bf16[1,80,128]{2,1,0:T(8,128)(2,1)S(1)} %bitcast.14), channel_id=1, source_target_pairs={{0,9},{1,8},{2,11},{3,10},{4,13},{5,12},{6,15},{7,14},{8,1},{9,0},... | collective-permute-start | bytes 61448 | tf_op jit(solution)/shard_map/ppermute | solution.py:492
  5.6 0.7 %pad_add_fusion.refs_0_ = s32[3,128]{1,0:T(4,128)S(1)} fusion(s32[1,128]{1,0:T(1,128)S(1)} %pad_bitcast_fusion, s32[1,128]{1,0:T(1,128)} %bitcast.29, s32[1,128]{1,0:T(1,128)} %bitcast.30), kind=kLoop, calls=%fused_computation.17 | loop fusion | flops 768 | bytes 3072 | tf_op jit(solution)/shard_map/stack | solution.py:444
  6.5 1.9 %collective-permute-start.1 = (bf16[2,80,128]{2,1,0:T(8,128)(2,1)S(1)}, bf16[2,80,128]{2,1,0:T(8,128)(2,1)S(1)}, u32[]{:S(2)}, u32[]{:S(2)}) collective-permute-start(bf16[2,80,128]{2,1,0:T(8,128)(2,1)S(1)} %pad_maximum_fusion.4.refs_0_), channel_id=1, source_target_pairs={{0,5},{1,4},{2,7},{3,6},{4,1},{5,0},{6,3},{7,2},{8,13},{9,12},{10,... | collective-permute-start | bytes 122888 | tf_op jit(solution)/shard_map/ppermute | solution.py:492
  8.7 1.2 %part.4 = (f32[1024,256]{1,0:T(8,128)S(1)}, bf16[1,256,1024]{2,1,0:T(8,128)(2,1)S(1)}, f32[2,72,512]{2,1,0:T(8,128)S(1)}) custom-call(bf16[2,80,128]{2,1,0:T(8,128)(2,1)S(1)} %pad_maximum_fusion.4.refs_0_), custom_call_target="tpu_custom_call" | custom-call | flops 1000000000 | tf_op jit(solution)/shard_map/part/pallas_call | solution.py:477
  10.2 1.7 %collective-permute-start.2 = (bf16[4,80,128]{2,1,0:T(8,128)(2,1)S(1)}, bf16[4,80,128]{2,1,0:T(8,128)(2,1)S(1)}, u32[]{:S(2)}, u32[]{:S(2)}) collective-permute-start(bf16[4,80,128]{2,1,0:T(8,128)(2,1)S(1)} %pad_maximum_fusion.2), channel_id=1, source_target_pairs={{0,3},{1,2},{2,1},{3,0},{4,7},{5,6},{6,5},{7,4},{8,11},{9,10},{10,... | collective-permute-start | bytes 245768 | tf_op jit(solution)/shard_map/ppermute | solution.py:492
  11.9 1.0 %spectral.1 = (f32[8,256,128]{2,1,0:T(8,128)S(1)}, f32[8,128]{1,0:T(8,128)S(1)}) custom-call(s32[3,128]{1,0:T(4,128)S(1)} %pad_add_fusion.refs_0_, f32[8,128,128]{2,1,0:T(8,128)S(1)} %copy-done.1), custom_call_target="tpu_custom_call" | custom-call | flops 2000000000 | tf_op jit(solution)/shard_map/spectral/pallas_call | solution.py:447
  12.9 1.3 %part.5 = (f32[1024,256]{1,0:T(8,128)S(1)}, bf16[1,256,1024]{2,1,0:T(8,128)(2,1)S(1)}, f32[2,72,512]{2,1,0:T(8,128)S(1)}) custom-call(bf16[2,80,128]{2,1,0:T(8,128)(2,1)S(1)} %collective-permute-done.1.refs_0_, f32[1024,256]{1,0:T(8,128)S(1)} %get-tuple-element.26.refs_1_), custom_call_target="tpu_custom_call", output_to_operand_aliasing={{0}: (1, {})} | custom-call | flops 1000000000 | tf_op jit(solution)/shard_map/part/pallas_call | solution.py:477
  14.9 1.7 %leaving.2 = (bf16[512,256]{1,0:T(8,128)(2,1)S(1)}, bf16[1,256,2048]{2,1,0:T(8,128)(2,1)S(1)}, f32[4,72,512]{2,1,0:T(8,128)S(1)}) custom-call(bf16[4,80,128]{2,1,0:T(8,128)(2,1)S(1)} %collective-permute-done.2.refs_0_, f32[1024,256]{1,0:T(8,128)S(1)} %get-tuple-element.27.refs_1_.refs_3_), custom_call_target="tpu_custom_call" | custom-call | flops 1000000000 | tf_op jit(solution)/shard_map/leaving/pallas_call | solution.py:477
  17.0 0.8 %staying.2.refs_0_ = f32[512,256]{1,0:T(8,128)S(1)} custom-call(bf16[4,80,128]{2,1,0:T(8,128)(2,1)S(1)} %collective-permute-done.2.refs_0_, bf16[1,256,2048]{2,1,0:T(8,128)(2,1)S(1)} %get-tuple-element.28.refs_1_, f32[4,72,512]{2,1,0:T(8,128)S(1)} %get-tuple-element.29.refs_2_, f32[1024,256]{1,0:T(8,128)S(1)} %get-tuple-element.27.refs_1_.refs_3_), custom_call_target="tpu_custom_call" | custom-call | flops 2000000000 | tf_op jit(solution)/shard_map/staying/pallas_call | solution.py:477
  18.3 0.8 %far.2 = (f32[32,128]{1,0:T(8,128)S(1)}, f32[32,128]{1,0:T(8,128)S(1)}) custom-call(f32[512,256]{1,0:T(8,128)S(1)} %staying.2.refs_0_, bf16[512,256]{1,0:T(8,128)(2,1)S(1)} %collective-permute-done.4.refs_1_, f32[8,256,128]{2,1,0:T(8,128)S(1)} %get-tuple-element.32.refs_2_, bf16[1,256,1024]{2,1,0:T(8,128)(2,1)S(1)} %get-tuple-element.33.refs_3_.refs_1_, ...), custom_call_target="tpu_custom_call" | custom-call | flops 1000000000 | tf_op jit(solution)/shard_map/far/pallas_call | solution.py:506
  19.5 0.9 %near.2.refs_1_ = f32[64,128]{1,0:T(8,128)S(1)} custom-call(bf16[16,80,128]{2,1,0:T(8,128)(2,1)S(1)} %constant_dynamic-update-slice_fusion.refs_0_, bf16[4,9,2,128,128]{4,3,2,1,0:T(8,128)(2,1)S(1)} %bitcast.22, s32[4,9]{1,0:T(4,128)S(1)} %bitcast.25), custom_call_target="tpu_custom_call" | custom-call | flops 2000000000 | tf_op jit(solution)/shard_map/near/pallas_call | solution.py:522
  20.4 3.2 %collective-permute-start.7 = (bf16[1,64,128]{2,1,0:T(8,128)(2,1)S(1)}, bf16[1,64,128]{2,1,0:T(8,128)(2,1)S(1)}, u32[]{:S(2)}, u32[]{:S(2)}) collective-permute-start(bf16[1,64,128]{2,1,0:T(8,128)(2,1)S(1)} %bitcast.18), channel_id=1, source_target_pairs={{0,9},{1,8},{2,11},{3,10},{4,13},{5,12},{6,15},{7,14},{8,1},{9,0},... | collective-permute-start | bytes 49160 | tf_op jit(solution)/shard_map/ppermute | solution.py:492
  23.6 1.4 %collective-permute-done.7 = bf16[1,64,128]{2,1,0:T(8,128)(2,1)S(1)} collective-permute-done((bf16[1,64,128]{2,1,0:T(8,128)(2,1)S(1)}, bf16[1,64,128]{2,1,0:T(8,128)(2,1)S(1)}, u32[]{:S(2)}, u32[]{:S(2)}) %collective-permute-start.7) | collective-permute-done | bytes 16416 | tf_op jit(solution)/shard_map/ppermute | solution.py:492
  25.0 1.9 %collective-permute-start.8 = (bf16[2,64,128]{2,1,0:T(8,128)(2,1)S(1)}, bf16[2,64,128]{2,1,0:T(8,128)(2,1)S(1)}, u32[]{:S(2)}, u32[]{:S(2)}) collective-permute-start(bf16[2,64,128]{2,1,0:T(8,128)(2,1)S(1)} %pad_maximum_fusion.6.refs_0_), channel_id=1, source_target_pairs={{0,5},{1,4},{2,7},{3,6},{4,1},{5,0},{6,3},{7,2},{8,13},{9,12},{10,... | collective-permute-start | bytes 98312 | tf_op jit(solution)/shard_map/ppermute | solution.py:492
  26.9 0.8 %part.6.refs_3_ = f32[1024,256]{1,0:T(8,128)S(1)} custom-call(bf16[2,64,128]{2,1,0:T(8,128)(2,1)S(1)} %pad_maximum_fusion.6.refs_0_, bf16[1,256,1024]{2,1,0:T(8,128)(2,1)S(1)} %get-tuple-element.33.refs_3_.refs_1_, f32[2,72,512]{2,1,0:T(8,128)S(1)} %get-tuple-element.34.refs_4_.refs_2_), custom_call_target="tpu_custom_call" | custom-call | flops 1000000000 | tf_op jit(solution)/shard_map/part/pallas_call | solution.py:477
  27.7 0.8 %collective-permute-done.8.refs_0_ = bf16[2,64,128]{2,1,0:T(8,128)(2,1)S(1)} collective-permute-done((bf16[2,64,128]{2,1,0:T(8,128)(2,1)S(1)}, bf16[2,64,128]{2,1,0:T(8,128)(2,1)S(1)}, u32[]{:S(2)}, u32[]{:S(2)}) %collective-permute-start.8) | collective-permute-done | bytes 32800 | tf_op jit(solution)/shard_map/ppermute | solution.py:492
  28.5 1.4 %collective-permute-start.9 = (bf16[4,64,128]{2,1,0:T(8,128)(2,1)S(1)}, bf16[4,64,128]{2,1,0:T(8,128)(2,1)S(1)}, u32[]{:S(2)}, u32[]{:S(2)}) collective-permute-start(bf16[4,64,128]{2,1,0:T(8,128)(2,1)S(1)} %pad_maximum_fusion.3), channel_id=1, source_target_pairs={{0,3},{1,2},{2,1},{3,0},{4,7},{5,6},{6,5},{7,4},{8,11},{9,10},{10,... | collective-permute-start | bytes 196616 | tf_op jit(solution)/shard_map/ppermute | solution.py:492
  29.9 0.8 %part.7.refs_3_ = f32[1024,256]{1,0:T(8,128)S(1)} custom-call(bf16[2,64,128]{2,1,0:T(8,128)(2,1)S(1)} %collective-permute-done.8.refs_0_, bf16[1,256,1024]{2,1,0:T(8,128)(2,1)S(1)} %get-tuple-element.42.refs_1_, f32[2,72,512]{2,1,0:T(8,128)S(1)} %get-tuple-element.43.refs_2_, f32[1024,256]{1,0:T(8,128)S(1)} %part.6.refs_3_), custom_call_target="tpu_custom_call", output_to_operand_aliasing={{}: (3, {})} | custom-call | flops 1000000000 | tf_op jit(solution)/shard_map/part/pallas_call | solution.py:477
  30.7 1.9 %collective-permute-done.9.refs_0_ = bf16[4,64,128]{2,1,0:T(8,128)(2,1)S(1)} collective-permute-done((bf16[4,64,128]{2,1,0:T(8,128)(2,1)S(1)}, bf16[4,64,128]{2,1,0:T(8,128)(2,1)S(1)}, u32[]{:S(2)}, u32[]{:S(2)}) %collective-permute-start.9) | collective-permute-done | bytes 65568 | tf_op jit(solution)/shard_map/ppermute | solution.py:492
  32.9 0.8 %leaving.3 = bf16[512,256]{1,0:T(8,128)(2,1)S(1)} custom-call(bf16[4,64,128]{2,1,0:T(8,128)(2,1)S(1)} %collective-permute-done.9.refs_0_, bf16[1,256,2048]{2,1,0:T(8,128)(2,1)S(1)} %get-tuple-element.28.refs_1_, f32[4,72,512]{2,1,0:T(8,128)S(1)} %get-tuple-element.29.refs_2_, f32[1024,256]{1,0:T(8,128)S(1)} %part.7.refs_3_), custom_call_target="tpu_custom_call" | custom-call | flops 1000000000 | tf_op jit(solution)/shard_map/leaving/pallas_call | solution.py:477
  34.1 0.8 %staying.3.refs_0_ = f32[512,256]{1,0:T(8,128)S(1)} custom-call(bf16[4,64,128]{2,1,0:T(8,128)(2,1)S(1)} %collective-permute-done.9.refs_0_, bf16[1,256,2048]{2,1,0:T(8,128)(2,1)S(1)} %get-tuple-element.28.refs_1_, f32[4,72,512]{2,1,0:T(8,128)S(1)} %get-tuple-element.29.refs_2_, f32[1024,256]{1,0:T(8,128)S(1)} %part.7.refs_3_), custom_call_target="tpu_custom_call" | custom-call | flops 2000000000 | tf_op jit(solution)/shard_map/staying/pallas_call | solution.py:477
  35.3 0.8 %far.3 = (f32[32,128]{1,0:T(8,128)S(1)}, f32[32,128]{1,0:T(8,128)S(1)}) custom-call(f32[512,256]{1,0:T(8,128)S(1)} %staying.3.refs_0_, bf16[512,256]{1,0:T(8,128)(2,1)S(1)} %collective-permute-done.11.refs_1_, f32[8,256,128]{2,1,0:T(8,128)S(1)} %get-tuple-element.32.refs_2_, bf16[1,256,1024]{2,1,0:T(8,128)(2,1)S(1)} %get-tuple-element.33.refs_3_.refs_1_, ...), custom_call_target="tpu_custom_call" | custom-call | flops 1000000000 | tf_op jit(solution)/shard_map/far/pallas_call | solution.py:506
  36.5 0.9 %near.3.refs_1_ = f32[64,128]{1,0:T(8,128)S(1)} custom-call(bf16[16,64,128]{2,1,0:T(8,128)(2,1)S(1)} %constant_dynamic-update-slice_fusion.5.refs_0_.refs_1_, bf16[4,9,2,128,128]{4,3,2,1,0:T(8,128)(2,1)S(1)} %bitcast.23, s32[4,9]{1,0:T(4,128)S(1)} %bitcast.26), custom_call_target="tpu_custom_call" | custom-call | flops 2000000000 | tf_op jit(solution)/shard_map/near/pallas_call | solution.py:522
  (45 shorter events, 5.5 us)
Async XLA Ops:
  1.4 5.1 %collective-permute-start = (bf16[1,80,128]{2,1,0:T(8,128)(2,1)S(1)}, bf16[1,80,128]{2,1,0:T(8,128)(2,1)S(1)}, u32[]{:S(2)}, u32[]{:S(2)}) collective-permute-start(bf16[1,80,128]{2,1,0:T(8,128)(2,1)S(1)} %bitcast.14), channel_id=1, source_target_pairs={{0,9},{1,8},{2,11},{3,10},{4,13},{5,12},{6,15},{7,14},{8,1},{9,0},... | collective-permute-start | bytes 61448 | tf_op jit(solution)/shard_map/ppermute | solution.py:492
  6.5 3.7 %collective-permute-start.1 = (bf16[2,80,128]{2,1,0:T(8,128)(2,1)S(1)}, bf16[2,80,128]{2,1,0:T(8,128)(2,1)S(1)}, u32[]{:S(2)}, u32[]{:S(2)}) collective-permute-start(bf16[2,80,128]{2,1,0:T(8,128)(2,1)S(1)} %pad_maximum_fusion.4.refs_0_), channel_id=1, source_target_pairs={{0,5},{1,4},{2,7},{3,6},{4,1},{5,0},{6,3},{7,2},{8,13},{9,12},{10,... | collective-permute-start | bytes 122888 | tf_op jit(solution)/shard_map/ppermute | solution.py:492
  8.3 1.6 %collective-permute-start.5 = (bf16[80,128]{1,0:T(8,128)(2,1)S(1)}, bf16[80,128]{1,0:T(8,128)(2,1)S(1)}, u32[]{:S(2)}, u32[]{:S(2)}) collective-permute-start(bf16[80,128]{1,0:T(8,128)(2,1)S(1)} %pack.1.refs_0_), channel_id=1, source_target_pairs={{0,1},{1,0},{2,3},{3,2},{4,5},{5,4},{6,7},{7,6},{8,9},{9,8},{10,11... | collective-permute-start | bytes 61448 | tf_op jit(solution)/shard_map/ppermute | solution.py:78
  8.7 3.2 %copy-start.1 = (f32[8,128,128]{2,1,0:T(8,128)S(1)}, f32[8,128,128]{2,1,0:T(8,128)}, u32[]{:S(2)}) copy-start(f32[8,128,128]{2,1,0:T(8,128)} %refs_1_.1) | copy-start | bytes 1572868
  10.2 4.4 %collective-permute-start.2 = (bf16[4,80,128]{2,1,0:T(8,128)(2,1)S(1)}, bf16[4,80,128]{2,1,0:T(8,128)(2,1)S(1)}, u32[]{:S(2)}, u32[]{:S(2)}) collective-permute-start(bf16[4,80,128]{2,1,0:T(8,128)(2,1)S(1)} %pad_maximum_fusion.2), channel_id=1, source_target_pairs={{0,3},{1,2},{2,1},{3,0},{4,7},{5,6},{6,5},{7,4},{8,11},{9,10},{10,... | collective-permute-start | bytes 245768 | tf_op jit(solution)/shard_map/ppermute | solution.py:492
  14.6 3.3 %collective-permute-start.3 = (bf16[8,80,128]{2,1,0:T(8,128)(2,1)S(1)}, bf16[8,80,128]{2,1,0:T(8,128)(2,1)S(1)}, u32[]{:S(2)}, u32[]{:S(2)}) collective-permute-start(bf16[8,80,128]{2,1,0:T(8,128)(2,1)S(1)} %pad_maximum_fusion), channel_id=1, source_target_pairs={{0,1},{1,0},{2,3},{3,2},{4,5},{5,4},{6,7},{7,6},{8,9},{9,8},{10,11... | collective-permute-start | bytes 491528 | tf_op jit(solution)/shard_map/ppermute | solution.py:78
  16.7 1.6 %collective-permute-start.4 = (bf16[512,256]{1,0:T(8,128)(2,1)S(1)}, bf16[512,256]{1,0:T(8,128)(2,1)S(1)}, u32[]{:S(2)}, u32[]{:S(2)}) collective-permute-start(bf16[512,256]{1,0:T(8,128)(2,1)S(1)} %get-tuple-element.30), channel_id=1, source_target_pairs={{0,1},{1,0},{2,3},{3,2},{4,5},{5,4},{6,7},{7,6},{8,9},{9,8},{10,11... | collective-permute-start | bytes 786440 | tf_op jit(solution)/shard_map/ppermute | solution.py:78
  17.8 1.7 %copy-start = (bf16[1,4,9,2,128,128]{5,4,3,2,1,0:T(8,128)(2,1)S(1)}, bf16[1,4,9,2,128,128]{5,4,3,2,1,0:T(8,128)(2,1)}, u32[]{:S(2)}) copy-start(bf16[1,4,9,2,128,128]{5,4,3,2,1,0:T(8,128)(2,1)} %param.9) | copy-start | bytes 7077892
  17.8 1.7 %copy-start.2 = (s32[1,4,9]{2,1,0:T(4,128)S(1)}, s32[1,4,9]{2,1,0:T(4,128)}, u32[]{:S(2)}) copy-start(s32[1,4,9]{2,1,0:T(4,128)} %param.11) | copy-start | bytes 436
  19.1 1.3 %collective-permute-start.6 = (f32[32,128]{1,0:T(8,128)S(1)}, f32[32,128]{1,0:T(8,128)S(1)}, u32[]{:S(2)}, u32[]{:S(2)}) collective-permute-start(f32[32,128]{1,0:T(8,128)S(1)} %get-tuple-element.39), channel_id=1, source_target_pairs={{0,1},{1,0},{2,3},{3,2},{4,5},{5,4},{6,7},{7,6},{8,9},{9,8},{10,11... | collective-permute-start | bytes 49160 | tf_op jit(solution)/shard_map/ppermute | solution.py:78
  20.4 4.6 %collective-permute-start.7 = (bf16[1,64,128]{2,1,0:T(8,128)(2,1)S(1)}, bf16[1,64,128]{2,1,0:T(8,128)(2,1)S(1)}, u32[]{:S(2)}, u32[]{:S(2)}) collective-permute-start(bf16[1,64,128]{2,1,0:T(8,128)(2,1)S(1)} %bitcast.18), channel_id=1, source_target_pairs={{0,9},{1,8},{2,11},{3,10},{4,13},{5,12},{6,15},{7,14},{8,1},{9,0},... | collective-permute-start | bytes 49160 | tf_op jit(solution)/shard_map/ppermute | solution.py:492
  25.0 3.5 %collective-permute-start.8 = (bf16[2,64,128]{2,1,0:T(8,128)(2,1)S(1)}, bf16[2,64,128]{2,1,0:T(8,128)(2,1)S(1)}, u32[]{:S(2)}, u32[]{:S(2)}) collective-permute-start(bf16[2,64,128]{2,1,0:T(8,128)(2,1)S(1)} %pad_maximum_fusion.6.refs_0_), channel_id=1, source_target_pairs={{0,5},{1,4},{2,7},{3,6},{4,1},{5,0},{6,3},{7,2},{8,13},{9,12},{10,... | collective-permute-start | bytes 98312 | tf_op jit(solution)/shard_map/ppermute | solution.py:492
  28.5 4.1 %collective-permute-start.9 = (bf16[4,64,128]{2,1,0:T(8,128)(2,1)S(1)}, bf16[4,64,128]{2,1,0:T(8,128)(2,1)S(1)}, u32[]{:S(2)}, u32[]{:S(2)}) collective-permute-start(bf16[4,64,128]{2,1,0:T(8,128)(2,1)S(1)} %pad_maximum_fusion.3), channel_id=1, source_target_pairs={{0,3},{1,2},{2,1},{3,0},{4,7},{5,6},{6,5},{7,4},{8,11},{9,10},{10,... | collective-permute-start | bytes 196616 | tf_op jit(solution)/shard_map/ppermute | solution.py:492
  32.6 2.3 %collective-permute-start.10 = (bf16[8,64,128]{2,1,0:T(8,128)(2,1)S(1)}, bf16[8,64,128]{2,1,0:T(8,128)(2,1)S(1)}, u32[]{:S(2)}, u32[]{:S(2)}) collective-permute-start(bf16[8,64,128]{2,1,0:T(8,128)(2,1)S(1)} %pad_maximum_fusion.1), channel_id=1, source_target_pairs={{0,1},{1,0},{2,3},{3,2},{4,5},{5,4},{6,7},{7,6},{8,9},{9,8},{10,11... | collective-permute-start | bytes 393224 | tf_op jit(solution)/shard_map/ppermute | solution.py:78
  33.7 1.6 %collective-permute-start.11 = (bf16[512,256]{1,0:T(8,128)(2,1)S(1)}, bf16[512,256]{1,0:T(8,128)(2,1)S(1)}, u32[]{:S(2)}, u32[]{:S(2)}) collective-permute-start(bf16[512,256]{1,0:T(8,128)(2,1)S(1)} %leaving.3), channel_id=1, source_target_pairs={{0,1},{1,0},{2,3},{3,2},{4,5},{5,4},{6,7},{7,6},{8,9},{9,8},{10,11... | collective-permute-start | bytes 786440 | tf_op jit(solution)/shard_map/ppermute | solution.py:78
  36.1 1.3 %collective-permute-start.12 = (f32[32,128]{1,0:T(8,128)S(1)}, f32[32,128]{1,0:T(8,128)S(1)}, u32[]{:S(2)}, u32[]{:S(2)}) collective-permute-start(f32[32,128]{1,0:T(8,128)S(1)} %get-tuple-element.46), channel_id=1, source_target_pairs={{0,1},{1,0},{2,3},{3,2},{4,5},{5,4},{6,7},{7,6},{8,9},{9,8},{10,11... | collective-permute-start | bytes 49160 | tf_op jit(solution)/shard_map/ppermute | solution.py:78

commit v6 on v5

--- a/solution.py
+++ b/solution.py
@@ -8,7 +8,7 @@
 from jax.sharding import PartitionSpec as P
 
 eps_norm = 1e-06
-lengths = {"part": 1, "leaving": 1, "staying": 2, "spectral": 2, "other_tables": 0.5, "far": 1, "near": 2}
+lengths = {"part": 1, "leaving": 0.5, "staying": 0.8, "spectral": 2, "other_tables": 0.5, "far": 0.3, "near": 2}
 f32 = jnp.float32
 bf16 = jnp.bfloat16
 lanes = 128
@@ -129,11 +129,12 @@
         mean = jnp.sum(jnp.sum(moved, 0, keepdims=True), 1, keepdims=True)
         rows.append(jnp.broadcast_to(0.5 + mean, (1, lanes)))
         part = [moved[k * quarter : (k + 1) * quarter] for k in range(4)]
-        for k, (one, other) in enumerate(((part[1], part[3]), (part[2], part[0]), (part[0], part[2]), (part[3], part[1]))):
-            chosen = jnp.where(low, one, other)
-            turned = swap(chosen)
-            out[v, 2 * k * quarter : (2 * k + 1) * quarter, :] = chosen + turned
-            out[v, (2 * k + 1) * quarter : (2 * k + 2) * quarter, :] = chosen - turned
+        for k, choices in enumerate((((1, 3), (0, 2)), ((2, 0), (3, 1)))):
+            chosen = [jnp.where(low, part[one], part[other]) for one, other in choices]
+            turned = [swap(value) for value in chosen]
+            plus = jnp.where(low, chosen[0] + turned[0], chosen[1] + turned[1])
+            minus = jnp.where(low, chosen[0] - turned[0], turned[1] - chosen[1])
+            out[v, 2 * k * quarter : 2 * (k + 1) * quarter, :] = jnp.concatenate([plus, minus], 0)
     guess[...] = jnp.concatenate(rows, 0)
 
 
@@ -166,7 +167,8 @@
                 c, s = both_c[a : a + 1], both_s[a : a + 1]
                 cosines.append(c * fine_xc - s * fine_xs)
                 sines.append(s * fine_xc + c * fine_xs)
-            table_x[group, 2 * half * e : 2 * half * (e + 1), wide] = jnp.concatenate(cosines + sines, 0).astype(bf16)
+            table_x[group, half * e : half * (e + 1), wide] = jnp.concatenate(cosines, 0).astype(bf16)
+            table_x[group, half * (e + 2) : half * (e + 3), wide] = jnp.concatenate(sines, 0).astype(bf16)
         cosines, sines = [], []
         for a in range(quarter // 8):
             c, s = big_yc[a : a + 1], big_ys[a : a + 1]
@@ -249,26 +251,27 @@
 def weigh(layout, total, weight, scaled):
     quarter = layout.quarter
     first = lax.axis_index("wave") * layout.part_v
-    low = lax.broadcasted_iota(jnp.int32, (quarter, lanes), 1) < layout.half
-    sign = jnp.where(low, -1.0, 1.0)
     for v in range(layout.part_v):
-        for e in range(2):
-            span = slice(e * lanes, (e + 1) * lanes)
-            real = v * 4 * quarter
-            imag = real + 2 * quarter
-            cos_r = total[real : real + quarter, span]
-            sin_r = swap(total[real + quarter : real + 2 * quarter, span]) * sign
-            cos_i = total[imag : imag + quarter, span]
-            sin_i = swap(total[imag + quarter : imag + 2 * quarter, span]) * sign
-            out = []
-            for k, (mr, mi) in enumerate(((cos_r + sin_r, cos_i + sin_i), (cos_r - sin_r, cos_i - sin_i))):
-                start = 2 * (2 * e + k) * quarter
-                plus = weight[first + v, start : start + quarter, :]
-                minus = weight[first + v, start + quarter : start + 2 * quarter, :]
-                out.append((plus * mr + minus * swap(mi), plus * mi - minus * swap(mr)))
-            for start, k in ((real, 0), (imag, 1)):
-                scaled[start : start + quarter, span] = (out[0][k] + out[1][k]).astype(bf16)
-                scaled[start + quarter : start + 2 * quarter, span] = swap(sign * (out[0][k] - out[1][k])).astype(bf16)
+        plus_sum, plus_rest, minus_sum, minus_rest = [
+            weight[first + v, k * quarter : (k + 1) * quarter, :] for k in range(4)
+        ]
+        starts = [(4 * v + k) * quarter for k in range(4)]
+        cc, cs = [[total[starts[2 * part + k] : starts[2 * part + k] + quarter, :lanes] for part in range(2)] for k in range(2)]
+        sc, ss = [[total[starts[2 * part + k] : starts[2 * part + k] + quarter, lanes:] for part in range(2)] for k in range(2)]
+        ur, ui = [cc[part] - ss[part] for part in range(2)]
+        vr, vi = [sc[part] + cs[part] for part in range(2)]
+        one = plus_sum * ur + plus_rest * vi, plus_sum * ui - plus_rest * vr
+        one_sine = plus_sum * vr - plus_rest * ui, plus_sum * vi + plus_rest * ur
+        ur, ui = [cc[part] + ss[part] for part in range(2)]
+        vr, vi = [sc[part] - cs[part] for part in range(2)]
+        two = minus_sum * ur + minus_rest * vi, minus_sum * ui - minus_rest * vr
+        two_sine = minus_sum * vr - minus_rest * ui, minus_sum * vi + minus_rest * ur
+        for part in range(2):
+            cosine, sine = [slice(start, start + quarter) for start in starts[2 * part : 2 * part + 2]]
+            scaled[cosine, :lanes] = (one[part] + two[part]).astype(bf16)
+            scaled[cosine, lanes:] = (one_sine[part] + two_sine[part]).astype(bf16)
+            scaled[sine, :lanes] = (one_sine[part] - two_sine[part]).astype(bf16)
+            scaled[sine, lanes:] = (two[part] - one[part]).astype(bf16)
 
 
 def expand(layout, scaled, table_x, table_y, summed, result):
@@ -447,7 +450,7 @@
         return call(
             lambda *refs: spectral_kernel(layout, scale, *refs),
             "spectral",
-            (shape((vectors, 2 * modes_y, modes_x), f32), shape((vectors, lanes), f32)),
+            (shape((vectors, modes_y, modes_x), f32), shape((vectors, lanes), f32)),
             [vmem, vmem],
             4,
             [

time: 38.3 us -> 37.4 us (0.977)
  Pallas kernels: 13.7 us -> 12.9 us
    pallas_call x2, Pallas kernels: 1.6 us -> 1 us  [far_field(): call(lambda *refs: far_kernel(layout, *refs), 'far', tuple([shape((rows /...]
    ppermute x7, waiting for transfers between devices: 0.38 us -> 0.78 us  [swap_cores(): return lax.ppermute(array, 'wave', [(0, 1), (1, 0)])]
  transfers between devices with their start and end apart: 13 -> 13, of which waited for: 6 -> 9; matrix products, arithmetic and copies ran while one was open for 4% -> 4% of each run, Pallas kernels for 30% -> 30%
where the time goes in v6:
time: 37.4 us; the launch traced here: 37.2 us
  starting transfers between devices  15.9 us (43%)
  Pallas kernels  12.9 us (34%)
  waiting for transfers between devices  5.27 us (14%)
  other arithmetic  1.53 us (4%)
  between operations  0.83 us (2%)
  local copies, waits for them, and re-layouts  0.78 us (2%)
    ppermute x6, starting transfers between devices, gather_and_project(): arrived = lax.ppermute(array, ('tile', 'wave'), pairs)  13.6 us
    pallas_call x8, Pallas kernels, part_call(): call(lambda *refs: part_kernel(layout, base, with_start, not tables, halv...  8.05 us
    ppermute x6, waiting for transfers between devices, gather_and_project(): arrived = lax.ppermute(array, ('tile', 'wave'), pairs)  4.49 us
    ppermute x7, starting transfers between devices, swap_cores(): return lax.ppermute(array, 'wave', [(0, 1), (1, 0)])  2.3 us
    pallas_call x2, Pallas kernels, near_field(): call(lambda *refs: near_kernel(layout, *refs), 'near', shape((rows, lanes...  1.73 us
    pallas_call x2, Pallas kernels, far_field(): call(lambda *refs: far_kernel(layout, *refs), 'far', tuple([shape((rows /...  1 us
    pallas_call x1, Pallas kernels, spectral(): call(lambda *refs: spectral_kernel(layout, scale, *refs), 'spectral', (sh...  0.97 us
    ppermute x7, waiting for transfers between devices, swap_cores(): return lax.ppermute(array, 'wave', [(0, 1), (1, 0)])  0.78 us
  transfers between devices with their start and end apart: 13, of which 9 were waited for; matrix products, arithmetic and copies ran while one was open for 4% of the time, Pallas kernels for 30%

profile of v6, /device:TPU:0, one launch (start us, length us, event | category | flops | bytes accessed | tf_op | source)
XLA Modules:
  0.0 37.2 jit_solution(7154804688815029727)
XLA Ops:
  0.6 0.8 %pad_maximum_fusion.5.refs_0_ = f32[72,128]{1,0:T(8,128)S(1)} fusion(f32[8,128]{1,0:T(8,128)} %bitcast.28, f32[64,128]{1,0:T(8,128)} %bitcast.27), kind=kLoop, calls=%fused_computation.5 | loop fusion | flops 9216 | bytes 73728 | tf_op jit(solution)/shard_map/concatenate | solution.py:438
  1.4 3.5 %collective-permute-start = (bf16[1,80,128]{2,1,0:T(8,128)(2,1)S(1)}, bf16[1,80,128]{2,1,0:T(8,128)(2,1)S(1)}, u32[]{:S(2)}, u32[]{:S(2)}) collective-permute-start(bf16[1,80,128]{2,1,0:T(8,128)(2,1)S(1)} %bitcast.14), channel_id=1, source_target_pairs={{0,9},{1,8},{2,11},{3,10},{4,13},{5,12},{6,15},{7,14},{8,1},{9,0},... | collective-permute-start | bytes 61448 | tf_op jit(solution)/shard_map/ppermute | solution.py:495
  5.0 0.7 %pad_bitcast_fusion = s32[1,128]{1,0:T(1,128)S(1)} fusion(s32[8]{0:T(128)} %param.12), kind=kLoop, calls=%fused_computation.18 | loop fusion | bytes 544 | tf_op jit(solution)/shard_map/stack | solution.py:447
  5.6 0.7 %pad_add_fusion.refs_0_ = s32[3,128]{1,0:T(4,128)S(1)} fusion(s32[1,128]{1,0:T(1,128)S(1)} %pad_bitcast_fusion, s32[1,128]{1,0:T(1,128)} %bitcast.29, s32[1,128]{1,0:T(1,128)} %bitcast.30), kind=kLoop, calls=%fused_computation.17 | loop fusion | flops 768 | bytes 3072 | tf_op jit(solution)/shard_map/stack | solution.py:447
  6.5 1.9 %collective-permute-start.1 = (bf16[2,80,128]{2,1,0:T(8,128)(2,1)S(1)}, bf16[2,80,128]{2,1,0:T(8,128)(2,1)S(1)}, u32[]{:S(2)}, u32[]{:S(2)}) collective-permute-start(bf16[2,80,128]{2,1,0:T(8,128)(2,1)S(1)} %pad_maximum_fusion.4.refs_0_), channel_id=1, source_target_pairs={{0,5},{1,4},{2,7},{3,6},{4,1},{5,0},{6,3},{7,2},{8,13},{9,12},{10,... | collective-permute-start | bytes 122888 | tf_op jit(solution)/shard_map/ppermute | solution.py:495
  8.7 1.2 %part.4 = (f32[1024,256]{1,0:T(8,128)S(1)}, bf16[1,256,1024]{2,1,0:T(8,128)(2,1)S(1)}, f32[2,72,512]{2,1,0:T(8,128)S(1)}) custom-call(bf16[2,80,128]{2,1,0:T(8,128)(2,1)S(1)} %pad_maximum_fusion.4.refs_0_), custom_call_target="tpu_custom_call" | custom-call | flops 1000000000 | tf_op jit(solution)/shard_map/part/pallas_call | solution.py:480
  10.2 1.7 %collective-permute-start.2 = (bf16[4,80,128]{2,1,0:T(8,128)(2,1)S(1)}, bf16[4,80,128]{2,1,0:T(8,128)(2,1)S(1)}, u32[]{:S(2)}, u32[]{:S(2)}) collective-permute-start(bf16[4,80,128]{2,1,0:T(8,128)(2,1)S(1)} %pad_maximum_fusion.2), channel_id=1, source_target_pairs={{0,3},{1,2},{2,1},{3,0},{4,7},{5,6},{6,5},{7,4},{8,11},{9,10},{10,... | collective-permute-start | bytes 245768 | tf_op jit(solution)/shard_map/ppermute | solution.py:495
  11.9 1.0 %spectral.1 = (f32[8,128,128]{2,1,0:T(8,128)S(1)}, f32[8,128]{1,0:T(8,128)S(1)}) custom-call(s32[3,128]{1,0:T(4,128)S(1)} %pad_add_fusion.refs_0_, f32[8,128,128]{2,1,0:T(8,128)S(1)} %copy-done.1), custom_call_target="tpu_custom_call" | custom-call | flops 2000000000 | tf_op jit(solution)/shard_map/spectral/pallas_call | solution.py:450
  12.9 1.3 %part.5 = (f32[1024,256]{1,0:T(8,128)S(1)}, bf16[1,256,1024]{2,1,0:T(8,128)(2,1)S(1)}, f32[2,72,512]{2,1,0:T(8,128)S(1)}) custom-call(bf16[2,80,128]{2,1,0:T(8,128)(2,1)S(1)} %collective-permute-done.1.refs_0_, f32[1024,256]{1,0:T(8,128)S(1)} %get-tuple-element.26.refs_1_), custom_call_target="tpu_custom_call", output_to_operand_aliasing={{0}: (1, {})} | custom-call | flops 1000000000 | tf_op jit(solution)/shard_map/part/pallas_call | solution.py:480
  14.9 1.7 %leaving.2 = (bf16[512,256]{1,0:T(8,128)(2,1)S(1)}, bf16[1,256,2048]{2,1,0:T(8,128)(2,1)S(1)}, f32[4,72,512]{2,1,0:T(8,128)S(1)}) custom-call(bf16[4,80,128]{2,1,0:T(8,128)(2,1)S(1)} %collective-permute-done.2.refs_0_, f32[1024,256]{1,0:T(8,128)S(1)} %get-tuple-element.27.refs_1_.refs_3_), custom_call_target="tpu_custom_call" | custom-call | flops 500000000 | tf_op jit(solution)/shard_map/leaving/pallas_call | solution.py:480
  17.0 0.8 %staying.2.refs_0_ = f32[512,256]{1,0:T(8,128)S(1)} custom-call(bf16[4,80,128]{2,1,0:T(8,128)(2,1)S(1)} %collective-permute-done.2.refs_0_, bf16[1,256,2048]{2,1,0:T(8,128)(2,1)S(1)} %get-tuple-element.28.refs_1_, f32[4,72,512]{2,1,0:T(8,128)S(1)} %get-tuple-element.29.refs_2_, f32[1024,256]{1,0:T(8,128)S(1)} %get-tuple-element.27.refs_1_.refs_3_), custom_call_target="tpu_custom_call" | custom-call | flops 800000000 | tf_op jit(solution)/shard_map/staying/pallas_call | solution.py:480
  19.1 0.9 %near.2.refs_1_ = f32[64,128]{1,0:T(8,128)S(1)} custom-call(bf16[16,80,128]{2,1,0:T(8,128)(2,1)S(1)} %constant_dynamic-update-slice_fusion.refs_0_, bf16[4,9,2,128,128]{4,3,2,1,0:T(8,128)(2,1)S(1)} %bitcast.22, s32[4,9]{1,0:T(4,128)S(1)} %bitcast.25), custom_call_target="tpu_custom_call" | custom-call | flops 2000000000 | tf_op jit(solution)/shard_map/near/pallas_call | solution.py:525
  20.0 3.2 %collective-permute-start.7 = (bf16[1,64,128]{2,1,0:T(8,128)(2,1)S(1)}, bf16[1,64,128]{2,1,0:T(8,128)(2,1)S(1)}, u32[]{:S(2)}, u32[]{:S(2)}) collective-permute-start(bf16[1,64,128]{2,1,0:T(8,128)(2,1)S(1)} %bitcast.18), channel_id=1, source_target_pairs={{0,9},{1,8},{2,11},{3,10},{4,13},{5,12},{6,15},{7,14},{8,1},{9,0},... | collective-permute-start | bytes 49160 | tf_op jit(solution)/shard_map/ppermute | solution.py:495
  23.2 1.4 %collective-permute-done.7 = bf16[1,64,128]{2,1,0:T(8,128)(2,1)S(1)} collective-permute-done((bf16[1,64,128]{2,1,0:T(8,128)(2,1)S(1)}, bf16[1,64,128]{2,1,0:T(8,128)(2,1)S(1)}, u32[]{:S(2)}, u32[]{:S(2)}) %collective-permute-start.7) | collective-permute-done | bytes 16416 | tf_op jit(solution)/shard_map/ppermute | solution.py:495
  24.7 1.8 %collective-permute-start.8 = (bf16[2,64,128]{2,1,0:T(8,128)(2,1)S(1)}, bf16[2,64,128]{2,1,0:T(8,128)(2,1)S(1)}, u32[]{:S(2)}, u32[]{:S(2)}) collective-permute-start(bf16[2,64,128]{2,1,0:T(8,128)(2,1)S(1)} %pad_maximum_fusion.6.refs_0_), channel_id=1, source_target_pairs={{0,5},{1,4},{2,7},{3,6},{4,1},{5,0},{6,3},{7,2},{8,13},{9,12},{10,... | collective-permute-start | bytes 98312 | tf_op jit(solution)/shard_map/ppermute | solution.py:495
  26.5 0.8 %part.6.refs_3_ = f32[1024,256]{1,0:T(8,128)S(1)} custom-call(bf16[2,64,128]{2,1,0:T(8,128)(2,1)S(1)} %pad_maximum_fusion.6.refs_0_, bf16[1,256,1024]{2,1,0:T(8,128)(2,1)S(1)} %get-tuple-element.33.refs_3_.refs_1_, f32[2,72,512]{2,1,0:T(8,128)S(1)} %get-tuple-element.34.refs_4_.refs_2_), custom_call_target="tpu_custom_call" | custom-call | flops 1000000000 | tf_op jit(solution)/shard_map/part/pallas_call | solution.py:480
  27.3 0.8 %collective-permute-done.8.refs_0_ = bf16[2,64,128]{2,1,0:T(8,128)(2,1)S(1)} collective-permute-done((bf16[2,64,128]{2,1,0:T(8,128)(2,1)S(1)}, bf16[2,64,128]{2,1,0:T(8,128)(2,1)S(1)}, u32[]{:S(2)}, u32[]{:S(2)}) %collective-permute-start.8) | collective-permute-done | bytes 32800 | tf_op jit(solution)/shard_map/ppermute | solution.py:495
  28.1 1.5 %collective-permute-start.9 = (bf16[4,64,128]{2,1,0:T(8,128)(2,1)S(1)}, bf16[4,64,128]{2,1,0:T(8,128)(2,1)S(1)}, u32[]{:S(2)}, u32[]{:S(2)}) collective-permute-start(bf16[4,64,128]{2,1,0:T(8,128)(2,1)S(1)} %pad_maximum_fusion.3), channel_id=1, source_target_pairs={{0,3},{1,2},{2,1},{3,0},{4,7},{5,6},{6,5},{7,4},{8,11},{9,10},{10,... | collective-permute-start | bytes 196616 | tf_op jit(solution)/shard_map/ppermute | solution.py:495
  29.6 0.8 %part.7.refs_3_ = f32[1024,256]{1,0:T(8,128)S(1)} custom-call(bf16[2,64,128]{2,1,0:T(8,128)(2,1)S(1)} %collective-permute-done.8.refs_0_, bf16[1,256,1024]{2,1,0:T(8,128)(2,1)S(1)} %get-tuple-element.42.refs_1_, f32[2,72,512]{2,1,0:T(8,128)S(1)} %get-tuple-element.43.refs_2_, f32[1024,256]{1,0:T(8,128)S(1)} %part.6.refs_3_), custom_call_target="tpu_custom_call", output_to_operand_aliasing={{}: (3, {})} | custom-call | flops 1000000000 | tf_op jit(solution)/shard_map/part/pallas_call | solution.py:480
  30.4 1.7 %collective-permute-done.9.refs_0_ = bf16[4,64,128]{2,1,0:T(8,128)(2,1)S(1)} collective-permute-done((bf16[4,64,128]{2,1,0:T(8,128)(2,1)S(1)}, bf16[4,64,128]{2,1,0:T(8,128)(2,1)S(1)}, u32[]{:S(2)}, u32[]{:S(2)}) %collective-permute-start.9) | collective-permute-done | bytes 65568 | tf_op jit(solution)/shard_map/ppermute | solution.py:495
  32.4 0.8 %leaving.3 = bf16[512,256]{1,0:T(8,128)(2,1)S(1)} custom-call(bf16[4,64,128]{2,1,0:T(8,128)(2,1)S(1)} %collective-permute-done.9.refs_0_, bf16[1,256,2048]{2,1,0:T(8,128)(2,1)S(1)} %get-tuple-element.28.refs_1_, f32[4,72,512]{2,1,0:T(8,128)S(1)} %get-tuple-element.29.refs_2_, f32[1024,256]{1,0:T(8,128)S(1)} %part.7.refs_3_), custom_call_target="tpu_custom_call" | custom-call | flops 500000000 | tf_op jit(solution)/shard_map/leaving/pallas_call | solution.py:480
  33.5 0.8 %staying.3.refs_0_ = f32[512,256]{1,0:T(8,128)S(1)} custom-call(bf16[4,64,128]{2,1,0:T(8,128)(2,1)S(1)} %collective-permute-done.9.refs_0_, bf16[1,256,2048]{2,1,0:T(8,128)(2,1)S(1)} %get-tuple-element.28.refs_1_, f32[4,72,512]{2,1,0:T(8,128)S(1)} %get-tuple-element.29.refs_2_, f32[1024,256]{1,0:T(8,128)S(1)} %part.7.refs_3_), custom_call_target="tpu_custom_call" | custom-call | flops 800000000 | tf_op jit(solution)/shard_map/staying/pallas_call | solution.py:480
  35.7 0.9 %near.3.refs_1_ = f32[64,128]{1,0:T(8,128)S(1)} custom-call(bf16[16,64,128]{2,1,0:T(8,128)(2,1)S(1)} %constant_dynamic-update-slice_fusion.5.refs_0_.refs_1_, bf16[4,9,2,128,128]{4,3,2,1,0:T(8,128)(2,1)S(1)} %bitcast.23, s32[4,9]{1,0:T(4,128)S(1)} %bitcast.26), custom_call_target="tpu_custom_call" | custom-call | flops 2000000000 | tf_op jit(solution)/shard_map/near/pallas_call | solution.py:525
  36.6 0.6 %second.1 = (f32[64,128]{1,0:T(8,128)}, f32[4,8]{1,0:T(4,128)}) custom-call(bf16[64,128]{1,0:T(8,128)(2,1)S(1)} %get-tuple-element.41.refs_0_, f32[64,128]{1,0:T(8,128)S(1)} %near.3.refs_1_, f32[32,128]{1,0:T(8,128)S(1)} %get-tuple-element.45.refs_2_, f32[32,128]{1,0:T(8,128)S(1)} %collective-permute-done.12.refs_3_, ...), custom_call_target="tpu_custom_call" | custom-call | tf_op jit(solution)/shard_map/second/pallas_call | solution.py:566
  (45 shorter events, 5.3 us)
Async XLA Ops:
  1.4 5.1 %collective-permute-start = (bf16[1,80,128]{2,1,0:T(8,128)(2,1)S(1)}, bf16[1,80,128]{2,1,0:T(8,128)(2,1)S(1)}, u32[]{:S(2)}, u32[]{:S(2)}) collective-permute-start(bf16[1,80,128]{2,1,0:T(8,128)(2,1)S(1)} %bitcast.14), channel_id=1, source_target_pairs={{0,9},{1,8},{2,11},{3,10},{4,13},{5,12},{6,15},{7,14},{8,1},{9,0},... | collective-permute-start | bytes 61448 | tf_op jit(solution)/shard_map/ppermute | solution.py:495
  6.5 3.7 %collective-permute-start.1 = (bf16[2,80,128]{2,1,0:T(8,128)(2,1)S(1)}, bf16[2,80,128]{2,1,0:T(8,128)(2,1)S(1)}, u32[]{:S(2)}, u32[]{:S(2)}) collective-permute-start(bf16[2,80,128]{2,1,0:T(8,128)(2,1)S(1)} %pad_maximum_fusion.4.refs_0_), channel_id=1, source_target_pairs={{0,5},{1,4},{2,7},{3,6},{4,1},{5,0},{6,3},{7,2},{8,13},{9,12},{10,... | collective-permute-start | bytes 122888 | tf_op jit(solution)/shard_map/ppermute | solution.py:495
  8.3 1.6 %collective-permute-start.5 = (bf16[80,128]{1,0:T(8,128)(2,1)S(1)}, bf16[80,128]{1,0:T(8,128)(2,1)S(1)}, u32[]{:S(2)}, u32[]{:S(2)}) collective-permute-start(bf16[80,128]{1,0:T(8,128)(2,1)S(1)} %pack.1.refs_0_), channel_id=1, source_target_pairs={{0,1},{1,0},{2,3},{3,2},{4,5},{5,4},{6,7},{7,6},{8,9},{9,8},{10,11... | collective-permute-start | bytes 61448 | tf_op jit(solution)/shard_map/ppermute | solution.py:78
  8.7 3.2 %copy-start.1 = (f32[8,128,128]{2,1,0:T(8,128)S(1)}, f32[8,128,128]{2,1,0:T(8,128)}, u32[]{:S(2)}) copy-start(f32[8,128,128]{2,1,0:T(8,128)} %refs_1_.1) | copy-start | bytes 1572868
  10.2 4.4 %collective-permute-start.2 = (bf16[4,80,128]{2,1,0:T(8,128)(2,1)S(1)}, bf16[4,80,128]{2,1,0:T(8,128)(2,1)S(1)}, u32[]{:S(2)}, u32[]{:S(2)}) collective-permute-start(bf16[4,80,128]{2,1,0:T(8,128)(2,1)S(1)} %pad_maximum_fusion.2), channel_id=1, source_target_pairs={{0,3},{1,2},{2,1},{3,0},{4,7},{5,6},{6,5},{7,4},{8,11},{9,10},{10,... | collective-permute-start | bytes 245768 | tf_op jit(solution)/shard_map/ppermute | solution.py:495
  14.6 3.2 %collective-permute-start.3 = (bf16[8,80,128]{2,1,0:T(8,128)(2,1)S(1)}, bf16[8,80,128]{2,1,0:T(8,128)(2,1)S(1)}, u32[]{:S(2)}, u32[]{:S(2)}) collective-permute-start(bf16[8,80,128]{2,1,0:T(8,128)(2,1)S(1)} %pad_maximum_fusion), channel_id=1, source_target_pairs={{0,1},{1,0},{2,3},{3,2},{4,5},{5,4},{6,7},{7,6},{8,9},{9,8},{10,11... | collective-permute-start | bytes 491528 | tf_op jit(solution)/shard_map/ppermute | solution.py:78
  16.6 1.6 %collective-permute-start.4 = (bf16[512,256]{1,0:T(8,128)(2,1)S(1)}, bf16[512,256]{1,0:T(8,128)(2,1)S(1)}, u32[]{:S(2)}, u32[]{:S(2)}) collective-permute-start(bf16[512,256]{1,0:T(8,128)(2,1)S(1)} %get-tuple-element.30), channel_id=1, source_target_pairs={{0,1},{1,0},{2,3},{3,2},{4,5},{5,4},{6,7},{7,6},{8,9},{9,8},{10,11... | collective-permute-start | bytes 786440 | tf_op jit(solution)/shard_map/ppermute | solution.py:78
  16.9 2.1 %copy-start = (bf16[1,4,9,2,128,128]{5,4,3,2,1,0:T(8,128)(2,1)S(1)}, bf16[1,4,9,2,128,128]{5,4,3,2,1,0:T(8,128)(2,1)}, u32[]{:S(2)}) copy-start(bf16[1,4,9,2,128,128]{5,4,3,2,1,0:T(8,128)(2,1)} %param.9) | copy-start | bytes 7077892
  17.0 2.1 %copy-start.2 = (s32[1,4,9]{2,1,0:T(4,128)S(1)}, s32[1,4,9]{2,1,0:T(4,128)}, u32[]{:S(2)}) copy-start(s32[1,4,9]{2,1,0:T(4,128)} %param.11) | copy-start | bytes 436
  18.8 1.2 %collective-permute-start.6 = (f32[32,128]{1,0:T(8,128)S(1)}, f32[32,128]{1,0:T(8,128)S(1)}, u32[]{:S(2)}, u32[]{:S(2)}) collective-permute-start(f32[32,128]{1,0:T(8,128)S(1)} %get-tuple-element.39), channel_id=1, source_target_pairs={{0,1},{1,0},{2,3},{3,2},{4,5},{5,4},{6,7},{7,6},{8,9},{9,8},{10,11... | collective-permute-start | bytes 49160 | tf_op jit(solution)/shard_map/ppermute | solution.py:78
  20.0 4.6 %collective-permute-start.7 = (bf16[1,64,128]{2,1,0:T(8,128)(2,1)S(1)}, bf16[1,64,128]{2,1,0:T(8,128)(2,1)S(1)}, u32[]{:S(2)}, u32[]{:S(2)}) collective-permute-start(bf16[1,64,128]{2,1,0:T(8,128)(2,1)S(1)} %bitcast.18), channel_id=1, source_target_pairs={{0,9},{1,8},{2,11},{3,10},{4,13},{5,12},{6,15},{7,14},{8,1},{9,0},... | collective-permute-start | bytes 49160 | tf_op jit(solution)/shard_map/ppermute | solution.py:495
  24.7 3.4 %collective-permute-start.8 = (bf16[2,64,128]{2,1,0:T(8,128)(2,1)S(1)}, bf16[2,64,128]{2,1,0:T(8,128)(2,1)S(1)}, u32[]{:S(2)}, u32[]{:S(2)}) collective-permute-start(bf16[2,64,128]{2,1,0:T(8,128)(2,1)S(1)} %pad_maximum_fusion.6.refs_0_), channel_id=1, source_target_pairs={{0,5},{1,4},{2,7},{3,6},{4,1},{5,0},{6,3},{7,2},{8,13},{9,12},{10,... | collective-permute-start | bytes 98312 | tf_op jit(solution)/shard_map/ppermute | solution.py:495
  28.1 4.0 %collective-permute-start.9 = (bf16[4,64,128]{2,1,0:T(8,128)(2,1)S(1)}, bf16[4,64,128]{2,1,0:T(8,128)(2,1)S(1)}, u32[]{:S(2)}, u32[]{:S(2)}) collective-permute-start(bf16[4,64,128]{2,1,0:T(8,128)(2,1)S(1)} %pad_maximum_fusion.3), channel_id=1, source_target_pairs={{0,3},{1,2},{2,1},{3,0},{4,7},{5,6},{6,5},{7,4},{8,11},{9,10},{10,... | collective-permute-start | bytes 196616 | tf_op jit(solution)/shard_map/ppermute | solution.py:495
  32.1 2.2 %collective-permute-start.10 = (bf16[8,64,128]{2,1,0:T(8,128)(2,1)S(1)}, bf16[8,64,128]{2,1,0:T(8,128)(2,1)S(1)}, u32[]{:S(2)}, u32[]{:S(2)}) collective-permute-start(bf16[8,64,128]{2,1,0:T(8,128)(2,1)S(1)} %pad_maximum_fusion.1), channel_id=1, source_target_pairs={{0,1},{1,0},{2,3},{3,2},{4,5},{5,4},{6,7},{7,6},{8,9},{9,8},{10,11... | collective-permute-start | bytes 393224 | tf_op jit(solution)/shard_map/ppermute | solution.py:78
  33.2 1.6 %collective-permute-start.11 = (bf16[512,256]{1,0:T(8,128)(2,1)S(1)}, bf16[512,256]{1,0:T(8,128)(2,1)S(1)}, u32[]{:S(2)}, u32[]{:S(2)}) collective-permute-start(bf16[512,256]{1,0:T(8,128)(2,1)S(1)} %leaving.3), channel_id=1, source_target_pairs={{0,1},{1,0},{2,3},{3,2},{4,5},{5,4},{6,7},{7,6},{8,9},{9,8},{10,11... | collective-permute-start | bytes 786440 | tf_op jit(solution)/shard_map/ppermute | solution.py:78
  35.3 1.2 %collective-permute-start.12 = (f32[32,128]{1,0:T(8,128)S(1)}, f32[32,128]{1,0:T(8,128)S(1)}, u32[]{:S(2)}, u32[]{:S(2)}) collective-permute-start(f32[32,128]{1,0:T(8,128)S(1)} %get-tuple-element.46), channel_id=1, source_target_pairs={{0,1},{1,0},{2,3},{3,2},{4,5},{5,4},{6,7},{7,6},{8,9},{9,8},{10,11... | collective-permute-start | bytes 49160 | tf_op jit(solution)/shard_map/ppermute | solution.py:78

commit v7 on v6

--- a/solution.py
+++ b/solution.py
@@ -8,7 +8,7 @@
 from jax.sharding import PartitionSpec as P
 
 eps_norm = 1e-06
-lengths = {"part": 1, "leaving": 0.5, "staying": 0.8, "spectral": 2, "other_tables": 0.5, "far": 0.3, "near": 2}
+lengths = {"part": 1, "leaving": 2, "staying": 0.8, "spectral": 2, "other_tables": 0.5, "far": 0.3, "near": 2, "tables": 0.5, "whole": 0.8}
 f32 = jnp.float32
 bf16 = jnp.bfloat16
 lanes = 128
@@ -53,6 +53,12 @@
 
     def me(self):
         return lax.axis_index("tile") * self.waves + lax.axis_index("wave")
+
+    def half_index(self):
+        column, half = lax.axis_index("tile"), lax.axis_index("wave")
+        for b in range(len(self.chip_masks)):
+            half = half ^ ((column >> b) & 1)
+        return half
 
     def device_of(self, block):
         device = self.me()
@@ -180,13 +186,13 @@
 
 def pick_half(layout, rows, other):
     count = layout.part_v
-    core = lax.axis_index("wave")
+    core = layout.half_index()
     upper = jnp.broadcast_to(1 - core if other else core, (count, lanes)) == 1
     return jnp.where(upper, rows[count:], rows[:count])
 
 
 def both_halves(layout, own, other):
-    upper = jnp.broadcast_to(lax.axis_index("wave"), own.shape) == 1
+    upper = jnp.broadcast_to(layout.half_index(), own.shape) == 1
     return jnp.concatenate([jnp.where(upper, other, own), jnp.where(upper, own, other)], 0)
 
 
@@ -227,6 +233,50 @@
         lax.fori_loop(1, groups, lambda group, carry: step(group, total) or carry, 0)
 
 
+def of_core(core, rows):
+    return jnp.where(jnp.broadcast_to(core, (rows.shape[0] // 2, lanes)) == 1, rows[rows.shape[0] // 2 :], rows[: rows.shape[0] // 2])
+
+
+def twist_chip(layout, block, core, k, density, table_y, out):
+    count, group = layout.part_v, 2 * layout.quarter
+    for i in range(layout.tiles):
+        span = slice(i * lanes, (i + 1) * lanes)
+        wide = slice(k * layout.local + i * lanes, k * layout.local + (i + 1) * lanes)
+        values = of_core(core, density[block, i * 4 * count : (i + 1) * 4 * count, :].astype(f32))
+        waves = table_y[block, :group, span]
+        c, s = table_y[block, group : group + 1, span], table_y[block, group + 1 : group + 2, span]
+        real, imag = values[:count], values[count:]
+        turned = (real * c - imag * s, imag * c + real * s)
+        for v in range(count):
+            for part in range(2):
+                start = (2 * v + part) * group
+                out[start : start + group, wide] = (turned[part][v : v + 1] * waves).astype(bf16)
+
+
+def chips_kernel(layout, base, with_start, density, own_x, own_y, other_x, other_y, *refs):
+    start = refs[0] if with_start else None
+    total, own_twisted, other_twisted = refs[-3:]
+    size = layout.group_of(density)
+
+    def step(group, before):
+        for k in range(size):
+            block = size * group + k
+            core = layout.device_of(base + block) & 1
+            twist_chip(layout, block, core, k, density, own_y, own_twisted)
+            twist_chip(layout, block, 1 - core, k, density, other_y, other_twisted)
+        product = 0.0
+        for twisted, table in ((own_twisted, own_x), (other_twisted, other_x)):
+            product = product + lax.dot_general(
+                twisted[...], table[group], (((1,), (1,)), ((), ())), preferred_element_type=f32
+            )
+        total[...] = product if before is None else before[...] + product
+
+    step(0, start)
+    groups = density.shape[0] // size
+    if groups > 1:
+        lax.fori_loop(1, groups, lambda group, carry: step(group, total) or carry, 0)
+
+
 def part_kernel(layout, base, with_start, with_tables, halves, *refs):
     refs = list(refs)
     density = refs.pop(0)
@@ -245,12 +295,22 @@
 
 
 def table_kernel(layout, base, density, table_x, table_y):
-    make_tables(layout, base, 0, 0, density, table_x, table_y)
+    size = layout.group_of(density)
+
+    def step(group, carry):
+        for k in range(size):
+            make_tables(layout, base, group, k, density, table_x, table_y)
+        return carry
+
+    step(0, 0)
+    groups = density.shape[0] // size
+    if groups > 1:
+        lax.fori_loop(1, groups, step, 0)
 
 
 def weigh(layout, total, weight, scaled):
     quarter = layout.quarter
-    first = lax.axis_index("wave") * layout.part_v
+    first = layout.half_index() * layout.part_v
     for v in range(layout.part_v):
         plus_sum, plus_rest, minus_sum, minus_rest = [
             weight[first + v, k * quarter : (k + 1) * quarter, :] for k in range(4)
@@ -288,14 +348,17 @@
         result[2 * count * i : 2 * count * (i + 1), :] = jnp.concatenate([real * c + imag * s, imag * c - real * s], 0)
 
 
-def far_kernel(layout, own, arrived, weight, own_x, own_y, other_x, other_y, far_own, far_other, total, scaled, summed, summed_other):
-    total[...] = own[...] + arrived[...].astype(f32)
-    weigh(layout, total, weight, scaled)
+def far_kernel(layout, *refs):
+    own, weight, own_x, own_y, other_x, other_y, far_own, far_other, total, scaled, summed, summed_other = refs[-12:]
+    if len(refs) > 12:
+        total[...] = own[...] + refs[0][...].astype(f32)
+        own = total
+    weigh(layout, own, weight, scaled)
     expand(layout, scaled, other_x, other_y, summed_other, far_other)
     expand(layout, scaled, own_x, own_y, summed, far_own)
 
 
-def far_rows(layout, i, own, other):
+def all_rows(layout, i, own, other):
     count = layout.part_v
     real, imag = [
         both_halves(layout, own[start : start + count, :], other[start : start + count, :])
@@ -304,8 +367,7 @@
     return real, imag
 
 
-def near_tile(layout, i, neighbor, density, kernel):
-    vectors = layout.vectors
+def near_tile(layout, i, neighbor, values_of, kernel):
     g = lax.axis_index("tile") * layout.strips + i // layout.tiles_y
     h = lax.axis_index("wave") * layout.tiles_y + i % layout.tiles_y
     values = []
@@ -314,48 +376,83 @@
         step_x = lax.div(slot, 3)
         gx = lax.rem(g + step_x - 1 + layout.count_x, layout.count_x)
         hy = lax.rem(h + slot - 3 * step_x - 1 + layout.count_y, layout.count_y)
-        block = layout.block_of(lax.div(gx, layout.strips) * layout.waves + lax.div(hy, layout.tiles_y))
+        core = lax.div(hy, layout.tiles_y)
+        block = layout.block_of(lax.div(gx, layout.strips) * layout.waves + core)
         tile = lax.rem(gx, layout.strips) * layout.tiles_y + lax.rem(hy, layout.tiles_y)
-        start = pl.multiple_of(tile * 2 * vectors, 2 * vectors)
-        values.append(density[block, pl.ds(start, 2 * vectors), :])
+        values.append(values_of(block, core, pl.multiple_of(tile * 2 * layout.vectors, 2 * layout.vectors)))
     total = 0.0
     for j in range(0, 9, 2):
         span = range(j, min(j + 2, 9))
         left = jnp.concatenate([values[k] for k in span], 1)
         right = jnp.concatenate([jnp.concatenate([kernel[i, k, 0], kernel[i, k, 1]], 1) for k in span], 0)
         total += jnp.dot(left, right, preferred_element_type=f32)
-    upper, lower = total[:vectors], total[vectors:]
-    return jnp.concatenate([upper[:, :lanes] - lower[:, lanes:], upper[:, lanes:] + lower[:, :lanes]], 0)
-
-
-def near_kernel(layout, density, blocks, neighbor, out):
+    return total
+
+
+def turn(upper, lower):
+    return upper[:, :lanes] - lower[:, lanes:], upper[:, lanes:] + lower[:, :lanes]
+
+
+def near_kernel(layout, whole, density, blocks, neighbor, near_own, near_other):
     places = neighbor[...]
-    tall = 2 * layout.vectors
+    count, vectors, tall = layout.part_v, layout.vectors, 2 * layout.vectors
+    chips = layout.devices // 2
+
+    def of_device(block, core, start):
+        return density[block, pl.ds(start, tall), :]
+
+    def of_chip(block, core, start):
+        chip = block & (chips - 1)
+        parts = [density[chip + first, pl.ds(start, tall), :].astype(f32) for first in (0, chips)]
+        return jnp.concatenate([of_core(core, part) for part in parts], 0).astype(bf16)
+
     for i in range(layout.tiles):
-        out[i * tall : (i + 1) * tall, :] = near_tile(layout, i, places, density, blocks)
-
-
-def first_kernel(layout, density, near, far_own, far_other, guess, basis, image):
-    vectors, tall = layout.vectors, 2 * layout.vectors
-    hint = guess[...]
+        total = near_tile(layout, i, places, of_device if whole else of_chip, blocks)
+        span = slice(i * 2 * count, (i + 1) * 2 * count)
+        if whole:
+            parts = turn(total[:vectors], total[vectors:])
+            near_own[span, :] = jnp.concatenate([pick_half(layout, part, False) for part in parts], 0)
+            near_other[span, :] = jnp.concatenate([pick_half(layout, part, True) for part in parts], 0)
+        else:
+            near_own[span, :] = jnp.concatenate(turn(total[:count], total[count : 2 * count]), 0)
+            near_other[span, :] = jnp.concatenate(turn(total[2 * count : 3 * count], total[3 * count :]), 0)
+
+
+def first_kernel(layout, own, other, near_own, near_other, far_own, far_other, guess, basis, image_own, image_other):
+    count, vectors, tall = layout.part_v, layout.vectors, 2 * layout.vectors
+    hint = pick_half(layout, guess[...], False)
+    core = lax.axis_index("wave")
     for i in range(layout.tiles):
-        first = i * tall
-        far_real, far_imag = far_rows(layout, i, far_own, far_other)
-        own = density[first : first + tall, :].astype(f32)
-        rr, ri = own[:vectors], own[vectors:]
-        wr = 0.5 * rr + near[first : first + vectors, :] + far_real
-        wi = 0.5 * ri + near[first + vectors : first + tall, :] + far_imag
-        image[first : first + tall, :] = jnp.concatenate([wr, wi], 0)
-        basis[first : first + tall, :] = jnp.concatenate([wr - hint * rr, wi - hint * ri], 0).astype(bf16)
+        span = slice(i * 2 * count, (i + 1) * 2 * count)
+        rests = []
+        for density, near, far, image in ((own, near_own, far_own, image_own), (other, near_other, far_other, image_other)):
+            values = density[i * tall : (i + 1) * tall, :].astype(f32)
+            rr, ri = pick_half(layout, values[:vectors], False), pick_half(layout, values[vectors:], False)
+            value = 0.5 * jnp.concatenate([rr, ri], 0) + near[span, :] + far[span, :]
+            image[span, :] = value
+            rests.append(value - jnp.concatenate([hint * rr, hint * ri], 0))
+        upper = jnp.broadcast_to(core, rests[0].shape) == 1
+        lines = [jnp.where(upper, rests[1], rests[0]), jnp.where(upper, rests[0], rests[1])]
+        basis[i * tall : (i + 1) * tall, :] = jnp.concatenate(lines, 0).astype(bf16)
+
+
+def chip_rows(layout, i, density, block, core):
+    count, tall = layout.part_v, 2 * layout.vectors
+    chips = layout.devices // 2
+    halves = [
+        of_core(core, density[block + first, i * tall : (i + 1) * tall, :].astype(f32)) for first in (0, chips)
+    ]
+    return [both_halves(layout, *[half[start : start + count] for half in halves]) for start in (0, count)]
 
 
 def block_sums(layout, start, density, block):
     vectors, tall = layout.vectors, 2 * layout.vectors
+    core = layout.device_of(block) & 1
     total = None
     for i in range(layout.tiles):
         r = start[block, i * tall : (i + 1) * tall, :].astype(f32)
-        z = density[block, i * tall : (i + 1) * tall, :].astype(f32)
-        rr, ri, zr, zi = r[:vectors], r[vectors:], z[:vectors], z[vectors:]
+        rr, ri = r[:vectors], r[vectors:]
+        zr, zi = chip_rows(layout, i, density, block % (layout.devices // 2), core)
         terms = (rr * rr + ri * ri, rr * zr + ri * zi, rr * zi - ri * zr, zr * zr + zi * zi)
         total = terms if total is None else [a + b for a, b in zip(total, terms)]
     return total
@@ -393,18 +490,20 @@
     factors[...] = jnp.concatenate([more_real, more_imag, 1.0 / (scale * update_scale)] + lines, 0)
 
 
-def second_kernel(layout, density, near, far_own, far_other, image, factors, result, scalars):
+def second_kernel(layout, density, near_own, near_other, far_own, far_other, image_own, image_other, factors, result, scalars):
     vectors, tall = layout.vectors, 2 * layout.vectors
     more_real, more_imag = factors[:vectors, :], factors[vectors : 2 * vectors, :]
     inverse = factors[2 * vectors : 3 * vectors, :]
     scalars[...] = factors[3 * vectors : 3 * vectors + 4, :vectors]
+    core = lax.axis_index("wave")
     for i in range(layout.tiles):
         first = i * tall
-        far_real, far_imag = far_rows(layout, i, far_own, far_other)
-        own = density[first : first + tall, :].astype(f32)
-        wr, wi = image[first : first + vectors, :], image[first + vectors : first + tall, :]
-        real = 0.5 * own[:vectors] + near[first : first + vectors, :] + far_real
-        imag = 0.5 * own[vectors:] + near[first + vectors : first + tall, :] + far_imag
+        far_real, far_imag = all_rows(layout, i, far_own, far_other)
+        near_real, near_imag = all_rows(layout, i, near_own, near_other)
+        wr, wi = all_rows(layout, i, image_own, image_other)
+        zr, zi = chip_rows(layout, i, density, 0, core)
+        real = 0.5 * zr + near_real + far_real
+        imag = 0.5 * zi + near_imag + far_imag
         result[first : first + vectors, :] = (real - (more_real * wr - more_imag * wi)) * inverse
         result[first + vectors : first + tall, :] = (imag - (more_real * wi + more_imag * wr)) * inverse
 
@@ -502,15 +601,52 @@
                 made.append(new or tables[k])
         leaving, *new = part_call("leaving", base, part, tables and tables[-1], total, (1,), bf16)
         made.append(new or tables[-1])
-        (staying,) = part_call("staying", base, part, made[-1], total, (0,), f32)
-        return seen, leaving, staying, made
-
-    def far_field(leaving, staying, weight, own_tables, other_tables):
-        far_own, far_other = call(
+
+        def stay(first):
+            return part_call("staying", base, after(part, first), made[-1], total, (0,), f32)[0]
+
+        return seen, leaving, stay, made
+
+    def make(name, base, density):
+        return call(
+            lambda *refs: table_kernel(layout, base, *refs),
+            name,
+            table_shapes(density.shape[0]),
+            [vmem],
+            8,
+        )(density)
+
+    def gather_chips(array, tables, other):
+        array = array[None]
+        total, base, seen = None, 0, []
+        for k, mask in enumerate(layout.chip_masks):
+            pairs = [(i, i ^ mask) for i in range(devices)]
+            arrived = lax.ppermute(array, ("tile", "wave"), pairs)
+            array = jnp.concatenate([array, arrived])
+            seen.append(array)
+            part = arrived if k else array
+            wait = seen[min(k, 1)]
+            more = make("tables", devices // 2 + base, after(other, wait)[base : base + part.shape[0]])
+            given = [part, *tables[k], *more] + ([] if total is None else [total])
+            width = layout.group_of(part) * layout.local
+            total = call(
+                lambda *refs, base=base, start=total is not None: chips_kernel(layout, base, start, *refs),
+                "part" if k < len(layout.chip_masks) - 1 else "whole",
+                shape((tall // 2, wide), f32),
+                [vmem] * len(given),
+                24,
+                [pltpu.VMEM((tall // 2, width), bf16)] * 2,
+                aliases={} if total is None else {len(given) - 1: 0},
+            )(*given)
+            base += part.shape[0]
+        return seen, total
+
+    def far_field(sums, weight, own_tables, other_tables):
+        return call(
             lambda *refs: far_kernel(layout, *refs),
             "far",
             tuple([shape((rows // 2, lanes), f32)] * 2),
-            [vmem] * 7,
+            [vmem] * (5 + len(sums)),
             24,
             [
                 pltpu.VMEM((tall // 2, wide), f32),
@@ -518,14 +654,13 @@
                 pltpu.VMEM((tall // 2, layout.local), f32),
                 pltpu.VMEM((tall // 2, layout.local), f32),
             ],
-        )(staying, swap_cores(leaving), weight, *own_tables, *other_tables)
-        return far_own, swap_cores(far_other)
-
-    def near_field(density):
+        )(*sums, weight, *own_tables, *other_tables)
+
+    def near_field(density, whole):
         return call(
-            lambda *refs: near_kernel(layout, *refs),
+            lambda *refs: near_kernel(layout, whole, *refs),
             "near",
-            shape((rows, lanes), f32),
+            tuple([shape((rows // 2, lanes), f32)] * 2),
             [vmem] * 3,
             12,
         )(density, blocks, neighbor)
@@ -533,26 +668,21 @@
     def with_other_core(array):
         return jnp.concatenate([array, swap_cores(array)])
 
-    seen, leaving, staying, tables = gather_and_project(packed, None)
-    other_tables = call(
-        lambda *refs: table_kernel(layout, devices // 2, *refs),
-        "other_tables",
-        table_shapes(1),
-        [vmem],
-        8,
-    )(swap_cores(after(packed, seen[0]))[None])
+    seen, leaving, stay, tables = gather_and_project(packed, None)
+    other_packed = swap_cores(after(packed, seen[0]))
+    beside = make("other_tables", devices // 2, other_packed[None])
     weight, guess = spectral(after(integers, seen[1]))
     start = with_other_core(seen[-1])
-    near_one = near_field(start)
-    far_own, far_other = far_field(leaving, staying, weight, tables[0], other_tables)
-    basis, image = call(
+    near_own, near_other = near_field(start, True)
+    far_own, far_other = far_field((swap_cores(leaving), stay(near_own)), weight, tables[0], beside)
+    basis, image_own, image_other = call(
         lambda *refs: first_kernel(layout, *refs),
         "first",
-        (shape((rows, lanes), bf16), shape((rows, lanes), f32)),
-        [vmem] * 5,
+        (shape((rows, lanes), bf16), shape((rows // 2, lanes), f32), shape((rows // 2, lanes), f32)),
+        [vmem] * 7,
         2,
-    )(packed, near_one, far_own, far_other, guess)
-    seen, leaving, staying, _ = gather_and_project(basis, tables)
+    )(packed, other_packed, near_own, swap_cores(near_other), far_own, far_other, guess)
+    seen, total = gather_chips(basis, tables, start[devices // 2 :])
     everything = with_other_core(seen[-1])
     factors = call(
         lambda *refs: scalar_kernel(layout, *refs),
@@ -561,15 +691,24 @@
         [vmem] * 3,
         1 + devices / 8,
     )(start, everything, guess)
-    near_two = near_field(everything)
-    far_own, far_other = far_field(leaving, after(staying, factors), weight, tables[0], other_tables)
+    near_own, near_other = near_field(everything, False)
+    far_own, far_other = far_field((total,), weight, tables[0], beside)
     result, scalars = call(
         lambda *refs: second_kernel(layout, *refs),
         "second",
         (shape((rows, lanes), f32), shape((4, vectors), f32)),
-        [vmem] * 6,
+        [vmem] * 8,
         2,
-    )(basis, near_two, far_own, far_other, image, factors)
+    )(
+        everything,
+        near_own,
+        near_other,
+        far_own,
+        swap_cores(far_other),
+        image_own,
+        swap_cores(image_other),
+        factors,
+    )
     return result.reshape(residual.shape), scalars
 
 

time: 37.4 us -> 36.1 us (0.965)
  waiting for transfers between devices: 5.27 us -> 2.68 us
  Pallas kernels: 12.9 us -> 14.3 us
    ppermute x0 -> x3, starting transfers between devices: none -> 6.52 us  [gather_chips(): arrived = lax.ppermute(array, ('tile', 'wave'), pairs)]
    ppermute x6 -> x3, starting transfers between devices: 13.6 us -> 7.12 us  [gather_and_project(): arrived = lax.ppermute(array, ('tile', 'wave'), pairs)]
    pallas_call x3 -> x9, Pallas kernels: 1.92 us -> 6.28 us  [the longest x3 2.9 us: gather_chips(): call(lambda *refs, base=base, start=total is not None: chips_kernel(layou...]
    ppermute x6 -> x3, waiting for transfers between devices: 4.49 us -> 0.53 us  [gather_and_project(): arrived = lax.ppermute(array, ('tile', 'wave'), pairs)]
    pallas_call x8 -> x4, Pallas kernels: 8.05 us -> 4.95 us  [part_call(): call(lambda *refs: part_kernel(layout, base, with_start, not tables, halv...]
    ppermute x0 -> x3, waiting for transfers between devices: none -> 2.13 us  [gather_chips(): arrived = lax.ppermute(array, ('tile', 'wave'), pairs)]
    ppermute x7, waiting for transfers between devices: 0.78 us -> 0.02 us  [swap_cores(): return lax.ppermute(array, 'wave', [(0, 1), (1, 0)])]
  transfers between devices with their start and end apart: 13 -> 13, of which waited for: 9 -> 5; matrix products, arithmetic and copies ran while one was open for 4% -> 4% of each run, Pallas kernels for 30% -> 38%
where the time goes in v7:
time: 36.1 us; the launch traced here: 35.9 us
  starting transfers between devices  15.8 us (44%)
  Pallas kernels  14.3 us (40%)
  waiting for transfers between devices  2.68 us (7%)
  other arithmetic  1.52 us (4%)
  between operations  0.9 us (2%)
  local copies, waits for them, and re-layouts  0.8 us (2%)
    ppermute x3, starting transfers between devices, gather_and_project(): arrived = lax.ppermute(array, ('tile', 'wave'), pairs)  7.12 us
    ppermute x3, starting transfers between devices, gather_chips(): arrived = lax.ppermute(array, ('tile', 'wave'), pairs)  6.52 us
    pallas_call x4, Pallas kernels, part_call(): call(lambda *refs: part_kernel(layout, base, with_start, not tables, halv...  4.95 us
    pallas_call x3, Pallas kernels, gather_chips(): call(lambda *refs, base=base, start=total is not None: chips_kernel(layou...  2.9 us
    ppermute x3, waiting for transfers between devices, gather_chips(): arrived = lax.ppermute(array, ('tile', 'wave'), pairs)  2.13 us
    ppermute x7, starting transfers between devices, swap_cores(): return lax.ppermute(array, 'wave', [(0, 1), (1, 0)])  2.12 us
    pallas_call x2, Pallas kernels, near_field(): call(lambda *refs: near_kernel(layout, whole, *refs), 'near', tuple([shap...  1.76 us
    pallas_call x4, Pallas kernels, make(): call(lambda *refs: table_kernel(layout, base, *refs), name, table_shapes(...  1.62 us
  transfers between devices with their start and end apart: 13, of which 5 were waited for; matrix products, arithmetic and copies ran while one was open for 4% of the time, Pallas kernels for 38%

profile of v7, /device:TPU:0, one launch (start us, length us, event | category | flops | bytes accessed | tf_op | source)
XLA Modules:
  0.0 35.9 jit_solution(14973330228586663766)
XLA Ops:
  0.6 0.8 %pad_maximum_fusion.5.refs_0_ = f32[72,128]{1,0:T(8,128)S(1)} fusion(f32[8,128]{1,0:T(8,128)} %bitcast.28, f32[64,128]{1,0:T(8,128)} %bitcast.27), kind=kLoop, calls=%fused_computation.5 | loop fusion | flops 9216 | bytes 73728 | tf_op jit(solution)/shard_map/concatenate | solution.py:537
  1.4 3.5 %collective-permute-start = (bf16[1,80,128]{2,1,0:T(8,128)(2,1)S(1)}, bf16[1,80,128]{2,1,0:T(8,128)(2,1)S(1)}, u32[]{:S(2)}, u32[]{:S(2)}) collective-permute-start(bf16[1,80,128]{2,1,0:T(8,128)(2,1)S(1)} %bitcast.14), channel_id=1, source_target_pairs={{0,9},{1,8},{2,11},{3,10},{4,13},{5,12},{6,15},{7,14},{8,1},{9,0},... | collective-permute-start | bytes 61448 | tf_op jit(solution)/shard_map/ppermute | solution.py:594
  5.0 0.7 %pad_bitcast_fusion = s32[1,128]{1,0:T(1,128)S(1)} fusion(s32[8]{0:T(128)} %param.12), kind=kLoop, calls=%fused_computation.18 | loop fusion | bytes 544 | tf_op jit(solution)/shard_map/stack | solution.py:546
  5.6 0.7 %pad_add_fusion.refs_0_ = s32[3,128]{1,0:T(4,128)S(1)} fusion(s32[1,128]{1,0:T(1,128)S(1)} %pad_bitcast_fusion, s32[1,128]{1,0:T(1,128)} %bitcast.29, s32[1,128]{1,0:T(1,128)} %bitcast.30), kind=kLoop, calls=%fused_computation.17 | loop fusion | flops 768 | bytes 3072 | tf_op jit(solution)/shard_map/stack | solution.py:546
  6.5 1.9 %collective-permute-start.2 = (bf16[2,80,128]{2,1,0:T(8,128)(2,1)S(1)}, bf16[2,80,128]{2,1,0:T(8,128)(2,1)S(1)}, u32[]{:S(2)}, u32[]{:S(2)}) collective-permute-start(bf16[2,80,128]{2,1,0:T(8,128)(2,1)S(1)} %pad_maximum_fusion.4.refs_0_), channel_id=1, source_target_pairs={{0,5},{1,4},{2,7},{3,6},{4,1},{5,0},{6,3},{7,2},{8,13},{9,12},{10,... | collective-permute-start | bytes 122888 | tf_op jit(solution)/shard_map/ppermute | solution.py:594
  8.7 1.2 %part.4 = (f32[1024,256]{1,0:T(8,128)S(1)}, bf16[1,256,1024]{2,1,0:T(8,128)(2,1)S(1)}, f32[2,72,512]{2,1,0:T(8,128)S(1)}) custom-call(bf16[2,80,128]{2,1,0:T(8,128)(2,1)S(1)} %pad_maximum_fusion.4.refs_0_), custom_call_target="tpu_custom_call" | custom-call | flops 1000000000 | tf_op jit(solution)/shard_map/part/pallas_call | solution.py:579
  10.2 1.7 %collective-permute-start.3 = (bf16[4,80,128]{2,1,0:T(8,128)(2,1)S(1)}, bf16[4,80,128]{2,1,0:T(8,128)(2,1)S(1)}, u32[]{:S(2)}, u32[]{:S(2)}) collective-permute-start(bf16[4,80,128]{2,1,0:T(8,128)(2,1)S(1)} %pad_maximum_fusion.2), channel_id=1, source_target_pairs={{0,3},{1,2},{2,1},{3,0},{4,7},{5,6},{6,5},{7,4},{8,11},{9,10},{10,... | collective-permute-start | bytes 245768 | tf_op jit(solution)/shard_map/ppermute | solution.py:594
  11.9 1.0 %spectral.1 = (f32[8,128,128]{2,1,0:T(8,128)S(1)}, f32[8,128]{1,0:T(8,128)S(1)}) custom-call(s32[3,128]{1,0:T(4,128)S(1)} %pad_add_fusion.refs_0_, f32[8,128,128]{2,1,0:T(8,128)S(1)} %copy-done.1), custom_call_target="tpu_custom_call" | custom-call | flops 2000000000 | tf_op jit(solution)/shard_map/spectral/pallas_call | solution.py:549
  12.9 1.3 %part.5 = (f32[1024,256]{1,0:T(8,128)S(1)}, bf16[1,256,1024]{2,1,0:T(8,128)(2,1)S(1)}, f32[2,72,512]{2,1,0:T(8,128)S(1)}) custom-call(bf16[2,80,128]{2,1,0:T(8,128)(2,1)S(1)} %collective-permute-done.2.refs_0_, f32[1024,256]{1,0:T(8,128)S(1)} %get-tuple-element.42.refs_1_), custom_call_target="tpu_custom_call", output_to_operand_aliasing={{0}: (1, {})} | custom-call | flops 1000000000 | tf_op jit(solution)/shard_map/part/pallas_call | solution.py:579
  14.9 1.7 %leaving.1 = (bf16[512,256]{1,0:T(8,128)(2,1)S(1)}, bf16[1,256,2048]{2,1,0:T(8,128)(2,1)S(1)}, f32[4,72,512]{2,1,0:T(8,128)S(1)}) custom-call(bf16[4,80,128]{2,1,0:T(8,128)(2,1)S(1)} %collective-permute-done.3.refs_0_, f32[1024,256]{1,0:T(8,128)S(1)} %get-tuple-element.43.refs_1_.refs_3_), custom_call_target="tpu_custom_call" | custom-call | flops 2000000000 | tf_op jit(solution)/shard_map/leaving/pallas_call | solution.py:579
  17.0 0.9 %near.2 = (f32[32,128]{1,0:T(8,128)S(1)}, f32[32,128]{1,0:T(8,128)S(1)}) custom-call(bf16[16,80,128]{2,1,0:T(8,128)(2,1)S(1)} %constant_dynamic-update-slice_fusion.refs_0_, bf16[4,9,2,128,128]{4,3,2,1,0:T(8,128)(2,1)S(1)} %bitcast.23, s32[4,9]{1,0:T(4,128)S(1)} %bitcast.25), custom_call_target="tpu_custom_call" | custom-call | flops 2000000000 | tf_op jit(solution)/shard_map/near/pallas_call | solution.py:660
  18.2 0.8 %staying.1.refs_1_ = f32[512,256]{1,0:T(8,128)S(1)} custom-call(bf16[4,80,128]{2,1,0:T(8,128)(2,1)S(1)} %collective-permute-done.3.refs_0_, bf16[1,256,2048]{2,1,0:T(8,128)(2,1)S(1)} %get-tuple-element.46.refs_1_, f32[4,72,512]{2,1,0:T(8,128)S(1)} %get-tuple-element.47.refs_2_, f32[1024,256]{1,0:T(8,128)S(1)} %get-tuple-element.43.refs_1_.refs_3_), custom_call_target="tpu_custom_call" | custom-call | flops 800000000 | tf_op jit(solution)/shard_map/staying/pallas_call | solution.py:579
  19.0 0.5 %far.2 = (f32[32,128]{1,0:T(8,128)S(1)}, f32[32,128]{1,0:T(8,128)S(1)}) custom-call(bf16[512,256]{1,0:T(8,128)(2,1)S(1)} %collective-permute-done.6.refs_0_, f32[512,256]{1,0:T(8,128)S(1)} %staying.1.refs_1_, f32[8,128,128]{2,1,0:T(8,128)S(1)} %get-tuple-element.49.refs_2_.refs_1_, bf16[1,256,1024]{2,1,0:T(8,128)(2,1)S(1)} %get-tuple-element.50.refs_3_.refs_1_.refs_2_, ...), custom_call_target="tpu_custom_call" | custom-call | flops 300000000 | tf_op jit(solution)/shard_map/far/pallas_call | solution.py:645
  19.5 3.2 %collective-permute-start.7 = (bf16[1,64,128]{2,1,0:T(8,128)(2,1)S(1)}, bf16[1,64,128]{2,1,0:T(8,128)(2,1)S(1)}, u32[]{:S(2)}, u32[]{:S(2)}) collective-permute-start(bf16[1,64,128]{2,1,0:T(8,128)(2,1)S(1)} %bitcast.18), channel_id=1, source_target_pairs={{0,9},{1,8},{2,11},{3,10},{4,13},{5,12},{6,15},{7,14},{8,1},{9,0},... | collective-permute-start | bytes 49160 | tf_op jit(solution)/shard_map/ppermute | solution.py:624
  22.9 1.3 %collective-permute-done.7 = bf16[1,64,128]{2,1,0:T(8,128)(2,1)S(1)} collective-permute-done((bf16[1,64,128]{2,1,0:T(8,128)(2,1)S(1)}, bf16[1,64,128]{2,1,0:T(8,128)(2,1)S(1)}, u32[]{:S(2)}, u32[]{:S(2)}) %collective-permute-start.7) | collective-permute-done | bytes 16416 | tf_op jit(solution)/shard_map/ppermute | solution.py:624
  24.2 1.7 %collective-permute-start.8 = (bf16[2,64,128]{2,1,0:T(8,128)(2,1)S(1)}, bf16[2,64,128]{2,1,0:T(8,128)(2,1)S(1)}, u32[]{:S(2)}, u32[]{:S(2)}) collective-permute-start(bf16[2,64,128]{2,1,0:T(8,128)(2,1)S(1)} %pad_maximum_fusion.6.refs_0_), channel_id=1, source_target_pairs={{0,5},{1,4},{2,7},{3,6},{4,1},{5,0},{6,3},{7,2},{8,13},{9,12},{10,... | collective-permute-start | bytes 98312 | tf_op jit(solution)/shard_map/ppermute | solution.py:624
  26.3 0.8 %part.6.refs_5_ = f32[512,256]{1,0:T(8,128)S(1)} custom-call(bf16[2,64,128]{2,1,0:T(8,128)(2,1)S(1)} %pad_maximum_fusion.6.refs_0_, bf16[1,256,1024]{2,1,0:T(8,128)(2,1)S(1)} %get-tuple-element.50.refs_3_.refs_1_.refs_2_, f32[2,72,512]{2,1,0:T(8,128)S(1)} %get-tuple-element.51.refs_4_.refs_2_.refs_3_, bf16[1,256,1024]{2,1,0:T(8,128)(2,1)S(1)} %get-tuple-element.68.refs_3_, ...), custom_call_target="tpu_custom_call" | custom-call | flops 1000000000 | tf_op jit(solution)/shard_map/part/pallas_call | solution.py:632
  27.5 1.6 %collective-permute-start.9 = (bf16[4,64,128]{2,1,0:T(8,128)(2,1)S(1)}, bf16[4,64,128]{2,1,0:T(8,128)(2,1)S(1)}, u32[]{:S(2)}, u32[]{:S(2)}) collective-permute-start(bf16[4,64,128]{2,1,0:T(8,128)(2,1)S(1)} %pad_maximum_fusion.3), channel_id=1, source_target_pairs={{0,3},{1,2},{2,1},{3,0},{4,7},{5,6},{6,5},{7,4},{8,11},{9,10},{10,... | collective-permute-start | bytes 196616 | tf_op jit(solution)/shard_map/ppermute | solution.py:624
  29.5 0.8 %part.7.refs_5_ = f32[512,256]{1,0:T(8,128)S(1)} custom-call(bf16[2,64,128]{2,1,0:T(8,128)(2,1)S(1)} %collective-permute-done.8.refs_0_, bf16[1,256,1024]{2,1,0:T(8,128)(2,1)S(1)} %get-tuple-element.63.refs_1_, f32[2,72,512]{2,1,0:T(8,128)S(1)} %get-tuple-element.64.refs_2_, ...), custom_call_target="tpu_custom_call", output_to_operand_aliasing={{}: (5, {})} | custom-call | flops 1000000000 | tf_op jit(solution)/shard_map/part/pallas_call | solution.py:632
  30.3 0.7 %tables.3 = (bf16[1,256,2048]{2,1,0:T(8,128)(2,1)S(1)}, f32[4,72,512]{2,1,0:T(8,128)S(1)}) custom-call(bf16[4,80,128]{2,1,0:T(8,128)(2,1)S(1)} %slice.9.refs_0_), custom_call_target="tpu_custom_call" | custom-call | flops 500000000 | tf_op jit(solution)/shard_map/tables/pallas_call | solution.py:611
  31.9 1.4 %whole.1.refs_0_ = f32[512,256]{1,0:T(8,128)S(1)} custom-call(bf16[4,64,128]{2,1,0:T(8,128)(2,1)S(1)} %collective-permute-done.9.refs_0_, bf16[1,256,2048]{2,1,0:T(8,128)(2,1)S(1)} %get-tuple-element.46.refs_1_, f32[4,72,512]{2,1,0:T(8,128)S(1)} %get-tuple-element.47.refs_2_, ...), custom_call_target="tpu_custom_call", output_to_operand_aliasing={{}: (5, {})} | custom-call | flops 800000000 | tf_op jit(solution)/shard_map/whole/pallas_call | solution.py:632
  33.2 0.5 %far.3 = (f32[32,128]{1,0:T(8,128)S(1)}, f32[32,128]{1,0:T(8,128)S(1)}) custom-call(f32[512,256]{1,0:T(8,128)S(1)} %whole.1.refs_0_, f32[8,128,128]{2,1,0:T(8,128)S(1)} %get-tuple-element.49.refs_2_.refs_1_, bf16[1,256,1024]{2,1,0:T(8,128)(2,1)S(1)} %get-tuple-element.50.refs_3_.refs_1_.refs_2_, f32[2,72,512]{2,1,0:T(8,128)S(1)} %get-tuple-element.51.refs_4_.refs_2_.refs_3_, ...), custom_call_target="tpu_custom_call" | custom-call | flops 300000000 | tf_op jit(solution)/shard_map/far/pallas_call | solution.py:645
  34.0 0.9 %near.3 = (f32[32,128]{1,0:T(8,128)S(1)}, f32[32,128]{1,0:T(8,128)S(1)}) custom-call(bf16[16,64,128]{2,1,0:T(8,128)(2,1)S(1)} %constant_dynamic-update-slice_fusion.5.refs_0_.refs_1_, bf16[4,9,2,128,128]{4,3,2,1,0:T(8,128)(2,1)S(1)} %bitcast.24, s32[4,9]{1,0:T(4,128)S(1)} %bitcast.26), custom_call_target="tpu_custom_call" | custom-call | flops 2000000000 | tf_op jit(solution)/shard_map/near/pallas_call | solution.py:660
  35.3 0.7 %second.1 = (f32[64,128]{1,0:T(8,128)}, f32[4,8]{1,0:T(4,128)}) custom-call(bf16[16,64,128]{2,1,0:T(8,128)(2,1)S(1)} %constant_dynamic-update-slice_fusion.5.refs_0_.refs_1_, f32[32,128]{1,0:T(8,128)S(1)} %get-tuple-element.58.refs_1_, f32[32,128]{1,0:T(8,128)S(1)} %get-tuple-element.59.refs_2_, f32[32,128]{1,0:T(8,128)S(1)} %get-tuple-element.70.refs_3_, ...), custom_call_target="tpu_custom_call" | custom-call | tf_op jit(solution)/shard_map/second/pallas_call | solution.py:696
  (50 shorter events, 5.1 us)
Async XLA Ops:
  1.4 5.1 %collective-permute-start = (bf16[1,80,128]{2,1,0:T(8,128)(2,1)S(1)}, bf16[1,80,128]{2,1,0:T(8,128)(2,1)S(1)}, u32[]{:S(2)}, u32[]{:S(2)}) collective-permute-start(bf16[1,80,128]{2,1,0:T(8,128)(2,1)S(1)} %bitcast.14), channel_id=1, source_target_pairs={{0,9},{1,8},{2,11},{3,10},{4,13},{5,12},{6,15},{7,14},{8,1},{9,0},... | collective-permute-start | bytes 61448 | tf_op jit(solution)/shard_map/ppermute | solution.py:594
  6.5 3.7 %collective-permute-start.2 = (bf16[2,80,128]{2,1,0:T(8,128)(2,1)S(1)}, bf16[2,80,128]{2,1,0:T(8,128)(2,1)S(1)}, u32[]{:S(2)}, u32[]{:S(2)}) collective-permute-start(bf16[2,80,128]{2,1,0:T(8,128)(2,1)S(1)} %pad_maximum_fusion.4.refs_0_), channel_id=1, source_target_pairs={{0,5},{1,4},{2,7},{3,6},{4,1},{5,0},{6,3},{7,2},{8,13},{9,12},{10,... | collective-permute-start | bytes 122888 | tf_op jit(solution)/shard_map/ppermute | solution.py:594
  8.3 1.6 %collective-permute-start.1 = (bf16[80,128]{1,0:T(8,128)(2,1)S(1)}, bf16[80,128]{1,0:T(8,128)(2,1)S(1)}, u32[]{:S(2)}, u32[]{:S(2)}) collective-permute-start(bf16[80,128]{1,0:T(8,128)(2,1)S(1)} %pack.1.refs_0_), channel_id=1, source_target_pairs={{0,1},{1,0},{2,3},{3,2},{4,5},{5,4},{6,7},{7,6},{8,9},{9,8},{10,11... | collective-permute-start | bytes 61448 | tf_op jit(solution)/shard_map/ppermute | solution.py:84
  8.7 3.2 %copy-start.1 = (f32[8,128,128]{2,1,0:T(8,128)S(1)}, f32[8,128,128]{2,1,0:T(8,128)}, u32[]{:S(2)}) copy-start(f32[8,128,128]{2,1,0:T(8,128)} %refs_1_.1) | copy-start | bytes 1572868
  10.2 4.4 %collective-permute-start.3 = (bf16[4,80,128]{2,1,0:T(8,128)(2,1)S(1)}, bf16[4,80,128]{2,1,0:T(8,128)(2,1)S(1)}, u32[]{:S(2)}, u32[]{:S(2)}) collective-permute-start(bf16[4,80,128]{2,1,0:T(8,128)(2,1)S(1)} %pad_maximum_fusion.2), channel_id=1, source_target_pairs={{0,3},{1,2},{2,1},{3,0},{4,7},{5,6},{6,5},{7,4},{8,11},{9,10},{10,... | collective-permute-start | bytes 245768 | tf_op jit(solution)/shard_map/ppermute | solution.py:594
  14.6 2.4 %collective-permute-start.4 = (bf16[8,80,128]{2,1,0:T(8,128)(2,1)S(1)}, bf16[8,80,128]{2,1,0:T(8,128)(2,1)S(1)}, u32[]{:S(2)}, u32[]{:S(2)}) collective-permute-start(bf16[8,80,128]{2,1,0:T(8,128)(2,1)S(1)} %pad_maximum_fusion), channel_id=1, source_target_pairs={{0,1},{1,0},{2,3},{3,2},{4,5},{5,4},{6,7},{7,6},{8,9},{9,8},{10,11... | collective-permute-start | bytes 491528 | tf_op jit(solution)/shard_map/ppermute | solution.py:84
  14.9 2.1 %copy-start = (bf16[1,4,9,2,128,128]{5,4,3,2,1,0:T(8,128)(2,1)S(1)}, bf16[1,4,9,2,128,128]{5,4,3,2,1,0:T(8,128)(2,1)}, u32[]{:S(2)}) copy-start(bf16[1,4,9,2,128,128]{5,4,3,2,1,0:T(8,128)(2,1)} %param.9) | copy-start | bytes 7077892
  14.9 2.1 %copy-start.2 = (s32[1,4,9]{2,1,0:T(4,128)S(1)}, s32[1,4,9]{2,1,0:T(4,128)}, u32[]{:S(2)}) copy-start(s32[1,4,9]{2,1,0:T(4,128)} %param.11) | copy-start | bytes 436
  16.7 2.3 %collective-permute-start.6 = (bf16[512,256]{1,0:T(8,128)(2,1)S(1)}, bf16[512,256]{1,0:T(8,128)(2,1)S(1)}, u32[]{:S(2)}, u32[]{:S(2)}) collective-permute-start(bf16[512,256]{1,0:T(8,128)(2,1)S(1)} %get-tuple-element.44), channel_id=1, source_target_pairs={{0,1},{1,0},{2,3},{3,2},{4,5},{5,4},{6,7},{7,6},{8,9},{9,8},{10,11... | collective-permute-start | bytes 786440 | tf_op jit(solution)/shard_map/ppermute | solution.py:84
  17.9 1.6 %collective-permute-start.5 = (f32[32,128]{1,0:T(8,128)S(1)}, f32[32,128]{1,0:T(8,128)S(1)}, u32[]{:S(2)}, u32[]{:S(2)}) collective-permute-start(f32[32,128]{1,0:T(8,128)S(1)} %get-tuple-element.41), channel_id=1, source_target_pairs={{0,1},{1,0},{2,3},{3,2},{4,5},{5,4},{6,7},{7,6},{8,9},{9,8},{10,11... | collective-permute-start | bytes 49160 | tf_op jit(solution)/shard_map/ppermute | solution.py:84
  19.5 4.6 %collective-permute-start.7 = (bf16[1,64,128]{2,1,0:T(8,128)(2,1)S(1)}, bf16[1,64,128]{2,1,0:T(8,128)(2,1)S(1)}, u32[]{:S(2)}, u32[]{:S(2)}) collective-permute-start(bf16[1,64,128]{2,1,0:T(8,128)(2,1)S(1)} %bitcast.18), channel_id=1, source_target_pairs={{0,9},{1,8},{2,11},{3,10},{4,13},{5,12},{6,15},{7,14},{8,1},{9,0},... | collective-permute-start | bytes 49160 | tf_op jit(solution)/shard_map/ppermute | solution.py:624
  22.7 12.5 %collective-permute-start.12 = (f32[32,128]{1,0:T(8,128)S(1)}, f32[32,128]{1,0:T(8,128)S(1)}, u32[]{:S(2)}, u32[]{:S(2)}) collective-permute-start(f32[32,128]{1,0:T(8,128)S(1)} %get-tuple-element.73), channel_id=1, source_target_pairs={{0,1},{1,0},{2,3},{3,2},{4,5},{5,4},{6,7},{7,6},{8,9},{9,8},{10,11... | collective-permute-start | bytes 49160 | tf_op jit(solution)/shard_map/ppermute | solution.py:84
  24.2 3.3 %collective-permute-start.8 = (bf16[2,64,128]{2,1,0:T(8,128)(2,1)S(1)}, bf16[2,64,128]{2,1,0:T(8,128)(2,1)S(1)}, u32[]{:S(2)}, u32[]{:S(2)}) collective-permute-start(bf16[2,64,128]{2,1,0:T(8,128)(2,1)S(1)} %pad_maximum_fusion.6.refs_0_), channel_id=1, source_target_pairs={{0,5},{1,4},{2,7},{3,6},{4,1},{5,0},{6,3},{7,2},{8,13},{9,12},{10,... | collective-permute-start | bytes 98312 | tf_op jit(solution)/shard_map/ppermute | solution.py:624
  27.5 3.9 %collective-permute-start.9 = (bf16[4,64,128]{2,1,0:T(8,128)(2,1)S(1)}, bf16[4,64,128]{2,1,0:T(8,128)(2,1)S(1)}, u32[]{:S(2)}, u32[]{:S(2)}) collective-permute-start(bf16[4,64,128]{2,1,0:T(8,128)(2,1)S(1)} %pad_maximum_fusion.3), channel_id=1, source_target_pairs={{0,3},{1,2},{2,1},{3,0},{4,7},{5,6},{6,5},{7,4},{8,11},{9,10},{10,... | collective-permute-start | bytes 196616 | tf_op jit(solution)/shard_map/ppermute | solution.py:624
  31.4 2.5 %collective-permute-start.10 = (bf16[8,64,128]{2,1,0:T(8,128)(2,1)S(1)}, bf16[8,64,128]{2,1,0:T(8,128)(2,1)S(1)}, u32[]{:S(2)}, u32[]{:S(2)}) collective-permute-start(bf16[8,64,128]{2,1,0:T(8,128)(2,1)S(1)} %pad_maximum_fusion.1), channel_id=1, source_target_pairs={{0,1},{1,0},{2,3},{3,2},{4,5},{5,4},{6,7},{7,6},{8,9},{9,8},{10,11... | collective-permute-start | bytes 393224 | tf_op jit(solution)/shard_map/ppermute | solution.py:84
  33.7 1.5 %collective-permute-start.11 = (f32[32,128]{1,0:T(8,128)S(1)}, f32[32,128]{1,0:T(8,128)S(1)}, u32[]{:S(2)}, u32[]{:S(2)}) collective-permute-start(f32[32,128]{1,0:T(8,128)S(1)} %get-tuple-element.71), channel_id=1, source_target_pairs={{0,1},{1,0},{2,3},{3,2},{4,5},{5,4},{6,7},{7,6},{8,9},{9,8},{10,11... | collective-permute-start | bytes 49160 | tf_op jit(solution)/shard_map/ppermute | solution.py:84

commit v8 on v7

--- a/solution.py
+++ b/solution.py
@@ -44,6 +44,8 @@
         self.rows = self.tiles * 2 * vectors
         self.offset_rows = -(-4 * self.tiles // 16) * 16
         self.part_v = vectors // 2
+        self.x_bits, self.y_bits = (strips - 1).bit_length(), (tiles_y - 1).bit_length()
+        assert strips == 1 << self.x_bits and tiles_y == 1 << self.y_bits
         self.half = modes // 2
         self.quarter = modes // 4
         chip_bits = (self.columns - 1).bit_length()
@@ -144,44 +146,51 @@
     guess[...] = jnp.concatenate(rows, 0)
 
 
+def climb(start, step, count):
+    (c, s), (step_c, step_s) = start, step
+    cosines, sines = [c], [s]
+    for _ in range(count - 1):
+        c, s = c * step_c - s * step_s, s * step_c + c * step_s
+        cosines.append(c)
+        sines.append(s)
+    return jnp.concatenate(cosines, 0), jnp.concatenate(sines, 0)
+
+
 def make_tables(layout, base, group, k, density, table_x, table_y):
     tiles, half, quarter = layout.tiles, layout.half, layout.quarter
     block = layout.group_of(density) * group + k
     device = layout.device_of(base + block)
     column, row_index = device // layout.waves, device % layout.waves
     pieces = density[block, layout.rows :, :].astype(f32)
-    offset = pieces[: 2 * tiles] + pieces[2 * tiles : 4 * tiles]
-    eight = lax.broadcasted_iota(jnp.int32, (8, lanes), 0).astype(f32)
-    coarse_y = jnp.where(eight < 4, quarter / 2 + 0.5 + 8 * eight, jnp.where(eight < 5, quarter / 2.0, 0.5))
+    spot = lax.broadcasted_iota(jnp.int32, (2 * tiles, lanes), 0)
+    along_x = (spot & 1) == 0
+    tile = spot >> 1
+    corner = jnp.where(
+        along_x,
+        column * layout.strips + (tile >> layout.y_bits),
+        row_index * layout.tiles_y + (tile & (layout.tiles_y - 1)),
+    )
+    size = jnp.where(along_x, 1.0 / layout.count_x, 1.0 / layout.count_y)
+    position = (pieces[: 2 * tiles] + pieces[2 * tiles : 4 * tiles] + corner.astype(f32)) * size
+    steps = cos_sin(8.0 * position)
+    phases = cos_sin(0.5 * (position + pltpu.roll(position, 2 * tiles - 1, 0)))
+    eight = lax.broadcasted_iota(jnp.int32, (8, lanes), 0).astype(f32) + 0.5
+
+    def row(array, index):
+        return jnp.broadcast_to(array[index : index + 1], (8, lanes))
+
     for i in range(tiles):
-        g = (column * layout.strips + i // layout.tiles_y).astype(f32)
-        h = (row_index * layout.tiles_y + i % layout.tiles_y).astype(f32)
-        x = jnp.broadcast_to((offset[2 * i : 2 * i + 1] + g) * (1.0 / layout.count_x), (8, lanes))
-        y = jnp.broadcast_to((offset[2 * i + 1 : 2 * i + 2] + h) * (1.0 / layout.count_y), (8, lanes))
-        fine_xc, fine_xs = cos_sin(eight * x)
-        big_xc, big_xs = cos_sin((8 * eight + 0.5) * x)
-        fine_yc, fine_ys = cos_sin(eight * y)
-        big_yc, big_ys = cos_sin(coarse_y * y + jnp.where(eight == 5, 0.5, 0.0) * x)
-        shift_c, shift_s = big_yc[4:5], big_ys[4:5]
+        x, y = row(position, 2 * i), row(position, 2 * i + 1)
+        step_x, step_y = [[row(step, 2 * i + n) for step in steps] for n in range(2)]
         span = slice(i * lanes, (i + 1) * lanes)
         wide = slice(k * layout.local + i * lanes, k * layout.local + (i + 1) * lanes)
-        for e, sign in ((0, 1.0), (1, -1.0)):
-            both_c = big_xc * shift_c - sign * (big_xs * shift_s)
-            both_s = big_xs * shift_c + sign * (big_xc * shift_s)
-            cosines, sines = [], []
-            for a in range(half // 8):
-                c, s = both_c[a : a + 1], both_s[a : a + 1]
-                cosines.append(c * fine_xc - s * fine_xs)
-                sines.append(s * fine_xc + c * fine_xs)
-            table_x[group, half * e : half * (e + 1), wide] = jnp.concatenate(cosines, 0).astype(bf16)
-            table_x[group, half * (e + 2) : half * (e + 3), wide] = jnp.concatenate(sines, 0).astype(bf16)
-        cosines, sines = [], []
-        for a in range(quarter // 8):
-            c, s = big_yc[a : a + 1], big_ys[a : a + 1]
-            cosines.append(c * fine_yc - s * fine_ys)
-            sines.append(s * fine_yc + c * fine_ys)
-        last = jnp.concatenate([big_yc[5:6], big_ys[5:6], jnp.zeros((6, lanes), f32)], 0)
-        table_y[block, :, span] = jnp.concatenate(cosines + sines + [last], 0)
+        for e, shift in ((0, quarter / 2), (1, -quarter / 2)):
+            cosines, sines = climb(cos_sin(eight * x + shift * y), step_x, half // 8)
+            table_x[group, half * e : half * (e + 1), wide] = cosines.astype(bf16)
+            table_x[group, half * (e + 2) : half * (e + 3), wide] = sines.astype(bf16)
+        cosines, sines = climb(cos_sin((eight + quarter / 2) * y), step_y, quarter // 8)
+        last = [phase[2 * i : 2 * i + 1] for phase in phases]
+        table_y[block, :, span] = jnp.concatenate([cosines, sines] + last + [jnp.zeros((6, lanes), f32)], 0)
 
 
 def pick_half(layout, rows, other):
@@ -367,19 +376,20 @@
     return real, imag
 
 
-def near_tile(layout, i, neighbor, values_of, kernel):
-    g = lax.axis_index("tile") * layout.strips + i // layout.tiles_y
-    h = lax.axis_index("wave") * layout.tiles_y + i % layout.tiles_y
-    values = []
-    for j in range(9):
-        slot = neighbor[i, j]
-        step_x = lax.div(slot, 3)
-        gx = lax.rem(g + step_x - 1 + layout.count_x, layout.count_x)
-        hy = lax.rem(h + slot - 3 * step_x - 1 + layout.count_y, layout.count_y)
-        core = lax.div(hy, layout.tiles_y)
-        block = layout.block_of(lax.div(gx, layout.strips) * layout.waves + core)
-        tile = lax.rem(gx, layout.strips) * layout.tiles_y + lax.rem(hy, layout.tiles_y)
-        values.append(values_of(block, core, pl.multiple_of(tile * 2 * layout.vectors, 2 * layout.vectors)))
+def near_places(layout, neighbor, block_rows, mask):
+    tile = lax.broadcasted_iota(jnp.int32, neighbor.shape, 0)
+    step_x = (neighbor * 11) >> 5
+    gx = lax.axis_index("tile") * layout.strips + (tile >> layout.y_bits) + step_x - 1
+    hy = lax.axis_index("wave") * layout.tiles_y + (tile & (layout.tiles_y - 1)) + neighbor - 3 * step_x - 1
+    gx, hy = gx & (layout.count_x - 1), hy & (layout.count_y - 1)
+    core = hy >> layout.y_bits
+    block = layout.block_of((gx >> layout.x_bits) * layout.waves + core) & mask
+    source = ((gx & (layout.strips - 1)) << layout.y_bits) + (hy & (layout.tiles_y - 1))
+    return 2 * (block * block_rows + source * 2 * layout.vectors) + core
+
+
+def near_tile(layout, i, places, values_of, kernel):
+    values = [values_of(places[i, j]) for j in range(9)]
     total = 0.0
     for j in range(0, 9, 2):
         span = range(j, min(j + 2, 9))
@@ -394,17 +404,20 @@
 
 
 def near_kernel(layout, whole, density, blocks, neighbor, near_own, near_other):
-    places = neighbor[...]
     count, vectors, tall = layout.part_v, layout.vectors, 2 * layout.vectors
     chips = layout.devices // 2
-
-    def of_device(block, core, start):
-        return density[block, pl.ds(start, tall), :]
-
-    def of_chip(block, core, start):
-        chip = block & (chips - 1)
-        parts = [density[chip + first, pl.ds(start, tall), :].astype(f32) for first in (0, chips)]
-        return jnp.concatenate([of_core(core, part) for part in parts], 0).astype(bf16)
+    block_rows = density.shape[0] // layout.devices
+    places = near_places(layout, neighbor[...], block_rows, layout.devices - 1 if whole else chips - 1)
+
+    def of_device(place):
+        return density[pl.ds(pl.multiple_of(place >> 1, tall), tall), :]
+
+    def of_chip(place):
+        start = place >> 1
+        parts = [
+            density[pl.ds(pl.multiple_of(start + first, tall), tall), :].astype(f32) for first in (0, chips * block_rows)
+        ]
+        return jnp.concatenate([of_core(place & 1, part) for part in parts], 0).astype(bf16)
 
     for i in range(layout.tiles):
         total = near_tile(layout, i, places, of_device if whole else of_chip, blocks)
@@ -445,30 +458,38 @@
     return [both_halves(layout, *[half[start : start + count] for half in halves]) for start in (0, count)]
 
 
-def block_sums(layout, start, density, block):
-    vectors, tall = layout.vectors, 2 * layout.vectors
-    core = layout.device_of(block) & 1
+def chip_sums(layout, start, density, chip):
+    vectors, tall, count = layout.vectors, 2 * layout.vectors, layout.part_v
+    chips = layout.devices // 2
+    swapped = layout.device_of(chip) & 1
+    half = layout.half_index()
+    upper = lax.broadcasted_iota(jnp.int32, (vectors, lanes), 0) >= count
     total = None
     for i in range(layout.tiles):
-        r = start[block, i * tall : (i + 1) * tall, :].astype(f32)
-        rr, ri = r[:vectors], r[vectors:]
-        zr, zi = chip_rows(layout, i, density, block % (layout.devices // 2), core)
-        terms = (rr * rr + ri * ri, rr * zr + ri * zi, rr * zi - ri * zr, zr * zr + zi * zi)
-        total = terms if total is None else [a + b for a, b in zip(total, terms)]
+        span = slice(i * tall, (i + 1) * tall)
+        low, high = [density[chip + chips * which, span, :].astype(f32) for which in (half, 1 - half)]
+        for core in range(2):
+            r = start[chip + chips * (core ^ swapped), span, :].astype(f32)
+            rr, ri = r[:vectors], r[vectors:]
+            one, two = [z[core * vectors : (core + 1) * vectors] for z in (low, high)]
+            zr = jnp.where(upper, pltpu.roll(two, count, 0), one)
+            zi = jnp.where(upper, two, pltpu.roll(one, count, 0))
+            terms = (rr * rr + ri * ri, rr * zr + ri * zi, rr * zi - ri * zr, zr * zr + zi * zi)
+            total = terms if total is None else [a + b for a, b in zip(total, terms)]
     return total
 
 
-def tree_sums(layout, start, density, block, count):
+def tree_sums(layout, start, density, chip, count):
     if count == 1:
-        return block_sums(layout, start, density, block)
-    lower = tree_sums(layout, start, density, block, count // 2)
-    upper = tree_sums(layout, start, density, block + count // 2, count // 2)
+        return chip_sums(layout, start, density, chip)
+    lower = tree_sums(layout, start, density, chip, count // 2)
+    upper = tree_sums(layout, start, density, chip + count // 2, count // 2)
     return [a + b for a, b in zip(lower, upper)]
 
 
 def scalar_kernel(layout, start, density, guess, factors):
     vectors = layout.vectors
-    sums = tree_sums(layout, start, density, 0, layout.devices)
+    sums = tree_sums(layout, start, density, 0, layout.devices // 2)
     squares, real, imag, rest = [
         jnp.broadcast_to(jnp.sum(value, 1, keepdims=True) * (1.0 / layout.panels), (vectors, lanes)) for value in sums
     ]
@@ -663,7 +684,7 @@
             tuple([shape((rows // 2, lanes), f32)] * 2),
             [vmem] * 3,
             12,
-        )(density, blocks, neighbor)
+        )(density.reshape(-1, lanes), blocks, neighbor)
 
     def with_other_core(array):
         return jnp.concatenate([array, swap_cores(array)])

time: 36.1 us -> 35.3 us (0.978)
  Pallas kernels: 14.3 us -> 12.7 us
  waiting for transfers between devices: 2.68 us -> 3.09 us
    pallas_call x2, Pallas kernels: 1.76 us -> 1.14 us  [near_field(): call(lambda *refs: near_kernel(layout, whole, *refs), 'near', tuple([shap...]
    pallas_call x4, Pallas kernels: 4.95 us -> 4.47 us  [part_call(): call(lambda *refs: part_kernel(layout, base, with_start, not tables, halv...]
    pallas_call x4, Pallas kernels: 1.62 us -> 1.25 us  [make(): call(lambda *refs: table_kernel(layout, base, *refs), name, table_shapes(...]
  transfers between devices with their start and end apart: 13 -> 13, of which waited for: 5 -> 6; matrix products, arithmetic and copies ran while one was open for 4% -> 4% of each run, Pallas kernels for 38% -> 34%
where the time goes in v8:
time: 35.3 us; the launch traced here: 35.1 us
  starting transfers between devices  16.1 us (46%)
  Pallas kernels  12.7 us (36%)
  waiting for transfers between devices  3.09 us (9%)
  other arithmetic  1.52 us (4%)
  between operations  0.89 us (3%)
  local copies, waits for them, and re-layouts  0.8 us (2%)
    ppermute x3, starting transfers between devices, gather_and_project(): arrived = lax.ppermute(array, ('tile', 'wave'), pairs)  7.28 us
    ppermute x3, starting transfers between devices, gather_chips(): arrived = lax.ppermute(array, ('tile', 'wave'), pairs)  6.6 us
    pallas_call x4, Pallas kernels, part_call(): call(lambda *refs: part_kernel(layout, base, with_start, not tables, halv...  4.47 us
    pallas_call x3, Pallas kernels, gather_chips(): call(lambda *refs, base=base, start=total is not None: chips_kernel(layou...  2.9 us
    ppermute x3, waiting for transfers between devices, gather_chips(): arrived = lax.ppermute(array, ('tile', 'wave'), pairs)  2.41 us
    ppermute x7, starting transfers between devices, swap_cores(): return lax.ppermute(array, 'wave', [(0, 1), (1, 0)])  2.21 us
    pallas_call x4, Pallas kernels, make(): call(lambda *refs: table_kernel(layout, base, *refs), name, table_shapes(...  1.25 us
    pallas_call x2, Pallas kernels, near_field(): call(lambda *refs: near_kernel(layout, whole, *refs), 'near', tuple([shap...  1.14 us
  transfers between devices with their start and end apart: 13, of which 6 were waited for; matrix products, arithmetic and copies ran while one was open for 4% of the time, Pallas kernels for 34%

profile of v8, /device:TPU:0, one launch (start us, length us, event | category | flops | bytes accessed | tf_op | source)
XLA Modules:
  0.0 35.1 jit_solution(12073916046520115076)
XLA Ops:
  0.6 0.8 %pad_maximum_fusion.5.refs_0_ = f32[72,128]{1,0:T(8,128)S(1)} fusion(f32[8,128]{1,0:T(8,128)} %bitcast.32, f32[64,128]{1,0:T(8,128)} %bitcast.31), kind=kLoop, calls=%fused_computation.5 | loop fusion | flops 9216 | bytes 73728 | tf_op jit(solution)/shard_map/concatenate | solution.py:558
  1.4 3.5 %collective-permute-start = (bf16[1,80,128]{2,1,0:T(8,128)(2,1)S(1)}, bf16[1,80,128]{2,1,0:T(8,128)(2,1)S(1)}, u32[]{:S(2)}, u32[]{:S(2)}) collective-permute-start(bf16[1,80,128]{2,1,0:T(8,128)(2,1)S(1)} %bitcast.17), channel_id=1, source_target_pairs={{0,9},{1,8},{2,11},{3,10},{4,13},{5,12},{6,15},{7,14},{8,1},{9,0},... | collective-permute-start | bytes 61448 | tf_op jit(solution)/shard_map/ppermute | solution.py:615
  5.0 0.7 %pad_bitcast_fusion = s32[1,128]{1,0:T(1,128)S(1)} fusion(s32[8]{0:T(128)} %param.12), kind=kLoop, calls=%fused_computation.18 | loop fusion | bytes 544 | tf_op jit(solution)/shard_map/stack | solution.py:567
  5.6 0.7 %pad_add_fusion.refs_0_ = s32[3,128]{1,0:T(4,128)S(1)} fusion(s32[1,128]{1,0:T(1,128)S(1)} %pad_bitcast_fusion, s32[1,128]{1,0:T(1,128)} %bitcast.33, s32[1,128]{1,0:T(1,128)} %bitcast.34), kind=kLoop, calls=%fused_computation.17 | loop fusion | flops 768 | bytes 3072 | tf_op jit(solution)/shard_map/stack | solution.py:567
  6.5 1.9 %collective-permute-start.2 = (bf16[2,80,128]{2,1,0:T(8,128)(2,1)S(1)}, bf16[2,80,128]{2,1,0:T(8,128)(2,1)S(1)}, u32[]{:S(2)}, u32[]{:S(2)}) collective-permute-start(bf16[2,80,128]{2,1,0:T(8,128)(2,1)S(1)} %pad_maximum_fusion.4.refs_0_), channel_id=1, source_target_pairs={{0,5},{1,4},{2,7},{3,6},{4,1},{5,0},{6,3},{7,2},{8,13},{9,12},{10,... | collective-permute-start | bytes 122888 | tf_op jit(solution)/shard_map/ppermute | solution.py:615
  8.7 1.1 %part.4 = (f32[1024,256]{1,0:T(8,128)S(1)}, bf16[1,256,1024]{2,1,0:T(8,128)(2,1)S(1)}, f32[2,72,512]{2,1,0:T(8,128)S(1)}) custom-call(bf16[2,80,128]{2,1,0:T(8,128)(2,1)S(1)} %pad_maximum_fusion.4.refs_0_), custom_call_target="tpu_custom_call" | custom-call | flops 1000000000 | tf_op jit(solution)/shard_map/part/pallas_call | solution.py:600
  10.0 1.9 %collective-permute-start.3 = (bf16[4,80,128]{2,1,0:T(8,128)(2,1)S(1)}, bf16[4,80,128]{2,1,0:T(8,128)(2,1)S(1)}, u32[]{:S(2)}, u32[]{:S(2)}) collective-permute-start(bf16[4,80,128]{2,1,0:T(8,128)(2,1)S(1)} %pad_maximum_fusion.2), channel_id=1, source_target_pairs={{0,3},{1,2},{2,1},{3,0},{4,7},{5,6},{6,5},{7,4},{8,11},{9,10},{10,... | collective-permute-start | bytes 245768 | tf_op jit(solution)/shard_map/ppermute | solution.py:615
  11.9 1.0 %spectral.1 = (f32[8,128,128]{2,1,0:T(8,128)S(1)}, f32[8,128]{1,0:T(8,128)S(1)}) custom-call(s32[3,128]{1,0:T(4,128)S(1)} %pad_add_fusion.refs_0_, f32[8,128,128]{2,1,0:T(8,128)S(1)} %copy-done.1), custom_call_target="tpu_custom_call" | custom-call | flops 2000000000 | tf_op jit(solution)/shard_map/spectral/pallas_call | solution.py:570
  12.9 1.1 %part.5 = (f32[1024,256]{1,0:T(8,128)S(1)}, bf16[1,256,1024]{2,1,0:T(8,128)(2,1)S(1)}, f32[2,72,512]{2,1,0:T(8,128)S(1)}) custom-call(bf16[2,80,128]{2,1,0:T(8,128)(2,1)S(1)} %collective-permute-done.2.refs_0_, f32[1024,256]{1,0:T(8,128)S(1)} %get-tuple-element.42.refs_1_), custom_call_target="tpu_custom_call", output_to_operand_aliasing={{0}: (1, {})} | custom-call | flops 1000000000 | tf_op jit(solution)/shard_map/part/pallas_call | solution.py:600
  14.9 1.5 %leaving.1 = (bf16[512,256]{1,0:T(8,128)(2,1)S(1)}, bf16[1,256,2048]{2,1,0:T(8,128)(2,1)S(1)}, f32[4,72,512]{2,1,0:T(8,128)S(1)}) custom-call(bf16[4,80,128]{2,1,0:T(8,128)(2,1)S(1)} %collective-permute-done.3.refs_0_, f32[1024,256]{1,0:T(8,128)S(1)} %get-tuple-element.43.refs_1_.refs_3_), custom_call_target="tpu_custom_call" | custom-call | flops 2000000000 | tf_op jit(solution)/shard_map/leaving/pallas_call | solution.py:600
  16.7 0.6 %near.2 = (f32[32,128]{1,0:T(8,128)S(1)}, f32[32,128]{1,0:T(8,128)S(1)}) custom-call(bf16[1280,128]{1,0:T(8,128)(2,1)S(1)} %bitcast.21, bf16[4,9,2,128,128]{4,3,2,1,0:T(8,128)(2,1)S(1)} %bitcast.27, s32[4,9]{1,0:T(4,128)S(1)} %bitcast.29), custom_call_target="tpu_custom_call" | custom-call | flops 2000000000 | tf_op jit(solution)/shard_map/near/pallas_call | solution.py:681
  17.6 0.8 %staying.1.refs_1_ = f32[512,256]{1,0:T(8,128)S(1)} custom-call(bf16[4,80,128]{2,1,0:T(8,128)(2,1)S(1)} %collective-permute-done.3.refs_0_, bf16[1,256,2048]{2,1,0:T(8,128)(2,1)S(1)} %get-tuple-element.46.refs_1_, f32[4,72,512]{2,1,0:T(8,128)S(1)} %get-tuple-element.47.refs_2_, f32[1024,256]{1,0:T(8,128)S(1)} %get-tuple-element.43.refs_1_.refs_3_), custom_call_target="tpu_custom_call" | custom-call | flops 800000000 | tf_op jit(solution)/shard_map/staying/pallas_call | solution.py:600
  19.0 3.2 %collective-permute-start.7 = (bf16[1,64,128]{2,1,0:T(8,128)(2,1)S(1)}, bf16[1,64,128]{2,1,0:T(8,128)(2,1)S(1)}, u32[]{:S(2)}, u32[]{:S(2)}) collective-permute-start(bf16[1,64,128]{2,1,0:T(8,128)(2,1)S(1)} %bitcast.22), channel_id=1, source_target_pairs={{0,9},{1,8},{2,11},{3,10},{4,13},{5,12},{6,15},{7,14},{8,1},{9,0},... | collective-permute-start | bytes 49160 | tf_op jit(solution)/shard_map/ppermute | solution.py:645
  22.3 1.3 %collective-permute-done.7 = bf16[1,64,128]{2,1,0:T(8,128)(2,1)S(1)} collective-permute-done((bf16[1,64,128]{2,1,0:T(8,128)(2,1)S(1)}, bf16[1,64,128]{2,1,0:T(8,128)(2,1)S(1)}, u32[]{:S(2)}, u32[]{:S(2)}) %collective-permute-start.7) | collective-permute-done | bytes 16416 | tf_op jit(solution)/shard_map/ppermute | solution.py:645
  23.6 1.8 %collective-permute-start.8 = (bf16[2,64,128]{2,1,0:T(8,128)(2,1)S(1)}, bf16[2,64,128]{2,1,0:T(8,128)(2,1)S(1)}, u32[]{:S(2)}, u32[]{:S(2)}) collective-permute-start(bf16[2,64,128]{2,1,0:T(8,128)(2,1)S(1)} %pad_maximum_fusion.6.refs_0_), channel_id=1, source_target_pairs={{0,5},{1,4},{2,7},{3,6},{4,1},{5,0},{6,3},{7,2},{8,13},{9,12},{10,... | collective-permute-start | bytes 98312 | tf_op jit(solution)/shard_map/ppermute | solution.py:645
  25.7 0.8 %part.6.refs_5_ = f32[512,256]{1,0:T(8,128)S(1)} custom-call(bf16[2,64,128]{2,1,0:T(8,128)(2,1)S(1)} %pad_maximum_fusion.6.refs_0_, bf16[1,256,1024]{2,1,0:T(8,128)(2,1)S(1)} %get-tuple-element.50.refs_3_.refs_1_.refs_2_, f32[2,72,512]{2,1,0:T(8,128)S(1)} %get-tuple-element.51.refs_4_.refs_2_.refs_3_, bf16[1,256,1024]{2,1,0:T(8,128)(2,1)S(1)} %get-tuple-element.68.refs_3_, ...), custom_call_target="tpu_custom_call" | custom-call | flops 1000000000 | tf_op jit(solution)/shard_map/part/pallas_call | solution.py:653
  26.5 0.5 %collective-permute-done.8.refs_0_ = bf16[2,64,128]{2,1,0:T(8,128)(2,1)S(1)} collective-permute-done((bf16[2,64,128]{2,1,0:T(8,128)(2,1)S(1)}, bf16[2,64,128]{2,1,0:T(8,128)(2,1)S(1)}, u32[]{:S(2)}, u32[]{:S(2)}) %collective-permute-start.8) | collective-permute-done | bytes 32800 | tf_op jit(solution)/shard_map/ppermute | solution.py:645
  27.0 1.6 %collective-permute-start.9 = (bf16[4,64,128]{2,1,0:T(8,128)(2,1)S(1)}, bf16[4,64,128]{2,1,0:T(8,128)(2,1)S(1)}, u32[]{:S(2)}, u32[]{:S(2)}) collective-permute-start(bf16[4,64,128]{2,1,0:T(8,128)(2,1)S(1)} %pad_maximum_fusion.3), channel_id=1, source_target_pairs={{0,3},{1,2},{2,1},{3,0},{4,7},{5,6},{6,5},{7,4},{8,11},{9,10},{10,... | collective-permute-start | bytes 196616 | tf_op jit(solution)/shard_map/ppermute | solution.py:645
  28.9 0.8 %part.7.refs_5_ = f32[512,256]{1,0:T(8,128)S(1)} custom-call(bf16[2,64,128]{2,1,0:T(8,128)(2,1)S(1)} %collective-permute-done.8.refs_0_, bf16[1,256,1024]{2,1,0:T(8,128)(2,1)S(1)} %get-tuple-element.63.refs_1_, f32[2,72,512]{2,1,0:T(8,128)S(1)} %get-tuple-element.64.refs_2_, ...), custom_call_target="tpu_custom_call", output_to_operand_aliasing={{}: (5, {})} | custom-call | flops 1000000000 | tf_op jit(solution)/shard_map/part/pallas_call | solution.py:653
  29.7 0.5 %tables.3 = (bf16[1,256,2048]{2,1,0:T(8,128)(2,1)S(1)}, f32[4,72,512]{2,1,0:T(8,128)S(1)}) custom-call(bf16[4,80,128]{2,1,0:T(8,128)(2,1)S(1)} %slice.9.refs_0_), custom_call_target="tpu_custom_call" | custom-call | flops 500000000 | tf_op jit(solution)/shard_map/tables/pallas_call | solution.py:632
  30.3 0.6 %collective-permute-done.9.refs_0_ = bf16[4,64,128]{2,1,0:T(8,128)(2,1)S(1)} collective-permute-done((bf16[4,64,128]{2,1,0:T(8,128)(2,1)S(1)}, bf16[4,64,128]{2,1,0:T(8,128)(2,1)S(1)}, u32[]{:S(2)}, u32[]{:S(2)}) %collective-permute-start.9) | collective-permute-done | bytes 65568 | tf_op jit(solution)/shard_map/ppermute | solution.py:645
  31.4 1.4 %whole.1.refs_0_ = f32[512,256]{1,0:T(8,128)S(1)} custom-call(bf16[4,64,128]{2,1,0:T(8,128)(2,1)S(1)} %collective-permute-done.9.refs_0_, bf16[1,256,2048]{2,1,0:T(8,128)(2,1)S(1)} %get-tuple-element.46.refs_1_, f32[4,72,512]{2,1,0:T(8,128)S(1)} %get-tuple-element.47.refs_2_, ...), custom_call_target="tpu_custom_call", output_to_operand_aliasing={{}: (5, {})} | custom-call | flops 800000000 | tf_op jit(solution)/shard_map/whole/pallas_call | solution.py:653
  33.5 0.6 %near.3 = (f32[32,128]{1,0:T(8,128)S(1)}, f32[32,128]{1,0:T(8,128)S(1)}) custom-call(bf16[1024,128]{1,0:T(8,128)(2,1)S(1)} %bitcast.16, bf16[4,9,2,128,128]{4,3,2,1,0:T(8,128)(2,1)S(1)} %bitcast.28, s32[4,9]{1,0:T(4,128)S(1)} %bitcast.30), custom_call_target="tpu_custom_call" | custom-call | flops 2000000000 | tf_op jit(solution)/shard_map/near/pallas_call | solution.py:681
  34.5 0.7 %second.1 = (f32[64,128]{1,0:T(8,128)}, f32[4,8]{1,0:T(4,128)}) custom-call(bf16[16,64,128]{2,1,0:T(8,128)(2,1)S(1)} %constant_dynamic-update-slice_fusion.5.refs_1_.refs_0_, f32[32,128]{1,0:T(8,128)S(1)} %get-tuple-element.58.refs_1_, f32[32,128]{1,0:T(8,128)S(1)} %get-tuple-element.59.refs_2_, f32[32,128]{1,0:T(8,128)S(1)} %get-tuple-element.70.refs_3_, ...), custom_call_target="tpu_custom_call" | custom-call | tf_op jit(solution)/shard_map/second/pallas_call | solution.py:717
  (50 shorter events, 5.2 us)
Async XLA Ops:
  1.4 5.1 %collective-permute-start = (bf16[1,80,128]{2,1,0:T(8,128)(2,1)S(1)}, bf16[1,80,128]{2,1,0:T(8,128)(2,1)S(1)}, u32[]{:S(2)}, u32[]{:S(2)}) collective-permute-start(bf16[1,80,128]{2,1,0:T(8,128)(2,1)S(1)} %bitcast.17), channel_id=1, source_target_pairs={{0,9},{1,8},{2,11},{3,10},{4,13},{5,12},{6,15},{7,14},{8,1},{9,0},... | collective-permute-start | bytes 61448 | tf_op jit(solution)/shard_map/ppermute | solution.py:615
  6.5 3.5 %collective-permute-start.2 = (bf16[2,80,128]{2,1,0:T(8,128)(2,1)S(1)}, bf16[2,80,128]{2,1,0:T(8,128)(2,1)S(1)}, u32[]{:S(2)}, u32[]{:S(2)}) collective-permute-start(bf16[2,80,128]{2,1,0:T(8,128)(2,1)S(1)} %pad_maximum_fusion.4.refs_0_), channel_id=1, source_target_pairs={{0,5},{1,4},{2,7},{3,6},{4,1},{5,0},{6,3},{7,2},{8,13},{9,12},{10,... | collective-permute-start | bytes 122888 | tf_op jit(solution)/shard_map/ppermute | solution.py:615
  8.3 1.5 %collective-permute-start.1 = (bf16[80,128]{1,0:T(8,128)(2,1)S(1)}, bf16[80,128]{1,0:T(8,128)(2,1)S(1)}, u32[]{:S(2)}, u32[]{:S(2)}) collective-permute-start(bf16[80,128]{1,0:T(8,128)(2,1)S(1)} %pack.1.refs_0_), channel_id=1, source_target_pairs={{0,1},{1,0},{2,3},{3,2},{4,5},{5,4},{6,7},{7,6},{8,9},{9,8},{10,11... | collective-permute-start | bytes 61448 | tf_op jit(solution)/shard_map/ppermute | solution.py:86
  8.7 3.2 %copy-start.1 = (f32[8,128,128]{2,1,0:T(8,128)S(1)}, f32[8,128,128]{2,1,0:T(8,128)}, u32[]{:S(2)}) copy-start(f32[8,128,128]{2,1,0:T(8,128)} %refs_1_.1) | copy-start | bytes 1572868
  10.0 4.4 %collective-permute-start.3 = (bf16[4,80,128]{2,1,0:T(8,128)(2,1)S(1)}, bf16[4,80,128]{2,1,0:T(8,128)(2,1)S(1)}, u32[]{:S(2)}, u32[]{:S(2)}) collective-permute-start(bf16[4,80,128]{2,1,0:T(8,128)(2,1)S(1)} %pad_maximum_fusion.2), channel_id=1, source_target_pairs={{0,3},{1,2},{2,1},{3,0},{4,7},{5,6},{6,5},{7,4},{8,11},{9,10},{10,... | collective-permute-start | bytes 245768 | tf_op jit(solution)/shard_map/ppermute | solution.py:615
  14.5 2.1 %collective-permute-start.4 = (bf16[8,80,128]{2,1,0:T(8,128)(2,1)S(1)}, bf16[8,80,128]{2,1,0:T(8,128)(2,1)S(1)}, u32[]{:S(2)}, u32[]{:S(2)}) collective-permute-start(bf16[8,80,128]{2,1,0:T(8,128)(2,1)S(1)} %pad_maximum_fusion), channel_id=1, source_target_pairs={{0,1},{1,0},{2,3},{3,2},{4,5},{5,4},{6,7},{7,6},{8,9},{9,8},{10,11... | collective-permute-start | bytes 491528 | tf_op jit(solution)/shard_map/ppermute | solution.py:86
  14.8 1.8 %copy-start = (bf16[1,4,9,2,128,128]{5,4,3,2,1,0:T(8,128)(2,1)S(1)}, bf16[1,4,9,2,128,128]{5,4,3,2,1,0:T(8,128)(2,1)}, u32[]{:S(2)}) copy-start(bf16[1,4,9,2,128,128]{5,4,3,2,1,0:T(8,128)(2,1)} %param.9) | copy-start | bytes 7077892
  14.8 1.8 %copy-start.2 = (s32[1,4,9]{2,1,0:T(4,128)S(1)}, s32[1,4,9]{2,1,0:T(4,128)}, u32[]{:S(2)}) copy-start(s32[1,4,9]{2,1,0:T(4,128)} %param.11) | copy-start | bytes 436
  16.3 2.1 %collective-permute-start.6 = (bf16[512,256]{1,0:T(8,128)(2,1)S(1)}, bf16[512,256]{1,0:T(8,128)(2,1)S(1)}, u32[]{:S(2)}, u32[]{:S(2)}) collective-permute-start(bf16[512,256]{1,0:T(8,128)(2,1)S(1)} %get-tuple-element.44), channel_id=1, source_target_pairs={{0,1},{1,0},{2,3},{3,2},{4,5},{5,4},{6,7},{7,6},{8,9},{9,8},{10,11... | collective-permute-start | bytes 786440 | tf_op jit(solution)/shard_map/ppermute | solution.py:86
  17.3 1.7 %collective-permute-start.5 = (f32[32,128]{1,0:T(8,128)S(1)}, f32[32,128]{1,0:T(8,128)S(1)}, u32[]{:S(2)}, u32[]{:S(2)}) collective-permute-start(f32[32,128]{1,0:T(8,128)S(1)} %get-tuple-element.41), channel_id=1, source_target_pairs={{0,1},{1,0},{2,3},{3,2},{4,5},{5,4},{6,7},{7,6},{8,9},{9,8},{10,11... | collective-permute-start | bytes 49160 | tf_op jit(solution)/shard_map/ppermute | solution.py:86
  19.0 4.6 %collective-permute-start.7 = (bf16[1,64,128]{2,1,0:T(8,128)(2,1)S(1)}, bf16[1,64,128]{2,1,0:T(8,128)(2,1)S(1)}, u32[]{:S(2)}, u32[]{:S(2)}) collective-permute-start(bf16[1,64,128]{2,1,0:T(8,128)(2,1)S(1)} %bitcast.22), channel_id=1, source_target_pairs={{0,9},{1,8},{2,11},{3,10},{4,13},{5,12},{6,15},{7,14},{8,1},{9,0},... | collective-permute-start | bytes 49160 | tf_op jit(solution)/shard_map/ppermute | solution.py:645
  22.2 12.2 %collective-permute-start.12 = (f32[32,128]{1,0:T(8,128)S(1)}, f32[32,128]{1,0:T(8,128)S(1)}, u32[]{:S(2)}, u32[]{:S(2)}) collective-permute-start(f32[32,128]{1,0:T(8,128)S(1)} %get-tuple-element.73), channel_id=1, source_target_pairs={{0,1},{1,0},{2,3},{3,2},{4,5},{5,4},{6,7},{7,6},{8,9},{9,8},{10,11... | collective-permute-start | bytes 49160 | tf_op jit(solution)/shard_map/ppermute | solution.py:86
  23.6 3.4 %collective-permute-start.8 = (bf16[2,64,128]{2,1,0:T(8,128)(2,1)S(1)}, bf16[2,64,128]{2,1,0:T(8,128)(2,1)S(1)}, u32[]{:S(2)}, u32[]{:S(2)}) collective-permute-start(bf16[2,64,128]{2,1,0:T(8,128)(2,1)S(1)} %pad_maximum_fusion.6.refs_0_), channel_id=1, source_target_pairs={{0,5},{1,4},{2,7},{3,6},{4,1},{5,0},{6,3},{7,2},{8,13},{9,12},{10,... | collective-permute-start | bytes 98312 | tf_op jit(solution)/shard_map/ppermute | solution.py:645
  27.0 3.9 %collective-permute-start.9 = (bf16[4,64,128]{2,1,0:T(8,128)(2,1)S(1)}, bf16[4,64,128]{2,1,0:T(8,128)(2,1)S(1)}, u32[]{:S(2)}, u32[]{:S(2)}) collective-permute-start(bf16[4,64,128]{2,1,0:T(8,128)(2,1)S(1)} %pad_maximum_fusion.3), channel_id=1, source_target_pairs={{0,3},{1,2},{2,1},{3,0},{4,7},{5,6},{6,5},{7,4},{8,11},{9,10},{10,... | collective-permute-start | bytes 196616 | tf_op jit(solution)/shard_map/ppermute | solution.py:645
  30.9 2.5 %collective-permute-start.10 = (bf16[8,64,128]{2,1,0:T(8,128)(2,1)S(1)}, bf16[8,64,128]{2,1,0:T(8,128)(2,1)S(1)}, u32[]{:S(2)}, u32[]{:S(2)}) collective-permute-start(bf16[8,64,128]{2,1,0:T(8,128)(2,1)S(1)} %pad_maximum_fusion.1), channel_id=1, source_target_pairs={{0,1},{1,0},{2,3},{3,2},{4,5},{5,4},{6,7},{7,6},{8,9},{9,8},{10,11... | collective-permute-start | bytes 393224 | tf_op jit(solution)/shard_map/ppermute | solution.py:86
  33.2 1.2 %collective-permute-start.11 = (f32[32,128]{1,0:T(8,128)S(1)}, f32[32,128]{1,0:T(8,128)S(1)}, u32[]{:S(2)}, u32[]{:S(2)}) collective-permute-start(f32[32,128]{1,0:T(8,128)S(1)} %get-tuple-element.71), channel_id=1, source_target_pairs={{0,1},{1,0},{2,3},{3,2},{4,5},{5,4},{6,7},{7,6},{8,9},{9,8},{10,11... | collective-permute-start | bytes 49160 | tf_op jit(solution)/shard_map/ppermute | solution.py:86

commit v9 on v8

--- a/solution.py
+++ b/solution.py
@@ -8,7 +8,7 @@
 from jax.sharding import PartitionSpec as P
 
 eps_norm = 1e-06
-lengths = {"part": 1, "leaving": 2, "staying": 0.8, "spectral": 2, "other_tables": 0.5, "far": 0.3, "near": 2, "tables": 0.5, "whole": 0.8}
+lengths = {"part": 1, "leaving": 0.5, "staying": 0.8, "spectral": 2, "other_tables": 0.5, "far": 0.3, "near": 2, "tables": 0.5, "whole": 0.8}
 f32 = jnp.float32
 bf16 = jnp.bfloat16
 lanes = 128
@@ -607,6 +607,15 @@
             aliases={len(given) - 1: 0} if with_start and len(halves) == 2 else None,
         )(*given)
 
+    def make(name, base, density):
+        return call(
+            lambda *refs: table_kernel(layout, base, *refs),
+            name,
+            table_shapes(density.shape[0]),
+            [vmem],
+            8,
+        )(density)
+
     def gather_and_project(array, tables):
         array = array[None]
         total, base, made, seen = None, 0, [], []
@@ -620,22 +629,13 @@
                 total, *new = part_call("part", base, part, tables and tables[k], total, (0, 1), f32)
                 base += part.shape[0]
                 made.append(new or tables[k])
-        leaving, *new = part_call("leaving", base, part, tables and tables[-1], total, (1,), bf16)
-        made.append(new or tables[-1])
+        made.append(make("tables", base, part))
+        (leaving,) = part_call("leaving", base, part, made[-1], total, (1,), bf16)
 
         def stay(first):
             return part_call("staying", base, after(part, first), made[-1], total, (0,), f32)[0]
 
         return seen, leaving, stay, made
-
-    def make(name, base, density):
-        return call(
-            lambda *refs: table_kernel(layout, base, *refs),
-            name,
-            table_shapes(density.shape[0]),
-            [vmem],
-            8,
-        )(density)
 
     def gather_chips(array, tables, other):
         array = array[None]

time: 35.3 us -> 35.2 us (level)
    pallas_call x4, Pallas kernels: 4.47 us -> 3.76 us  [part_call(): call(lambda *refs: part_kernel(layout, base, with_start, not tables, halv...]
    pallas_call x4 -> x5, Pallas kernels: 1.25 us -> 1.78 us  [make(): call(lambda *refs: table_kernel(layout, base, *refs), name, table_shapes(...]
where the time goes in v9:
time: 35.2 us; the launch traced here: 35 us
  starting transfers between devices  16.1 us (46%)
  Pallas kernels  12.5 us (36%)
  waiting for transfers between devices  3.11 us (9%)
  other arithmetic  1.53 us (4%)
  between operations  0.91 us (3%)
  local copies, waits for them, and re-layouts  0.8 us (2%)
    ppermute x3, starting transfers between devices, gather_and_project(): arrived = lax.ppermute(array, ('tile', 'wave'), pairs)  7.28 us
    ppermute x3, starting transfers between devices, gather_chips(): arrived = lax.ppermute(array, ('tile', 'wave'), pairs)  6.6 us
    pallas_call x4, Pallas kernels, part_call(): call(lambda *refs: part_kernel(layout, base, with_start, not tables, halv...  3.76 us
    pallas_call x3, Pallas kernels, gather_chips(): call(lambda *refs, base=base, start=total is not None: chips_kernel(layou...  2.89 us
    ppermute x3, waiting for transfers between devices, gather_chips(): arrived = lax.ppermute(array, ('tile', 'wave'), pairs)  2.42 us
    ppermute x7, starting transfers between devices, swap_cores(): return lax.ppermute(array, 'wave', [(0, 1), (1, 0)])  2.21 us
    pallas_call x5, Pallas kernels, make(): call(lambda *refs: table_kernel(layout, base, *refs), name, table_shapes(...  1.78 us
    pallas_call x2, Pallas kernels, near_field(): call(lambda *refs: near_kernel(layout, whole, *refs), 'near', tuple([shap...  1.14 us
  transfers between devices with their start and end apart: 13, of which 6 were waited for; matrix products, arithmetic and copies ran while one was open for 4% of the time, Pallas kernels for 34%

profile of v9, /device:TPU:0, one launch (start us, length us, event | category | flops | bytes accessed | tf_op | source)
XLA Modules:
  0.0 35.0 jit_solution(5178494126129549165)
XLA Ops:
  0.6 0.8 %pad_maximum_fusion.5.refs_0_ = f32[72,128]{1,0:T(8,128)S(1)} fusion(f32[8,128]{1,0:T(8,128)} %bitcast.32, f32[64,128]{1,0:T(8,128)} %bitcast.31), kind=kLoop, calls=%fused_computation.5 | loop fusion | flops 9216 | bytes 73728 | tf_op jit(solution)/shard_map/concatenate | solution.py:558
  1.4 3.5 %collective-permute-start = (bf16[1,80,128]{2,1,0:T(8,128)(2,1)S(1)}, bf16[1,80,128]{2,1,0:T(8,128)(2,1)S(1)}, u32[]{:S(2)}, u32[]{:S(2)}) collective-permute-start(bf16[1,80,128]{2,1,0:T(8,128)(2,1)S(1)} %bitcast.17), channel_id=1, source_target_pairs={{0,9},{1,8},{2,11},{3,10},{4,13},{5,12},{6,15},{7,14},{8,1},{9,0},... | collective-permute-start | bytes 61448 | tf_op jit(solution)/shard_map/ppermute | solution.py:624
  5.0 0.7 %pad_bitcast_fusion = s32[1,128]{1,0:T(1,128)S(1)} fusion(s32[8]{0:T(128)} %param.12), kind=kLoop, calls=%fused_computation.18 | loop fusion | bytes 544 | tf_op jit(solution)/shard_map/stack | solution.py:567
  5.6 0.7 %pad_add_fusion.refs_0_ = s32[3,128]{1,0:T(4,128)S(1)} fusion(s32[1,128]{1,0:T(1,128)S(1)} %pad_bitcast_fusion, s32[1,128]{1,0:T(1,128)} %bitcast.33, s32[1,128]{1,0:T(1,128)} %bitcast.34), kind=kLoop, calls=%fused_computation.17 | loop fusion | flops 768 | bytes 3072 | tf_op jit(solution)/shard_map/stack | solution.py:567
  6.5 1.9 %collective-permute-start.2 = (bf16[2,80,128]{2,1,0:T(8,128)(2,1)S(1)}, bf16[2,80,128]{2,1,0:T(8,128)(2,1)S(1)}, u32[]{:S(2)}, u32[]{:S(2)}) collective-permute-start(bf16[2,80,128]{2,1,0:T(8,128)(2,1)S(1)} %pad_maximum_fusion.4.refs_0_), channel_id=1, source_target_pairs={{0,5},{1,4},{2,7},{3,6},{4,1},{5,0},{6,3},{7,2},{8,13},{9,12},{10,... | collective-permute-start | bytes 122888 | tf_op jit(solution)/shard_map/ppermute | solution.py:624
  8.7 1.1 %part.4 = (f32[1024,256]{1,0:T(8,128)S(1)}, bf16[1,256,1024]{2,1,0:T(8,128)(2,1)S(1)}, f32[2,72,512]{2,1,0:T(8,128)S(1)}) custom-call(bf16[2,80,128]{2,1,0:T(8,128)(2,1)S(1)} %pad_maximum_fusion.4.refs_0_), custom_call_target="tpu_custom_call" | custom-call | flops 1000000000 | tf_op jit(solution)/shard_map/part/pallas_call | solution.py:600
  10.1 1.9 %collective-permute-start.3 = (bf16[4,80,128]{2,1,0:T(8,128)(2,1)S(1)}, bf16[4,80,128]{2,1,0:T(8,128)(2,1)S(1)}, u32[]{:S(2)}, u32[]{:S(2)}) collective-permute-start(bf16[4,80,128]{2,1,0:T(8,128)(2,1)S(1)} %pad_maximum_fusion.2), channel_id=1, source_target_pairs={{0,3},{1,2},{2,1},{3,0},{4,7},{5,6},{6,5},{7,4},{8,11},{9,10},{10,... | collective-permute-start | bytes 245768 | tf_op jit(solution)/shard_map/ppermute | solution.py:624
  11.9 1.0 %spectral.1 = (f32[8,128,128]{2,1,0:T(8,128)S(1)}, f32[8,128]{1,0:T(8,128)S(1)}) custom-call(s32[3,128]{1,0:T(4,128)S(1)} %pad_add_fusion.refs_0_, f32[8,128,128]{2,1,0:T(8,128)S(1)} %copy-done.1), custom_call_target="tpu_custom_call" | custom-call | flops 2000000000 | tf_op jit(solution)/shard_map/spectral/pallas_call | solution.py:570
  12.9 1.1 %part.5 = (f32[1024,256]{1,0:T(8,128)S(1)}, bf16[1,256,1024]{2,1,0:T(8,128)(2,1)S(1)}, f32[2,72,512]{2,1,0:T(8,128)S(1)}) custom-call(bf16[2,80,128]{2,1,0:T(8,128)(2,1)S(1)} %collective-permute-done.2.refs_0_, f32[1024,256]{1,0:T(8,128)S(1)} %get-tuple-element.43.refs_1_), custom_call_target="tpu_custom_call", output_to_operand_aliasing={{0}: (1, {})} | custom-call | flops 1000000000 | tf_op jit(solution)/shard_map/part/pallas_call | solution.py:600
  15.4 0.8 %leaving.1 = bf16[512,256]{1,0:T(8,128)(2,1)S(1)} custom-call(bf16[4,80,128]{2,1,0:T(8,128)(2,1)S(1)} %collective-permute-done.3.refs_0_, bf16[1,256,2048]{2,1,0:T(8,128)(2,1)S(1)} %get-tuple-element.41.refs_1_, f32[4,72,512]{2,1,0:T(8,128)S(1)} %get-tuple-element.42.refs_2_, f32[1024,256]{1,0:T(8,128)S(1)} %get-tuple-element.44.refs_3_), custom_call_target="tpu_custom_call" | custom-call | flops 500000000 | tf_op jit(solution)/shard_map/leaving/pallas_call | solution.py:600
  16.6 0.6 %near.2 = (f32[32,128]{1,0:T(8,128)S(1)}, f32[32,128]{1,0:T(8,128)S(1)}) custom-call(bf16[1280,128]{1,0:T(8,128)(2,1)S(1)} %bitcast.21, bf16[4,9,2,128,128]{4,3,2,1,0:T(8,128)(2,1)S(1)} %bitcast.27, s32[4,9]{1,0:T(4,128)S(1)} %bitcast.29), custom_call_target="tpu_custom_call" | custom-call | flops 2000000000 | tf_op jit(solution)/shard_map/near/pallas_call | solution.py:681
  17.5 0.8 %staying.1.refs_1_ = f32[512,256]{1,0:T(8,128)S(1)} custom-call(bf16[4,80,128]{2,1,0:T(8,128)(2,1)S(1)} %collective-permute-done.3.refs_0_, bf16[1,256,2048]{2,1,0:T(8,128)(2,1)S(1)} %get-tuple-element.41.refs_1_, f32[4,72,512]{2,1,0:T(8,128)S(1)} %get-tuple-element.42.refs_2_, f32[1024,256]{1,0:T(8,128)S(1)} %get-tuple-element.44.refs_3_), custom_call_target="tpu_custom_call" | custom-call | flops 800000000 | tf_op jit(solution)/shard_map/staying/pallas_call | solution.py:600
  18.8 3.2 %collective-permute-start.7 = (bf16[1,64,128]{2,1,0:T(8,128)(2,1)S(1)}, bf16[1,64,128]{2,1,0:T(8,128)(2,1)S(1)}, u32[]{:S(2)}, u32[]{:S(2)}) collective-permute-start(bf16[1,64,128]{2,1,0:T(8,128)(2,1)S(1)} %bitcast.22), channel_id=1, source_target_pairs={{0,9},{1,8},{2,11},{3,10},{4,13},{5,12},{6,15},{7,14},{8,1},{9,0},... | collective-permute-start | bytes 49160 | tf_op jit(solution)/shard_map/ppermute | solution.py:645
  22.2 1.3 %collective-permute-done.7 = bf16[1,64,128]{2,1,0:T(8,128)(2,1)S(1)} collective-permute-done((bf16[1,64,128]{2,1,0:T(8,128)(2,1)S(1)}, bf16[1,64,128]{2,1,0:T(8,128)(2,1)S(1)}, u32[]{:S(2)}, u32[]{:S(2)}) %collective-permute-start.7) | collective-permute-done | bytes 16416 | tf_op jit(solution)/shard_map/ppermute | solution.py:645
  23.4 1.8 %collective-permute-start.8 = (bf16[2,64,128]{2,1,0:T(8,128)(2,1)S(1)}, bf16[2,64,128]{2,1,0:T(8,128)(2,1)S(1)}, u32[]{:S(2)}, u32[]{:S(2)}) collective-permute-start(bf16[2,64,128]{2,1,0:T(8,128)(2,1)S(1)} %pad_maximum_fusion.6.refs_0_), channel_id=1, source_target_pairs={{0,5},{1,4},{2,7},{3,6},{4,1},{5,0},{6,3},{7,2},{8,13},{9,12},{10,... | collective-permute-start | bytes 98312 | tf_op jit(solution)/shard_map/ppermute | solution.py:645
  25.6 0.8 %part.6.refs_5_ = f32[512,256]{1,0:T(8,128)S(1)} custom-call(bf16[2,64,128]{2,1,0:T(8,128)(2,1)S(1)} %pad_maximum_fusion.6.refs_0_, bf16[1,256,1024]{2,1,0:T(8,128)(2,1)S(1)} %get-tuple-element.48.refs_3_.refs_1_.refs_2_, f32[2,72,512]{2,1,0:T(8,128)S(1)} %get-tuple-element.49.refs_4_.refs_2_.refs_3_, bf16[1,256,1024]{2,1,0:T(8,128)(2,1)S(1)} %get-tuple-element.66.refs_3_, ...), custom_call_target="tpu_custom_call" | custom-call | flops 1000000000 | tf_op jit(solution)/shard_map/part/pallas_call | solution.py:653
  26.3 0.5 %collective-permute-done.8.refs_0_ = bf16[2,64,128]{2,1,0:T(8,128)(2,1)S(1)} collective-permute-done((bf16[2,64,128]{2,1,0:T(8,128)(2,1)S(1)}, bf16[2,64,128]{2,1,0:T(8,128)(2,1)S(1)}, u32[]{:S(2)}, u32[]{:S(2)}) %collective-permute-start.8) | collective-permute-done | bytes 32800 | tf_op jit(solution)/shard_map/ppermute | solution.py:645
  26.9 1.6 %collective-permute-start.9 = (bf16[4,64,128]{2,1,0:T(8,128)(2,1)S(1)}, bf16[4,64,128]{2,1,0:T(8,128)(2,1)S(1)}, u32[]{:S(2)}, u32[]{:S(2)}) collective-permute-start(bf16[4,64,128]{2,1,0:T(8,128)(2,1)S(1)} %pad_maximum_fusion.3), channel_id=1, source_target_pairs={{0,3},{1,2},{2,1},{3,0},{4,7},{5,6},{6,5},{7,4},{8,11},{9,10},{10,... | collective-permute-start | bytes 196616 | tf_op jit(solution)/shard_map/ppermute | solution.py:645
  28.8 0.8 %part.7.refs_5_ = f32[512,256]{1,0:T(8,128)S(1)} custom-call(bf16[2,64,128]{2,1,0:T(8,128)(2,1)S(1)} %collective-permute-done.8.refs_0_, bf16[1,256,1024]{2,1,0:T(8,128)(2,1)S(1)} %get-tuple-element.61.refs_1_, f32[2,72,512]{2,1,0:T(8,128)S(1)} %get-tuple-element.62.refs_2_, ...), custom_call_target="tpu_custom_call", output_to_operand_aliasing={{}: (5, {})} | custom-call | flops 1000000000 | tf_op jit(solution)/shard_map/part/pallas_call | solution.py:653
  29.6 0.5 %tables.5 = (bf16[1,256,2048]{2,1,0:T(8,128)(2,1)S(1)}, f32[4,72,512]{2,1,0:T(8,128)S(1)}) custom-call(bf16[4,80,128]{2,1,0:T(8,128)(2,1)S(1)} %slice.9.refs_0_), custom_call_target="tpu_custom_call" | custom-call | flops 500000000 | tf_op jit(solution)/shard_map/tables/pallas_call | solution.py:611
  30.1 0.6 %collective-permute-done.9.refs_0_ = bf16[4,64,128]{2,1,0:T(8,128)(2,1)S(1)} collective-permute-done((bf16[4,64,128]{2,1,0:T(8,128)(2,1)S(1)}, bf16[4,64,128]{2,1,0:T(8,128)(2,1)S(1)}, u32[]{:S(2)}, u32[]{:S(2)}) %collective-permute-start.9) | collective-permute-done | bytes 65568 | tf_op jit(solution)/shard_map/ppermute | solution.py:645
  31.2 1.4 %whole.1.refs_0_ = f32[512,256]{1,0:T(8,128)S(1)} custom-call(bf16[4,64,128]{2,1,0:T(8,128)(2,1)S(1)} %collective-permute-done.9.refs_0_, bf16[1,256,2048]{2,1,0:T(8,128)(2,1)S(1)} %get-tuple-element.41.refs_1_, f32[4,72,512]{2,1,0:T(8,128)S(1)} %get-tuple-element.42.refs_2_, ...), custom_call_target="tpu_custom_call", output_to_operand_aliasing={{}: (5, {})} | custom-call | flops 800000000 | tf_op jit(solution)/shard_map/whole/pallas_call | solution.py:653
  33.3 0.6 %near.3 = (f32[32,128]{1,0:T(8,128)S(1)}, f32[32,128]{1,0:T(8,128)S(1)}) custom-call(bf16[1024,128]{1,0:T(8,128)(2,1)S(1)} %bitcast.16, bf16[4,9,2,128,128]{4,3,2,1,0:T(8,128)(2,1)S(1)} %bitcast.28, s32[4,9]{1,0:T(4,128)S(1)} %bitcast.30), custom_call_target="tpu_custom_call" | custom-call | flops 2000000000 | tf_op jit(solution)/shard_map/near/pallas_call | solution.py:681
  34.3 0.7 %second.1 = (f32[64,128]{1,0:T(8,128)}, f32[4,8]{1,0:T(4,128)}) custom-call(bf16[16,64,128]{2,1,0:T(8,128)(2,1)S(1)} %constant_dynamic-update-slice_fusion.5.refs_1_.refs_0_, f32[32,128]{1,0:T(8,128)S(1)} %get-tuple-element.56.refs_1_, f32[32,128]{1,0:T(8,128)S(1)} %get-tuple-element.57.refs_2_, f32[32,128]{1,0:T(8,128)S(1)} %get-tuple-element.68.refs_3_, ...), custom_call_target="tpu_custom_call" | custom-call | tf_op jit(solution)/shard_map/second/pallas_call | solution.py:717
  (51 shorter events, 5.7 us)
Async XLA Ops:
  1.4 5.1 %collective-permute-start = (bf16[1,80,128]{2,1,0:T(8,128)(2,1)S(1)}, bf16[1,80,128]{2,1,0:T(8,128)(2,1)S(1)}, u32[]{:S(2)}, u32[]{:S(2)}) collective-permute-start(bf16[1,80,128]{2,1,0:T(8,128)(2,1)S(1)} %bitcast.17), channel_id=1, source_target_pairs={{0,9},{1,8},{2,11},{3,10},{4,13},{5,12},{6,15},{7,14},{8,1},{9,0},... | collective-permute-start | bytes 61448 | tf_op jit(solution)/shard_map/ppermute | solution.py:624
  6.5 3.5 %collective-permute-start.2 = (bf16[2,80,128]{2,1,0:T(8,128)(2,1)S(1)}, bf16[2,80,128]{2,1,0:T(8,128)(2,1)S(1)}, u32[]{:S(2)}, u32[]{:S(2)}) collective-permute-start(bf16[2,80,128]{2,1,0:T(8,128)(2,1)S(1)} %pad_maximum_fusion.4.refs_0_), channel_id=1, source_target_pairs={{0,5},{1,4},{2,7},{3,6},{4,1},{5,0},{6,3},{7,2},{8,13},{9,12},{10,... | collective-permute-start | bytes 122888 | tf_op jit(solution)/shard_map/ppermute | solution.py:624
  8.3 1.5 %collective-permute-start.1 = (bf16[80,128]{1,0:T(8,128)(2,1)S(1)}, bf16[80,128]{1,0:T(8,128)(2,1)S(1)}, u32[]{:S(2)}, u32[]{:S(2)}) collective-permute-start(bf16[80,128]{1,0:T(8,128)(2,1)S(1)} %pack.1.refs_0_), channel_id=1, source_target_pairs={{0,1},{1,0},{2,3},{3,2},{4,5},{5,4},{6,7},{7,6},{8,9},{9,8},{10,11... | collective-permute-start | bytes 61448 | tf_op jit(solution)/shard_map/ppermute | solution.py:86
  8.7 3.2 %copy-start.1 = (f32[8,128,128]{2,1,0:T(8,128)S(1)}, f32[8,128,128]{2,1,0:T(8,128)}, u32[]{:S(2)}) copy-start(f32[8,128,128]{2,1,0:T(8,128)} %refs_1_.1) | copy-start | bytes 1572868
  10.1 4.4 %collective-permute-start.3 = (bf16[4,80,128]{2,1,0:T(8,128)(2,1)S(1)}, bf16[4,80,128]{2,1,0:T(8,128)(2,1)S(1)}, u32[]{:S(2)}, u32[]{:S(2)}) collective-permute-start(bf16[4,80,128]{2,1,0:T(8,128)(2,1)S(1)} %pad_maximum_fusion.2), channel_id=1, source_target_pairs={{0,3},{1,2},{2,1},{3,0},{4,7},{5,6},{6,5},{7,4},{8,11},{9,10},{10,... | collective-permute-start | bytes 245768 | tf_op jit(solution)/shard_map/ppermute | solution.py:624
  14.5 2.0 %copy-start = (bf16[1,4,9,2,128,128]{5,4,3,2,1,0:T(8,128)(2,1)S(1)}, bf16[1,4,9,2,128,128]{5,4,3,2,1,0:T(8,128)(2,1)}, u32[]{:S(2)}) copy-start(bf16[1,4,9,2,128,128]{5,4,3,2,1,0:T(8,128)(2,1)} %param.9) | copy-start | bytes 7077892
  14.5 2.0 %copy-start.2 = (s32[1,4,9]{2,1,0:T(4,128)S(1)}, s32[1,4,9]{2,1,0:T(4,128)}, u32[]{:S(2)}) copy-start(s32[1,4,9]{2,1,0:T(4,128)} %param.11) | copy-start | bytes 436
  14.5 2.0 %collective-permute-start.4 = (bf16[8,80,128]{2,1,0:T(8,128)(2,1)S(1)}, bf16[8,80,128]{2,1,0:T(8,128)(2,1)S(1)}, u32[]{:S(2)}, u32[]{:S(2)}) collective-permute-start(bf16[8,80,128]{2,1,0:T(8,128)(2,1)S(1)} %pad_maximum_fusion), channel_id=1, source_target_pairs={{0,1},{1,0},{2,3},{3,2},{4,5},{5,4},{6,7},{7,6},{8,9},{9,8},{10,11... | collective-permute-start | bytes 491528 | tf_op jit(solution)/shard_map/ppermute | solution.py:86
  16.2 2.1 %collective-permute-start.6 = (bf16[512,256]{1,0:T(8,128)(2,1)S(1)}, bf16[512,256]{1,0:T(8,128)(2,1)S(1)}, u32[]{:S(2)}, u32[]{:S(2)}) collective-permute-start(bf16[512,256]{1,0:T(8,128)(2,1)S(1)} %leaving.1), channel_id=1, source_target_pairs={{0,1},{1,0},{2,3},{3,2},{4,5},{5,4},{6,7},{7,6},{8,9},{9,8},{10,11... | collective-permute-start | bytes 786440 | tf_op jit(solution)/shard_map/ppermute | solution.py:86
  17.1 1.6 %collective-permute-start.5 = (f32[32,128]{1,0:T(8,128)S(1)}, f32[32,128]{1,0:T(8,128)S(1)}, u32[]{:S(2)}, u32[]{:S(2)}) collective-permute-start(f32[32,128]{1,0:T(8,128)S(1)} %get-tuple-element.40), channel_id=1, source_target_pairs={{0,1},{1,0},{2,3},{3,2},{4,5},{5,4},{6,7},{7,6},{8,9},{9,8},{10,11... | collective-permute-start | bytes 49160 | tf_op jit(solution)/shard_map/ppermute | solution.py:86
  18.8 4.6 %collective-permute-start.7 = (bf16[1,64,128]{2,1,0:T(8,128)(2,1)S(1)}, bf16[1,64,128]{2,1,0:T(8,128)(2,1)S(1)}, u32[]{:S(2)}, u32[]{:S(2)}) collective-permute-start(bf16[1,64,128]{2,1,0:T(8,128)(2,1)S(1)} %bitcast.22), channel_id=1, source_target_pairs={{0,9},{1,8},{2,11},{3,10},{4,13},{5,12},{6,15},{7,14},{8,1},{9,0},... | collective-permute-start | bytes 49160 | tf_op jit(solution)/shard_map/ppermute | solution.py:645
  22.0 12.2 %collective-permute-start.12 = (f32[32,128]{1,0:T(8,128)S(1)}, f32[32,128]{1,0:T(8,128)S(1)}, u32[]{:S(2)}, u32[]{:S(2)}) collective-permute-start(f32[32,128]{1,0:T(8,128)S(1)} %get-tuple-element.71), channel_id=1, source_target_pairs={{0,1},{1,0},{2,3},{3,2},{4,5},{5,4},{6,7},{7,6},{8,9},{9,8},{10,11... | collective-permute-start | bytes 49160 | tf_op jit(solution)/shard_map/ppermute | solution.py:86
  23.4 3.4 %collective-permute-start.8 = (bf16[2,64,128]{2,1,0:T(8,128)(2,1)S(1)}, bf16[2,64,128]{2,1,0:T(8,128)(2,1)S(1)}, u32[]{:S(2)}, u32[]{:S(2)}) collective-permute-start(bf16[2,64,128]{2,1,0:T(8,128)(2,1)S(1)} %pad_maximum_fusion.6.refs_0_), channel_id=1, source_target_pairs={{0,5},{1,4},{2,7},{3,6},{4,1},{5,0},{6,3},{7,2},{8,13},{9,12},{10,... | collective-permute-start | bytes 98312 | tf_op jit(solution)/shard_map/ppermute | solution.py:645
  26.9 3.9 %collective-permute-start.9 = (bf16[4,64,128]{2,1,0:T(8,128)(2,1)S(1)}, bf16[4,64,128]{2,1,0:T(8,128)(2,1)S(1)}, u32[]{:S(2)}, u32[]{:S(2)}) collective-permute-start(bf16[4,64,128]{2,1,0:T(8,128)(2,1)S(1)} %pad_maximum_fusion.3), channel_id=1, source_target_pairs={{0,3},{1,2},{2,1},{3,0},{4,7},{5,6},{6,5},{7,4},{8,11},{9,10},{10,... | collective-permute-start | bytes 196616 | tf_op jit(solution)/shard_map/ppermute | solution.py:645
  30.8 2.5 %collective-permute-start.10 = (bf16[8,64,128]{2,1,0:T(8,128)(2,1)S(1)}, bf16[8,64,128]{2,1,0:T(8,128)(2,1)S(1)}, u32[]{:S(2)}, u32[]{:S(2)}) collective-permute-start(bf16[8,64,128]{2,1,0:T(8,128)(2,1)S(1)} %pad_maximum_fusion.1), channel_id=1, source_target_pairs={{0,1},{1,0},{2,3},{3,2},{4,5},{5,4},{6,7},{7,6},{8,9},{9,8},{10,11... | collective-permute-start | bytes 393224 | tf_op jit(solution)/shard_map/ppermute | solution.py:86
  33.1 1.2 %collective-permute-start.11 = (f32[32,128]{1,0:T(8,128)S(1)}, f32[32,128]{1,0:T(8,128)S(1)}, u32[]{:S(2)}, u32[]{:S(2)}) collective-permute-start(f32[32,128]{1,0:T(8,128)S(1)} %get-tuple-element.69), channel_id=1, source_target_pairs={{0,1},{1,0},{2,3},{3,2},{4,5},{5,4},{6,7},{7,6},{8,9},{9,8},{10,11... | collective-permute-start | bytes 49160 | tf_op jit(solution)/shard_map/ppermute | solution.py:86

commit v10 on v9

--- a/solution.py
+++ b/solution.py
@@ -14,8 +14,8 @@
 lanes = 128
 mib = 1024 * 1024
 
-sine_terms = (6.283185160087918, -10.3354137577709, 5.100062753380459, -1.1960903419427114, 0.1544402466966843)
-cosine_terms = (0.9999999534659573, -4.93479285858416, 4.058411912342187, -1.331880149557601, 0.21969677520430975)
+sine_terms = (6.2831640439986325, -10.334285583027317, 5.083797977378017, -1.1092722161777626)
+cosine_terms = (0.9999932951314766, -4.933938004239768, 4.041283709560866, -1.2221267509458762)
 
 
 def horner(terms, value):

time: 35.2 us -> 35.1 us (level)
  transfers between devices with their start and end apart: 13 -> 13, of which waited for: 6 -> 6; matrix products, arithmetic and copies ran while one was open for 4% -> 4% of each run, Pallas kernels for 34% -> 33%
where the time goes in v10:
time: 35.1 us; the launch traced here: 34.9 us
  starting transfers between devices  16.1 us (46%)
  Pallas kernels  12.4 us (35%)
  waiting for transfers between devices  3.22 us (9%)
  other arithmetic  1.53 us (4%)
  between operations  0.91 us (3%)
  local copies, waits for them, and re-layouts  0.8 us (2%)
    ppermute x3, starting transfers between devices, gather_and_project(): arrived = lax.ppermute(array, ('tile', 'wave'), pairs)  7.29 us
    ppermute x3, starting transfers between devices, gather_chips(): arrived = lax.ppermute(array, ('tile', 'wave'), pairs)  6.6 us
    pallas_call x4, Pallas kernels, part_call(): call(lambda *refs: part_kernel(layout, base, with_start, not tables, halv...  3.69 us
    pallas_call x3, Pallas kernels, gather_chips(): call(lambda *refs, base=base, start=total is not None: chips_kernel(layou...  2.89 us
    ppermute x3, waiting for transfers between devices, gather_chips(): arrived = lax.ppermute(array, ('tile', 'wave'), pairs)  2.47 us
    ppermute x7, starting transfers between devices, swap_cores(): return lax.ppermute(array, 'wave', [(0, 1), (1, 0)])  2.21 us
    pallas_call x5, Pallas kernels, make(): call(lambda *refs: table_kernel(layout, base, *refs), name, table_shapes(...  1.69 us
    pallas_call x2, Pallas kernels, near_field(): call(lambda *refs: near_kernel(layout, whole, *refs), 'near', tuple([shap...  1.14 us
  transfers between devices with their start and end apart: 13, of which 6 were waited for; matrix products, arithmetic and copies ran while one was open for 4% of the time, Pallas kernels for 33%

profile of v10, /device:TPU:0, one launch (start us, length us, event | category | flops | bytes accessed | tf_op | source)
XLA Modules:
  0.0 34.9 jit_solution(6607745232335304937)
XLA Ops:
  0.6 0.8 %pad_maximum_fusion.5.refs_0_ = f32[72,128]{1,0:T(8,128)S(1)} fusion(f32[8,128]{1,0:T(8,128)} %bitcast.32, f32[64,128]{1,0:T(8,128)} %bitcast.31), kind=kLoop, calls=%fused_computation.5 | loop fusion | flops 9216 | bytes 73728 | tf_op jit(solution)/shard_map/concatenate | solution.py:558
  1.4 3.5 %collective-permute-start = (bf16[1,80,128]{2,1,0:T(8,128)(2,1)S(1)}, bf16[1,80,128]{2,1,0:T(8,128)(2,1)S(1)}, u32[]{:S(2)}, u32[]{:S(2)}) collective-permute-start(bf16[1,80,128]{2,1,0:T(8,128)(2,1)S(1)} %bitcast.17), channel_id=1, source_target_pairs={{0,9},{1,8},{2,11},{3,10},{4,13},{5,12},{6,15},{7,14},{8,1},{9,0},... | collective-permute-start | bytes 61448 | tf_op jit(solution)/shard_map/ppermute | solution.py:624
  5.0 0.7 %pad_bitcast_fusion = s32[1,128]{1,0:T(1,128)S(1)} fusion(s32[8]{0:T(128)} %param.12), kind=kLoop, calls=%fused_computation.18 | loop fusion | bytes 544 | tf_op jit(solution)/shard_map/stack | solution.py:567
  5.6 0.7 %pad_add_fusion.refs_0_ = s32[3,128]{1,0:T(4,128)S(1)} fusion(s32[1,128]{1,0:T(1,128)S(1)} %pad_bitcast_fusion, s32[1,128]{1,0:T(1,128)} %bitcast.33, s32[1,128]{1,0:T(1,128)} %bitcast.34), kind=kLoop, calls=%fused_computation.17 | loop fusion | flops 768 | bytes 3072 | tf_op jit(solution)/shard_map/stack | solution.py:567
  6.5 1.9 %collective-permute-start.2 = (bf16[2,80,128]{2,1,0:T(8,128)(2,1)S(1)}, bf16[2,80,128]{2,1,0:T(8,128)(2,1)S(1)}, u32[]{:S(2)}, u32[]{:S(2)}) collective-permute-start(bf16[2,80,128]{2,1,0:T(8,128)(2,1)S(1)} %pad_maximum_fusion.4.refs_0_), channel_id=1, source_target_pairs={{0,5},{1,4},{2,7},{3,6},{4,1},{5,0},{6,3},{7,2},{8,13},{9,12},{10,... | collective-permute-start | bytes 122888 | tf_op jit(solution)/shard_map/ppermute | solution.py:624
  8.7 1.1 %part.4 = (f32[1024,256]{1,0:T(8,128)S(1)}, bf16[1,256,1024]{2,1,0:T(8,128)(2,1)S(1)}, f32[2,72,512]{2,1,0:T(8,128)S(1)}) custom-call(bf16[2,80,128]{2,1,0:T(8,128)(2,1)S(1)} %pad_maximum_fusion.4.refs_0_), custom_call_target="tpu_custom_call" | custom-call | flops 1000000000 | tf_op jit(solution)/shard_map/part/pallas_call | solution.py:600
  10.0 1.9 %collective-permute-start.3 = (bf16[4,80,128]{2,1,0:T(8,128)(2,1)S(1)}, bf16[4,80,128]{2,1,0:T(8,128)(2,1)S(1)}, u32[]{:S(2)}, u32[]{:S(2)}) collective-permute-start(bf16[4,80,128]{2,1,0:T(8,128)(2,1)S(1)} %pad_maximum_fusion.2), channel_id=1, source_target_pairs={{0,3},{1,2},{2,1},{3,0},{4,7},{5,6},{6,5},{7,4},{8,11},{9,10},{10,... | collective-permute-start | bytes 245768 | tf_op jit(solution)/shard_map/ppermute | solution.py:624
  11.9 1.0 %spectral.1 = (f32[8,128,128]{2,1,0:T(8,128)S(1)}, f32[8,128]{1,0:T(8,128)S(1)}) custom-call(s32[3,128]{1,0:T(4,128)S(1)} %pad_add_fusion.refs_0_, f32[8,128,128]{2,1,0:T(8,128)S(1)} %copy-done.1), custom_call_target="tpu_custom_call" | custom-call | flops 2000000000 | tf_op jit(solution)/shard_map/spectral/pallas_call | solution.py:570
  12.9 1.1 %part.5 = (f32[1024,256]{1,0:T(8,128)S(1)}, bf16[1,256,1024]{2,1,0:T(8,128)(2,1)S(1)}, f32[2,72,512]{2,1,0:T(8,128)S(1)}) custom-call(bf16[2,80,128]{2,1,0:T(8,128)(2,1)S(1)} %collective-permute-done.2.refs_0_, f32[1024,256]{1,0:T(8,128)S(1)} %get-tuple-element.43.refs_1_), custom_call_target="tpu_custom_call", output_to_operand_aliasing={{0}: (1, {})} | custom-call | flops 1000000000 | tf_op jit(solution)/shard_map/part/pallas_call | solution.py:600
  15.4 0.8 %leaving.1 = bf16[512,256]{1,0:T(8,128)(2,1)S(1)} custom-call(bf16[4,80,128]{2,1,0:T(8,128)(2,1)S(1)} %collective-permute-done.3.refs_0_, bf16[1,256,2048]{2,1,0:T(8,128)(2,1)S(1)} %get-tuple-element.41.refs_1_, f32[4,72,512]{2,1,0:T(8,128)S(1)} %get-tuple-element.42.refs_2_, f32[1024,256]{1,0:T(8,128)S(1)} %get-tuple-element.44.refs_3_), custom_call_target="tpu_custom_call" | custom-call | flops 500000000 | tf_op jit(solution)/shard_map/leaving/pallas_call | solution.py:600
  16.5 0.6 %near.2 = (f32[32,128]{1,0:T(8,128)S(1)}, f32[32,128]{1,0:T(8,128)S(1)}) custom-call(bf16[1280,128]{1,0:T(8,128)(2,1)S(1)} %bitcast.21, bf16[4,9,2,128,128]{4,3,2,1,0:T(8,128)(2,1)S(1)} %bitcast.27, s32[4,9]{1,0:T(4,128)S(1)} %bitcast.29), custom_call_target="tpu_custom_call" | custom-call | flops 2000000000 | tf_op jit(solution)/shard_map/near/pallas_call | solution.py:681
  17.4 0.8 %staying.1.refs_1_ = f32[512,256]{1,0:T(8,128)S(1)} custom-call(bf16[4,80,128]{2,1,0:T(8,128)(2,1)S(1)} %collective-permute-done.3.refs_0_, bf16[1,256,2048]{2,1,0:T(8,128)(2,1)S(1)} %get-tuple-element.41.refs_1_, f32[4,72,512]{2,1,0:T(8,128)S(1)} %get-tuple-element.42.refs_2_, f32[1024,256]{1,0:T(8,128)S(1)} %get-tuple-element.44.refs_3_), custom_call_target="tpu_custom_call" | custom-call | flops 800000000 | tf_op jit(solution)/shard_map/staying/pallas_call | solution.py:600
  18.8 3.2 %collective-permute-start.7 = (bf16[1,64,128]{2,1,0:T(8,128)(2,1)S(1)}, bf16[1,64,128]{2,1,0:T(8,128)(2,1)S(1)}, u32[]{:S(2)}, u32[]{:S(2)}) collective-permute-start(bf16[1,64,128]{2,1,0:T(8,128)(2,1)S(1)} %bitcast.22), channel_id=1, source_target_pairs={{0,9},{1,8},{2,11},{3,10},{4,13},{5,12},{6,15},{7,14},{8,1},{9,0},... | collective-permute-start | bytes 49160 | tf_op jit(solution)/shard_map/ppermute | solution.py:645
  22.2 1.3 %collective-permute-done.7 = bf16[1,64,128]{2,1,0:T(8,128)(2,1)S(1)} collective-permute-done((bf16[1,64,128]{2,1,0:T(8,128)(2,1)S(1)}, bf16[1,64,128]{2,1,0:T(8,128)(2,1)S(1)}, u32[]{:S(2)}, u32[]{:S(2)}) %collective-permute-start.7) | collective-permute-done | bytes 16416 | tf_op jit(solution)/shard_map/ppermute | solution.py:645
  23.4 1.8 %collective-permute-start.8 = (bf16[2,64,128]{2,1,0:T(8,128)(2,1)S(1)}, bf16[2,64,128]{2,1,0:T(8,128)(2,1)S(1)}, u32[]{:S(2)}, u32[]{:S(2)}) collective-permute-start(bf16[2,64,128]{2,1,0:T(8,128)(2,1)S(1)} %pad_maximum_fusion.6.refs_0_), channel_id=1, source_target_pairs={{0,5},{1,4},{2,7},{3,6},{4,1},{5,0},{6,3},{7,2},{8,13},{9,12},{10,... | collective-permute-start | bytes 98312 | tf_op jit(solution)/shard_map/ppermute | solution.py:645
  25.5 0.8 %part.6.refs_5_ = f32[512,256]{1,0:T(8,128)S(1)} custom-call(bf16[2,64,128]{2,1,0:T(8,128)(2,1)S(1)} %pad_maximum_fusion.6.refs_0_, bf16[1,256,1024]{2,1,0:T(8,128)(2,1)S(1)} %get-tuple-element.48.refs_3_.refs_1_.refs_2_, f32[2,72,512]{2,1,0:T(8,128)S(1)} %get-tuple-element.49.refs_4_.refs_2_.refs_3_, bf16[1,256,1024]{2,1,0:T(8,128)(2,1)S(1)} %get-tuple-element.66.refs_3_, ...), custom_call_target="tpu_custom_call" | custom-call | flops 1000000000 | tf_op jit(solution)/shard_map/part/pallas_call | solution.py:653
  26.3 0.5 %collective-permute-done.8.refs_0_ = bf16[2,64,128]{2,1,0:T(8,128)(2,1)S(1)} collective-permute-done((bf16[2,64,128]{2,1,0:T(8,128)(2,1)S(1)}, bf16[2,64,128]{2,1,0:T(8,128)(2,1)S(1)}, u32[]{:S(2)}, u32[]{:S(2)}) %collective-permute-start.8) | collective-permute-done | bytes 32800 | tf_op jit(solution)/shard_map/ppermute | solution.py:645
  26.8 1.6 %collective-permute-start.9 = (bf16[4,64,128]{2,1,0:T(8,128)(2,1)S(1)}, bf16[4,64,128]{2,1,0:T(8,128)(2,1)S(1)}, u32[]{:S(2)}, u32[]{:S(2)}) collective-permute-start(bf16[4,64,128]{2,1,0:T(8,128)(2,1)S(1)} %pad_maximum_fusion.3), channel_id=1, source_target_pairs={{0,3},{1,2},{2,1},{3,0},{4,7},{5,6},{6,5},{7,4},{8,11},{9,10},{10,... | collective-permute-start | bytes 196616 | tf_op jit(solution)/shard_map/ppermute | solution.py:645
  28.7 0.8 %part.7.refs_5_ = f32[512,256]{1,0:T(8,128)S(1)} custom-call(bf16[2,64,128]{2,1,0:T(8,128)(2,1)S(1)} %collective-permute-done.8.refs_0_, bf16[1,256,1024]{2,1,0:T(8,128)(2,1)S(1)} %get-tuple-element.61.refs_1_, f32[2,72,512]{2,1,0:T(8,128)S(1)} %get-tuple-element.62.refs_2_, ...), custom_call_target="tpu_custom_call", output_to_operand_aliasing={{}: (5, {})} | custom-call | flops 1000000000 | tf_op jit(solution)/shard_map/part/pallas_call | solution.py:653
  29.5 0.5 %tables.5 = (bf16[1,256,2048]{2,1,0:T(8,128)(2,1)S(1)}, f32[4,72,512]{2,1,0:T(8,128)S(1)}) custom-call(bf16[4,80,128]{2,1,0:T(8,128)(2,1)S(1)} %slice.9.refs_0_), custom_call_target="tpu_custom_call" | custom-call | flops 500000000 | tf_op jit(solution)/shard_map/tables/pallas_call | solution.py:611
  30.1 0.7 %collective-permute-done.9.refs_0_ = bf16[4,64,128]{2,1,0:T(8,128)(2,1)S(1)} collective-permute-done((bf16[4,64,128]{2,1,0:T(8,128)(2,1)S(1)}, bf16[4,64,128]{2,1,0:T(8,128)(2,1)S(1)}, u32[]{:S(2)}, u32[]{:S(2)}) %collective-permute-start.9) | collective-permute-done | bytes 65568 | tf_op jit(solution)/shard_map/ppermute | solution.py:645
  31.2 1.4 %whole.1.refs_0_ = f32[512,256]{1,0:T(8,128)S(1)} custom-call(bf16[4,64,128]{2,1,0:T(8,128)(2,1)S(1)} %collective-permute-done.9.refs_0_, bf16[1,256,2048]{2,1,0:T(8,128)(2,1)S(1)} %get-tuple-element.41.refs_1_, f32[4,72,512]{2,1,0:T(8,128)S(1)} %get-tuple-element.42.refs_2_, ...), custom_call_target="tpu_custom_call", output_to_operand_aliasing={{}: (5, {})} | custom-call | flops 800000000 | tf_op jit(solution)/shard_map/whole/pallas_call | solution.py:653
  33.3 0.6 %near.3 = (f32[32,128]{1,0:T(8,128)S(1)}, f32[32,128]{1,0:T(8,128)S(1)}) custom-call(bf16[1024,128]{1,0:T(8,128)(2,1)S(1)} %bitcast.16, bf16[4,9,2,128,128]{4,3,2,1,0:T(8,128)(2,1)S(1)} %bitcast.28, s32[4,9]{1,0:T(4,128)S(1)} %bitcast.30), custom_call_target="tpu_custom_call" | custom-call | flops 2000000000 | tf_op jit(solution)/shard_map/near/pallas_call | solution.py:681
  34.3 0.7 %second.1 = (f32[64,128]{1,0:T(8,128)}, f32[4,8]{1,0:T(4,128)}) custom-call(bf16[16,64,128]{2,1,0:T(8,128)(2,1)S(1)} %constant_dynamic-update-slice_fusion.5.refs_1_.refs_0_, f32[32,128]{1,0:T(8,128)S(1)} %get-tuple-element.56.refs_1_, f32[32,128]{1,0:T(8,128)S(1)} %get-tuple-element.57.refs_2_, f32[32,128]{1,0:T(8,128)S(1)} %get-tuple-element.68.refs_3_, ...), custom_call_target="tpu_custom_call" | custom-call | tf_op jit(solution)/shard_map/second/pallas_call | solution.py:717
  (51 shorter events, 5.7 us)
Async XLA Ops:
  1.4 5.1 %collective-permute-start = (bf16[1,80,128]{2,1,0:T(8,128)(2,1)S(1)}, bf16[1,80,128]{2,1,0:T(8,128)(2,1)S(1)}, u32[]{:S(2)}, u32[]{:S(2)}) collective-permute-start(bf16[1,80,128]{2,1,0:T(8,128)(2,1)S(1)} %bitcast.17), channel_id=1, source_target_pairs={{0,9},{1,8},{2,11},{3,10},{4,13},{5,12},{6,15},{7,14},{8,1},{9,0},... | collective-permute-start | bytes 61448 | tf_op jit(solution)/shard_map/ppermute | solution.py:624
  6.5 3.5 %collective-permute-start.2 = (bf16[2,80,128]{2,1,0:T(8,128)(2,1)S(1)}, bf16[2,80,128]{2,1,0:T(8,128)(2,1)S(1)}, u32[]{:S(2)}, u32[]{:S(2)}) collective-permute-start(bf16[2,80,128]{2,1,0:T(8,128)(2,1)S(1)} %pad_maximum_fusion.4.refs_0_), channel_id=1, source_target_pairs={{0,5},{1,4},{2,7},{3,6},{4,1},{5,0},{6,3},{7,2},{8,13},{9,12},{10,... | collective-permute-start | bytes 122888 | tf_op jit(solution)/shard_map/ppermute | solution.py:624
  8.3 1.5 %collective-permute-start.1 = (bf16[80,128]{1,0:T(8,128)(2,1)S(1)}, bf16[80,128]{1,0:T(8,128)(2,1)S(1)}, u32[]{:S(2)}, u32[]{:S(2)}) collective-permute-start(bf16[80,128]{1,0:T(8,128)(2,1)S(1)} %pack.1.refs_0_), channel_id=1, source_target_pairs={{0,1},{1,0},{2,3},{3,2},{4,5},{5,4},{6,7},{7,6},{8,9},{9,8},{10,11... | collective-permute-start | bytes 61448 | tf_op jit(solution)/shard_map/ppermute | solution.py:86
  8.7 3.2 %copy-start.1 = (f32[8,128,128]{2,1,0:T(8,128)S(1)}, f32[8,128,128]{2,1,0:T(8,128)}, u32[]{:S(2)}) copy-start(f32[8,128,128]{2,1,0:T(8,128)} %refs_1_.1) | copy-start | bytes 1572868
  10.0 4.4 %collective-permute-start.3 = (bf16[4,80,128]{2,1,0:T(8,128)(2,1)S(1)}, bf16[4,80,128]{2,1,0:T(8,128)(2,1)S(1)}, u32[]{:S(2)}, u32[]{:S(2)}) collective-permute-start(bf16[4,80,128]{2,1,0:T(8,128)(2,1)S(1)} %pad_maximum_fusion.2), channel_id=1, source_target_pairs={{0,3},{1,2},{2,1},{3,0},{4,7},{5,6},{6,5},{7,4},{8,11},{9,10},{10,... | collective-permute-start | bytes 245768 | tf_op jit(solution)/shard_map/ppermute | solution.py:624
  14.5 2.0 %copy-start = (bf16[1,4,9,2,128,128]{5,4,3,2,1,0:T(8,128)(2,1)S(1)}, bf16[1,4,9,2,128,128]{5,4,3,2,1,0:T(8,128)(2,1)}, u32[]{:S(2)}) copy-start(bf16[1,4,9,2,128,128]{5,4,3,2,1,0:T(8,128)(2,1)} %param.9) | copy-start | bytes 7077892
  14.5 2.0 %copy-start.2 = (s32[1,4,9]{2,1,0:T(4,128)S(1)}, s32[1,4,9]{2,1,0:T(4,128)}, u32[]{:S(2)}) copy-start(s32[1,4,9]{2,1,0:T(4,128)} %param.11) | copy-start | bytes 436
  14.5 1.9 %collective-permute-start.4 = (bf16[8,80,128]{2,1,0:T(8,128)(2,1)S(1)}, bf16[8,80,128]{2,1,0:T(8,128)(2,1)S(1)}, u32[]{:S(2)}, u32[]{:S(2)}) collective-permute-start(bf16[8,80,128]{2,1,0:T(8,128)(2,1)S(1)} %pad_maximum_fusion), channel_id=1, source_target_pairs={{0,1},{1,0},{2,3},{3,2},{4,5},{5,4},{6,7},{7,6},{8,9},{9,8},{10,11... | collective-permute-start | bytes 491528 | tf_op jit(solution)/shard_map/ppermute | solution.py:86
  16.2 2.1 %collective-permute-start.6 = (bf16[512,256]{1,0:T(8,128)(2,1)S(1)}, bf16[512,256]{1,0:T(8,128)(2,1)S(1)}, u32[]{:S(2)}, u32[]{:S(2)}) collective-permute-start(bf16[512,256]{1,0:T(8,128)(2,1)S(1)} %leaving.1), channel_id=1, source_target_pairs={{0,1},{1,0},{2,3},{3,2},{4,5},{5,4},{6,7},{7,6},{8,9},{9,8},{10,11... | collective-permute-start | bytes 786440 | tf_op jit(solution)/shard_map/ppermute | solution.py:86
  17.1 1.6 %collective-permute-start.5 = (f32[32,128]{1,0:T(8,128)S(1)}, f32[32,128]{1,0:T(8,128)S(1)}, u32[]{:S(2)}, u32[]{:S(2)}) collective-permute-start(f32[32,128]{1,0:T(8,128)S(1)} %get-tuple-element.40), channel_id=1, source_target_pairs={{0,1},{1,0},{2,3},{3,2},{4,5},{5,4},{6,7},{7,6},{8,9},{9,8},{10,11... | collective-permute-start | bytes 49160 | tf_op jit(solution)/shard_map/ppermute | solution.py:86
  18.8 4.6 %collective-permute-start.7 = (bf16[1,64,128]{2,1,0:T(8,128)(2,1)S(1)}, bf16[1,64,128]{2,1,0:T(8,128)(2,1)S(1)}, u32[]{:S(2)}, u32[]{:S(2)}) collective-permute-start(bf16[1,64,128]{2,1,0:T(8,128)(2,1)S(1)} %bitcast.22), channel_id=1, source_target_pairs={{0,9},{1,8},{2,11},{3,10},{4,13},{5,12},{6,15},{7,14},{8,1},{9,0},... | collective-permute-start | bytes 49160 | tf_op jit(solution)/shard_map/ppermute | solution.py:645
  22.0 12.2 %collective-permute-start.12 = (f32[32,128]{1,0:T(8,128)S(1)}, f32[32,128]{1,0:T(8,128)S(1)}, u32[]{:S(2)}, u32[]{:S(2)}) collective-permute-start(f32[32,128]{1,0:T(8,128)S(1)} %get-tuple-element.71), channel_id=1, source_target_pairs={{0,1},{1,0},{2,3},{3,2},{4,5},{5,4},{6,7},{7,6},{8,9},{9,8},{10,11... | collective-permute-start | bytes 49160 | tf_op jit(solution)/shard_map/ppermute | solution.py:86
  23.4 3.4 %collective-permute-start.8 = (bf16[2,64,128]{2,1,0:T(8,128)(2,1)S(1)}, bf16[2,64,128]{2,1,0:T(8,128)(2,1)S(1)}, u32[]{:S(2)}, u32[]{:S(2)}) collective-permute-start(bf16[2,64,128]{2,1,0:T(8,128)(2,1)S(1)} %pad_maximum_fusion.6.refs_0_), channel_id=1, source_target_pairs={{0,5},{1,4},{2,7},{3,6},{4,1},{5,0},{6,3},{7,2},{8,13},{9,12},{10,... | collective-permute-start | bytes 98312 | tf_op jit(solution)/shard_map/ppermute | solution.py:645
  26.8 3.9 %collective-permute-start.9 = (bf16[4,64,128]{2,1,0:T(8,128)(2,1)S(1)}, bf16[4,64,128]{2,1,0:T(8,128)(2,1)S(1)}, u32[]{:S(2)}, u32[]{:S(2)}) collective-permute-start(bf16[4,64,128]{2,1,0:T(8,128)(2,1)S(1)} %pad_maximum_fusion.3), channel_id=1, source_target_pairs={{0,3},{1,2},{2,1},{3,0},{4,7},{5,6},{6,5},{7,4},{8,11},{9,10},{10,... | collective-permute-start | bytes 196616 | tf_op jit(solution)/shard_map/ppermute | solution.py:645
  30.8 2.5 %collective-permute-start.10 = (bf16[8,64,128]{2,1,0:T(8,128)(2,1)S(1)}, bf16[8,64,128]{2,1,0:T(8,128)(2,1)S(1)}, u32[]{:S(2)}, u32[]{:S(2)}) collective-permute-start(bf16[8,64,128]{2,1,0:T(8,128)(2,1)S(1)} %pad_maximum_fusion.1), channel_id=1, source_target_pairs={{0,1},{1,0},{2,3},{3,2},{4,5},{5,4},{6,7},{7,6},{8,9},{9,8},{10,11... | collective-permute-start | bytes 393224 | tf_op jit(solution)/shard_map/ppermute | solution.py:86
  33.0 1.2 %collective-permute-start.11 = (f32[32,128]{1,0:T(8,128)S(1)}, f32[32,128]{1,0:T(8,128)S(1)}, u32[]{:S(2)}, u32[]{:S(2)}) collective-permute-start(f32[32,128]{1,0:T(8,128)S(1)} %get-tuple-element.69), channel_id=1, source_target_pairs={{0,1},{1,0},{2,3},{3,2},{4,5},{5,4},{6,7},{7,6},{8,9},{9,8},{10,11... | collective-permute-start | bytes 49160 | tf_op jit(solution)/shard_map/ppermute | solution.py:86
